TPU v7x, 32 devices: a whole 2x2x4 slice. The times are simulated.
32 devices in a mesh: groups: 2 (over y), ctx: 4 (over z), head: 4 (over x, core).
Axes of the slice: x: 2, y: 2, z: 4, core: 2. Of those that a mesh axis runs over, the one named last changes fastest.
Arguments:
- doc_lengths: int32 [32], P('groups'), parts along dimension 0, may hold values from 1 to 256, as said below
- owners: int32 [1024], P(('groups', 'ctx')), parts along dimension 0, may hold values from 0 to 3, as said below
- queries: bfloat16 [1024, 2048], P(('groups', 'ctx'), 'head'), parts along dimension 0, may hold values from -7 to 7
- key_head_rows: bfloat16 [1024, 512], P(('groups', 'ctx'), 'head'), parts along dimension 0, may hold values from -6 to 6
- value_head_rows: bfloat16 [1024, 512], P(('groups', 'ctx'), 'head'), parts along dimension 0, may hold values from -5 to 5
- forward_out: bfloat16 [1024, 2048], P(('groups', 'ctx'), 'head'), parts along dimension 0, may hold values from -5 to 5
- grad_out: bfloat16 [1024, 2048], P(('groups', 'ctx'), 'head'), parts along dimension 0, may hold values from -5 to 5
Outputs:
- grad_queries: float32 [1024, 2048], P(('groups', 'ctx'), 'head'), parts along dimension 0
- key_gradient_rows: float32 [1024, 512], P(('groups', 'ctx'), 'head'), parts along dimension 0
- value_gradient_rows: float32 [1024, 512], P(('groups', 'ctx'), 'head'), parts along dimension 0
There are 2 independent parts, one for each index of `groups`. A program takes and returns all parts, laid end to end along the dimension named above; each array names one. Nothing has to cross between parts.
Inputs may be any that keep to these rules, and one draw needn't show every extreme that they name: `doc_lengths`: 16 lengths in sequence order that sum to 512; exactly one document has 256 tokens, all others fewer. Every owner is given exactly 128 tokens. Of the 128 tokens of one device at most 64 go to one owner, and every device gives exactly 64 tokens to some owner. The tokens of one device that go to one owner form one contiguous run, the runs following in the order of the owners.
All inputs are finite; a program needn't handle non-finite values.
Results may differ from a plain program's by a relative error of at most 0.0031.
Values may be sent and summed in bfloat16 or wider, within the bound.
No kernel may reach another device: no remote copies, remote signals or barrier semaphores. Data moves between devices by JAX's collectives and lax.ppermute only.
A program may use at most 64 MiB of HBM per device.

v0:
```python
import math

import jax
import jax.numpy as jnp
from jax import lax
from jax.sharding import PartitionSpec as P

HEAD_WIDTH = 128
GROUP = 4


NEG = -1e30
BLOCK = 512


def shifted(value, axis, by):
    count = lax.axis_size(axis)
    return lax.ppermute(value, axis, [(i, (i + by) % count) for i in range(count)])


def document_of(positions, doc_lengths):
    ends = jnp.cumsum(doc_lengths)
    return jnp.sum((positions[:, None] >= ends[None, :]).astype(jnp.int32), axis=1)


def allowed_between(query_positions, query_docs, key_positions, key_docs):
    return (query_docs[:, None] == key_docs[None, :]) & (
        key_positions[None, :] <= query_positions[:, None]
    )


def head_rows(matrix, group_size, head_dim):
    row_count = matrix.shape[0]
    return matrix.reshape(row_count * group_size, head_dim)


def block_scores(query_flat, key_head, row_count, group_size, head_dim):
    scores = lax.dot_general(
        query_flat, key_head, (((1,), (1,)), ((), ())), preferred_element_type=jnp.float32
    )
    return (scores * (1.0 / math.sqrt(head_dim))).reshape(row_count, group_size, key_head.shape[0])


def update_stats(running, query_local, key_block, allowed, group_size, head_dim):
    running_max, totals = running
    row_count = query_local.shape[0]
    scores = block_scores(
        head_rows(query_local, group_size, head_dim), key_block, row_count, group_size, head_dim
    )
    masked = jnp.where(allowed[:, None, :], scores, NEG)
    new_max = jnp.maximum(running_max, jnp.max(masked, axis=2))
    weights = jnp.where(allowed[:, None, :], jnp.exp(masked - new_max[:, :, None]), 0.0)
    new_totals = [totals * jnp.exp(running_max - new_max) + jnp.sum(weights, axis=2)]
    new_maxima = [new_max]
    return (jnp.concatenate(new_maxima, axis=1), jnp.concatenate(new_totals, axis=1))


def backward_block(
    query_local,
    grad_local,
    log_norm,
    row_delta,
    key_block,
    value_block,
    allowed,
    group_size,
    head_dim,
):
    row_count = query_local.shape[0]
    query_flat = head_rows(query_local, group_size, head_dim)
    grad_flat = head_rows(grad_local, group_size, head_dim)
    scores = block_scores(query_flat, key_block, row_count, group_size, head_dim)
    masked = jnp.where(allowed[:, None, :], scores, NEG)
    weights = jnp.exp(masked - log_norm[:, 0:group_size, None])
    grad_weights = lax.dot_general(
        grad_flat, value_block, (((1,), (1,)), ((), ())), preferred_element_type=jnp.float32
    ).reshape(row_count, group_size, -1)
    grad_scores = weights * (grad_weights - row_delta[:, 0:group_size, None])
    rounded_weights = weights.astype(jnp.bfloat16).reshape(row_count * group_size, -1)
    rounded_grads = grad_scores.astype(jnp.bfloat16).reshape(row_count * group_size, -1)
    value_parts = [
        lax.dot_general(
            rounded_weights, grad_flat, (((0,), (0,)), ((), ())), preferred_element_type=jnp.float32
        )
    ]
    key_parts = [
        lax.dot_general(
            rounded_grads, query_flat, (((0,), (0,)), ((), ())), preferred_element_type=jnp.float32
        )
    ]
    query_parts = [
        jnp.dot(rounded_grads, key_block, preferred_element_type=jnp.float32).reshape(
            row_count, group_size * head_dim
        )
    ]
    return (
        jnp.concatenate(query_parts, axis=1),
        jnp.concatenate(key_parts, axis=1),
        jnp.concatenate(value_parts, axis=1),
    )


def per_device(doc_lengths, owners, queries, key_head_rows, value_head_rows, forward_out, grad_out):
    context_size = lax.axis_size("ctx")
    context_index = lax.axis_index("ctx")
    row_count = queries.shape[0]
    head_dim = HEAD_WIDTH
    group_size = GROUP
    query_heads = queries.shape[1] // head_dim
    slot_count = 2 * row_count // context_size
    everyone = lax.all_gather(owners, "ctx", axis=0, tiled=True)
    row_arrangement = jnp.argsort(everyone, stable=True)
    layout_docs = document_of(row_arrangement, doc_lengths)
    own_positions = lax.dynamic_slice_in_dim(
        row_arrangement, context_index * row_count, row_count, 0
    )
    own_documents = lax.dynamic_slice_in_dim(layout_docs, context_index * row_count, row_count, 0)
    owner_ids = jnp.arange(context_size, dtype=jnp.int32)
    owner_hot = (owners[:, None] == owner_ids[None, :]).astype(jnp.int32)
    earlier = jnp.cumsum(owner_hot, axis=0) - owner_hot
    rank_within = jnp.sum(earlier * owner_hot, axis=1)
    slot_rows = owners * slot_count + rank_within

    def packed(matrix):
        empty = jnp.zeros((context_size * slot_count,) + matrix.shape[1:], matrix.dtype)
        return empty.at[slot_rows].set(matrix)

    owner_grid = everyone.reshape(context_size, row_count)
    counts = jnp.sum((owner_grid == context_index).astype(jnp.int32), axis=1)
    count_ends = jnp.cumsum(counts)
    starts = count_ends - counts
    wanted = jnp.arange(row_count, dtype=jnp.int32)
    source = jnp.sum((wanted[:, None] >= count_ends[None, :]).astype(jnp.int32), axis=1)
    source_hot = (source[:, None] == owner_ids[None, :]).astype(jnp.int32)
    take_rows = source * slot_count + wanted - jnp.sum(source_hot * starts[None, :], axis=1)

    def compact(received):
        return jnp.take(received, take_rows, axis=0)

    local_delta = jnp.sum(
        (grad_out.astype(jnp.float32) * forward_out.astype(jnp.float32)).reshape(
            row_count, query_heads, head_dim
        ),
        axis=2,
    )
    arrived = (
        lax.all_to_all(packed(queries), "ctx", split_axis=0, concat_axis=0, tiled=True),
        lax.all_to_all(packed(key_head_rows), "ctx", split_axis=0, concat_axis=0, tiled=True),
        lax.all_to_all(packed(value_head_rows), "ctx", split_axis=0, concat_axis=0, tiled=True),
        lax.all_to_all(packed(grad_out), "ctx", split_axis=0, concat_axis=0, tiled=True),
    )
    query_local, key_local, value_local, grad_local = [compact(received) for received in arrived]
    row_delta = compact(
        lax.all_to_all(packed(local_delta), "ctx", split_axis=0, concat_axis=0, tiled=True)
    )

    def fold_keys(running, shard_rows, first_row):
        piece_count = shard_rows.shape[0]
        step_rows = math.gcd(piece_count, BLOCK) if piece_count > BLOCK else piece_count

        def one_block(partial_value, block_index):
            offset = first_row + block_index * step_rows
            key_block = lax.dynamic_slice_in_dim(shard_rows, block_index * step_rows, step_rows, 0)
            key_positions = lax.dynamic_slice_in_dim(row_arrangement, offset, step_rows, 0)
            key_docs = lax.dynamic_slice_in_dim(layout_docs, offset, step_rows, 0)
            allowed = allowed_between(own_positions, own_documents, key_positions, key_docs)
            return (
                update_stats(partial_value, query_local, key_block, allowed, group_size, head_dim),
                None,
            )

        if piece_count == step_rows:
            return one_block(running, 0)[0]
        return lax.scan(one_block, running, jnp.arange(piece_count // step_rows, dtype=jnp.int32))[
            0
        ]

    start_stats = (
        jnp.full((row_count, query_heads), NEG, jnp.float32),
        jnp.zeros((row_count, query_heads), jnp.float32),
    )
    top_scores, totals = fold_keys(
        start_stats, lax.all_gather(key_local, "ctx", axis=0, tiled=True), jnp.int32(0)
    )
    log_norm = top_scores + jnp.log(totals)

    def block_meta(owner_index, offset, size):
        first = owner_index * row_count + offset
        key_positions = lax.dynamic_slice_in_dim(row_arrangement, first, size, 0)
        key_docs = lax.dynamic_slice_in_dim(layout_docs, first, size, 0)
        return (key_positions, key_docs)

    query_zero = jnp.zeros(query_local.shape, jnp.float32)
    key_zero = jnp.zeros(key_local.shape, jnp.float32)

    def one_turn(turn_index, loop_state):
        key_moving, value_moving, key_grad, value_grad, query_grad = loop_state
        owner_index = (context_index - turn_index) % context_size
        key_positions, key_docs = block_meta(owner_index, 0, row_count)
        allowed = allowed_between(own_positions, own_documents, key_positions, key_docs)
        query_part, key_part, value_part = backward_block(
            query_local,
            grad_local,
            log_norm,
            row_delta,
            key_moving,
            value_moving,
            allowed,
            group_size,
            head_dim,
        )
        return (
            key_moving,
            value_moving,
            key_grad + key_part,
            value_grad + value_part,
            query_grad + query_part,
        )

    def moved_turn(turn_index, loop_state):
        key_moving, value_moving, key_grad, value_grad, query_grad = loop_state
        key_moving, value_moving = shifted((key_moving, value_moving), "ctx", 1)
        key_grad, value_grad = shifted((key_grad, value_grad), "ctx", 1)
        return one_turn(turn_index, (key_moving, value_moving, key_grad, value_grad, query_grad))

    loop_state = one_turn(0, (key_local, value_local, key_zero, key_zero, query_zero))
    loop_state = lax.fori_loop(1, context_size, moved_turn, loop_state)
    key_grad, value_grad = shifted((loop_state[2], loop_state[3]), "ctx", 1)
    query_grad = loop_state[4]
    inverse_root = 1.0 / math.sqrt(head_dim)
    return (query_grad * inverse_root, key_grad * inverse_root, value_grad)


def solution(mesh):
    return jax.shard_map(
        per_device,
        mesh=mesh,
        in_specs=(
            P("groups"),
            P(("groups", "ctx")),
            P(("groups", "ctx"), "head"),
            P(("groups", "ctx"), "head"),
            P(("groups", "ctx"), "head"),
            P(("groups", "ctx"), "head"),
            P(("groups", "ctx"), "head"),
        ),
        out_specs=(
            P(("groups", "ctx"), "head"),
            P(("groups", "ctx"), "head"),
            P(("groups", "ctx"), "head"),
        ),
        check_vma=False,
    )
```

profile of v0, /device:TPU:0, one launch (start us, length us, event | category | flops | bytes accessed | tf_op | source)
XLA Modules:
  0.0 119.2 jit_solution(11992509436393600767)
XLA Ops:
  4.6 6.3 %all-to-all-start.4 = ((f32[4,1,256]{2,1,0:T(1,128)}), f32[4,1,256]{2,1,0:T(1,128)S(1)}, u32[]{:S(2)}, u32[]{:S(2)}) async-start(f32[4,1,256]{2,1,0:T(1,128)} %reshape.531), calls=%async_computation.4 | async-start | bytes 8192 | tf_op jit(solution)/shard_map/all_to_all | solution.py:154
  10.9 11.3 %all-gather = s32[4,1,128]{2,1,0:T(1,128)S(1)} all-gather(s32[1,1,128]{2,1,0:T(1,128)S(1)} %bitcast.129), channel_id=1, replica_groups=mesh['groups'=2,'ctx'=4,'head'=4] {'ctx'}, dimensions={0}, use_global_device_ids=true | all-gather | bytes 2560 | tf_op jit(solution)/shard_map/all_gather | solution.py:111
  22.4 3.8 %sort.17 = (s32[512]{0:T(512)}, s32[512]{0:T(512)S(1)}) sort(s32[512]{0:T(512)S(1)} %bitcast.128, s32[512]{0:T(512)S(1)} %iota.18), dimensions={0}, to_apply=%region_8.10 | sort | flops 4608 | bytes 8192 | tf_op jit(solution)/shard_map/jit(argsort)/sort | solution.py:112
  27.8 1.7 %scatter_custom_fusion = bf16[256,128]{1,0:T(8,128)(2,1)} fusion(s32[128]{0:T(128)S(1)} %compare_select_fusion.2, bf16[128,128]{1,0:T(8,128)(2,1)} %param.16, bf16[]{:T(256)} %constant.155.clone.1), kind=kCustom, calls=%fused_computation.67 | custom fusion | bytes 66048 | tf_op jit(solution)/shard_map/scatter | solution.py:126
  29.5 3.3 %all-to-all-start = ((bf16[4,64,128]{2,1,0:T(8,128)(2,1)}), bf16[4,64,128]{2,1,0:T(8,128)(2,1)S(1)}, u32[]{:S(2)}, u32[]{:S(2)}) async-start(bf16[4,64,128]{2,1,0:T(8,128)(2,1)} %bitcast.9), calls=%async_computation | async-start | bytes 131072 | tf_op jit(solution)/shard_map/all_to_all | solution.py:148
  32.8 1.7 %scatter_custom_fusion.1 = bf16[256,128]{1,0:T(8,128)(2,1)} fusion(s32[128]{0:T(128)S(1)} %compare_select_fusion.2, bf16[128,128]{1,0:T(8,128)(2,1)} %param.17, bf16[]{:T(256)} %constant.155.clone.1), kind=kCustom, calls=%fused_computation.65 | custom fusion | bytes 66048 | tf_op jit(solution)/shard_map/scatter | solution.py:126
  34.5 4.0 %all-to-all-done = bf16[4,64,128]{2,1,0:T(8,128)(2,1)S(1)} async-done(((bf16[4,64,128]{2,1,0:T(8,128)(2,1)}), bf16[4,64,128]{2,1,0:T(8,128)(2,1)S(1)}, u32[]{:S(2)}, u32[]{:S(2)}) %all-to-all-start) | async-done | bytes 65568 | tf_op jit(solution)/shard_map/all_to_all | solution.py:148
  38.5 3.3 %all-to-all-start.1 = ((bf16[4,64,128]{2,1,0:T(8,128)(2,1)}), bf16[4,64,128]{2,1,0:T(8,128)(2,1)S(1)}, u32[]{:S(2)}, u32[]{:S(2)}) async-start(bf16[4,64,128]{2,1,0:T(8,128)(2,1)} %bitcast.11), calls=%async_computation.1 | async-start | bytes 131072 | tf_op jit(solution)/shard_map/all_to_all | solution.py:149
  41.8 2.1 %scatter_custom_fusion.2 = bf16[256,512]{1,0:T(8,128)(2,1)} fusion(s32[128]{0:T(128)S(1)} %compare_select_fusion.2, bf16[128,512]{1,0:T(8,128)(2,1)} %param.15, bf16[]{:T(256)} %constant.155.clone.1), kind=kCustom, calls=%fused_computation.48 | custom fusion | bytes 262656 | tf_op jit(solution)/shard_map/scatter | solution.py:126
  43.9 3.6 %all-to-all-done.1 = bf16[4,64,128]{2,1,0:T(8,128)(2,1)S(1)} async-done(((bf16[4,64,128]{2,1,0:T(8,128)(2,1)}), bf16[4,64,128]{2,1,0:T(8,128)(2,1)S(1)}, u32[]{:S(2)}, u32[]{:S(2)}) %all-to-all-start.1) | async-done | bytes 65568 | tf_op jit(solution)/shard_map/all_to_all | solution.py:149
  47.5 3.4 %all-to-all-start.2 = ((bf16[4,64,512]{2,1,0:T(8,128)(2,1)}), bf16[4,64,512]{2,1,0:T(8,128)(2,1)S(1)}, u32[]{:S(2)}, u32[]{:S(2)}) async-start(bf16[4,64,512]{2,1,0:T(8,128)(2,1)} %bitcast.14), calls=%async_computation.2 | async-start | bytes 524288 | tf_op jit(solution)/shard_map/all_to_all | solution.py:147
  50.9 1.7 %scatter_custom_fusion.3 = bf16[256,512]{1,0:T(8,128)(2,1)} fusion(s32[128]{0:T(128)S(1)} %compare_select_fusion.2, bf16[128,512]{1,0:T(8,128)(2,1)S(1)} %copy-done.2, bf16[]{:T(256)} %constant.155.clone.1), kind=kCustom, calls=%fused_computation.46 | custom fusion | bytes 262146 | tf_op jit(solution)/shard_map/scatter | solution.py:126
  55.6 2.0 %all-to-all-done.2 = bf16[4,64,512]{2,1,0:T(8,128)(2,1)S(1)} async-done(((bf16[4,64,512]{2,1,0:T(8,128)(2,1)}), bf16[4,64,512]{2,1,0:T(8,128)(2,1)S(1)}, u32[]{:S(2)}, u32[]{:S(2)}) %all-to-all-start.2) | async-done | bytes 262176 | tf_op jit(solution)/shard_map/all_to_all | solution.py:147
  57.6 3.4 %all-to-all-start.3 = ((bf16[4,64,512]{2,1,0:T(8,128)(2,1)}), bf16[4,64,512]{2,1,0:T(8,128)(2,1)S(1)}, u32[]{:S(2)}, u32[]{:S(2)}) async-start(bf16[4,64,512]{2,1,0:T(8,128)(2,1)} %bitcast.17), calls=%async_computation.3 | async-start | bytes 524288 | tf_op jit(solution)/shard_map/all_to_all | solution.py:150
  62.8 13.9 %all_gather.7 = bf16[512,128]{1,0:T(8,128)(2,1)S(1)} all-gather(bf16[128,128]{1,0:T(8,128)(2,1)S(1)} %get-tuple-element.667), channel_id=1, replica_groups=mesh['groups'=2,'ctx'=4,'head'=4] {'ctx'}, dimensions={0}, use_global_device_ids=true | all-gather | bytes 163840 | tf_op jit(solution)/shard_map/all_gather | solution.py:183
  81.4 30.3 %while.24 = (s32[]{:T(128)}, bf16[128,128]{1,0:T(8,128)(2,1)S(1)}, bf16[128,128]{1,0:T(8,128)(2,1)S(1)}, f32[128,128]{1,0:T(8,128)S(1)}, f32[128,128]{1,0:T(8,12...) while((s32[]{:T(128)}, bf16[128,128]{1,0:T(8,128)(2,1)S(1)}, ...), condition=%wide.wide.region_18.21_spmd, body=%wide.wide.region_17.20_spmd.sunk | while | flops 84623360 | bytes 5012004 | solution.py:227
  81.4 1.5 %collective-permute-start = (bf16[128,128]{1,0:T(8,128)(2,1)S(1)}, bf16[128,128]{1,0:T(8,128)(2,1)S(1)}, u32[]{:S(2)}, u32[]{:S(2)}) collective-permute-start(bf16[128,128]{1,0:T(8,128)(2,1)S(1)} %get-tuple-element.691), channel_id=1, source_target_pairs={{0,4},{4,8},{8,12},{12,0},{1,5},{5,9},{9,13},{13,1},{2,6},{6,10},{... | collective-permute-start | bytes 98312 | tf_op jit(solution)/shard_map/while/body/eval_jaxpr/ppermute | solution.py:18
  82.9 2.9 %collective-permute-start.3 = (f32[128,128]{1,0:T(8,128)S(1)}, f32[128,128]{1,0:T(8,128)S(1)}, u32[]{:S(2)}, u32[]{:S(2)}) collective-permute-start(f32[128,128]{1,0:T(8,128)S(1)} %get-tuple-element.694), channel_id=1, source_target_pairs={{0,4},{4,8},{8,12},{12,0},{1,5},{5,9},{9,13},{13,1},{2,6},{6,10},{... | collective-permute-start | bytes 196616 | tf_op jit(solution)/shard_map/while/body/eval_jaxpr/ppermute | solution.py:18
  89.5 2.5 %collective-permute-done.2 = f32[128,128]{1,0:T(8,128)S(1)} collective-permute-done((f32[128,128]{1,0:T(8,128)S(1)}, f32[128,128]{1,0:T(8,128)S(1)}, u32[]{:S(2)}, u32[]{:S(2)}) %collective-permute-start.2) | collective-permute-done | bytes 65568 | tf_op jit(solution)/shard_map/while/body/eval_jaxpr/ppermute | solution.py:18
  93.5 4.1 %collective-permute-start.2 = (f32[128,128]{1,0:T(8,128)S(1)}, f32[128,128]{1,0:T(8,128)S(1)}, u32[]{:S(2)}, u32[]{:S(2)}) collective-permute-start(f32[128,128]{1,0:T(8,128)S(1)} %get-tuple-element.693), channel_id=1, source_target_pairs={{0,4},{4,8},{8,12},{12,0},{1,5},{5,9},{9,13},{13,1},{2,6},{6,10},{... | collective-permute-start | bytes 196616 | tf_op jit(solution)/shard_map/while/body/eval_jaxpr/ppermute | solution.py:18
  100.8 2.5 %collective-permute-start = (bf16[128,128]{1,0:T(8,128)(2,1)S(1)}, bf16[128,128]{1,0:T(8,128)(2,1)S(1)}, u32[]{:S(2)}, u32[]{:S(2)}) collective-permute-start(bf16[128,128]{1,0:T(8,128)(2,1)S(1)} %get-tuple-element.691), channel_id=1, source_target_pairs={{0,4},{4,8},{8,12},{12,0},{1,5},{5,9},{9,13},{13,1},{2,6},{6,10},{... | collective-permute-start | bytes 98312 | tf_op jit(solution)/shard_map/while/body/eval_jaxpr/ppermute | solution.py:18
  106.7 2.2 %collective-permute-done.1 = bf16[128,128]{1,0:T(8,128)(2,1)S(1)} collective-permute-done((bf16[128,128]{1,0:T(8,128)(2,1)S(1)}, bf16[128,128]{1,0:T(8,128)(2,1)S(1)}, u32[]{:S(2)}, u32[]{:S(2)}) %collective-permute-start.1) | collective-permute-done | bytes 32800 | tf_op jit(solution)/shard_map/while/body/eval_jaxpr/ppermute | solution.py:18
  109.6 1.5 %collective-permute-done.2 = f32[128,128]{1,0:T(8,128)S(1)} collective-permute-done((f32[128,128]{1,0:T(8,128)S(1)}, f32[128,128]{1,0:T(8,128)S(1)}, u32[]{:S(2)}, u32[]{:S(2)}) %collective-permute-start.2) | collective-permute-done | bytes 65568 | tf_op jit(solution)/shard_map/while/body/eval_jaxpr/ppermute | solution.py:18
  113.9 3.9 %collective-permute-done.4 = f32[128,128]{1,0:T(8,128)S(1)} collective-permute-done((f32[128,128]{1,0:T(8,128)S(1)}, f32[128,128]{1,0:T(8,128)S(1)}, u32[]{:S(2)}, u32[]{:S(2)}) %collective-permute-start.4) | collective-permute-done | bytes 65568 | tf_op jit(solution)/shard_map/ppermute | solution.py:18
  (144 shorter events, 31.3 us)
Async XLA Ops:
  0.6 1.9 %copy-start.2 = (bf16[128,512]{1,0:T(8,128)(2,1)S(1)}, bf16[128,512]{1,0:T(8,128)(2,1)}, u32[]{:S(2)}) copy-start(bf16[128,512]{1,0:T(8,128)(2,1)} %param.19) | copy-start | bytes 393220
  0.6 1.9 %copy-start.1 = (bf16[128,512]{1,0:T(8,128)(2,1)S(1)}, bf16[128,512]{1,0:T(8,128)(2,1)}, u32[]{:S(2)}) copy-start(bf16[128,512]{1,0:T(8,128)(2,1)} %param.18) | copy-start | bytes 393220
  1.6 0.9 copy-start.3
  4.6 24.9 %all-to-all-start.4 = ((f32[4,1,256]{2,1,0:T(1,128)}), f32[4,1,256]{2,1,0:T(1,128)S(1)}, u32[]{:S(2)}, u32[]{:S(2)}) async-start(f32[4,1,256]{2,1,0:T(1,128)} %reshape.531), calls=%async_computation.4 | async-start | bytes 8192 | tf_op jit(solution)/shard_map/all_to_all | solution.py:154
  26.1 0.7 copy-start.4
  29.5 9.0 %all-to-all-start = ((bf16[4,64,128]{2,1,0:T(8,128)(2,1)}), bf16[4,64,128]{2,1,0:T(8,128)(2,1)S(1)}, u32[]{:S(2)}, u32[]{:S(2)}) async-start(bf16[4,64,128]{2,1,0:T(8,128)(2,1)} %bitcast.9), calls=%async_computation | async-start | bytes 131072 | tf_op jit(solution)/shard_map/all_to_all | solution.py:148
  38.5 9.0 %all-to-all-start.1 = ((bf16[4,64,128]{2,1,0:T(8,128)(2,1)}), bf16[4,64,128]{2,1,0:T(8,128)(2,1)S(1)}, u32[]{:S(2)}, u32[]{:S(2)}) async-start(bf16[4,64,128]{2,1,0:T(8,128)(2,1)} %bitcast.11), calls=%async_computation.1 | async-start | bytes 131072 | tf_op jit(solution)/shard_map/all_to_all | solution.py:149
  47.5 10.2 %all-to-all-start.2 = ((bf16[4,64,512]{2,1,0:T(8,128)(2,1)}), bf16[4,64,512]{2,1,0:T(8,128)(2,1)S(1)}, u32[]{:S(2)}, u32[]{:S(2)}) async-start(bf16[4,64,512]{2,1,0:T(8,128)(2,1)} %bitcast.14), calls=%async_computation.2 | async-start | bytes 524288 | tf_op jit(solution)/shard_map/all_to_all | solution.py:147
  57.6 19.9 %all-to-all-start.3 = ((bf16[4,64,512]{2,1,0:T(8,128)(2,1)}), bf16[4,64,512]{2,1,0:T(8,128)(2,1)S(1)}, u32[]{:S(2)}, u32[]{:S(2)}) async-start(bf16[4,64,512]{2,1,0:T(8,128)(2,1)} %bitcast.17), calls=%async_computation.3 | async-start | bytes 524288 | tf_op jit(solution)/shard_map/all_to_all | solution.py:150
  78.5 2.3 %copy-start = (bf16[128,512]{1,0:T(8,128)(2,1)}, bf16[128,512]{1,0:T(8,128)(2,1)S(1)}, u32[]{:S(2)}) copy-start(bf16[128,512]{1,0:T(8,128)(2,1)S(1)} %get-tuple-element.677) | copy-start | bytes 393220
  81.4 6.1 %collective-permute-start = (bf16[128,128]{1,0:T(8,128)(2,1)S(1)}, bf16[128,128]{1,0:T(8,128)(2,1)S(1)}, u32[]{:S(2)}, u32[]{:S(2)}) collective-permute-start(bf16[128,128]{1,0:T(8,128)(2,1)S(1)} %get-tuple-element.691), channel_id=1, source_target_pairs={{0,4},{4,8},{8,12},{12,0},{1,5},{5,9},{9,13},{13,1},{2,6},{6,10},{... | collective-permute-start | bytes 98312 | tf_op jit(solution)/shard_map/while/body/eval_jaxpr/ppermute | solution.py:18
  82.9 5.9 %collective-permute-start.1 = (bf16[128,128]{1,0:T(8,128)(2,1)S(1)}, bf16[128,128]{1,0:T(8,128)(2,1)S(1)}, u32[]{:S(2)}, u32[]{:S(2)}) collective-permute-start(bf16[128,128]{1,0:T(8,128)(2,1)S(1)} %get-tuple-element.692), channel_id=1, source_target_pairs={{0,4},{4,8},{8,12},{12,0},{1,5},{5,9},{9,13},{13,1},{2,6},{6,10},{... | collective-permute-start | bytes 98312 | tf_op jit(solution)/shard_map/while/body/eval_jaxpr/ppermute | solution.py:18
  82.9 9.2 %collective-permute-start.3 = (f32[128,128]{1,0:T(8,128)S(1)}, f32[128,128]{1,0:T(8,128)S(1)}, u32[]{:S(2)}, u32[]{:S(2)}) collective-permute-start(f32[128,128]{1,0:T(8,128)S(1)} %get-tuple-element.694), channel_id=1, source_target_pairs={{0,4},{4,8},{8,12},{12,0},{1,5},{5,9},{9,13},{13,1},{2,6},{6,10},{... | collective-permute-start | bytes 196616 | tf_op jit(solution)/shard_map/while/body/eval_jaxpr/ppermute | solution.py:18
  85.9 6.1 %collective-permute-start.2 = (f32[128,128]{1,0:T(8,128)S(1)}, f32[128,128]{1,0:T(8,128)S(1)}, u32[]{:S(2)}, u32[]{:S(2)}) collective-permute-start(f32[128,128]{1,0:T(8,128)S(1)} %get-tuple-element.693), channel_id=1, source_target_pairs={{0,4},{4,8},{8,12},{12,0},{1,5},{5,9},{9,13},{13,1},{2,6},{6,10},{... | collective-permute-start | bytes 196616 | tf_op jit(solution)/shard_map/while/body/eval_jaxpr/ppermute | solution.py:18
  92.6 5.8 %collective-permute-start = (bf16[128,128]{1,0:T(8,128)(2,1)S(1)}, bf16[128,128]{1,0:T(8,128)(2,1)S(1)}, u32[]{:S(2)}, u32[]{:S(2)}) collective-permute-start(bf16[128,128]{1,0:T(8,128)(2,1)S(1)} %get-tuple-element.691), channel_id=1, source_target_pairs={{0,4},{4,8},{8,12},{12,0},{1,5},{5,9},{9,13},{13,1},{2,6},{6,10},{... | collective-permute-start | bytes 98312 | tf_op jit(solution)/shard_map/while/body/eval_jaxpr/ppermute | solution.py:18
  92.6 6.0 %collective-permute-start.1 = (bf16[128,128]{1,0:T(8,128)(2,1)S(1)}, bf16[128,128]{1,0:T(8,128)(2,1)S(1)}, u32[]{:S(2)}, u32[]{:S(2)}) collective-permute-start(bf16[128,128]{1,0:T(8,128)(2,1)S(1)} %get-tuple-element.692), channel_id=1, source_target_pairs={{0,4},{4,8},{8,12},{12,0},{1,5},{5,9},{9,13},{13,1},{2,6},{6,10},{... | collective-permute-start | bytes 98312 | tf_op jit(solution)/shard_map/while/body/eval_jaxpr/ppermute | solution.py:18
  92.8 7.5 %collective-permute-start.3 = (f32[128,128]{1,0:T(8,128)S(1)}, f32[128,128]{1,0:T(8,128)S(1)}, u32[]{:S(2)}, u32[]{:S(2)}) collective-permute-start(f32[128,128]{1,0:T(8,128)S(1)} %get-tuple-element.694), channel_id=1, source_target_pairs={{0,4},{4,8},{8,12},{12,0},{1,5},{5,9},{9,13},{13,1},{2,6},{6,10},{... | collective-permute-start | bytes 196616 | tf_op jit(solution)/shard_map/while/body/eval_jaxpr/ppermute | solution.py:18
  93.5 6.6 %collective-permute-start.2 = (f32[128,128]{1,0:T(8,128)S(1)}, f32[128,128]{1,0:T(8,128)S(1)}, u32[]{:S(2)}, u32[]{:S(2)}) collective-permute-start(f32[128,128]{1,0:T(8,128)S(1)} %get-tuple-element.693), channel_id=1, source_target_pairs={{0,4},{4,8},{8,12},{12,0},{1,5},{5,9},{9,13},{13,1},{2,6},{6,10},{... | collective-permute-start | bytes 196616 | tf_op jit(solution)/shard_map/while/body/eval_jaxpr/ppermute | solution.py:18
  100.8 5.8 %collective-permute-start = (bf16[128,128]{1,0:T(8,128)(2,1)S(1)}, bf16[128,128]{1,0:T(8,128)(2,1)S(1)}, u32[]{:S(2)}, u32[]{:S(2)}) collective-permute-start(bf16[128,128]{1,0:T(8,128)(2,1)S(1)} %get-tuple-element.691), channel_id=1, source_target_pairs={{0,4},{4,8},{8,12},{12,0},{1,5},{5,9},{9,13},{13,1},{2,6},{6,10},{... | collective-permute-start | bytes 98312 | tf_op jit(solution)/shard_map/while/body/eval_jaxpr/ppermute | solution.py:18
  103.2 5.7 %collective-permute-start.1 = (bf16[128,128]{1,0:T(8,128)(2,1)S(1)}, bf16[128,128]{1,0:T(8,128)(2,1)S(1)}, u32[]{:S(2)}, u32[]{:S(2)}) collective-permute-start(bf16[128,128]{1,0:T(8,128)(2,1)S(1)} %get-tuple-element.692), channel_id=1, source_target_pairs={{0,4},{4,8},{8,12},{12,0},{1,5},{5,9},{9,13},{13,1},{2,6},{6,10},{... | collective-permute-start | bytes 98312 | tf_op jit(solution)/shard_map/while/body/eval_jaxpr/ppermute | solution.py:18
  104.3 7.0 %collective-permute-start.3 = (f32[128,128]{1,0:T(8,128)S(1)}, f32[128,128]{1,0:T(8,128)S(1)}, u32[]{:S(2)}, u32[]{:S(2)}) collective-permute-start(f32[128,128]{1,0:T(8,128)S(1)} %get-tuple-element.694), channel_id=1, source_target_pairs={{0,4},{4,8},{8,12},{12,0},{1,5},{5,9},{9,13},{13,1},{2,6},{6,10},{... | collective-permute-start | bytes 196616 | tf_op jit(solution)/shard_map/while/body/eval_jaxpr/ppermute | solution.py:18
  104.4 6.7 %collective-permute-start.2 = (f32[128,128]{1,0:T(8,128)S(1)}, f32[128,128]{1,0:T(8,128)S(1)}, u32[]{:S(2)}, u32[]{:S(2)}) collective-permute-start(f32[128,128]{1,0:T(8,128)S(1)} %get-tuple-element.693), channel_id=1, source_target_pairs={{0,4},{4,8},{8,12},{12,0},{1,5},{5,9},{9,13},{13,1},{2,6},{6,10},{... | collective-permute-start | bytes 196616 | tf_op jit(solution)/shard_map/while/body/eval_jaxpr/ppermute | solution.py:18
  111.7 6.1 %collective-permute-start.4 = (f32[128,128]{1,0:T(8,128)S(1)}, f32[128,128]{1,0:T(8,128)S(1)}, u32[]{:S(2)}, u32[]{:S(2)}) collective-permute-start(f32[128,128]{1,0:T(8,128)S(1)} %get-tuple-element.363), channel_id=1, source_target_pairs={{0,4},{4,8},{8,12},{12,0},{1,5},{5,9},{9,13},{13,1},{2,6},{6,10},{... | collective-permute-start | bytes 196616 | tf_op jit(solution)/shard_map/ppermute | solution.py:18
  112.5 6.1 %collective-permute-start.5 = (f32[128,128]{1,0:T(8,128)S(1)}, f32[128,128]{1,0:T(8,128)S(1)}, u32[]{:S(2)}, u32[]{:S(2)}) collective-permute-start(f32[128,128]{1,0:T(8,128)S(1)} %get-tuple-element.364), channel_id=1, source_target_pairs={{0,4},{4,8},{8,12},{12,0},{1,5},{5,9},{9,13},{13,1},{2,6},{6,10},{... | collective-permute-start | bytes 196616 | tf_op jit(solution)/shard_map/ppermute | solution.py:18
where the time goes:
time: 120 us; the launch traced here: 119 us
  starting transfers between devices  36.2 us (30%)
  blocking collectives  25.2 us (21%)
  waiting for transfers between devices  23.5 us (20%)
  local copies, waits for them, and re-layouts  18.1 us (15%)
  other arithmetic  10 us (8%)
  matrix products  4.84 us (4%)
    ppermute x14, starting transfers between devices, shifted(): lax.ppermute(value, axis, [(i, (i + by) % count) for i in range(count)])  16.4 us
    all_gather x1, blocking collectives, per_device(): lax.all_gather(key_local, 'ctx', axis=0, tiled=True)  13.9 us
    ppermute x14, waiting for transfers between devices, shifted(): lax.ppermute(value, axis, [(i, (i + by) % count) for i in range(count)])  13.9 us
    all_gather x1, blocking collectives, per_device(): everyone = lax.all_gather(owners, 'ctx', axis=0, tiled=True)  11.3 us
    scatter x5, local copies, waits for them, and re-layouts, packed(): return empty.at[slot_rows].set(matrix)  8.14 us
    all_to_all x1, starting transfers between devices, per_device(): lax.all_to_all(packed(local_delta), 'ctx', split_axis=0, concat_axis=0, t...  6.32 us
    all_to_all x1, waiting for transfers between devices, per_device(): lax.all_to_all(packed(key_head_rows), 'ctx', split_axis=0, concat_axis=0,...  4 us
    gather x5, local copies, waits for them, and re-layouts, compact(): return jnp.take(received, take_rows, axis=0)  3.78 us
  transfers between devices with their start and end apart: 19, of which 14 were waited for; matrix products, arithmetic and copies ran while one was open for 19% of the time, Pallas kernels for 0%

commit v1 on v0

--- a/solution.py
+++ b/solution.py
@@ -1,8 +1,11 @@
+import functools
 import math
 
 import jax
 import jax.numpy as jnp
 from jax import lax
+from jax.experimental import pallas as pl
+from jax.experimental.pallas import tpu as pltpu
 from jax.sharding import PartitionSpec as P
 
 HEAD_WIDTH = 128
@@ -100,7 +103,7 @@
     )
 
 
-def per_device(doc_lengths, owners, queries, key_head_rows, value_head_rows, forward_out, grad_out):
+def ring_plan(doc_lengths, owners, queries, key_head_rows, value_head_rows, forward_out, grad_out):
     context_size = lax.axis_size("ctx")
     context_index = lax.axis_index("ctx")
     row_count = queries.shape[0]
@@ -231,6 +234,204 @@
     return (query_grad * inverse_root, key_grad * inverse_root, value_grad)
 
 
+META = 16
+
+
+def contract(left, right, left_dim, right_dim, **kw):
+    return lax.dot_general(
+        left,
+        right,
+        (((left_dim,), (right_dim,)), ((), ())),
+        preferred_element_type=jnp.float32,
+        **kw,
+    )
+
+
+def attend_kernel(count, halo, docs, *refs):
+    doc_ref, owner_ref, query_ref, grad_ref, saved_ref, key_ref, value_ref = refs[:7]
+    near = refs[7 : 7 + halo]
+    outs = refs[7 + halo :]
+    rows, width = query_ref.shape
+    depth = key_ref.shape[1]
+    heads = width // depth
+    slot = 2 * rows // count
+    scale = 1.0 / math.sqrt(depth)
+    index = lax.axis_index("ctx")
+    lane = lax.broadcasted_iota(jnp.int32, (1, rows), 1)
+
+    def stacked(ref):
+        return jnp.concatenate([ref[:, h * depth : (h + 1) * depth] for h in range(heads)], axis=0)
+
+    position = index * rows + lane
+    first = jnp.zeros((1, rows), jnp.int32)
+    end = jnp.int32(0)
+    for d in range(docs):
+        end = end + doc_ref[d]
+        first = jnp.where(end <= position, end, first)
+    key_rows = (halo + 1) * rows
+    key_position = (index - halo) * rows + lax.broadcasted_iota(jnp.int32, (key_rows, rows), 0)
+    allowed = (key_position >= first) & (key_position <= position)
+    allowed = jnp.concatenate([allowed] * heads, axis=1)
+
+    keys = jnp.concatenate([n[0:rows, :] for n in near[::-1]] + [key_ref[...]], axis=0)
+    values = jnp.concatenate([n[rows : 2 * rows, :] for n in near[::-1]] + [value_ref[...]], axis=0)
+    queries = stacked(query_ref)
+    grads = stacked(grad_ref)
+    product = grads.astype(jnp.float32) * stacked(saved_ref).astype(jnp.float32)
+    delta = contract(
+        jnp.ones((8, depth), jnp.float32), product, 1, 1, precision=lax.Precision.HIGHEST
+    )[0:1, :]
+    scores = jnp.where(allowed, contract(keys, queries, 1, 1) * scale, NEG)
+    raised = jnp.exp(scores - jnp.max(scores, axis=0, keepdims=True))
+    weights = raised * (1.0 / jnp.sum(raised, axis=0, keepdims=True))
+    grad_scores = weights * (contract(values, grads, 1, 1) - delta)
+    weights = weights.astype(jnp.bfloat16)
+    grad_scores = grad_scores.astype(jnp.bfloat16)
+    value_parts = contract(weights, grads, 1, 0).astype(jnp.bfloat16)
+    key_parts = (contract(grad_scores, queries, 1, 0) * scale).astype(jnp.bfloat16)
+    query_grad = (contract(keys, grad_scores, 0, 0) * scale).astype(jnp.bfloat16)
+
+    def by_owner(owner):
+        counts = [
+            jnp.sum(jnp.where(owner == p, 1.0, 0.0), axis=1, keepdims=True) for p in range(count)
+        ]
+        before = jnp.zeros((1, rows), jnp.float32)
+        for p in range(count - 1):
+            before = before + jnp.where(owner > p, counts[p], 0.0)
+        ahead = lax.rem(owner - index + count, count)
+        target = ahead * slot + lane - before.astype(jnp.int32)
+        places = lax.broadcasted_iota(jnp.int32, (count * slot, rows), 0)
+        return counts, jnp.where(places == target, 1.0, 0.0).astype(jnp.bfloat16)
+
+    counts, spread = by_owner(owner_ref[...])
+    tall = jnp.concatenate(
+        [query_grad[:, h * rows : (h + 1) * rows] for h in range(heads)], axis=0
+    )
+    query_slots = contract(spread, tall, 1, 1).astype(jnp.bfloat16)
+    pieces = [query_slots[:, h * depth : (h + 1) * depth] for h in range(heads)]
+    for back in range(halo + 1):
+        if back:
+            owner = near[back - 1][2 * rows : 2 * rows + 1, :].astype(jnp.int32)
+            _, spread = by_owner(owner)
+        at = slice((halo - back) * rows, (halo - back + 1) * rows)
+        pieces.append(contract(spread, key_parts[at, :], 1, 0).astype(jnp.bfloat16))
+        pieces.append(contract(spread, value_parts[at, :], 1, 0).astype(jnp.bfloat16))
+    for ahead in range(count):
+        owner = lax.rem(index + ahead, count)
+        for n, piece in enumerate(pieces):
+            outs[ahead][n * slot : (n + 1) * slot, :] = piece[ahead * slot : (ahead + 1) * slot, :]
+        given = jnp.zeros((1, 1), jnp.float32)
+        for p in range(count):
+            given = jnp.where(owner == p, counts[p], given)
+        outs[ahead][len(pieces) * slot :, :] = jnp.broadcast_to(given, (META, depth)).astype(
+            jnp.bfloat16
+        )
+
+
+def place_kernel(count, halo, *refs):
+    ins = refs[:count]
+    query_out, key_out, value_out = refs[count:]
+    rows, width = query_out.shape
+    depth = key_out.shape[1]
+    heads = width // depth
+    slot = 2 * rows // count
+    index = lax.axis_index("ctx")
+    pieces = heads + 2 * (halo + 1)
+    source = [lax.rem(index - k + count, count) for k in range(count)]
+    given = [
+        ins[k][pieces * slot : pieces * slot + 1, 0:1].astype(jnp.float32).astype(jnp.int32)
+        for k in range(count)
+    ]
+    lane = lax.broadcasted_iota(jnp.int32, (1, count * slot), 1)
+    target = jnp.full((1, count * slot), -1, jnp.int32)
+    for k in range(count):
+        before = jnp.zeros((1, 1), jnp.int32)
+        for other in range(count):
+            before = before + jnp.where(source[other] < source[k], given[other], 0)
+        step = lane - k * slot
+        inside = (step >= 0) & (step < given[k])
+        target = jnp.where(inside, before + step, target)
+    places = lax.broadcasted_iota(jnp.int32, (rows, count * slot), 0)
+    spread = jnp.where(places == target, 1.0, 0.0).astype(jnp.bfloat16)
+
+    def gathered(piece, back):
+        return jnp.concatenate(
+            [
+                ins[(k - back) % count][piece * slot : (piece + 1) * slot, :]
+                for k in range(count)
+            ],
+            axis=0,
+        )
+
+    for h in range(heads):
+        query_out[:, h * depth : (h + 1) * depth] = contract(spread, gathered(h, 0), 1, 0)
+    for n, out in enumerate((key_out, value_out)):
+        total = contract(spread, gathered(heads + n, 0), 1, 0)
+        for back in range(1, halo + 1):
+            total = total + contract(spread, gathered(heads + 2 * back + n, back), 1, 0)
+        out[...] = total
+
+
+def near_plan(doc_lengths, owners, queries, key_head_rows, value_head_rows, forward_out, grad_out):
+    count = lax.axis_size("ctx")
+    rows, width = queries.shape
+    depth = key_head_rows.shape[1]
+    halo = count // 2
+    slot = 2 * rows // count
+    pieces = width // depth + 2 * (halo + 1)
+    whole = pl.BlockSpec(memory_space=pltpu.VMEM)
+    params = pltpu.CompilerParams(vmem_limit_bytes=40 * 1024 * 1024)
+    packet = jnp.concatenate(
+        [
+            key_head_rows,
+            value_head_rows,
+            jnp.broadcast_to(owners.astype(jnp.bfloat16)[None, :], (META, rows)),
+        ],
+        axis=0,
+    )
+    near = [
+        lax.ppermute(packet, "ctx", [(i, i + back) for i in range(count - back)])
+        for back in range(1, halo + 1)
+    ]
+    sent = pl.pallas_call(
+        functools.partial(attend_kernel, count, halo, doc_lengths.shape[0]),
+        out_shape=[jax.ShapeDtypeStruct((pieces * slot + META, depth), jnp.bfloat16)] * count,
+        in_specs=[pl.BlockSpec(memory_space=pltpu.SMEM)] + [whole] * (6 + halo),
+        out_specs=[whole] * count,
+        compiler_params=params,
+    )(
+        doc_lengths,
+        owners.reshape(1, rows),
+        queries,
+        grad_out,
+        forward_out,
+        key_head_rows,
+        value_head_rows,
+        *near,
+    )
+    received = [sent[0]] + [
+        lax.ppermute(sent[k], "ctx", [(i, (i + k) % count) for i in range(count)])
+        for k in range(1, count)
+    ]
+    return pl.pallas_call(
+        functools.partial(place_kernel, count, halo),
+        out_shape=[
+            jax.ShapeDtypeStruct((rows, width), jnp.float32),
+            jax.ShapeDtypeStruct((rows, depth), jnp.float32),
+            jax.ShapeDtypeStruct((rows, depth), jnp.float32),
+        ],
+        in_specs=[whole] * count,
+        out_specs=[whole] * 3,
+        compiler_params=params,
+    )(*received)
+
+
+def per_device(*args):
+    if lax.axis_size("ctx") <= 4:
+        return near_plan(*args)
+    return ring_plan(*args)
+
+
 def solution(mesh):
     return jax.shard_map(
         per_device,

time: 120 us -> 34.8 us (0.29)
  the two profiles are of different devices: /device:TPU:0 before, /device:TPU:8 now
where the time goes in v1:
time: 34.8 us; the launch traced here: 34.5 us
  waiting for transfers between devices  17.4 us (50%)
  starting transfers between devices  9.11 us (26%)
  Pallas kernels  3 us (9%)
  local copies, waits for them, and re-layouts  2.73 us (8%)
  other arithmetic  1.5 us (4%)
  between operations  0.69 us (2%)
    ppermute x3, waiting for transfers between devices, near_plan(): lax.ppermute(sent[k], 'ctx', [(i, (i + k) % count) for i in range(count)])  13.2 us
    ppermute x2, starting transfers between devices, near_plan(): lax.ppermute(packet, 'ctx', [(i, i + back) for i in range(count - back)])  6.55 us
    ppermute x2, waiting for transfers between devices, near_plan(): lax.ppermute(packet, 'ctx', [(i, i + back) for i in range(count - back)])  4.27 us
    unnamed x14, local copies, waits for them, and re-layouts  2.72 us
    ppermute x3, starting transfers between devices, near_plan(): lax.ppermute(sent[k], 'ctx', [(i, (i + k) % count) for i in range(count)])  2.56 us
    pallas_call x1, Pallas kernels, near_plan(): pl.pallas_call(functools.partial(attend_kernel, count, halo, doc_lengths....  1.96 us
    pallas_call x1, Pallas kernels, near_plan(): pl.pallas_call(functools.partial(place_kernel, count, halo), out_shape=[j...  1.04 us
    concatenate x1, other arithmetic, near_plan(): jnp.concatenate([key_head_rows, value_head_rows, jnp.broadcast_to(owners....  0.84 us
  transfers between devices with their start and end apart: 5, of which 5 were waited for; matrix products, arithmetic and copies ran while one was open for 0% of the time, Pallas kernels for 0%

profile of v1, /device:TPU:8, one launch (start us, length us, event | category | flops | bytes accessed | tf_op | source)
XLA Modules:
  0.0 34.5 jit_solution(18377103142264867656)
XLA Ops:
  0.6 0.7 %convert_element_type.3 = bf16[128]{0:T(256)(128)(2,1)S(1)} convert(s32[128]{0:T(128)} %param.8) | non-fusion elementwise | flops 128 | bytes 768 | tf_op jit(solution)/shard_map/convert_element_type | solution.py:388
  1.3 0.0 copy-start
  1.3 0.8 %pad_maximum_fusion = bf16[272,128]{1,0:T(8,128)(2,1)S(1)} fusion(bf16[16,128]{1,0:T(8,128)(2,1)S(1)} %broadcast_in_dim.2, bf16[128,128]{1,0:T(8,128)(2,1)} %refs_6_.1, bf16[128,128]{1,0:T(8,128)(2,1)} %refs_5_.1), kind=kLoop, calls=%fused_computation | loop fusion | flops 208896 | bytes 139264 | tf_op jit(solution)/shard_map/concatenate | solution.py:384
  2.1 0.0 copy-start.6
  2.2 4.6 %collective-permute-start.1 = (bf16[272,128]{1,0:T(8,128)(2,1)S(1)}, bf16[272,128]{1,0:T(8,128)(2,1)S(1)}, u32[]{:S(2)}, u32[]{:S(2)}) collective-permute-start(bf16[272,128]{1,0:T(8,128)(2,1)S(1)} %pad_maximum_fusion), channel_id=1, source_target_pairs={{0,8},{4,12},{1,9},{5,13},{2,10},{6,14},{3,11},{7,15},{16,24},{20,... | collective-permute-start | bytes 208904 | tf_op jit(solution)/shard_map/ppermute | solution.py:393
  6.8 1.9 %collective-permute-start = (bf16[272,128]{1,0:T(8,128)(2,1)S(1)}, bf16[272,128]{1,0:T(8,128)(2,1)S(1)}, u32[]{:S(2)}, u32[]{:S(2)}) collective-permute-start(bf16[272,128]{1,0:T(8,128)(2,1)S(1)} %pad_maximum_fusion), channel_id=1, source_target_pairs={{0,4},{4,8},{8,12},{1,5},{5,9},{9,13},{2,6},{6,10},{10,14},{3,7},{... | collective-permute-start | bytes 208904 | tf_op jit(solution)/shard_map/ppermute | solution.py:393
  8.7 1.3 %collective-permute-done.1.refs_8_ = bf16[272,128]{1,0:T(8,128)(2,1)S(1)} collective-permute-done((bf16[272,128]{1,0:T(8,128)(2,1)S(1)}, bf16[272,128]{1,0:T(8,128)(2,1)S(1)}, u32[]{:S(2)}, u32[]{:S(2)}) %collective-permute-start.1) | collective-permute-done | bytes 69664 | tf_op jit(solution)/shard_map/ppermute | solution.py:393
  10.0 3.0 %collective-permute-done.refs_7_ = bf16[272,128]{1,0:T(8,128)(2,1)S(1)} collective-permute-done((bf16[272,128]{1,0:T(8,128)(2,1)S(1)}, bf16[272,128]{1,0:T(8,128)(2,1)S(1)}, u32[]{:S(2)}, u32[]{:S(2)}) %collective-permute-start) | collective-permute-done | bytes 69664 | tf_op jit(solution)/shard_map/ppermute | solution.py:393
  13.0 0.0 copy-done
  13.0 0.0 copy-done.1
  13.0 0.0 copy-done.5
  13.0 0.0 copy-done.6
  13.0 0.0 copy-start.2
  13.0 0.9 %copy-done.2 = bf16[128,512]{1,0:T(8,128)(2,1)S(1)} copy-done((bf16[128,512]{1,0:T(8,128)(2,1)S(1)}, bf16[128,512]{1,0:T(8,128)(2,1)}, u32[]{:S(2)}) %copy-start.2) | copy-done | bytes 131096
  13.9 0.9 %copy-done.3 = bf16[128,512]{1,0:T(8,128)(2,1)S(1)} copy-done((bf16[128,512]{1,0:T(8,128)(2,1)S(1)}, bf16[128,512]{1,0:T(8,128)(2,1)}, u32[]{:S(2)}) %copy-start.3) | copy-done | bytes 131096
  14.8 0.9 %copy-done.4 = bf16[128,512]{1,0:T(8,128)(2,1)S(1)} copy-done((bf16[128,512]{1,0:T(8,128)(2,1)S(1)}, bf16[128,512]{1,0:T(8,128)(2,1)}, u32[]{:S(2)}) %copy-start.4) | copy-done | bytes 131096
  15.7 2.0 %shard_map.94 = (bf16[656,128]{1,0:T(8,128)(2,1)S(1)}, bf16[656,128]{1,0:T(8,128)(2,1)S(1)}, bf16[656,128]{1,0:T(8,128)(2,1)S(1)}, bf16[656,128]{1,0:T(8,128)(2,1)S(1)}) custom-call(s32[16]{0:T(128)S(1)} %copy-done.5, s32[1,128]{1,0:T(1,128)S(1)} %bitcast.1, bf16[128,512]{1,0:T(8,128)(2,1)S(1)} %copy-done.2, bf16[128,512]{1,0:T(8,128)(2,1)S(1)} %copy-done.3, ...), custom_call_target="tpu_custom_call" | custom-call | tf_op jit(solution)/shard_map/pallas_call | solution.py:396
  17.7 0.6 %collective-permute-start.2 = (bf16[656,128]{1,0:T(8,128)(2,1)S(1)}, bf16[656,128]{1,0:T(8,128)(2,1)S(1)}, u32[]{:S(2)}, u32[]{:S(2)}) collective-permute-start(bf16[656,128]{1,0:T(8,128)(2,1)S(1)} %get-tuple-element.8), channel_id=1, source_target_pairs={{0,4},{4,8},{8,12},{12,0},{1,5},{5,9},{9,13},{13,1},{2,6},{6,10},{... | collective-permute-start | bytes 503816 | tf_op jit(solution)/shard_map/ppermute | solution.py:413
  18.3 1.4 %collective-permute-start.3 = (bf16[656,128]{1,0:T(8,128)(2,1)S(1)}, bf16[656,128]{1,0:T(8,128)(2,1)S(1)}, u32[]{:S(2)}, u32[]{:S(2)}) collective-permute-start(bf16[656,128]{1,0:T(8,128)(2,1)S(1)} %get-tuple-element.9), channel_id=1, source_target_pairs={{0,8},{4,12},{8,0},{12,4},{1,9},{5,13},{9,1},{13,5},{2,10},{6,14},... | collective-permute-start | bytes 503816 | tf_op jit(solution)/shard_map/ppermute | solution.py:413
  19.8 0.5 %collective-permute-start.4 = (bf16[656,128]{1,0:T(8,128)(2,1)S(1)}, bf16[656,128]{1,0:T(8,128)(2,1)S(1)}, u32[]{:S(2)}, u32[]{:S(2)}) collective-permute-start(bf16[656,128]{1,0:T(8,128)(2,1)S(1)} %get-tuple-element.10), channel_id=1, source_target_pairs={{0,12},{4,0},{8,4},{12,8},{1,13},{5,1},{9,5},{13,9},{2,14},{6,2},{... | collective-permute-start | bytes 503816 | tf_op jit(solution)/shard_map/ppermute | solution.py:413
  20.3 10.0 %collective-permute-done.2.refs_1_ = bf16[656,128]{1,0:T(8,128)(2,1)S(1)} collective-permute-done((bf16[656,128]{1,0:T(8,128)(2,1)S(1)}, bf16[656,128]{1,0:T(8,128)(2,1)S(1)}, u32[]{:S(2)}, u32[]{:S(2)}) %collective-permute-start.2) | collective-permute-done | bytes 167968 | tf_op jit(solution)/shard_map/ppermute | solution.py:413
  30.2 2.3 %collective-permute-done.3.refs_2_ = bf16[656,128]{1,0:T(8,128)(2,1)S(1)} collective-permute-done((bf16[656,128]{1,0:T(8,128)(2,1)S(1)}, bf16[656,128]{1,0:T(8,128)(2,1)S(1)}, u32[]{:S(2)}, u32[]{:S(2)}) %collective-permute-start.3) | collective-permute-done | bytes 167968 | tf_op jit(solution)/shard_map/ppermute | solution.py:413
  32.5 0.9 %collective-permute-done.4.refs_3_ = bf16[656,128]{1,0:T(8,128)(2,1)S(1)} collective-permute-done((bf16[656,128]{1,0:T(8,128)(2,1)S(1)}, bf16[656,128]{1,0:T(8,128)(2,1)S(1)}, u32[]{:S(2)}, u32[]{:S(2)}) %collective-permute-start.4) | collective-permute-done | bytes 167968 | tf_op jit(solution)/shard_map/ppermute | solution.py:413
  33.4 1.0 %shard_map.95 = (f32[128,512]{1,0:T(8,128)}, f32[128,128]{1,0:T(8,128)}, f32[128,128]{1,0:T(8,128)}) custom-call(bf16[656,128]{1,0:T(8,128)(2,1)S(1)} %get-tuple-element.7.refs_0_, bf16[656,128]{1,0:T(8,128)(2,1)S(1)} %collective-permute-done.2.refs_1_, bf16[656,128]{1,0:T(8,128)(2,1)S(1)} %collective-permute-done.3.refs_2_, ...), custom_call_target="tpu_custom_call" | custom-call | tf_op jit(solution)/shard_map/pallas_call | solution.py:416
  (5 shorter events, 0.0 us)
Async XLA Ops:
  1.3 11.7 %copy-start = (bf16[128,128]{1,0:T(8,128)(2,1)S(1)}, bf16[128,128]{1,0:T(8,128)(2,1)}, u32[]{:S(2)}) copy-start(bf16[128,128]{1,0:T(8,128)(2,1)} %refs_5_.1) | copy-start | bytes 98308
  1.3 11.7 %copy-start.1 = (bf16[128,128]{1,0:T(8,128)(2,1)S(1)}, bf16[128,128]{1,0:T(8,128)(2,1)}, u32[]{:S(2)}) copy-start(bf16[128,128]{1,0:T(8,128)(2,1)} %refs_6_.1) | copy-start | bytes 98308
  2.1 10.9 %copy-start.5 = (s32[16]{0:T(128)S(1)}, s32[16]{0:T(128)}, u32[]{:S(2)}) copy-start(s32[16]{0:T(128)} %refs_0_.1) | copy-start | bytes 196
  2.1 10.9 %copy-start.6 = (s32[128]{0:T(128)S(1)}, s32[128]{0:T(128)}, u32[]{:S(2)}) copy-start(s32[128]{0:T(128)} %param.8) | copy-start | bytes 1540
  2.2 7.8 %collective-permute-start.1 = (bf16[272,128]{1,0:T(8,128)(2,1)S(1)}, bf16[272,128]{1,0:T(8,128)(2,1)S(1)}, u32[]{:S(2)}, u32[]{:S(2)}) collective-permute-start(bf16[272,128]{1,0:T(8,128)(2,1)S(1)} %pad_maximum_fusion), channel_id=1, source_target_pairs={{0,8},{4,12},{1,9},{5,13},{2,10},{6,14},{3,11},{7,15},{16,24},{20,... | collective-permute-start | bytes 208904 | tf_op jit(solution)/shard_map/ppermute | solution.py:393
  6.8 6.2 %collective-permute-start = (bf16[272,128]{1,0:T(8,128)(2,1)S(1)}, bf16[272,128]{1,0:T(8,128)(2,1)S(1)}, u32[]{:S(2)}, u32[]{:S(2)}) collective-permute-start(bf16[272,128]{1,0:T(8,128)(2,1)S(1)} %pad_maximum_fusion), channel_id=1, source_target_pairs={{0,4},{4,8},{8,12},{1,5},{5,9},{9,13},{2,6},{6,10},{10,14},{3,7},{... | collective-permute-start | bytes 208904 | tf_op jit(solution)/shard_map/ppermute | solution.py:393
  13.0 0.9 %copy-start.2 = (bf16[128,512]{1,0:T(8,128)(2,1)S(1)}, bf16[128,512]{1,0:T(8,128)(2,1)}, u32[]{:S(2)}) copy-start(bf16[128,512]{1,0:T(8,128)(2,1)} %refs_2_.1) | copy-start | bytes 393220
  13.9 0.9 %copy-start.3 = (bf16[128,512]{1,0:T(8,128)(2,1)S(1)}, bf16[128,512]{1,0:T(8,128)(2,1)}, u32[]{:S(2)}) copy-start(bf16[128,512]{1,0:T(8,128)(2,1)} %refs_3_.1) | copy-start | bytes 393220
  14.8 0.9 %copy-start.4 = (bf16[128,512]{1,0:T(8,128)(2,1)S(1)}, bf16[128,512]{1,0:T(8,128)(2,1)}, u32[]{:S(2)}) copy-start(bf16[128,512]{1,0:T(8,128)(2,1)} %refs_4_.1) | copy-start | bytes 393220
  17.7 12.5 %collective-permute-start.2 = (bf16[656,128]{1,0:T(8,128)(2,1)S(1)}, bf16[656,128]{1,0:T(8,128)(2,1)S(1)}, u32[]{:S(2)}, u32[]{:S(2)}) collective-permute-start(bf16[656,128]{1,0:T(8,128)(2,1)S(1)} %get-tuple-element.8), channel_id=1, source_target_pairs={{0,4},{4,8},{8,12},{12,0},{1,5},{5,9},{9,13},{13,1},{2,6},{6,10},{... | collective-permute-start | bytes 503816 | tf_op jit(solution)/shard_map/ppermute | solution.py:413
  18.3 14.2 %collective-permute-start.3 = (bf16[656,128]{1,0:T(8,128)(2,1)S(1)}, bf16[656,128]{1,0:T(8,128)(2,1)S(1)}, u32[]{:S(2)}, u32[]{:S(2)}) collective-permute-start(bf16[656,128]{1,0:T(8,128)(2,1)S(1)} %get-tuple-element.9), channel_id=1, source_target_pairs={{0,8},{4,12},{8,0},{12,4},{1,9},{5,13},{9,1},{13,5},{2,10},{6,14},... | collective-permute-start | bytes 503816 | tf_op jit(solution)/shard_map/ppermute | solution.py:413
  19.8 13.7 %collective-permute-start.4 = (bf16[656,128]{1,0:T(8,128)(2,1)S(1)}, bf16[656,128]{1,0:T(8,128)(2,1)S(1)}, u32[]{:S(2)}, u32[]{:S(2)}) collective-permute-start(bf16[656,128]{1,0:T(8,128)(2,1)S(1)} %get-tuple-element.10), channel_id=1, source_target_pairs={{0,12},{4,0},{8,4},{12,8},{1,13},{5,1},{9,5},{13,9},{2,14},{6,2},{... | collective-permute-start | bytes 503816 | tf_op jit(solution)/shard_map/ppermute | solution.py:413

commit v2 on v0

--- a/solution.py
+++ b/solution.py
@@ -1,8 +1,11 @@
+import functools
 import math
 
 import jax
 import jax.numpy as jnp
 from jax import lax
+from jax.experimental import pallas as pl
+from jax.experimental.pallas import tpu as pltpu
 from jax.sharding import PartitionSpec as P
 
 HEAD_WIDTH = 128
@@ -100,7 +103,7 @@
     )
 
 
-def per_device(doc_lengths, owners, queries, key_head_rows, value_head_rows, forward_out, grad_out):
+def ring_plan(doc_lengths, owners, queries, key_head_rows, value_head_rows, forward_out, grad_out):
     context_size = lax.axis_size("ctx")
     context_index = lax.axis_index("ctx")
     row_count = queries.shape[0]
@@ -231,6 +234,292 @@
     return (query_grad * inverse_root, key_grad * inverse_root, value_grad)
 
 
+META = 16
+
+
+def contract(left, right, left_dim, right_dim, **kw):
+    return lax.dot_general(
+        left,
+        right,
+        (((left_dim,), (right_dim,)), ((), ())),
+        preferred_element_type=jnp.float32,
+        **kw,
+    )
+
+
+def one_hot(row_count, target):
+    places = lax.broadcasted_iota(jnp.int32, (row_count, target.shape[1]), 0)
+    return jnp.where(places == target, 1.0, 0.0).astype(jnp.bfloat16)
+
+
+def side_by_side(stack, heads):
+    rows = stack.shape[0] // heads
+    return jnp.concatenate([stack[h * rows : (h + 1) * rows, :] for h in range(heads)], axis=1)
+
+
+def end_to_end(matrix, heads):
+    width = matrix.shape[1] // heads
+    return jnp.concatenate([matrix[:, h * width : (h + 1) * width] for h in range(heads)], axis=0)
+
+
+def own_kernel(
+    docs,
+    doc_ref,
+    packet_ref,
+    query_ref,
+    grad_ref,
+    saved_ref,
+    query_out,
+    grad_out,
+    raised_out,
+    change_out,
+    row_out,
+    query_in,
+    grad_in,
+    saved_in,
+    sems,
+):
+    copies = [
+        pltpu.make_async_copy(far, here, sems.at[n])
+        for n, (far, here) in enumerate(
+            ((query_ref, query_in), (grad_ref, grad_in), (saved_ref, saved_in))
+        )
+    ]
+    for copy in copies:
+        copy.start()
+    rows, width = query_in.shape
+    depth = packet_ref.shape[1]
+    heads = width // depth
+    index = lax.axis_index("ctx")
+    lane = lax.broadcasted_iota(jnp.int32, (1, rows), 1)
+    position = index * rows + lane
+    first = jnp.zeros((1, rows), jnp.int32)
+    end = jnp.int32(0)
+    for d in range(docs):
+        end = end + doc_ref[d]
+        first = jnp.where(end <= position, end, first)
+    key_position = index * rows + lax.broadcasted_iota(jnp.int32, (rows, rows), 0)
+    allowed = (key_position >= first) & (key_position <= position)
+    allowed = jnp.concatenate([allowed] * heads, axis=1)
+
+    copies[0].wait()
+    queries = end_to_end(query_in[...], heads)
+    query_out[...] = queries
+    scores = contract(packet_ref[0:rows, :], queries, 1, 1) * (1.0 / math.sqrt(depth))
+    scores = jnp.where(allowed, scores, NEG)
+    top = jnp.max(scores, axis=0, keepdims=True)
+    raised = jnp.exp(scores - top)
+    raised_out[...] = raised
+    copies[1].wait()
+    grads = end_to_end(grad_in[...], heads)
+    grad_out[...] = grads
+    copies[2].wait()
+    product = grads.astype(jnp.float32) * end_to_end(saved_in[...], heads).astype(jnp.float32)
+    delta = contract(
+        jnp.ones((8, depth), jnp.float32), product, 1, 1, precision=lax.Precision.HIGHEST
+    )[0:1, :]
+    change_out[...] = contract(packet_ref[rows : 2 * rows, :], grads, 1, 1) - delta
+    row_out[0:1, :] = delta
+    row_out[1:2, :] = top
+    row_out[2:3, :] = jnp.sum(raised, axis=0, keepdims=True)
+    row_out[3:4, :] = jnp.concatenate([first.astype(jnp.float32)] * heads, axis=1)
+    row_out[4:8, :] = jnp.zeros((4, width), jnp.float32)
+
+
+def attend_kernel(count, halo, *refs):
+    query_ref, grad_ref, raised_ref, change_ref, row_ref = refs[:5]
+    own = refs[5]
+    near = refs[6 : 6 + halo]
+    outs = refs[6 + halo :]
+    rows, columns = raised_ref.shape
+    depth = query_ref.shape[1]
+    heads = columns // rows
+    slot = 2 * rows // count
+    scale = 1.0 / math.sqrt(depth)
+    index = lax.axis_index("ctx")
+    before = near[::-1]
+    delta, top, total = (row_ref[n : n + 1, :] for n in range(3))
+    first = row_ref[3:4, :].astype(jnp.int32)
+
+    key_position = (index - halo) * rows + lax.broadcasted_iota(
+        jnp.int32, (halo * rows, columns), 0
+    )
+    queries = query_ref[...]
+    grads = grad_ref[...]
+    keys = jnp.concatenate([n[0:rows, :] for n in before], axis=0)
+    values = jnp.concatenate([n[rows : 2 * rows, :] for n in before], axis=0)
+    scores = jnp.where(key_position >= first, contract(keys, queries, 1, 1) * scale, NEG)
+    new_top = jnp.maximum(top, jnp.max(scores, axis=0, keepdims=True))
+    raised = jnp.exp(scores - new_top)
+    shrink = jnp.exp(top - new_top)
+    inverse = 1.0 / (total * shrink + jnp.sum(raised, axis=0, keepdims=True))
+    weights = raised * inverse
+    own_weights = raised_ref[...] * (shrink * inverse)
+    grad_scores = weights * (contract(values, grads, 1, 1) - delta)
+    own_grad_scores = own_weights * change_ref[...]
+    weights = jnp.concatenate([weights, own_weights], axis=0).astype(jnp.bfloat16)
+    grad_scores = jnp.concatenate([grad_scores, own_grad_scores], axis=0).astype(jnp.bfloat16)
+    keys = jnp.concatenate([keys, own[0:rows, :]], axis=0)
+    value_parts = contract(weights, grads, 1, 0).astype(jnp.bfloat16)
+    key_parts = (contract(grad_scores, queries, 1, 0) * scale).astype(jnp.bfloat16)
+    query_grad = (contract(keys, grad_scores, 0, 0) * scale).astype(jnp.bfloat16)
+
+    lane = lax.broadcasted_iota(jnp.int32, (1, rows), 1)
+    filled = jnp.zeros((count, 1), jnp.float32)
+    targets = []
+    for block, ref in enumerate(before + (own,)):
+        hot = ref[2 * rows : 2 * rows + count, :].astype(jnp.float32)
+        counts = jnp.sum(hot, axis=1, keepdims=True)
+        owner = jnp.zeros((1, rows), jnp.int32)
+        earlier = jnp.zeros((1, rows), jnp.float32)
+        base = jnp.zeros((1, rows), jnp.float32)
+        for p in range(count):
+            mine = hot[p : p + 1, :] > 0.0
+            owner = jnp.where(mine, p, owner)
+            base = jnp.where(mine, filled[p : p + 1, :], base)
+            for less in range(p):
+                earlier = earlier + jnp.where(mine, counts[less : less + 1, :], 0.0)
+        ahead = lax.rem(owner - index + count, count)
+        rank = lane - earlier.astype(jnp.int32)
+        target = ahead * rows + base.astype(jnp.int32) + rank
+        targets.append(jnp.where(index - halo + block >= 0, target, -1))
+        filled = filled + counts
+    spread = one_hot(count * slot, ahead * slot + rank)
+    query_slots = contract(spread, end_to_end(query_grad, heads), 1, 1).astype(jnp.bfloat16)
+    spread = one_hot(count * rows, jnp.concatenate(targets, axis=1))
+    key_slots = contract(spread, key_parts, 1, 0).astype(jnp.bfloat16)
+    value_slots = contract(spread, value_parts, 1, 0).astype(jnp.bfloat16)
+    for k in range(count):
+        out = outs[k]
+        for h in range(heads):
+            out[h * slot : (h + 1) * slot, :] = query_slots[
+                k * slot : (k + 1) * slot, h * depth : (h + 1) * depth
+            ]
+        at = heads * slot
+        out[at : at + rows, :] = key_slots[k * rows : (k + 1) * rows, :]
+        out[at + rows : at + 2 * rows, :] = value_slots[k * rows : (k + 1) * rows, :]
+        owner = lax.rem(index + k, count)
+        given = jnp.zeros((1, 1), jnp.float32)
+        for p in range(count):
+            given = jnp.where(owner == p, counts[p : p + 1, :], given)
+        out[at + 2 * rows :, :] = jnp.broadcast_to(given, (META, depth)).astype(jnp.bfloat16)
+
+
+def place_kernel(count, halo, *refs):
+    ins = refs[:count]
+    query_out, key_out, value_out = refs[count:]
+    rows, width = query_out.shape
+    depth = key_out.shape[1]
+    heads = width // depth
+    slot = 2 * rows // count
+    at = heads * slot
+    index = lax.axis_index("ctx")
+    source = [lax.rem(index - k + count, count) for k in range(count)]
+    given = [
+        ref[at + 2 * rows : at + 2 * rows + 1, 0:1].astype(jnp.float32).astype(jnp.int32)
+        for ref in ins
+    ]
+    query_targets = []
+    key_targets = []
+    for k in range(count):
+        start = jnp.zeros((1, 1), jnp.int32)
+        key_start = jnp.zeros((1, 1), jnp.int32)
+        for other in range(count):
+            start = start + jnp.where(source[other] < source[k], given[other], 0)
+            key_start = key_start + jnp.where(source[other] < source[k] - halo, given[other], 0)
+        query_targets.append(start)
+        key_targets.append(key_start)
+
+    def spread_of(starts, size, limits):
+        lane = lax.broadcasted_iota(jnp.int32, (1, count * size), 1)
+        target = jnp.full((1, count * size), -1, jnp.int32)
+        for k in range(count):
+            step = lane - k * size
+            inside = (step >= 0) & (step < limits[k])
+            target = jnp.where(inside, starts[k] + step, target)
+        return one_hot(rows, target)
+
+    spread = spread_of(query_targets, slot, given)
+    for h in range(heads):
+        taken = jnp.concatenate([ref[h * slot : (h + 1) * slot, :] for ref in ins], axis=0)
+        query_out[:, h * depth : (h + 1) * depth] = contract(spread, taken, 1, 0)
+    spread = spread_of(key_targets, rows, [rows] * count)
+    for n, out in enumerate((key_out, value_out)):
+        first = at + n * rows
+        taken = jnp.concatenate([ref[first : first + rows, :] for ref in ins], axis=0)
+        out[...] = contract(spread, taken, 1, 0)
+
+
+def near_plan(doc_lengths, owners, queries, key_head_rows, value_head_rows, forward_out, grad_out):
+    count = lax.axis_size("ctx")
+    rows, width = queries.shape
+    depth = key_head_rows.shape[1]
+    heads = width // depth
+    columns = heads * rows
+    halo = count // 2
+    slot = 2 * rows // count
+    packet_rows = heads * slot + 2 * rows + META
+    whole = pl.BlockSpec(memory_space=pltpu.VMEM)
+    anywhere = pl.BlockSpec(memory_space=pltpu.HBM)
+    params = pltpu.CompilerParams(vmem_limit_bytes=40 * 1024 * 1024)
+    bf16, f32 = jnp.bfloat16, jnp.float32
+
+    packet = jnp.concatenate(
+        [
+            key_head_rows,
+            value_head_rows,
+            (owners[None, :] == jnp.arange(META, dtype=jnp.int32)[:, None]).astype(bf16),
+        ],
+        axis=0,
+    )
+    near = [
+        lax.ppermute(packet, "ctx", [(i, i + back) for i in range(count - back)])
+        for back in range(1, halo + 1)
+    ]
+    own = pl.pallas_call(
+        functools.partial(own_kernel, doc_lengths.shape[0]),
+        out_shape=[
+            jax.ShapeDtypeStruct((columns, depth), bf16),
+            jax.ShapeDtypeStruct((columns, depth), bf16),
+            jax.ShapeDtypeStruct((rows, columns), f32),
+            jax.ShapeDtypeStruct((rows, columns), f32),
+            jax.ShapeDtypeStruct((8, columns), f32),
+        ],
+        in_specs=[pl.BlockSpec(memory_space=pltpu.SMEM), whole] + [anywhere] * 3,
+        out_specs=[whole] * 5,
+        scratch_shapes=[pltpu.VMEM((rows, width), bf16)] * 3 + [pltpu.SemaphoreType.DMA((3,))],
+        compiler_params=params,
+    )(doc_lengths, packet, queries, grad_out, forward_out)
+    sent = pl.pallas_call(
+        functools.partial(attend_kernel, count, halo),
+        out_shape=[jax.ShapeDtypeStruct((packet_rows, depth), bf16)] * count,
+        in_specs=[whole] * (6 + halo),
+        out_specs=[whole] * count,
+        compiler_params=params,
+    )(*own, packet, *near)
+    received = [sent[0]] + [
+        lax.ppermute(sent[k], "ctx", [(i, (i + k) % count) for i in range(count)])
+        for k in range(1, count)
+    ]
+    return pl.pallas_call(
+        functools.partial(place_kernel, count, halo),
+        out_shape=[
+            jax.ShapeDtypeStruct((rows, width), f32),
+            jax.ShapeDtypeStruct((rows, depth), f32),
+            jax.ShapeDtypeStruct((rows, depth), f32),
+        ],
+        in_specs=[whole] * count,
+        out_specs=[whole] * 3,
+        compiler_params=params,
+    )(*received)
+
+
+def per_device(*args):
+    if lax.axis_size("ctx") <= 4:
+        return near_plan(*args)
+    return ring_plan(*args)
+
+
 def solution(mesh):
     return jax.shard_map(
         per_device,

time: 120 us -> 30.4 us (0.25)
  blocking collectives: 25.2 us -> 0 us
  starting transfers between devices: 36.2 us -> 13.3 us
  local copies, waits for them, and re-layouts: 18.1 us -> 1.81 us
  waiting for transfers between devices: 23.5 us -> 8.7 us
  other arithmetic: 10 us -> 1.49 us
  matrix products: 4.84 us -> 0 us
  Pallas kernels: 0 us -> 4.13 us
    all_gather x2 -> x0, blocking collectives: 25.2 us -> none  [the longest x1 13.9 us: per_device(): lax.all_gather(key_local, 'ctx', axis=0, tiled=True)]
    all_to_all x5 -> x0, starting transfers between devices: 19.7 us -> none  [the longest x1 6.32 us: per_device(): lax.all_to_all(packed(local_delta), 'ctx', split_axis=0, concat_axis=0, t...]
    all_to_all x5 -> x0, waiting for transfers between devices: 9.6 us -> none  [the longest x1 4 us: per_device(): lax.all_to_all(packed(key_head_rows), 'ctx', split_axis=0, concat_axis=0,...]
    scatter x5 -> x0, local copies, waits for them, and re-layouts: 8.14 us -> none  [packed(): return empty.at[slot_rows].set(matrix)]
    ppermute x14 -> x5, waiting for transfers between devices: 13.9 us -> 8.7 us  [the longest x3 8.69 us: near_plan(): lax.ppermute(sent[k], 'ctx', [(i, (i + k) % count) for i in range(count)])]
    dot_general x21 -> x0, matrix products: 4.84 us -> none  [the longest x4 1.33 us: backward_block(): lax.dot_general(rounded_weights, grad_flat, (((0,), (0,)), ((), ())), pre...]
    pallas_call x0 -> x3, Pallas kernels: none -> 4.13 us  [the longest x1 1.8 us: near_plan(): pl.pallas_call(functools.partial(own_kernel, doc_lengths.shape[0]), out_s...]
    gather x5 -> x0, local copies, waits for them, and re-layouts: 3.78 us -> none  [compact(): return jnp.take(received, take_rows, axis=0)]
  transfers between devices with their start and end apart: 19 -> 5, of which waited for: 14 -> 2; matrix products, arithmetic and copies ran while one was open for 19% -> 0% of each run, Pallas kernels for 0% -> 6%
where the time goes in v2:
time: 30.4 us; the launch traced here: 30.1 us
  starting transfers between devices  13.3 us (44%)
  waiting for transfers between devices  8.7 us (29%)
  Pallas kernels  4.13 us (14%)
  local copies, waits for them, and re-layouts  1.81 us (6%)
  other arithmetic  1.49 us (5%)
  between operations  0.72 us (2%)
    ppermute x2, starting transfers between devices, near_plan(): lax.ppermute(packet, 'ctx', [(i, i + back) for i in range(count - back)])  9.42 us
    ppermute x3, waiting for transfers between devices, near_plan(): lax.ppermute(sent[k], 'ctx', [(i, (i + k) % count) for i in range(count)])  8.69 us
    ppermute x3, starting transfers between devices, near_plan(): lax.ppermute(sent[k], 'ctx', [(i, (i + k) % count) for i in range(count)])  3.88 us
    unnamed x8, local copies, waits for them, and re-layouts  1.81 us
    pallas_call x1, Pallas kernels, near_plan(): pl.pallas_call(functools.partial(own_kernel, doc_lengths.shape[0]), out_s...  1.8 us
    pallas_call x1, Pallas kernels, near_plan(): pl.pallas_call(functools.partial(attend_kernel, count, halo), out_shape=[...  1.28 us
    pallas_call x1, Pallas kernels, near_plan(): pl.pallas_call(functools.partial(place_kernel, count, halo), out_shape=[j...  1.05 us
    concatenate x1, other arithmetic, near_plan(): jnp.concatenate([key_head_rows, value_head_rows, (owners[None, :] == jnp....  0.79 us
  transfers between devices with their start and end apart: 5, of which 2 were waited for; matrix products, arithmetic and copies ran while one was open for 0% of the time, Pallas kernels for 6%

profile of v2, /device:TPU:0, one launch (start us, length us, event | category | flops | bytes accessed | tf_op | source)
XLA Modules:
  0.0 30.1 jit_solution(15316867201401097920)
XLA Ops:
  0.6 0.0 copy-start
  0.6 0.7 %fusion = bf16[16,128]{1,0:T(8,128)(2,1)S(1)} fusion(s32[128]{0:T(128)} %param.8), kind=kLoop, calls=%fused_computation.2 | loop fusion | flops 4096 | bytes 4608 | tf_op jit(solution)/shard_map/convert_element_type | solution.py:471
  1.3 0.0 copy-start.3
  1.3 0.8 %pad_maximum_fusion.packet_ref.refs_5_ = bf16[272,128]{1,0:T(8,128)(2,1)S(1)} fusion(bf16[16,128]{1,0:T(8,128)(2,1)S(1)} %fusion, bf16[128,128]{1,0:T(8,128)(2,1)} %param.11, bf16[128,128]{1,0:T(8,128)(2,1)} %param.10), kind=kLoop, calls=%fused_computation | loop fusion | flops 208896 | bytes 139264 | tf_op jit(solution)/shard_map/concatenate | solution.py:467
  2.1 5.9 %collective-permute-start.1 = (bf16[272,128]{1,0:T(8,128)(2,1)S(1)}, bf16[272,128]{1,0:T(8,128)(2,1)S(1)}, u32[]{:S(2)}, u32[]{:S(2)}) collective-permute-start(bf16[272,128]{1,0:T(8,128)(2,1)S(1)} %pad_maximum_fusion.packet_ref.refs_5_), channel_id=1, source_target_pairs={{0,8},{4,12},{1,9},{5,13},{2,10},{6,14},{3,11},{7,15},{16,24},{20,... | collective-permute-start | bytes 208904 | tf_op jit(solution)/shard_map/ppermute | solution.py:476
  8.1 3.5 %collective-permute-start = (bf16[272,128]{1,0:T(8,128)(2,1)S(1)}, bf16[272,128]{1,0:T(8,128)(2,1)S(1)}, u32[]{:S(2)}, u32[]{:S(2)}) collective-permute-start(bf16[272,128]{1,0:T(8,128)(2,1)S(1)} %pad_maximum_fusion.packet_ref.refs_5_), channel_id=1, source_target_pairs={{0,4},{4,8},{8,12},{1,5},{5,9},{9,13},{2,6},{6,10},{10,14},{3,7},{... | collective-permute-start | bytes 208904 | tf_op jit(solution)/shard_map/ppermute | solution.py:476
  11.6 0.0 copy-done
  11.6 0.0 copy-done.3
  11.6 0.0 copy-start.1
  11.6 0.9 %copy-done.1 = bf16[128,512]{1,0:T(8,128)(2,1)S(1)} copy-done((bf16[128,512]{1,0:T(8,128)(2,1)S(1)}, bf16[128,512]{1,0:T(8,128)(2,1)}, u32[]{:S(2)}) %copy-start.1) | copy-done | bytes 131096
  12.5 0.0 copy-start.2
  12.5 0.9 %copy-done.2 = bf16[128,512]{1,0:T(8,128)(2,1)S(1)} copy-done((bf16[128,512]{1,0:T(8,128)(2,1)S(1)}, bf16[128,512]{1,0:T(8,128)(2,1)}, u32[]{:S(2)}) %copy-start.2) | copy-done | bytes 131096
  13.4 1.8 %shard_map.94 = (bf16[512,128]{1,0:T(8,128)(2,1)S(1)}, bf16[512,128]{1,0:T(8,128)(2,1)S(1)}, f32[128,512]{1,0:T(8,128)S(1)}, f32[128,512]{1,0:T(8,128)S(1)}, f32[8,512]{1,0:T(8,128)S(1)}) custom-call(s32[16]{0:T(128)S(1)} %copy-done.3, bf16[272,128]{1,0:T(8,128)(2,1)S(1)} %pad_maximum_fusion.packet_ref.refs_5_, bf16[128,512]{1,0:T(8,128)(2,1)S(1)} %copy-done, ...), custom_call_target="tpu_custom_call" | custom-call | tf_op jit(solution)/shard_map/pallas_call | solution.py:479
  15.2 0.0 collective-permute-done.1.refs_7_
  15.2 0.0 collective-permute-done.refs_6_
  15.2 1.3 %shard_map.95 = (bf16[528,128]{1,0:T(8,128)(2,1)S(1)}, bf16[528,128]{1,0:T(8,128)(2,1)S(1)}, bf16[528,128]{1,0:T(8,128)(2,1)S(1)}, bf16[528,128]{1,0:T(8,128)(2,1)S(1)}) custom-call(bf16[512,128]{1,0:T(8,128)(2,1)S(1)} %get-tuple-element.12.refs_0_, bf16[512,128]{1,0:T(8,128)(2,1)S(1)} %get-tuple-element.13.refs_1_, ...), custom_call_target="tpu_custom_call" | custom-call | tf_op jit(solution)/shard_map/pallas_call | solution.py:493
  16.5 0.7 %collective-permute-start.2 = (bf16[528,128]{1,0:T(8,128)(2,1)S(1)}, bf16[528,128]{1,0:T(8,128)(2,1)S(1)}, u32[]{:S(2)}, u32[]{:S(2)}) collective-permute-start(bf16[528,128]{1,0:T(8,128)(2,1)S(1)} %get-tuple-element.18), channel_id=1, source_target_pairs={{0,4},{4,8},{8,12},{12,0},{1,5},{5,9},{9,13},{13,1},{2,6},{6,10},{... | collective-permute-start | bytes 405512 | tf_op jit(solution)/shard_map/ppermute | solution.py:501
  17.2 0.5 %collective-permute-start.3 = (bf16[528,128]{1,0:T(8,128)(2,1)S(1)}, bf16[528,128]{1,0:T(8,128)(2,1)S(1)}, u32[]{:S(2)}, u32[]{:S(2)}) collective-permute-start(bf16[528,128]{1,0:T(8,128)(2,1)S(1)} %get-tuple-element.19), channel_id=1, source_target_pairs={{0,8},{4,12},{8,0},{12,4},{1,9},{5,13},{9,1},{13,5},{2,10},{6,14},... | collective-permute-start | bytes 405512 | tf_op jit(solution)/shard_map/ppermute | solution.py:501
  17.7 2.7 %collective-permute-start.4 = (bf16[528,128]{1,0:T(8,128)(2,1)S(1)}, bf16[528,128]{1,0:T(8,128)(2,1)S(1)}, u32[]{:S(2)}, u32[]{:S(2)}) collective-permute-start(bf16[528,128]{1,0:T(8,128)(2,1)S(1)} %get-tuple-element.20), channel_id=1, source_target_pairs={{0,12},{4,0},{8,4},{12,8},{1,13},{5,1},{9,5},{13,9},{2,14},{6,2},{... | collective-permute-start | bytes 405512 | tf_op jit(solution)/shard_map/ppermute | solution.py:501
  20.4 4.5 %collective-permute-done.2.refs_1_ = bf16[528,128]{1,0:T(8,128)(2,1)S(1)} collective-permute-done((bf16[528,128]{1,0:T(8,128)(2,1)S(1)}, bf16[528,128]{1,0:T(8,128)(2,1)S(1)}, u32[]{:S(2)}, u32[]{:S(2)}) %collective-permute-start.2) | collective-permute-done | bytes 135200 | tf_op jit(solution)/shard_map/ppermute | solution.py:501
  24.9 4.1 %collective-permute-done.3.refs_2_ = bf16[528,128]{1,0:T(8,128)(2,1)S(1)} collective-permute-done((bf16[528,128]{1,0:T(8,128)(2,1)S(1)}, bf16[528,128]{1,0:T(8,128)(2,1)S(1)}, u32[]{:S(2)}, u32[]{:S(2)}) %collective-permute-start.3) | collective-permute-done | bytes 135200 | tf_op jit(solution)/shard_map/ppermute | solution.py:501
  29.1 0.0 collective-permute-done.4.refs_3_
  29.1 1.1 %shard_map.96 = (f32[128,512]{1,0:T(8,128)}, f32[128,128]{1,0:T(8,128)}, f32[128,128]{1,0:T(8,128)}) custom-call(bf16[528,128]{1,0:T(8,128)(2,1)S(1)} %get-tuple-element.17.refs_0_, bf16[528,128]{1,0:T(8,128)(2,1)S(1)} %collective-permute-done.2.refs_1_, bf16[528,128]{1,0:T(8,128)(2,1)S(1)} %collective-permute-done.3.refs_2_, ...), custom_call_target="tpu_custom_call" | custom-call | tf_op jit(solution)/shard_map/pallas_call | solution.py:504
Async XLA Ops:
  0.6 10.9 %copy-start = (bf16[128,512]{1,0:T(8,128)(2,1)S(1)}, bf16[128,512]{1,0:T(8,128)(2,1)}, u32[]{:S(2)}) copy-start(bf16[128,512]{1,0:T(8,128)(2,1)} %query_ref.1) | copy-start | bytes 393220
  1.3 10.2 %copy-start.3 = (s32[16]{0:T(128)S(1)}, s32[16]{0:T(128)}, u32[]{:S(2)}) copy-start(s32[16]{0:T(128)} %doc_ref.1) | copy-start | bytes 196
  2.1 13.1 %collective-permute-start.1 = (bf16[272,128]{1,0:T(8,128)(2,1)S(1)}, bf16[272,128]{1,0:T(8,128)(2,1)S(1)}, u32[]{:S(2)}, u32[]{:S(2)}) collective-permute-start(bf16[272,128]{1,0:T(8,128)(2,1)S(1)} %pad_maximum_fusion.packet_ref.refs_5_), channel_id=1, source_target_pairs={{0,8},{4,12},{1,9},{5,13},{2,10},{6,14},{3,11},{7,15},{16,24},{20,... | collective-permute-start | bytes 208904 | tf_op jit(solution)/shard_map/ppermute | solution.py:476
  8.1 7.1 %collective-permute-start = (bf16[272,128]{1,0:T(8,128)(2,1)S(1)}, bf16[272,128]{1,0:T(8,128)(2,1)S(1)}, u32[]{:S(2)}, u32[]{:S(2)}) collective-permute-start(bf16[272,128]{1,0:T(8,128)(2,1)S(1)} %pad_maximum_fusion.packet_ref.refs_5_), channel_id=1, source_target_pairs={{0,4},{4,8},{8,12},{1,5},{5,9},{9,13},{2,6},{6,10},{10,14},{3,7},{... | collective-permute-start | bytes 208904 | tf_op jit(solution)/shard_map/ppermute | solution.py:476
  11.6 0.9 %copy-start.1 = (bf16[128,512]{1,0:T(8,128)(2,1)S(1)}, bf16[128,512]{1,0:T(8,128)(2,1)}, u32[]{:S(2)}) copy-start(bf16[128,512]{1,0:T(8,128)(2,1)} %grad_ref.1) | copy-start | bytes 393220
  12.5 0.9 %copy-start.2 = (bf16[128,512]{1,0:T(8,128)(2,1)S(1)}, bf16[128,512]{1,0:T(8,128)(2,1)}, u32[]{:S(2)}) copy-start(bf16[128,512]{1,0:T(8,128)(2,1)} %saved_ref.1) | copy-start | bytes 393220
  16.5 8.4 %collective-permute-start.2 = (bf16[528,128]{1,0:T(8,128)(2,1)S(1)}, bf16[528,128]{1,0:T(8,128)(2,1)S(1)}, u32[]{:S(2)}, u32[]{:S(2)}) collective-permute-start(bf16[528,128]{1,0:T(8,128)(2,1)S(1)} %get-tuple-element.18), channel_id=1, source_target_pairs={{0,4},{4,8},{8,12},{12,0},{1,5},{5,9},{9,13},{13,1},{2,6},{6,10},{... | collective-permute-start | bytes 405512 | tf_op jit(solution)/shard_map/ppermute | solution.py:501
  17.2 11.9 %collective-permute-start.3 = (bf16[528,128]{1,0:T(8,128)(2,1)S(1)}, bf16[528,128]{1,0:T(8,128)(2,1)S(1)}, u32[]{:S(2)}, u32[]{:S(2)}) collective-permute-start(bf16[528,128]{1,0:T(8,128)(2,1)S(1)} %get-tuple-element.19), channel_id=1, source_target_pairs={{0,8},{4,12},{8,0},{12,4},{1,9},{5,13},{9,1},{13,5},{2,10},{6,14},... | collective-permute-start | bytes 405512 | tf_op jit(solution)/shard_map/ppermute | solution.py:501
  17.7 11.4 %collective-permute-start.4 = (bf16[528,128]{1,0:T(8,128)(2,1)S(1)}, bf16[528,128]{1,0:T(8,128)(2,1)S(1)}, u32[]{:S(2)}, u32[]{:S(2)}) collective-permute-start(bf16[528,128]{1,0:T(8,128)(2,1)S(1)} %get-tuple-element.20), channel_id=1, source_target_pairs={{0,12},{4,0},{8,4},{12,8},{1,13},{5,1},{9,5},{13,9},{2,14},{6,2},{... | collective-permute-start | bytes 405512 | tf_op jit(solution)/shard_map/ppermute | solution.py:501

commit v3 on v2

--- a/solution.py
+++ b/solution.py
@@ -274,20 +274,8 @@
     raised_out,
     change_out,
     row_out,
-    query_in,
-    grad_in,
-    saved_in,
-    sems,
 ):
-    copies = [
-        pltpu.make_async_copy(far, here, sems.at[n])
-        for n, (far, here) in enumerate(
-            ((query_ref, query_in), (grad_ref, grad_in), (saved_ref, saved_in))
-        )
-    ]
-    for copy in copies:
-        copy.start()
-    rows, width = query_in.shape
+    rows, width = query_ref.shape
     depth = packet_ref.shape[1]
     heads = width // depth
     index = lax.axis_index("ctx")
@@ -302,19 +290,16 @@
     allowed = (key_position >= first) & (key_position <= position)
     allowed = jnp.concatenate([allowed] * heads, axis=1)
 
-    copies[0].wait()
-    queries = end_to_end(query_in[...], heads)
+    queries = end_to_end(query_ref[...], heads)
     query_out[...] = queries
     scores = contract(packet_ref[0:rows, :], queries, 1, 1) * (1.0 / math.sqrt(depth))
     scores = jnp.where(allowed, scores, NEG)
     top = jnp.max(scores, axis=0, keepdims=True)
     raised = jnp.exp(scores - top)
     raised_out[...] = raised
-    copies[1].wait()
-    grads = end_to_end(grad_in[...], heads)
+    grads = end_to_end(grad_ref[...], heads)
     grad_out[...] = grads
-    copies[2].wait()
-    product = grads.astype(jnp.float32) * end_to_end(saved_in[...], heads).astype(jnp.float32)
+    product = grads.astype(jnp.float32) * end_to_end(saved_ref[...], heads).astype(jnp.float32)
     delta = contract(
         jnp.ones((8, depth), jnp.float32), product, 1, 1, precision=lax.Precision.HIGHEST
     )[0:1, :]
@@ -369,6 +354,7 @@
     targets = []
     for block, ref in enumerate(before + (own,)):
         hot = ref[2 * rows : 2 * rows + count, :].astype(jnp.float32)
+        hot = jnp.where(index - halo + block >= 0, hot, 0.0)
         counts = jnp.sum(hot, axis=1, keepdims=True)
         owner = jnp.zeros((1, rows), jnp.int32)
         earlier = jnp.zeros((1, rows), jnp.float32)
@@ -460,20 +446,17 @@
     slot = 2 * rows // count
     packet_rows = heads * slot + 2 * rows + META
     whole = pl.BlockSpec(memory_space=pltpu.VMEM)
-    anywhere = pl.BlockSpec(memory_space=pltpu.HBM)
     params = pltpu.CompilerParams(vmem_limit_bytes=40 * 1024 * 1024)
     bf16, f32 = jnp.bfloat16, jnp.float32
 
-    packet = jnp.concatenate(
-        [
-            key_head_rows,
-            value_head_rows,
-            (owners[None, :] == jnp.arange(META, dtype=jnp.int32)[:, None]).astype(bf16),
-        ],
-        axis=0,
+    mark = lax.broadcasted_iota(jnp.int32, (2 * rows + META, rows), 0) - 2 * rows
+    packet = jnp.where(
+        mark < 0,
+        jnp.pad(jnp.concatenate([key_head_rows, value_head_rows], axis=0), ((0, META), (0, 0))),
+        (owners[None, :] == mark).astype(bf16),
     )
     near = [
-        lax.ppermute(packet, "ctx", [(i, i + back) for i in range(count - back)])
+        lax.ppermute(packet, "ctx", [(i, (i + back) % count) for i in range(count)])
         for back in range(1, halo + 1)
     ]
     own = pl.pallas_call(
@@ -485,9 +468,8 @@
             jax.ShapeDtypeStruct((rows, columns), f32),
             jax.ShapeDtypeStruct((8, columns), f32),
         ],
-        in_specs=[pl.BlockSpec(memory_space=pltpu.SMEM), whole] + [anywhere] * 3,
+        in_specs=[pl.BlockSpec(memory_space=pltpu.SMEM)] + [whole] * 4,
         out_specs=[whole] * 5,
-        scratch_shapes=[pltpu.VMEM((rows, width), bf16)] * 3 + [pltpu.SemaphoreType.DMA((3,))],
         compiler_params=params,
     )(doc_lengths, packet, queries, grad_out, forward_out)
     sent = pl.pallas_call(

time: 30.4 us -> 26.2 us (0.86)
  starting transfers between devices: 13.3 us -> 10.3 us
  Pallas kernels: 4.13 us -> 3.32 us
  other arithmetic: 1.49 us -> 0.96 us
    ppermute x2, starting transfers between devices: 9.42 us -> 5.68 us  [near_plan(): lax.ppermute(packet, 'ctx', [(i, (i + back) % count) for i in range(count)])]
    ppermute x2, waiting for transfers between devices: 0.01 us -> 1.7 us  [near_plan(): lax.ppermute(packet, 'ctx', [(i, (i + back) % count) for i in range(count)])]
    ppermute x3, waiting for transfers between devices: 8.69 us -> 7.23 us  [near_plan(): lax.ppermute(sent[k], 'ctx', [(i, (i + k) % count) for i in range(count)])]
    select_n x0 -> x1, other arithmetic: none -> 0.95 us  [near_plan(): jnp.where(mark < 0, jnp.pad(jnp.concatenate([key_head_rows, value_head_ro...]
    pallas_call x1, Pallas kernels: 1.8 us -> 1 us  [near_plan(): pl.pallas_call(functools.partial(own_kernel, doc_lengths.shape[0]), out_s...]
    concatenate x1 -> x0, other arithmetic: 0.79 us -> none  [near_plan(): jnp.concatenate([key_head_rows, value_head_rows, (owners[None, :] == jnp....]
    ppermute x3, starting transfers between devices: 3.88 us -> 4.67 us  [near_plan(): lax.ppermute(sent[k], 'ctx', [(i, (i + k) % count) for i in range(count)])]
    convert_element_type x1 -> x0, other arithmetic: 0.7 us -> none  [near_plan(): (owners[None, :] == jnp.arange(META, dtype=jnp.int32)[:, None]).astype(bf16)]
  transfers between devices with their start and end apart: 5 -> 5, of which waited for: 2 -> 3; matrix products, arithmetic and copies ran while one was open for 0% -> 0% of each run, Pallas kernels for 6% -> 4%
where the time goes in v3:
time: 26.2 us; the launch traced here: 26.1 us
  starting transfers between devices  10.3 us (39%)
  waiting for transfers between devices  8.92 us (34%)
  Pallas kernels  3.32 us (13%)
  local copies, waits for them, and re-layouts  1.82 us (7%)
  other arithmetic  0.96 us (4%)
  between operations  0.7 us (3%)
    ppermute x3, waiting for transfers between devices, near_plan(): lax.ppermute(sent[k], 'ctx', [(i, (i + k) % count) for i in range(count)])  7.23 us
    ppermute x2, starting transfers between devices, near_plan(): lax.ppermute(packet, 'ctx', [(i, (i + back) % count) for i in range(count)])  5.68 us
    ppermute x3, starting transfers between devices, near_plan(): lax.ppermute(sent[k], 'ctx', [(i, (i + k) % count) for i in range(count)])  4.67 us
    unnamed x8, local copies, waits for them, and re-layouts  1.82 us
    ppermute x2, waiting for transfers between devices, near_plan(): lax.ppermute(packet, 'ctx', [(i, (i + back) % count) for i in range(count)])  1.7 us
    pallas_call x1, Pallas kernels, near_plan(): pl.pallas_call(functools.partial(attend_kernel, count, halo), out_shape=[...  1.27 us
    pallas_call x1, Pallas kernels, near_plan(): pl.pallas_call(functools.partial(place_kernel, count, halo), out_shape=[j...  1.05 us
    pallas_call x1, Pallas kernels, near_plan(): pl.pallas_call(functools.partial(own_kernel, doc_lengths.shape[0]), out_s...  1 us
  transfers between devices with their start and end apart: 5, of which 3 were waited for; matrix products, arithmetic and copies ran while one was open for 0% of the time, Pallas kernels for 4%

profile of v3, /device:TPU:0, one launch (start us, length us, event | category | flops | bytes accessed | tf_op | source)
XLA Modules:
  0.0 26.1 jit_solution(6599475420000507254)
XLA Ops:
  0.6 0.0 copy-start
  0.7 0.0 copy-start.3
  0.7 0.9 %fusion.2.packet_ref.refs_5_ = bf16[272,128]{1,0:T(8,128)(2,1)S(1)} fusion(bf16[128,128]{1,0:T(8,128)(2,1)} %param.11, bf16[128,128]{1,0:T(8,128)(2,1)} %param.10, s32[128]{0:T(128)} %param.8, s32[272]{0:T(512)S(1)} %iota_add_fusion, pred[272]{0:T(512)(128)(4,1)S(1)} %broadcast_compare_fusion), kind=kLoop, calls=%fused_computation.4 | loop fusion | flops 348160 | bytes 137040 | tf_op jit(solution)/shard_map/jit(_where)/select_n | solution.py:453
  1.6 4.1 %collective-permute-start.1 = (bf16[272,128]{1,0:T(8,128)(2,1)S(1)}, bf16[272,128]{1,0:T(8,128)(2,1)S(1)}, u32[]{:S(2)}, u32[]{:S(2)}) collective-permute-start(bf16[272,128]{1,0:T(8,128)(2,1)S(1)} %fusion.2.packet_ref.refs_5_), channel_id=1, source_target_pairs={{0,8},{4,12},{8,0},{12,4},{1,9},{5,13},{9,1},{13,5},{2,10},{6,14},... | collective-permute-start | bytes 208904 | tf_op jit(solution)/shard_map/ppermute | solution.py:459
  5.7 1.6 %collective-permute-start = (bf16[272,128]{1,0:T(8,128)(2,1)S(1)}, bf16[272,128]{1,0:T(8,128)(2,1)S(1)}, u32[]{:S(2)}, u32[]{:S(2)}) collective-permute-start(bf16[272,128]{1,0:T(8,128)(2,1)S(1)} %fusion.2.packet_ref.refs_5_), channel_id=1, source_target_pairs={{0,4},{4,8},{8,12},{12,0},{1,5},{5,9},{9,13},{13,1},{2,6},{6,10},{... | collective-permute-start | bytes 208904 | tf_op jit(solution)/shard_map/ppermute | solution.py:459
  7.3 0.0 copy-done
  7.3 0.0 copy-done.3
  7.3 0.0 copy-start.1
  7.3 0.9 %copy-done.1 = bf16[128,512]{1,0:T(8,128)(2,1)S(1)} copy-done((bf16[128,512]{1,0:T(8,128)(2,1)S(1)}, bf16[128,512]{1,0:T(8,128)(2,1)}, u32[]{:S(2)}) %copy-start.1) | copy-done | bytes 131096
  8.2 0.0 copy-start.2
  8.2 0.9 %copy-done.2 = bf16[128,512]{1,0:T(8,128)(2,1)S(1)} copy-done((bf16[128,512]{1,0:T(8,128)(2,1)S(1)}, bf16[128,512]{1,0:T(8,128)(2,1)}, u32[]{:S(2)}) %copy-start.2) | copy-done | bytes 131096
  9.1 1.0 %shard_map.94 = (bf16[512,128]{1,0:T(8,128)(2,1)S(1)}, bf16[512,128]{1,0:T(8,128)(2,1)S(1)}, f32[128,512]{1,0:T(8,128)S(1)}, f32[128,512]{1,0:T(8,128)S(1)}, f32[8,512]{1,0:T(8,128)S(1)}) custom-call(s32[16]{0:T(128)S(1)} %copy-done.3, bf16[272,128]{1,0:T(8,128)(2,1)S(1)} %fusion.2.packet_ref.refs_5_, bf16[128,512]{1,0:T(8,128)(2,1)S(1)} %copy-done, ...), custom_call_target="tpu_custom_call" | custom-call | tf_op jit(solution)/shard_map/pallas_call | solution.py:462
  10.1 0.0 collective-permute-done.1.refs_7_
  10.1 1.7 %collective-permute-done.refs_6_ = bf16[272,128]{1,0:T(8,128)(2,1)S(1)} collective-permute-done((bf16[272,128]{1,0:T(8,128)(2,1)S(1)}, bf16[272,128]{1,0:T(8,128)(2,1)S(1)}, u32[]{:S(2)}, u32[]{:S(2)}) %collective-permute-start) | collective-permute-done | bytes 69664 | tf_op jit(solution)/shard_map/ppermute | solution.py:459
  11.8 1.3 %shard_map.95 = (bf16[528,128]{1,0:T(8,128)(2,1)S(1)}, bf16[528,128]{1,0:T(8,128)(2,1)S(1)}, bf16[528,128]{1,0:T(8,128)(2,1)S(1)}, bf16[528,128]{1,0:T(8,128)(2,1)S(1)}) custom-call(bf16[512,128]{1,0:T(8,128)(2,1)S(1)} %get-tuple-element.12.refs_0_, bf16[512,128]{1,0:T(8,128)(2,1)S(1)} %get-tuple-element.13.refs_1_, ...), custom_call_target="tpu_custom_call" | custom-call | tf_op jit(solution)/shard_map/pallas_call | solution.py:475
  13.1 0.1 collective-permute-start.2
  13.2 2.1 %collective-permute-start.3 = (bf16[528,128]{1,0:T(8,128)(2,1)S(1)}, bf16[528,128]{1,0:T(8,128)(2,1)S(1)}, u32[]{:S(2)}, u32[]{:S(2)}) collective-permute-start(bf16[528,128]{1,0:T(8,128)(2,1)S(1)} %get-tuple-element.19), channel_id=1, source_target_pairs={{0,8},{4,12},{8,0},{12,4},{1,9},{5,13},{9,1},{13,5},{2,10},{6,14},... | collective-permute-start | bytes 405512 | tf_op jit(solution)/shard_map/ppermute | solution.py:483
  15.2 2.6 %collective-permute-start.4 = (bf16[528,128]{1,0:T(8,128)(2,1)S(1)}, bf16[528,128]{1,0:T(8,128)(2,1)S(1)}, u32[]{:S(2)}, u32[]{:S(2)}) collective-permute-start(bf16[528,128]{1,0:T(8,128)(2,1)S(1)} %get-tuple-element.20), channel_id=1, source_target_pairs={{0,12},{4,0},{8,4},{12,8},{1,13},{5,1},{9,5},{13,9},{2,14},{6,2},{... | collective-permute-start | bytes 405512 | tf_op jit(solution)/shard_map/ppermute | solution.py:483
  17.8 3.7 %collective-permute-done.2.refs_1_ = bf16[528,128]{1,0:T(8,128)(2,1)S(1)} collective-permute-done((bf16[528,128]{1,0:T(8,128)(2,1)S(1)}, bf16[528,128]{1,0:T(8,128)(2,1)S(1)}, u32[]{:S(2)}, u32[]{:S(2)}) %collective-permute-start.2) | collective-permute-done | bytes 135200 | tf_op jit(solution)/shard_map/ppermute | solution.py:483
  21.4 3.6 %collective-permute-done.3.refs_2_ = bf16[528,128]{1,0:T(8,128)(2,1)S(1)} collective-permute-done((bf16[528,128]{1,0:T(8,128)(2,1)S(1)}, bf16[528,128]{1,0:T(8,128)(2,1)S(1)}, u32[]{:S(2)}, u32[]{:S(2)}) %collective-permute-start.3) | collective-permute-done | bytes 135200 | tf_op jit(solution)/shard_map/ppermute | solution.py:483
  25.0 0.0 collective-permute-done.4.refs_3_
  25.0 1.0 %shard_map.96 = (f32[128,512]{1,0:T(8,128)}, f32[128,128]{1,0:T(8,128)}, f32[128,128]{1,0:T(8,128)}) custom-call(bf16[528,128]{1,0:T(8,128)(2,1)S(1)} %get-tuple-element.17.refs_0_, bf16[528,128]{1,0:T(8,128)(2,1)S(1)} %collective-permute-done.2.refs_1_, bf16[528,128]{1,0:T(8,128)(2,1)S(1)} %collective-permute-done.3.refs_2_, ...), custom_call_target="tpu_custom_call" | custom-call | tf_op jit(solution)/shard_map/pallas_call | solution.py:486
  (2 shorter events, 0.0 us)
Async XLA Ops:
  0.6 6.7 %copy-start = (bf16[128,512]{1,0:T(8,128)(2,1)S(1)}, bf16[128,512]{1,0:T(8,128)(2,1)}, u32[]{:S(2)}) copy-start(bf16[128,512]{1,0:T(8,128)(2,1)} %query_ref.1) | copy-start | bytes 393220
  0.7 6.6 %copy-start.3 = (s32[16]{0:T(128)S(1)}, s32[16]{0:T(128)}, u32[]{:S(2)}) copy-start(s32[16]{0:T(128)} %doc_ref.1) | copy-start | bytes 196
  1.6 8.5 %collective-permute-start.1 = (bf16[272,128]{1,0:T(8,128)(2,1)S(1)}, bf16[272,128]{1,0:T(8,128)(2,1)S(1)}, u32[]{:S(2)}, u32[]{:S(2)}) collective-permute-start(bf16[272,128]{1,0:T(8,128)(2,1)S(1)} %fusion.2.packet_ref.refs_5_), channel_id=1, source_target_pairs={{0,8},{4,12},{8,0},{12,4},{1,9},{5,13},{9,1},{13,5},{2,10},{6,14},... | collective-permute-start | bytes 208904 | tf_op jit(solution)/shard_map/ppermute | solution.py:459
  5.7 6.1 %collective-permute-start = (bf16[272,128]{1,0:T(8,128)(2,1)S(1)}, bf16[272,128]{1,0:T(8,128)(2,1)S(1)}, u32[]{:S(2)}, u32[]{:S(2)}) collective-permute-start(bf16[272,128]{1,0:T(8,128)(2,1)S(1)} %fusion.2.packet_ref.refs_5_), channel_id=1, source_target_pairs={{0,4},{4,8},{8,12},{12,0},{1,5},{5,9},{9,13},{13,1},{2,6},{6,10},{... | collective-permute-start | bytes 208904 | tf_op jit(solution)/shard_map/ppermute | solution.py:459
  7.3 0.9 %copy-start.1 = (bf16[128,512]{1,0:T(8,128)(2,1)S(1)}, bf16[128,512]{1,0:T(8,128)(2,1)}, u32[]{:S(2)}) copy-start(bf16[128,512]{1,0:T(8,128)(2,1)} %grad_ref.1) | copy-start | bytes 393220
  8.2 0.9 %copy-start.2 = (bf16[128,512]{1,0:T(8,128)(2,1)S(1)}, bf16[128,512]{1,0:T(8,128)(2,1)}, u32[]{:S(2)}) copy-start(bf16[128,512]{1,0:T(8,128)(2,1)} %saved_ref.1) | copy-start | bytes 393220
  13.1 8.3 %collective-permute-start.2 = (bf16[528,128]{1,0:T(8,128)(2,1)S(1)}, bf16[528,128]{1,0:T(8,128)(2,1)S(1)}, u32[]{:S(2)}, u32[]{:S(2)}) collective-permute-start(bf16[528,128]{1,0:T(8,128)(2,1)S(1)} %get-tuple-element.18), channel_id=1, source_target_pairs={{0,4},{4,8},{8,12},{12,0},{1,5},{5,9},{9,13},{13,1},{2,6},{6,10},{... | collective-permute-start | bytes 405512 | tf_op jit(solution)/shard_map/ppermute | solution.py:483
  13.2 11.8 %collective-permute-start.3 = (bf16[528,128]{1,0:T(8,128)(2,1)S(1)}, bf16[528,128]{1,0:T(8,128)(2,1)S(1)}, u32[]{:S(2)}, u32[]{:S(2)}) collective-permute-start(bf16[528,128]{1,0:T(8,128)(2,1)S(1)} %get-tuple-element.19), channel_id=1, source_target_pairs={{0,8},{4,12},{8,0},{12,4},{1,9},{5,13},{9,1},{13,5},{2,10},{6,14},... | collective-permute-start | bytes 405512 | tf_op jit(solution)/shard_map/ppermute | solution.py:483
  15.2 9.8 %collective-permute-start.4 = (bf16[528,128]{1,0:T(8,128)(2,1)S(1)}, bf16[528,128]{1,0:T(8,128)(2,1)S(1)}, u32[]{:S(2)}, u32[]{:S(2)}) collective-permute-start(bf16[528,128]{1,0:T(8,128)(2,1)S(1)} %get-tuple-element.20), channel_id=1, source_target_pairs={{0,12},{4,0},{8,4},{12,8},{1,13},{5,1},{9,5},{13,9},{2,14},{6,2},{... | collective-permute-start | bytes 405512 | tf_op jit(solution)/shard_map/ppermute | solution.py:483

commit v4 on v3

--- a/solution.py
+++ b/solution.py
@@ -262,7 +262,22 @@
     return jnp.concatenate([matrix[:, h * width : (h + 1) * width] for h in range(heads)], axis=0)
 
 
+def runs_of(hot):
+    count, rows = hot.shape
+    counts = jnp.sum(hot, axis=1, keepdims=True)
+    owner = jnp.zeros((1, rows), jnp.int32)
+    earlier = jnp.zeros((1, rows), jnp.float32)
+    for p in range(count):
+        mine = hot[p : p + 1, :] > 0.0
+        owner = jnp.where(mine, p, owner)
+        for less in range(p):
+            earlier = earlier + jnp.where(mine, counts[less : less + 1, :], 0.0)
+    lane = lax.broadcasted_iota(jnp.int32, (1, rows), 1)
+    return owner, counts, lane - earlier.astype(jnp.int32)
+
+
 def own_kernel(
+    count,
     docs,
     doc_ref,
     packet_ref,
@@ -274,10 +289,12 @@
     raised_out,
     change_out,
     row_out,
+    spread_out,
 ):
     rows, width = query_ref.shape
     depth = packet_ref.shape[1]
     heads = width // depth
+    slot = 2 * rows // count
     index = lax.axis_index("ctx")
     lane = lax.broadcasted_iota(jnp.int32, (1, rows), 1)
     position = index * rows + lane
@@ -309,130 +326,140 @@
     row_out[2:3, :] = jnp.sum(raised, axis=0, keepdims=True)
     row_out[3:4, :] = jnp.concatenate([first.astype(jnp.float32)] * heads, axis=1)
     row_out[4:8, :] = jnp.zeros((4, width), jnp.float32)
+    owner, counts, rank = runs_of(packet_ref[2 * rows : 2 * rows + count, :].astype(jnp.float32))
+    ahead = lax.rem(owner - index + count, count)
+    spread_out[...] = one_hot(count * slot, ahead * slot + rank)
 
 
 def attend_kernel(count, halo, *refs):
-    query_ref, grad_ref, raised_ref, change_ref, row_ref = refs[:5]
-    own = refs[5]
-    near = refs[6 : 6 + halo]
-    outs = refs[6 + halo :]
+    query_ref, grad_ref, raised_ref, change_ref, row_ref, spread_ref = refs[:6]
+    own = refs[6]
+    before = refs[7 : 7 + halo][::-1]
+    weight_out, change_out = refs[7 + halo : 9 + halo]
+    outs = refs[9 + halo :]
     rows, columns = raised_ref.shape
     depth = query_ref.shape[1]
     heads = columns // rows
     slot = 2 * rows // count
     scale = 1.0 / math.sqrt(depth)
     index = lax.axis_index("ctx")
-    before = near[::-1]
     delta, top, total = (row_ref[n : n + 1, :] for n in range(3))
     first = row_ref[3:4, :].astype(jnp.int32)
 
     key_position = (index - halo) * rows + lax.broadcasted_iota(
         jnp.int32, (halo * rows, columns), 0
     )
-    queries = query_ref[...]
-    grads = grad_ref[...]
     keys = jnp.concatenate([n[0:rows, :] for n in before], axis=0)
     values = jnp.concatenate([n[rows : 2 * rows, :] for n in before], axis=0)
-    scores = jnp.where(key_position >= first, contract(keys, queries, 1, 1) * scale, NEG)
+    scores = contract(keys, query_ref[...], 1, 1) * scale
+    scores = jnp.where(key_position >= first, scores, NEG)
     new_top = jnp.maximum(top, jnp.max(scores, axis=0, keepdims=True))
     raised = jnp.exp(scores - new_top)
     shrink = jnp.exp(top - new_top)
     inverse = 1.0 / (total * shrink + jnp.sum(raised, axis=0, keepdims=True))
     weights = raised * inverse
     own_weights = raised_ref[...] * (shrink * inverse)
-    grad_scores = weights * (contract(values, grads, 1, 1) - delta)
-    own_grad_scores = own_weights * change_ref[...]
-    weights = jnp.concatenate([weights, own_weights], axis=0).astype(jnp.bfloat16)
-    grad_scores = jnp.concatenate([grad_scores, own_grad_scores], axis=0).astype(jnp.bfloat16)
+    changes = weights * (contract(values, grad_ref[...], 1, 1) - delta)
+    own_changes = own_weights * change_ref[...]
+    changes = jnp.concatenate([changes, own_changes], axis=0).astype(jnp.bfloat16)
+    weight_out[0 : halo * rows, :] = weights.astype(jnp.bfloat16)
+    weight_out[halo * rows :, :] = own_weights.astype(jnp.bfloat16)
+    change_out[...] = changes
     keys = jnp.concatenate([keys, own[0:rows, :]], axis=0)
-    value_parts = contract(weights, grads, 1, 0).astype(jnp.bfloat16)
-    key_parts = (contract(grad_scores, queries, 1, 0) * scale).astype(jnp.bfloat16)
-    query_grad = (contract(keys, grad_scores, 0, 0) * scale).astype(jnp.bfloat16)
-
-    lane = lax.broadcasted_iota(jnp.int32, (1, rows), 1)
+    query_grad = (contract(keys, changes, 0, 0) * scale).astype(jnp.bfloat16)
+
+    slots = contract(spread_ref[...], end_to_end(query_grad, heads), 1, 1).astype(jnp.bfloat16)
+    for k in range(count):
+        for h in range(heads):
+            outs[k][h * slot : (h + 1) * slot, :] = slots[
+                k * slot : (k + 1) * slot, h * depth : (h + 1) * depth
+            ]
+
+
+def key_kernel(count, halo, _, *refs):
+    query_ref, grad_ref, weight_ref, change_ref = refs[:4]
+    own = refs[4]
+    near = refs[5 : 5 + halo]
+    given_out = refs[5 + halo]
+    outs = refs[6 + halo :]
+    depth = query_ref.shape[1]
+    rows = weight_ref.shape[0] // (halo + 1)
+    index = lax.axis_index("ctx")
+    value_parts = contract(weight_ref[...], grad_ref[...], 1, 0).astype(jnp.bfloat16)
+    key_parts = contract(change_ref[...], query_ref[...], 1, 0) * (1.0 / math.sqrt(depth))
+    key_parts = key_parts.astype(jnp.bfloat16)
+
     filled = jnp.zeros((count, 1), jnp.float32)
     targets = []
-    for block, ref in enumerate(before + (own,)):
+    given = []
+    for block, ref in enumerate(near[::-1] + (own,)):
         hot = ref[2 * rows : 2 * rows + count, :].astype(jnp.float32)
-        hot = jnp.where(index - halo + block >= 0, hot, 0.0)
-        counts = jnp.sum(hot, axis=1, keepdims=True)
-        owner = jnp.zeros((1, rows), jnp.int32)
-        earlier = jnp.zeros((1, rows), jnp.float32)
+        owner, counts, rank = runs_of(hot)
+        mine = jnp.zeros((1, 1), jnp.float32)
         base = jnp.zeros((1, rows), jnp.float32)
         for p in range(count):
-            mine = hot[p : p + 1, :] > 0.0
-            owner = jnp.where(mine, p, owner)
-            base = jnp.where(mine, filled[p : p + 1, :], base)
-            for less in range(p):
-                earlier = earlier + jnp.where(mine, counts[less : less + 1, :], 0.0)
-        ahead = lax.rem(owner - index + count, count)
-        rank = lane - earlier.astype(jnp.int32)
-        target = ahead * rows + base.astype(jnp.int32) + rank
-        targets.append(jnp.where(index - halo + block >= 0, target, -1))
-        filled = filled + counts
-    spread = one_hot(count * slot, ahead * slot + rank)
-    query_slots = contract(spread, end_to_end(query_grad, heads), 1, 1).astype(jnp.bfloat16)
+            mine = jnp.where(index == p, counts[p : p + 1, :], mine)
+            base = base + jnp.where(owner == p, filled[p : p + 1, :], 0.0)
+        given.insert(0, mine)
+        target = lax.rem(owner - index + count, count) * rows + base.astype(jnp.int32) + rank
+        inside = index - halo + block >= 0
+        targets.append(jnp.where(inside, target, -1))
+        filled = filled + jnp.where(inside, counts, 0.0)
     spread = one_hot(count * rows, jnp.concatenate(targets, axis=1))
     key_slots = contract(spread, key_parts, 1, 0).astype(jnp.bfloat16)
     value_slots = contract(spread, value_parts, 1, 0).astype(jnp.bfloat16)
     for k in range(count):
-        out = outs[k]
-        for h in range(heads):
-            out[h * slot : (h + 1) * slot, :] = query_slots[
-                k * slot : (k + 1) * slot, h * depth : (h + 1) * depth
-            ]
-        at = heads * slot
-        out[at : at + rows, :] = key_slots[k * rows : (k + 1) * rows, :]
-        out[at + rows : at + 2 * rows, :] = value_slots[k * rows : (k + 1) * rows, :]
-        owner = lax.rem(index + k, count)
-        given = jnp.zeros((1, 1), jnp.float32)
-        for p in range(count):
-            given = jnp.where(owner == p, counts[p : p + 1, :], given)
-        out[at + 2 * rows :, :] = jnp.broadcast_to(given, (META, depth)).astype(jnp.bfloat16)
-
-
-def place_kernel(count, halo, *refs):
-    ins = refs[:count]
-    query_out, key_out, value_out = refs[count:]
-    rows, width = query_out.shape
-    depth = key_out.shape[1]
-    heads = width // depth
-    slot = 2 * rows // count
-    at = heads * slot
+        outs[k][0:rows, :] = key_slots[k * rows : (k + 1) * rows, :]
+        outs[k][rows:, :] = value_slots[k * rows : (k + 1) * rows, :]
+
+    if len(given) < count:
+        given.append(rows - sum(given))
+    for k in range(count):
+        given_out[k : k + 1, :] = jnp.broadcast_to(given[k], (1, depth))
+    given_out[count:, :] = jnp.zeros((8 - count, depth), jnp.float32)
+
+
+def starts_of(given_ref, count, back):
     index = lax.axis_index("ctx")
+    given = [given_ref[k : k + 1, 0:1].astype(jnp.int32) for k in range(count)]
     source = [lax.rem(index - k + count, count) for k in range(count)]
-    given = [
-        ref[at + 2 * rows : at + 2 * rows + 1, 0:1].astype(jnp.float32).astype(jnp.int32)
-        for ref in ins
-    ]
-    query_targets = []
-    key_targets = []
+    starts = []
     for k in range(count):
         start = jnp.zeros((1, 1), jnp.int32)
-        key_start = jnp.zeros((1, 1), jnp.int32)
         for other in range(count):
-            start = start + jnp.where(source[other] < source[k], given[other], 0)
-            key_start = key_start + jnp.where(source[other] < source[k] - halo, given[other], 0)
-        query_targets.append(start)
-        key_targets.append(key_start)
-
-    def spread_of(starts, size, limits):
-        lane = lax.broadcasted_iota(jnp.int32, (1, count * size), 1)
-        target = jnp.full((1, count * size), -1, jnp.int32)
-        for k in range(count):
-            step = lane - k * size
-            inside = (step >= 0) & (step < limits[k])
-            target = jnp.where(inside, starts[k] + step, target)
-        return one_hot(rows, target)
-
-    spread = spread_of(query_targets, slot, given)
-    for h in range(heads):
+            start = start + jnp.where(source[other] < source[k] - back, given[other], 0)
+        starts.append(start)
+    return starts, given
+
+
+def placement(rows, starts, size, limits):
+    lane = lax.broadcasted_iota(jnp.int32, (1, len(starts) * size), 1)
+    target = jnp.full(lane.shape, -1, jnp.int32)
+    for k, start in enumerate(starts):
+        step = lane - k * size
+        target = jnp.where((step >= 0) & (step < limits[k]), start + step, target)
+    return one_hot(rows, target)
+
+
+def place_queries_kernel(count, given_ref, *refs):
+    ins, out = refs[:count], refs[count]
+    rows, width = out.shape
+    slot = 2 * rows // count
+    depth = width * slot // ins[0].shape[0]
+    starts, given = starts_of(given_ref, count, 0)
+    spread = placement(rows, starts, slot, given)
+    for h in range(width // depth):
         taken = jnp.concatenate([ref[h * slot : (h + 1) * slot, :] for ref in ins], axis=0)
-        query_out[:, h * depth : (h + 1) * depth] = contract(spread, taken, 1, 0)
-    spread = spread_of(key_targets, rows, [rows] * count)
-    for n, out in enumerate((key_out, value_out)):
-        first = at + n * rows
-        taken = jnp.concatenate([ref[first : first + rows, :] for ref in ins], axis=0)
+        out[:, h * depth : (h + 1) * depth] = contract(spread, taken, 1, 0)
+
+
+def place_keys_kernel(count, halo, given_ref, *refs):
+    ins, outs = refs[:count], refs[count:]
+    rows = outs[0].shape[0]
+    starts, _ = starts_of(given_ref, count, halo)
+    spread = placement(rows, starts, rows, [rows] * count)
+    for n, out in enumerate(outs):
+        taken = jnp.concatenate([ref[n * rows : (n + 1) * rows, :] for ref in ins], axis=0)
         out[...] = contract(spread, taken, 1, 0)
 
 
@@ -441,13 +468,13 @@
     rows, width = queries.shape
     depth = key_head_rows.shape[1]
     heads = width // depth
+    bf16, f32 = jnp.bfloat16, jnp.float32
     columns = heads * rows
     halo = count // 2
     slot = 2 * rows // count
-    packet_rows = heads * slot + 2 * rows + META
+    spread_shape = jax.ShapeDtypeStruct((count * slot, rows), bf16)
     whole = pl.BlockSpec(memory_space=pltpu.VMEM)
     params = pltpu.CompilerParams(vmem_limit_bytes=40 * 1024 * 1024)
-    bf16, f32 = jnp.bfloat16, jnp.float32
 
     mark = lax.broadcasted_iota(jnp.int32, (2 * rows + META, rows), 0) - 2 * rows
     packet = jnp.where(
@@ -460,40 +487,59 @@
         for back in range(1, halo + 1)
     ]
     own = pl.pallas_call(
-        functools.partial(own_kernel, doc_lengths.shape[0]),
+        functools.partial(own_kernel, count, doc_lengths.shape[0]),
         out_shape=[
             jax.ShapeDtypeStruct((columns, depth), bf16),
             jax.ShapeDtypeStruct((columns, depth), bf16),
             jax.ShapeDtypeStruct((rows, columns), f32),
             jax.ShapeDtypeStruct((rows, columns), f32),
             jax.ShapeDtypeStruct((8, columns), f32),
+            spread_shape,
         ],
         in_specs=[pl.BlockSpec(memory_space=pltpu.SMEM)] + [whole] * 4,
-        out_specs=[whole] * 5,
+        out_specs=[whole] * 6,
         compiler_params=params,
     )(doc_lengths, packet, queries, grad_out, forward_out)
-    sent = pl.pallas_call(
+    weights, changes, *query_slots = pl.pallas_call(
         functools.partial(attend_kernel, count, halo),
-        out_shape=[jax.ShapeDtypeStruct((packet_rows, depth), bf16)] * count,
-        in_specs=[whole] * (6 + halo),
-        out_specs=[whole] * count,
+        out_shape=[jax.ShapeDtypeStruct(((halo + 1) * rows, columns), bf16)] * 2
+        + [jax.ShapeDtypeStruct((heads * slot, depth), bf16)] * count,
+        in_specs=[whole] * (7 + halo),
+        out_specs=[whole] * (2 + count),
         compiler_params=params,
     )(*own, packet, *near)
-    received = [sent[0]] + [
-        lax.ppermute(sent[k], "ctx", [(i, (i + k) % count) for i in range(count)])
-        for k in range(1, count)
-    ]
-    return pl.pallas_call(
-        functools.partial(place_kernel, count, halo),
-        out_shape=[
-            jax.ShapeDtypeStruct((rows, width), f32),
-            jax.ShapeDtypeStruct((rows, depth), f32),
-            jax.ShapeDtypeStruct((rows, depth), f32),
-        ],
-        in_specs=[whole] * count,
-        out_specs=[whole] * 3,
+
+    def exchanged(slots):
+        return [slots[0]] + [
+            lax.ppermute(slots[k], "ctx", [(i, (i + k) % count) for i in range(count)])
+            for k in range(1, count)
+        ]
+
+    query_slots = exchanged(query_slots)
+    given, *key_slots = pl.pallas_call(
+        functools.partial(key_kernel, count, halo),
+        out_shape=[jax.ShapeDtypeStruct((8, depth), f32)]
+        + [jax.ShapeDtypeStruct((2 * rows, depth), bf16)] * count,
+        in_specs=[pl.BlockSpec(memory_space=pl.ANY)] + [whole] * (5 + halo),
+        out_specs=[whole] * (1 + count),
         compiler_params=params,
-    )(*received)
+    )(query_slots[1], own[0], own[1], weights, changes, packet, *near)
+    key_slots = exchanged(key_slots)
+    grad_queries = pl.pallas_call(
+        functools.partial(place_queries_kernel, count),
+        out_shape=jax.ShapeDtypeStruct((rows, width), f32),
+        in_specs=[whole] * (1 + count),
+        out_specs=whole,
+        compiler_params=params,
+    )(given, *query_slots)
+    key_grads, value_grads = pl.pallas_call(
+        functools.partial(place_keys_kernel, count, halo),
+        out_shape=[jax.ShapeDtypeStruct((rows, depth), f32)] * 2,
+        in_specs=[whole] * (1 + count),
+        out_specs=[whole] * 2,
+        compiler_params=params,
+    )(given, *key_slots)
+    return grad_queries, key_grads, value_grads
 
 
 def per_device(*args):

time: 26.2 us -> 28.2 us (1.076)
  starting transfers between devices: 10.3 us -> 14.9 us
  waiting for transfers between devices: 8.92 us -> 5.06 us
  Pallas kernels: 3.32 us -> 4.54 us
    ppermute x3 -> x6, starting transfers between devices: 4.67 us -> 9.22 us  [exchanged(): lax.ppermute(slots[k], 'ctx', [(i, (i + k) % count) for i in range(count)])]
    ppermute x3 -> x6, waiting for transfers between devices: 7.23 us -> 3.36 us  [exchanged(): lax.ppermute(slots[k], 'ctx', [(i, (i + k) % count) for i in range(count)])]
    pallas_call x2 -> x4, Pallas kernels: 2.05 us -> 3.64 us  [the longest x1 1.01 us: near_plan(): pl.pallas_call(functools.partial(own_kernel, count, doc_lengths.shape[0])...]
    pallas_call x1, Pallas kernels: 1.27 us -> 0.9 us  [near_plan(): pl.pallas_call(functools.partial(attend_kernel, count, halo), out_shape=[...]
  transfers between devices with their start and end apart: 5 -> 8, of which waited for: 3 -> 4; matrix products, arithmetic and copies ran while one was open for 0% -> 0% of each run, Pallas kernels for 4% -> 10%
where the time goes in v4:
time: 28.2 us; the launch traced here: 28 us
  starting transfers between devices  14.9 us (53%)
  waiting for transfers between devices  5.06 us (18%)
  Pallas kernels  4.54 us (16%)
  local copies, waits for them, and re-layouts  1.82 us (6%)
  other arithmetic  0.96 us (3%)
  between operations  0.72 us (3%)
    ppermute x6, starting transfers between devices, exchanged(): lax.ppermute(slots[k], 'ctx', [(i, (i + k) % count) for i in range(count)])  9.22 us
    ppermute x2, starting transfers between devices, near_plan(): lax.ppermute(packet, 'ctx', [(i, (i + back) % count) for i in range(count)])  5.68 us
    ppermute x6, waiting for transfers between devices, exchanged(): lax.ppermute(slots[k], 'ctx', [(i, (i + k) % count) for i in range(count)])  3.36 us
    unnamed x8, local copies, waits for them, and re-layouts  1.82 us
    ppermute x2, waiting for transfers between devices, near_plan(): lax.ppermute(packet, 'ctx', [(i, (i + back) % count) for i in range(count)])  1.69 us
    pallas_call x1, Pallas kernels, near_plan(): pl.pallas_call(functools.partial(own_kernel, count, doc_lengths.shape[0])...  1.01 us
    pallas_call x1, Pallas kernels, near_plan(): pl.pallas_call(functools.partial(place_queries_kernel, count), out_shape=...  1 us
    select_n x1, other arithmetic, near_plan(): jnp.where(mark < 0, jnp.pad(jnp.concatenate([key_head_rows, value_head_ro...  0.95 us
  transfers between devices with their start and end apart: 8, of which 4 were waited for; matrix products, arithmetic and copies ran while one was open for 0% of the time, Pallas kernels for 10%

profile of v4, /device:TPU:0, one launch (start us, length us, event | category | flops | bytes accessed | tf_op | source)
XLA Modules:
  0.0 28.0 jit_solution(14165594483793243913)
XLA Ops:
  0.7 0.0 copy-start.3
  0.7 0.9 %fusion.2.packet_ref.refs_6_.refs_4_ = bf16[272,128]{1,0:T(8,128)(2,1)S(1)} fusion(bf16[128,128]{1,0:T(8,128)(2,1)} %param.11, bf16[128,128]{1,0:T(8,128)(2,1)} %param.10, s32[128]{0:T(128)} %param.8, s32[272]{0:T(512)S(1)} %iota_add_fusion, pred[272]{0:T(512)(128)(4,1)S(1)} %broadcast_compare_fusion), kind=kLoop, calls=%fused_computation.4 | loop fusion | flops 348160 | bytes 137040 | tf_op jit(solution)/shard_map/jit(_where)/select_n | solution.py:480
  1.6 4.1 %collective-permute-start.1 = (bf16[272,128]{1,0:T(8,128)(2,1)S(1)}, bf16[272,128]{1,0:T(8,128)(2,1)S(1)}, u32[]{:S(2)}, u32[]{:S(2)}) collective-permute-start(bf16[272,128]{1,0:T(8,128)(2,1)S(1)} %fusion.2.packet_ref.refs_6_.refs_4_), channel_id=1, source_target_pairs={{0,8},{4,12},{8,0},{12,4},{1,9},{5,13},{9,1},{13,5},{2,10},{6,14},... | collective-permute-start | bytes 208904 | tf_op jit(solution)/shard_map/ppermute | solution.py:486
  5.7 1.6 %collective-permute-start = (bf16[272,128]{1,0:T(8,128)(2,1)S(1)}, bf16[272,128]{1,0:T(8,128)(2,1)S(1)}, u32[]{:S(2)}, u32[]{:S(2)}) collective-permute-start(bf16[272,128]{1,0:T(8,128)(2,1)S(1)} %fusion.2.packet_ref.refs_6_.refs_4_), channel_id=1, source_target_pairs={{0,4},{4,8},{8,12},{12,0},{1,5},{5,9},{9,13},{13,1},{2,6},{6,10},{... | collective-permute-start | bytes 208904 | tf_op jit(solution)/shard_map/ppermute | solution.py:486
  7.3 0.9 %copy-done.1 = bf16[128,512]{1,0:T(8,128)(2,1)S(1)} copy-done((bf16[128,512]{1,0:T(8,128)(2,1)S(1)}, bf16[128,512]{1,0:T(8,128)(2,1)}, u32[]{:S(2)}) %copy-start.1) | copy-done | bytes 131096
  8.2 0.9 %copy-done.2 = bf16[128,512]{1,0:T(8,128)(2,1)S(1)} copy-done((bf16[128,512]{1,0:T(8,128)(2,1)S(1)}, bf16[128,512]{1,0:T(8,128)(2,1)}, u32[]{:S(2)}) %copy-start.2) | copy-done | bytes 131096
  9.1 1.0 %shard_map.94 = (bf16[512,128]{1,0:T(8,128)(2,1)S(1)}, bf16[512,128]{1,0:T(8,128)(2,1)S(1)}, f32[128,512]{1,0:T(8,128)S(1)}, f32[128,512]{1,0:T(8,128)S(1)}, f32...) custom-call(s32[16]{0:T(128)S(1)} %copy-done.3, bf16[272,128]{1,0:T(8,128)(2,1)S(1)} %fusion.2.packet_ref.refs_6_.refs_4_, ...), custom_call_target="tpu_custom_call" | custom-call | tf_op jit(solution)/shard_map/pallas_call | solution.py:489
  10.1 0.0 collective-permute-done.1.refs_8_.refs_6_
  10.1 1.7 %collective-permute-done.refs_7_.refs_5_ = bf16[272,128]{1,0:T(8,128)(2,1)S(1)} collective-permute-done((bf16[272,128]{1,0:T(8,128)(2,1)S(1)}, bf16[272,128]{1,0:T(8,128)(2,1)S(1)}, u32[]{:S(2)}, u32[]{:S(2)}) %collective-permute-start) | collective-permute-done | bytes 69664 | tf_op jit(solution)/shard_map/ppermute | solution.py:486
  11.8 0.9 %shard_map.95 = (bf16[384,512]{1,0:T(8,128)(2,1)S(1)}, bf16[384,512]{1,0:T(8,128)(2,1)S(1)}, bf16[256,128]{1,0:T(8,128)(2,1)S(1)}, bf16[256,128]{1,0:T(8,128)(2,...) custom-call(bf16[512,128]{1,0:T(8,128)(2,1)S(1)} %get-tuple-element.22.refs_0_, ...), custom_call_target="tpu_custom_call" | custom-call | tf_op jit(solution)/shard_map/pallas_call | solution.py:503
  12.7 0.1 collective-permute-start.2
  12.8 2.1 %collective-permute-start.3 = (bf16[256,128]{1,0:T(8,128)(2,1)S(1)}, bf16[256,128]{1,0:T(8,128)(2,1)S(1)}, u32[]{:S(2)}, u32[]{:S(2)}) collective-permute-start(bf16[256,128]{1,0:T(8,128)(2,1)S(1)} %get-tuple-element.33), channel_id=1, source_target_pairs={{0,8},{4,12},{8,0},{12,4},{1,9},{5,13},{9,1},{13,5},{2,10},{6,14},... | collective-permute-start | bytes 196616 | tf_op jit(solution)/shard_map/ppermute | solution.py:514
  14.9 2.5 %collective-permute-start.4 = (bf16[256,128]{1,0:T(8,128)(2,1)S(1)}, bf16[256,128]{1,0:T(8,128)(2,1)S(1)}, u32[]{:S(2)}, u32[]{:S(2)}) collective-permute-start(bf16[256,128]{1,0:T(8,128)(2,1)S(1)} %get-tuple-element.34), channel_id=1, source_target_pairs={{0,12},{4,0},{8,4},{12,8},{1,13},{5,1},{9,5},{13,9},{2,14},{6,2},{... | collective-permute-start | bytes 196616 | tf_op jit(solution)/shard_map/ppermute | solution.py:514
  17.4 2.1 %collective-permute-done.2._.refs_1_ = bf16[256,128]{1,0:T(8,128)(2,1)S(1)} collective-permute-done((bf16[256,128]{1,0:T(8,128)(2,1)S(1)}, bf16[256,128]{1,0:T(8,128)(2,1)S(1)}, u32[]{:S(2)}, u32[]{:S(2)}) %collective-permute-start.2) | collective-permute-done | bytes 65568 | tf_op jit(solution)/shard_map/ppermute | solution.py:514
  19.5 0.7 %shard_map.96 = (f32[8,128]{1,0:T(8,128)S(1)}, bf16[256,128]{1,0:T(8,128)(2,1)S(1)}, bf16[256,128]{1,0:T(8,128)(2,1)S(1)}, bf16[256,128]{1,0:T(8,128)(2,1)S(1)}, bf16[256,128]{1,0:T(8,128)(2,1)S(1)}) custom-call(bf16[256,128]{1,0:T(8,128)(2,1)S(1)} %collective-permute-done.2._.refs_1_, bf16[512,128]{1,0:T(8,128)(2,1)S(1)} %get-tuple-element.22.refs_0_, ...), custom_call_target="tpu_custom_call" | custom-call | tf_op jit(solution)/shard_map/pallas_call | solution.py:519
  20.2 0.1 collective-permute-start.5
  20.3 1.7 %collective-permute-start.6 = (bf16[256,128]{1,0:T(8,128)(2,1)S(1)}, bf16[256,128]{1,0:T(8,128)(2,1)S(1)}, u32[]{:S(2)}, u32[]{:S(2)}) collective-permute-start(bf16[256,128]{1,0:T(8,128)(2,1)S(1)} %get-tuple-element.37), channel_id=1, source_target_pairs={{0,8},{4,12},{8,0},{12,4},{1,9},{5,13},{9,1},{13,5},{2,10},{6,14},... | collective-permute-start | bytes 196616 | tf_op jit(solution)/shard_map/ppermute | solution.py:514
  22.0 2.8 %collective-permute-start.7 = (bf16[256,128]{1,0:T(8,128)(2,1)S(1)}, bf16[256,128]{1,0:T(8,128)(2,1)S(1)}, u32[]{:S(2)}, u32[]{:S(2)}) collective-permute-start(bf16[256,128]{1,0:T(8,128)(2,1)S(1)} %get-tuple-element.38), channel_id=1, source_target_pairs={{0,12},{4,0},{8,4},{12,8},{1,13},{5,1},{9,5},{13,9},{2,14},{6,2},{... | collective-permute-start | bytes 196616 | tf_op jit(solution)/shard_map/ppermute | solution.py:514
  24.8 0.0 collective-permute-done.3.refs_2_
  24.8 1.0 %shard_map.97 = f32[128,512]{1,0:T(8,128)} custom-call(f32[8,128]{1,0:T(8,128)S(1)} %get-tuple-element.31.given_ref, bf16[256,128]{1,0:T(8,128)(2,1)S(1)} %get-tuple-element.32.refs_0_, bf16[256,128]{1,0:T(8,128)(2,1)S(1)} %collective-permute-done.2._.refs_1_, bf16[256,128]{1,0:T(8,128)(2,1)S(1)} %collective-permute-done.3.refs_2_, ...), custom_call_target="tpu_custom_call" | custom-call | tf_op jit(solution)/shard_map/pallas_call | solution.py:528
  25.8 0.6 %collective-permute-done.5.refs_1_ = bf16[256,128]{1,0:T(8,128)(2,1)S(1)} collective-permute-done((bf16[256,128]{1,0:T(8,128)(2,1)S(1)}, bf16[256,128]{1,0:T(8,128)(2,1)S(1)}, u32[]{:S(2)}, u32[]{:S(2)}) %collective-permute-start.5) | collective-permute-done | bytes 65568 | tf_op jit(solution)/shard_map/ppermute | solution.py:514
  26.4 0.0 collective-permute-done.6.refs_2_
  26.4 0.7 %collective-permute-done.7.refs_3_ = bf16[256,128]{1,0:T(8,128)(2,1)S(1)} collective-permute-done((bf16[256,128]{1,0:T(8,128)(2,1)S(1)}, bf16[256,128]{1,0:T(8,128)(2,1)S(1)}, u32[]{:S(2)}, u32[]{:S(2)}) %collective-permute-start.7) | collective-permute-done | bytes 65568 | tf_op jit(solution)/shard_map/ppermute | solution.py:514
  27.1 0.9 %shard_map.98 = (f32[128,128]{1,0:T(8,128)}, f32[128,128]{1,0:T(8,128)}) custom-call(f32[8,128]{1,0:T(8,128)S(1)} %get-tuple-element.31.given_ref, bf16[256,128]{1,0:T(8,128)(2,1)S(1)} %get-tuple-element.35.refs_0_, bf16[256,128]{1,0:T(8,128)(2,1)S(1)} %collective-permute-done.5.refs_1_, bf16[256,128]{1,0:T(8,128)(2,1)S(1)} %collective-permute-done.6.refs_2_, ...), custom_call_target="tpu_custom_call" | custom-call | tf_op jit(solution)/shard_map/pallas_call | solution.py:535
  (8 shorter events, 0.0 us)
Async XLA Ops:
  0.6 6.7 %copy-start = (bf16[128,512]{1,0:T(8,128)(2,1)S(1)}, bf16[128,512]{1,0:T(8,128)(2,1)}, u32[]{:S(2)}) copy-start(bf16[128,512]{1,0:T(8,128)(2,1)} %query_ref.1) | copy-start | bytes 393220
  0.7 6.6 %copy-start.3 = (s32[16]{0:T(128)S(1)}, s32[16]{0:T(128)}, u32[]{:S(2)}) copy-start(s32[16]{0:T(128)} %doc_ref.1) | copy-start | bytes 196
  1.6 8.5 %collective-permute-start.1 = (bf16[272,128]{1,0:T(8,128)(2,1)S(1)}, bf16[272,128]{1,0:T(8,128)(2,1)S(1)}, u32[]{:S(2)}, u32[]{:S(2)}) collective-permute-start(bf16[272,128]{1,0:T(8,128)(2,1)S(1)} %fusion.2.packet_ref.refs_6_.refs_4_), channel_id=1, source_target_pairs={{0,8},{4,12},{8,0},{12,4},{1,9},{5,13},{9,1},{13,5},{2,10},{6,14},... | collective-permute-start | bytes 208904 | tf_op jit(solution)/shard_map/ppermute | solution.py:486
  5.7 6.1 %collective-permute-start = (bf16[272,128]{1,0:T(8,128)(2,1)S(1)}, bf16[272,128]{1,0:T(8,128)(2,1)S(1)}, u32[]{:S(2)}, u32[]{:S(2)}) collective-permute-start(bf16[272,128]{1,0:T(8,128)(2,1)S(1)} %fusion.2.packet_ref.refs_6_.refs_4_), channel_id=1, source_target_pairs={{0,4},{4,8},{8,12},{12,0},{1,5},{5,9},{9,13},{13,1},{2,6},{6,10},{... | collective-permute-start | bytes 208904 | tf_op jit(solution)/shard_map/ppermute | solution.py:486
  7.3 0.9 %copy-start.1 = (bf16[128,512]{1,0:T(8,128)(2,1)S(1)}, bf16[128,512]{1,0:T(8,128)(2,1)}, u32[]{:S(2)}) copy-start(bf16[128,512]{1,0:T(8,128)(2,1)} %grad_ref.1) | copy-start | bytes 393220
  8.2 0.9 %copy-start.2 = (bf16[128,512]{1,0:T(8,128)(2,1)S(1)}, bf16[128,512]{1,0:T(8,128)(2,1)}, u32[]{:S(2)}) copy-start(bf16[128,512]{1,0:T(8,128)(2,1)} %saved_ref.1) | copy-start | bytes 393220
  12.7 6.8 %collective-permute-start.2 = (bf16[256,128]{1,0:T(8,128)(2,1)S(1)}, bf16[256,128]{1,0:T(8,128)(2,1)S(1)}, u32[]{:S(2)}, u32[]{:S(2)}) collective-permute-start(bf16[256,128]{1,0:T(8,128)(2,1)S(1)} %get-tuple-element.28), channel_id=1, source_target_pairs={{0,4},{4,8},{8,12},{12,0},{1,5},{5,9},{9,13},{13,1},{2,6},{6,10},{... | collective-permute-start | bytes 196616 | tf_op jit(solution)/shard_map/ppermute | solution.py:514
  12.8 12.0 %collective-permute-start.3 = (bf16[256,128]{1,0:T(8,128)(2,1)S(1)}, bf16[256,128]{1,0:T(8,128)(2,1)S(1)}, u32[]{:S(2)}, u32[]{:S(2)}) collective-permute-start(bf16[256,128]{1,0:T(8,128)(2,1)S(1)} %get-tuple-element.33), channel_id=1, source_target_pairs={{0,8},{4,12},{8,0},{12,4},{1,9},{5,13},{9,1},{13,5},{2,10},{6,14},... | collective-permute-start | bytes 196616 | tf_op jit(solution)/shard_map/ppermute | solution.py:514
  14.9 9.9 %collective-permute-start.4 = (bf16[256,128]{1,0:T(8,128)(2,1)S(1)}, bf16[256,128]{1,0:T(8,128)(2,1)S(1)}, u32[]{:S(2)}, u32[]{:S(2)}) collective-permute-start(bf16[256,128]{1,0:T(8,128)(2,1)S(1)} %get-tuple-element.34), channel_id=1, source_target_pairs={{0,12},{4,0},{8,4},{12,8},{1,13},{5,1},{9,5},{13,9},{2,14},{6,2},{... | collective-permute-start | bytes 196616 | tf_op jit(solution)/shard_map/ppermute | solution.py:514
  20.2 6.1 %collective-permute-start.5 = (bf16[256,128]{1,0:T(8,128)(2,1)S(1)}, bf16[256,128]{1,0:T(8,128)(2,1)S(1)}, u32[]{:S(2)}, u32[]{:S(2)}) collective-permute-start(bf16[256,128]{1,0:T(8,128)(2,1)S(1)} %get-tuple-element.36), channel_id=1, source_target_pairs={{0,4},{4,8},{8,12},{12,0},{1,5},{5,9},{9,13},{13,1},{2,6},{6,10},{... | collective-permute-start | bytes 196616 | tf_op jit(solution)/shard_map/ppermute | solution.py:514
  20.3 6.1 %collective-permute-start.6 = (bf16[256,128]{1,0:T(8,128)(2,1)S(1)}, bf16[256,128]{1,0:T(8,128)(2,1)S(1)}, u32[]{:S(2)}, u32[]{:S(2)}) collective-permute-start(bf16[256,128]{1,0:T(8,128)(2,1)S(1)} %get-tuple-element.37), channel_id=1, source_target_pairs={{0,8},{4,12},{8,0},{12,4},{1,9},{5,13},{9,1},{13,5},{2,10},{6,14},... | collective-permute-start | bytes 196616 | tf_op jit(solution)/shard_map/ppermute | solution.py:514
  22.0 5.1 %collective-permute-start.7 = (bf16[256,128]{1,0:T(8,128)(2,1)S(1)}, bf16[256,128]{1,0:T(8,128)(2,1)S(1)}, u32[]{:S(2)}, u32[]{:S(2)}) collective-permute-start(bf16[256,128]{1,0:T(8,128)(2,1)S(1)} %get-tuple-element.38), channel_id=1, source_target_pairs={{0,12},{4,0},{8,4},{12,8},{1,13},{5,1},{9,5},{13,9},{2,14},{6,2},{... | collective-permute-start | bytes 196616 | tf_op jit(solution)/shard_map/ppermute | solution.py:514

commit v5 on v3

--- a/solution.py
+++ b/solution.py
@@ -262,7 +262,22 @@
     return jnp.concatenate([matrix[:, h * width : (h + 1) * width] for h in range(heads)], axis=0)
 
 
+def runs_of(hot):
+    count, rows = hot.shape
+    counts = jnp.sum(hot, axis=1, keepdims=True)
+    owner = jnp.zeros((1, rows), jnp.int32)
+    earlier = jnp.zeros((1, rows), jnp.float32)
+    for p in range(count):
+        mine = hot[p : p + 1, :] > 0.0
+        owner = jnp.where(mine, p, owner)
+        for less in range(p):
+            earlier = earlier + jnp.where(mine, counts[less : less + 1, :], 0.0)
+    lane = lax.broadcasted_iota(jnp.int32, (1, rows), 1)
+    return owner, counts, lane - earlier.astype(jnp.int32)
+
+
 def own_kernel(
+    count,
     docs,
     doc_ref,
     packet_ref,
@@ -274,10 +289,12 @@
     raised_out,
     change_out,
     row_out,
+    spread_out,
 ):
     rows, width = query_ref.shape
     depth = packet_ref.shape[1]
     heads = width // depth
+    slot = 2 * rows // count
     index = lax.axis_index("ctx")
     lane = lax.broadcasted_iota(jnp.int32, (1, rows), 1)
     position = index * rows + lane
@@ -309,28 +326,30 @@
     row_out[2:3, :] = jnp.sum(raised, axis=0, keepdims=True)
     row_out[3:4, :] = jnp.concatenate([first.astype(jnp.float32)] * heads, axis=1)
     row_out[4:8, :] = jnp.zeros((4, width), jnp.float32)
+    owner, counts, rank = runs_of(packet_ref[2 * rows : 2 * rows + count, :].astype(jnp.float32))
+    ahead = lax.rem(owner - index + count, count)
+    spread_out[...] = one_hot(count * slot, ahead * slot + rank)
 
 
 def attend_kernel(count, halo, *refs):
-    query_ref, grad_ref, raised_ref, change_ref, row_ref = refs[:5]
-    own = refs[5]
-    near = refs[6 : 6 + halo]
-    outs = refs[6 + halo :]
+    query_ref, grad_ref, raised_ref, change_ref, row_ref, spread_ref = refs[:6]
+    own = refs[6]
+    before = refs[7 : 7 + halo]
+    outs = refs[7 + halo :]
     rows, columns = raised_ref.shape
     depth = query_ref.shape[1]
     heads = columns // rows
     slot = 2 * rows // count
     scale = 1.0 / math.sqrt(depth)
     index = lax.axis_index("ctx")
-    before = near[::-1]
     delta, top, total = (row_ref[n : n + 1, :] for n in range(3))
     first = row_ref[3:4, :].astype(jnp.int32)
+    queries = query_ref[...]
+    grads = grad_ref[...]
 
     key_position = (index - halo) * rows + lax.broadcasted_iota(
         jnp.int32, (halo * rows, columns), 0
     )
-    queries = query_ref[...]
-    grads = grad_ref[...]
     keys = jnp.concatenate([n[0:rows, :] for n in before], axis=0)
     values = jnp.concatenate([n[rows : 2 * rows, :] for n in before], axis=0)
     scores = jnp.where(key_position >= first, contract(keys, queries, 1, 1) * scale, NEG)
@@ -340,100 +359,89 @@
     inverse = 1.0 / (total * shrink + jnp.sum(raised, axis=0, keepdims=True))
     weights = raised * inverse
     own_weights = raised_ref[...] * (shrink * inverse)
-    grad_scores = weights * (contract(values, grads, 1, 1) - delta)
-    own_grad_scores = own_weights * change_ref[...]
+    changes = weights * (contract(values, grads, 1, 1) - delta)
+    own_changes = own_weights * change_ref[...]
     weights = jnp.concatenate([weights, own_weights], axis=0).astype(jnp.bfloat16)
-    grad_scores = jnp.concatenate([grad_scores, own_grad_scores], axis=0).astype(jnp.bfloat16)
+    changes = jnp.concatenate([changes, own_changes], axis=0).astype(jnp.bfloat16)
     keys = jnp.concatenate([keys, own[0:rows, :]], axis=0)
+    query_grad = (contract(keys, changes, 0, 0) * scale).astype(jnp.bfloat16)
     value_parts = contract(weights, grads, 1, 0).astype(jnp.bfloat16)
-    key_parts = (contract(grad_scores, queries, 1, 0) * scale).astype(jnp.bfloat16)
-    query_grad = (contract(keys, grad_scores, 0, 0) * scale).astype(jnp.bfloat16)
-
-    lane = lax.broadcasted_iota(jnp.int32, (1, rows), 1)
+    key_parts = (contract(changes, queries, 1, 0) * scale).astype(jnp.bfloat16)
+
+    query_slots = contract(spread_ref[...], end_to_end(query_grad, heads), 1, 1)
+    query_slots = query_slots.astype(jnp.bfloat16)
     filled = jnp.zeros((count, 1), jnp.float32)
     targets = []
     for block, ref in enumerate(before + (own,)):
-        hot = ref[2 * rows : 2 * rows + count, :].astype(jnp.float32)
-        hot = jnp.where(index - halo + block >= 0, hot, 0.0)
-        counts = jnp.sum(hot, axis=1, keepdims=True)
-        owner = jnp.zeros((1, rows), jnp.int32)
-        earlier = jnp.zeros((1, rows), jnp.float32)
+        owner, counts, rank = runs_of(ref[2 * rows : 2 * rows + count, :].astype(jnp.float32))
         base = jnp.zeros((1, rows), jnp.float32)
         for p in range(count):
-            mine = hot[p : p + 1, :] > 0.0
-            owner = jnp.where(mine, p, owner)
-            base = jnp.where(mine, filled[p : p + 1, :], base)
-            for less in range(p):
-                earlier = earlier + jnp.where(mine, counts[less : less + 1, :], 0.0)
-        ahead = lax.rem(owner - index + count, count)
-        rank = lane - earlier.astype(jnp.int32)
-        target = ahead * rows + base.astype(jnp.int32) + rank
-        targets.append(jnp.where(index - halo + block >= 0, target, -1))
-        filled = filled + counts
-    spread = one_hot(count * slot, ahead * slot + rank)
-    query_slots = contract(spread, end_to_end(query_grad, heads), 1, 1).astype(jnp.bfloat16)
+            base = base + jnp.where(owner == p, filled[p : p + 1, :], 0.0)
+        target = lax.rem(owner - index + count, count) * rows + base.astype(jnp.int32) + rank
+        inside = index - halo + block >= 0
+        targets.append(jnp.where(inside, target, -1))
+        filled = filled + jnp.where(inside, counts, 0.0)
     spread = one_hot(count * rows, jnp.concatenate(targets, axis=1))
     key_slots = contract(spread, key_parts, 1, 0).astype(jnp.bfloat16)
     value_slots = contract(spread, value_parts, 1, 0).astype(jnp.bfloat16)
+    at = heads * slot
     for k in range(count):
         out = outs[k]
         for h in range(heads):
             out[h * slot : (h + 1) * slot, :] = query_slots[
                 k * slot : (k + 1) * slot, h * depth : (h + 1) * depth
             ]
-        at = heads * slot
         out[at : at + rows, :] = key_slots[k * rows : (k + 1) * rows, :]
-        out[at + rows : at + 2 * rows, :] = value_slots[k * rows : (k + 1) * rows, :]
-        owner = lax.rem(index + k, count)
-        given = jnp.zeros((1, 1), jnp.float32)
+        out[at + rows :, :] = value_slots[k * rows : (k + 1) * rows, :]
+
+
+def order_kernel(count, halo, _, *refs):
+    packets = refs[:1] + refs[1 : 1 + halo][::-1]
+    query_out, key_out = refs[1 + halo :]
+    rows = query_out.shape[0]
+    index = lax.axis_index("ctx")
+    given = []
+    for ref in packets:
+        hot = ref[2 * rows : 2 * rows + count, :].astype(jnp.float32)
+        counts = jnp.sum(hot, axis=1, keepdims=True)
+        mine = jnp.zeros((1, 1), jnp.float32)
         for p in range(count):
-            given = jnp.where(owner == p, counts[p : p + 1, :], given)
-        out[at + 2 * rows :, :] = jnp.broadcast_to(given, (META, depth)).astype(jnp.bfloat16)
-
-
-def place_kernel(count, halo, *refs):
+            mine = jnp.where(index == p, counts[p : p + 1, :], mine)
+        given.append(mine.astype(jnp.int32))
+    if len(given) < count:
+        given.append(rows - sum(given))
+    source = [lax.rem(index - k + count, count) for k in range(count)]
+
+    def placement(size, back, whole):
+        lane = lax.broadcasted_iota(jnp.int32, (1, count * size), 1)
+        target = jnp.full(lane.shape, -1, jnp.int32)
+        for k in range(count):
+            start = jnp.zeros((1, 1), jnp.int32)
+            for other in range(count):
+                start = start + jnp.where(source[other] < source[k] - back, given[other], 0)
+            step = lane - k * size
+            inside = (step >= 0) & (step < (size if whole else given[k]))
+            target = jnp.where(inside, start + step, target)
+        return one_hot(rows, target)
+
+    query_out[...] = placement(2 * rows // count, 0, False)
+    key_out[...] = placement(rows, halo, True)
+
+
+def place_kernel(count, query_spread, key_spread, *refs):
     ins = refs[:count]
     query_out, key_out, value_out = refs[count:]
     rows, width = query_out.shape
     depth = key_out.shape[1]
     heads = width // depth
     slot = 2 * rows // count
-    at = heads * slot
-    index = lax.axis_index("ctx")
-    source = [lax.rem(index - k + count, count) for k in range(count)]
-    given = [
-        ref[at + 2 * rows : at + 2 * rows + 1, 0:1].astype(jnp.float32).astype(jnp.int32)
-        for ref in ins
-    ]
-    query_targets = []
-    key_targets = []
-    for k in range(count):
-        start = jnp.zeros((1, 1), jnp.int32)
-        key_start = jnp.zeros((1, 1), jnp.int32)
-        for other in range(count):
-            start = start + jnp.where(source[other] < source[k], given[other], 0)
-            key_start = key_start + jnp.where(source[other] < source[k] - halo, given[other], 0)
-        query_targets.append(start)
-        key_targets.append(key_start)
-
-    def spread_of(starts, size, limits):
-        lane = lax.broadcasted_iota(jnp.int32, (1, count * size), 1)
-        target = jnp.full((1, count * size), -1, jnp.int32)
-        for k in range(count):
-            step = lane - k * size
-            inside = (step >= 0) & (step < limits[k])
-            target = jnp.where(inside, starts[k] + step, target)
-        return one_hot(rows, target)
-
-    spread = spread_of(query_targets, slot, given)
     for h in range(heads):
         taken = jnp.concatenate([ref[h * slot : (h + 1) * slot, :] for ref in ins], axis=0)
-        query_out[:, h * depth : (h + 1) * depth] = contract(spread, taken, 1, 0)
-    spread = spread_of(key_targets, rows, [rows] * count)
+        query_out[:, h * depth : (h + 1) * depth] = contract(query_spread[...], taken, 1, 0)
     for n, out in enumerate((key_out, value_out)):
-        first = at + n * rows
-        taken = jnp.concatenate([ref[first : first + rows, :] for ref in ins], axis=0)
-        out[...] = contract(spread, taken, 1, 0)
+        at = heads * slot + n * rows
+        taken = jnp.concatenate([ref[at : at + rows, :] for ref in ins], axis=0)
+        out[...] = contract(key_spread[...], taken, 1, 0)
 
 
 def near_plan(doc_lengths, owners, queries, key_head_rows, value_head_rows, forward_out, grad_out):
@@ -441,13 +449,13 @@
     rows, width = queries.shape
     depth = key_head_rows.shape[1]
     heads = width // depth
+    bf16, f32 = jnp.bfloat16, jnp.float32
     columns = heads * rows
     halo = count // 2
     slot = 2 * rows // count
-    packet_rows = heads * slot + 2 * rows + META
+    spread_shape = jax.ShapeDtypeStruct((count * slot, rows), bf16)
     whole = pl.BlockSpec(memory_space=pltpu.VMEM)
     params = pltpu.CompilerParams(vmem_limit_bytes=40 * 1024 * 1024)
-    bf16, f32 = jnp.bfloat16, jnp.float32
 
     mark = lax.broadcasted_iota(jnp.int32, (2 * rows + META, rows), 0) - 2 * rows
     packet = jnp.where(
@@ -457,25 +465,26 @@
     )
     near = [
         lax.ppermute(packet, "ctx", [(i, (i + back) % count) for i in range(count)])
-        for back in range(1, halo + 1)
+        for back in range(halo, 0, -1)
     ]
     own = pl.pallas_call(
-        functools.partial(own_kernel, doc_lengths.shape[0]),
+        functools.partial(own_kernel, count, doc_lengths.shape[0]),
         out_shape=[
             jax.ShapeDtypeStruct((columns, depth), bf16),
             jax.ShapeDtypeStruct((columns, depth), bf16),
             jax.ShapeDtypeStruct((rows, columns), f32),
             jax.ShapeDtypeStruct((rows, columns), f32),
             jax.ShapeDtypeStruct((8, columns), f32),
+            spread_shape,
         ],
         in_specs=[pl.BlockSpec(memory_space=pltpu.SMEM)] + [whole] * 4,
-        out_specs=[whole] * 5,
+        out_specs=[whole] * 6,
         compiler_params=params,
     )(doc_lengths, packet, queries, grad_out, forward_out)
     sent = pl.pallas_call(
         functools.partial(attend_kernel, count, halo),
-        out_shape=[jax.ShapeDtypeStruct((packet_rows, depth), bf16)] * count,
-        in_specs=[whole] * (6 + halo),
+        out_shape=[jax.ShapeDtypeStruct((heads * slot + 2 * rows, depth), bf16)] * count,
+        in_specs=[whole] * (7 + halo),
         out_specs=[whole] * count,
         compiler_params=params,
     )(*own, packet, *near)
@@ -483,17 +492,27 @@
         lax.ppermute(sent[k], "ctx", [(i, (i + k) % count) for i in range(count)])
         for k in range(1, count)
     ]
+    spreads = pl.pallas_call(
+        functools.partial(order_kernel, count, halo),
+        out_shape=[
+            jax.ShapeDtypeStruct((rows, count * slot), bf16),
+            jax.ShapeDtypeStruct((rows, count * rows), bf16),
+        ],
+        in_specs=[pl.BlockSpec(memory_space=pl.ANY)] + [whole] * (1 + halo),
+        out_specs=[whole] * 2,
+        compiler_params=params,
+    )(received[1], packet, *near)
     return pl.pallas_call(
-        functools.partial(place_kernel, count, halo),
+        functools.partial(place_kernel, count),
         out_shape=[
             jax.ShapeDtypeStruct((rows, width), f32),
             jax.ShapeDtypeStruct((rows, depth), f32),
             jax.ShapeDtypeStruct((rows, depth), f32),
         ],
-        in_specs=[whole] * count,
+        in_specs=[whole] * (2 + count),
         out_specs=[whole] * 3,
         compiler_params=params,
-    )(*received)
+    )(*spreads, *received)
 
 
 def per_device(*args):

time: 26.2 us -> 27.2 us (1.038)
  waiting for transfers between devices: 8.92 us -> 10.6 us
  starting transfers between devices: 10.3 us -> 9.54 us
    ppermute x3, waiting for transfers between devices: 7.23 us -> 8.88 us  [near_plan(): lax.ppermute(sent[k], 'ctx', [(i, (i + k) % count) for i in range(count)])]
    ppermute x3, starting transfers between devices: 4.67 us -> 3.87 us  [near_plan(): lax.ppermute(sent[k], 'ctx', [(i, (i + k) % count) for i in range(count)])]
    pallas_call x2 -> x3, Pallas kernels: 2.05 us -> 2.19 us  [the longest x1 1.01 us: near_plan(): pl.pallas_call(functools.partial(own_kernel, count, doc_lengths.shape[0])...]
  transfers between devices with their start and end apart: 5 -> 5, of which waited for: 3 -> 3; matrix products, arithmetic and copies ran while one was open for 0% -> 0% of each run, Pallas kernels for 4% -> 5%
where the time goes in v5:
time: 27.2 us; the launch traced here: 27.1 us
  waiting for transfers between devices  10.6 us (39%)
  starting transfers between devices  9.54 us (35%)
  Pallas kernels  3.4 us (12%)
  local copies, waits for them, and re-layouts  1.82 us (7%)
  other arithmetic  0.96 us (4%)
  between operations  0.71 us (3%)
    ppermute x3, waiting for transfers between devices, near_plan(): lax.ppermute(sent[k], 'ctx', [(i, (i + k) % count) for i in range(count)])  8.88 us
    ppermute x2, starting transfers between devices, near_plan(): lax.ppermute(packet, 'ctx', [(i, (i + back) % count) for i in range(count)])  5.67 us
    ppermute x3, starting transfers between devices, near_plan(): lax.ppermute(sent[k], 'ctx', [(i, (i + k) % count) for i in range(count)])  3.87 us
    unnamed x8, local copies, waits for them, and re-layouts  1.82 us
    ppermute x2, waiting for transfers between devices, near_plan(): lax.ppermute(packet, 'ctx', [(i, (i + back) % count) for i in range(count)])  1.76 us
    pallas_call x1, Pallas kernels, near_plan(): pl.pallas_call(functools.partial(attend_kernel, count, halo), out_shape=[...  1.21 us
    pallas_call x1, Pallas kernels, near_plan(): pl.pallas_call(functools.partial(own_kernel, count, doc_lengths.shape[0])...  1.01 us
    pallas_call x1, Pallas kernels, near_plan(): pl.pallas_call(functools.partial(place_kernel, count), out_shape=[jax.Sha...  0.96 us
  transfers between devices with their start and end apart: 5, of which 3 were waited for; matrix products, arithmetic and copies ran while one was open for 0% of the time, Pallas kernels for 5%

profile of v5, /device:TPU:0, one launch (start us, length us, event | category | flops | bytes accessed | tf_op | source)
XLA Modules:
  0.0 27.1 jit_solution(13349119952070477336)
XLA Ops:
  0.6 0.0 copy-start
  0.7 0.0 copy-start.3
  0.7 0.9 %fusion.2.packet_ref.refs_6_.refs_0_ = bf16[272,128]{1,0:T(8,128)(2,1)S(1)} fusion(bf16[128,128]{1,0:T(8,128)(2,1)} %param.11, bf16[128,128]{1,0:T(8,128)(2,1)} %param.10, s32[128]{0:T(128)} %param.8, s32[272]{0:T(512)S(1)} %iota_add_fusion, pred[272]{0:T(512)(128)(4,1)S(1)} %broadcast_compare_fusion), kind=kLoop, calls=%fused_computation.4 | loop fusion | flops 348160 | bytes 137040 | tf_op jit(solution)/shard_map/jit(_where)/select_n | solution.py:461
  1.6 3.1 %collective-permute-start.1 = (bf16[272,128]{1,0:T(8,128)(2,1)S(1)}, bf16[272,128]{1,0:T(8,128)(2,1)S(1)}, u32[]{:S(2)}, u32[]{:S(2)}) collective-permute-start(bf16[272,128]{1,0:T(8,128)(2,1)S(1)} %fusion.2.packet_ref.refs_6_.refs_0_), channel_id=1, source_target_pairs={{0,4},{4,8},{8,12},{12,0},{1,5},{5,9},{9,13},{13,1},{2,6},{6,10},{... | collective-permute-start | bytes 208904 | tf_op jit(solution)/shard_map/ppermute | solution.py:467
  4.7 2.6 %collective-permute-start = (bf16[272,128]{1,0:T(8,128)(2,1)S(1)}, bf16[272,128]{1,0:T(8,128)(2,1)S(1)}, u32[]{:S(2)}, u32[]{:S(2)}) collective-permute-start(bf16[272,128]{1,0:T(8,128)(2,1)S(1)} %fusion.2.packet_ref.refs_6_.refs_0_), channel_id=1, source_target_pairs={{0,8},{4,12},{8,0},{12,4},{1,9},{5,13},{9,1},{13,5},{2,10},{6,14},... | collective-permute-start | bytes 208904 | tf_op jit(solution)/shard_map/ppermute | solution.py:467
  7.3 0.0 copy-done
  7.3 0.0 copy-done.3
  7.3 0.0 copy-start.1
  7.3 0.9 %copy-done.1 = bf16[128,512]{1,0:T(8,128)(2,1)S(1)} copy-done((bf16[128,512]{1,0:T(8,128)(2,1)S(1)}, bf16[128,512]{1,0:T(8,128)(2,1)}, u32[]{:S(2)}) %copy-start.1) | copy-done | bytes 131096
  8.2 0.0 copy-start.2
  8.2 0.9 %copy-done.2 = bf16[128,512]{1,0:T(8,128)(2,1)S(1)} copy-done((bf16[128,512]{1,0:T(8,128)(2,1)S(1)}, bf16[128,512]{1,0:T(8,128)(2,1)}, u32[]{:S(2)}) %copy-start.2) | copy-done | bytes 131096
  9.1 1.0 %shard_map.94 = (bf16[512,128]{1,0:T(8,128)(2,1)S(1)}, bf16[512,128]{1,0:T(8,128)(2,1)S(1)}, f32[128,512]{1,0:T(8,128)S(1)}, f32[128,512]{1,0:T(8,128)S(1)}, f32...) custom-call(s32[16]{0:T(128)S(1)} %copy-done.3, bf16[272,128]{1,0:T(8,128)(2,1)S(1)} %fusion.2.packet_ref.refs_6_.refs_0_, ...), custom_call_target="tpu_custom_call" | custom-call | tf_op jit(solution)/shard_map/pallas_call | solution.py:470
  10.1 0.0 collective-permute-done.1.refs_8_.refs_2_
  10.1 1.8 %collective-permute-done.refs_7_.refs_1_ = bf16[272,128]{1,0:T(8,128)(2,1)S(1)} collective-permute-done((bf16[272,128]{1,0:T(8,128)(2,1)S(1)}, bf16[272,128]{1,0:T(8,128)(2,1)S(1)}, u32[]{:S(2)}, u32[]{:S(2)}) %collective-permute-start) | collective-permute-done | bytes 69664 | tf_op jit(solution)/shard_map/ppermute | solution.py:467
  11.9 1.2 %shard_map.95 = (bf16[512,128]{1,0:T(8,128)(2,1)S(1)}, bf16[512,128]{1,0:T(8,128)(2,1)S(1)}, bf16[512,128]{1,0:T(8,128)(2,1)S(1)}, bf16[512,128]{1,0:T(8,128)(2,1)S(1)}) custom-call(bf16[512,128]{1,0:T(8,128)(2,1)S(1)} %get-tuple-element.15.refs_0_, bf16[512,128]{1,0:T(8,128)(2,1)S(1)} %get-tuple-element.16.refs_1_, ...), custom_call_target="tpu_custom_call" | custom-call | tf_op jit(solution)/shard_map/pallas_call | solution.py:484
  13.1 0.1 collective-permute-start.2
  13.2 2.5 %collective-permute-start.3 = (bf16[512,128]{1,0:T(8,128)(2,1)S(1)}, bf16[512,128]{1,0:T(8,128)(2,1)S(1)}, u32[]{:S(2)}, u32[]{:S(2)}) collective-permute-start(bf16[512,128]{1,0:T(8,128)(2,1)S(1)} %get-tuple-element.25), channel_id=1, source_target_pairs={{0,8},{4,12},{8,0},{12,4},{1,9},{5,13},{9,1},{13,5},{2,10},{6,14},... | collective-permute-start | bytes 393224 | tf_op jit(solution)/shard_map/ppermute | solution.py:492
  15.7 1.3 %collective-permute-start.4 = (bf16[512,128]{1,0:T(8,128)(2,1)S(1)}, bf16[512,128]{1,0:T(8,128)(2,1)S(1)}, u32[]{:S(2)}, u32[]{:S(2)}) collective-permute-start(bf16[512,128]{1,0:T(8,128)(2,1)S(1)} %get-tuple-element.26), channel_id=1, source_target_pairs={{0,12},{4,0},{8,4},{12,8},{1,13},{5,1},{9,5},{13,9},{2,14},{6,2},{... | collective-permute-start | bytes 393224 | tf_op jit(solution)/shard_map/ppermute | solution.py:492
  17.0 4.5 %collective-permute-done.2._.refs_1_ = bf16[512,128]{1,0:T(8,128)(2,1)S(1)} collective-permute-done((bf16[512,128]{1,0:T(8,128)(2,1)S(1)}, bf16[512,128]{1,0:T(8,128)(2,1)S(1)}, u32[]{:S(2)}, u32[]{:S(2)}) %collective-permute-start.2) | collective-permute-done | bytes 131104 | tf_op jit(solution)/shard_map/ppermute | solution.py:492
  21.4 0.2 shard_map.96
  21.7 4.4 %collective-permute-done.3.refs_2_ = bf16[512,128]{1,0:T(8,128)(2,1)S(1)} collective-permute-done((bf16[512,128]{1,0:T(8,128)(2,1)S(1)}, bf16[512,128]{1,0:T(8,128)(2,1)S(1)}, u32[]{:S(2)}, u32[]{:S(2)}) %collective-permute-start.3) | collective-permute-done | bytes 131104 | tf_op jit(solution)/shard_map/ppermute | solution.py:492
  26.1 0.0 collective-permute-done.4.refs_3_
  26.1 1.0 %shard_map.97 = (f32[128,512]{1,0:T(8,128)}, f32[128,128]{1,0:T(8,128)}, f32[128,128]{1,0:T(8,128)}) custom-call(bf16[128,256]{1,0:T(8,128)(2,1)S(1)} %get-tuple-element.22.query_spread, bf16[128,512]{1,0:T(8,128)(2,1)S(1)} %get-tuple-element.23.key_spread, bf16[512,128]{1,0:T(8,128)(2,1)S(1)} %get-tuple-element.24.refs_0_, ...), custom_call_target="tpu_custom_call" | custom-call | tf_op jit(solution)/shard_map/pallas_call | solution.py:505
  (2 shorter events, 0.0 us)
Async XLA Ops:
  0.6 6.7 %copy-start = (bf16[128,512]{1,0:T(8,128)(2,1)S(1)}, bf16[128,512]{1,0:T(8,128)(2,1)}, u32[]{:S(2)}) copy-start(bf16[128,512]{1,0:T(8,128)(2,1)} %query_ref.1) | copy-start | bytes 393220
  0.7 6.6 %copy-start.3 = (s32[16]{0:T(128)S(1)}, s32[16]{0:T(128)}, u32[]{:S(2)}) copy-start(s32[16]{0:T(128)} %doc_ref.1) | copy-start | bytes 196
  1.6 8.5 %collective-permute-start.1 = (bf16[272,128]{1,0:T(8,128)(2,1)S(1)}, bf16[272,128]{1,0:T(8,128)(2,1)S(1)}, u32[]{:S(2)}, u32[]{:S(2)}) collective-permute-start(bf16[272,128]{1,0:T(8,128)(2,1)S(1)} %fusion.2.packet_ref.refs_6_.refs_0_), channel_id=1, source_target_pairs={{0,4},{4,8},{8,12},{12,0},{1,5},{5,9},{9,13},{13,1},{2,6},{6,10},{... | collective-permute-start | bytes 208904 | tf_op jit(solution)/shard_map/ppermute | solution.py:467
  4.7 7.2 %collective-permute-start = (bf16[272,128]{1,0:T(8,128)(2,1)S(1)}, bf16[272,128]{1,0:T(8,128)(2,1)S(1)}, u32[]{:S(2)}, u32[]{:S(2)}) collective-permute-start(bf16[272,128]{1,0:T(8,128)(2,1)S(1)} %fusion.2.packet_ref.refs_6_.refs_0_), channel_id=1, source_target_pairs={{0,8},{4,12},{8,0},{12,4},{1,9},{5,13},{9,1},{13,5},{2,10},{6,14},... | collective-permute-start | bytes 208904 | tf_op jit(solution)/shard_map/ppermute | solution.py:467
  7.3 0.9 %copy-start.1 = (bf16[128,512]{1,0:T(8,128)(2,1)S(1)}, bf16[128,512]{1,0:T(8,128)(2,1)}, u32[]{:S(2)}) copy-start(bf16[128,512]{1,0:T(8,128)(2,1)} %grad_ref.1) | copy-start | bytes 393220
  8.2 0.9 %copy-start.2 = (bf16[128,512]{1,0:T(8,128)(2,1)S(1)}, bf16[128,512]{1,0:T(8,128)(2,1)}, u32[]{:S(2)}) copy-start(bf16[128,512]{1,0:T(8,128)(2,1)} %saved_ref.1) | copy-start | bytes 393220
  13.1 8.3 %collective-permute-start.2 = (bf16[512,128]{1,0:T(8,128)(2,1)S(1)}, bf16[512,128]{1,0:T(8,128)(2,1)S(1)}, u32[]{:S(2)}, u32[]{:S(2)}) collective-permute-start(bf16[512,128]{1,0:T(8,128)(2,1)S(1)} %get-tuple-element.21), channel_id=1, source_target_pairs={{0,4},{4,8},{8,12},{12,0},{1,5},{5,9},{9,13},{13,1},{2,6},{6,10},{... | collective-permute-start | bytes 393224 | tf_op jit(solution)/shard_map/ppermute | solution.py:492
  13.2 12.9 %collective-permute-start.3 = (bf16[512,128]{1,0:T(8,128)(2,1)S(1)}, bf16[512,128]{1,0:T(8,128)(2,1)S(1)}, u32[]{:S(2)}, u32[]{:S(2)}) collective-permute-start(bf16[512,128]{1,0:T(8,128)(2,1)S(1)} %get-tuple-element.25), channel_id=1, source_target_pairs={{0,8},{4,12},{8,0},{12,4},{1,9},{5,13},{9,1},{13,5},{2,10},{6,14},... | collective-permute-start | bytes 393224 | tf_op jit(solution)/shard_map/ppermute | solution.py:492
  15.7 10.4 %collective-permute-start.4 = (bf16[512,128]{1,0:T(8,128)(2,1)S(1)}, bf16[512,128]{1,0:T(8,128)(2,1)S(1)}, u32[]{:S(2)}, u32[]{:S(2)}) collective-permute-start(bf16[512,128]{1,0:T(8,128)(2,1)S(1)} %get-tuple-element.26), channel_id=1, source_target_pairs={{0,12},{4,0},{8,4},{12,8},{1,13},{5,1},{9,5},{13,9},{2,14},{6,2},{... | collective-permute-start | bytes 393224 | tf_op jit(solution)/shard_map/ppermute | solution.py:492

commit v6 on v5

--- a/solution.py
+++ b/solution.py
@@ -327,8 +327,7 @@
     row_out[3:4, :] = jnp.concatenate([first.astype(jnp.float32)] * heads, axis=1)
     row_out[4:8, :] = jnp.zeros((4, width), jnp.float32)
     owner, counts, rank = runs_of(packet_ref[2 * rows : 2 * rows + count, :].astype(jnp.float32))
-    ahead = lax.rem(owner - index + count, count)
-    spread_out[...] = one_hot(count * slot, ahead * slot + rank)
+    spread_out[...] = one_hot(count * slot, (owner ^ index) * slot + rank)
 
 
 def attend_kernel(count, halo, *refs):
@@ -377,7 +376,7 @@
         base = jnp.zeros((1, rows), jnp.float32)
         for p in range(count):
             base = base + jnp.where(owner == p, filled[p : p + 1, :], 0.0)
-        target = lax.rem(owner - index + count, count) * rows + base.astype(jnp.int32) + rank
+        target = (owner ^ index) * rows + base.astype(jnp.int32) + rank
         inside = index - halo + block >= 0
         targets.append(jnp.where(inside, target, -1))
         filled = filled + jnp.where(inside, counts, 0.0)
@@ -410,18 +409,20 @@
         given.append(mine.astype(jnp.int32))
     if len(given) < count:
         given.append(rows - sum(given))
-    source = [lax.rem(index - k + count, count) for k in range(count)]
+    giver = [lax.rem(index - d + count, count) for d in range(count)]
 
     def placement(size, back, whole):
         lane = lax.broadcasted_iota(jnp.int32, (1, count * size), 1)
         target = jnp.full(lane.shape, -1, jnp.int32)
         for k in range(count):
             start = jnp.zeros((1, 1), jnp.int32)
-            for other in range(count):
-                start = start + jnp.where(source[other] < source[k] - back, given[other], 0)
+            limit = jnp.full((1, 1), size, jnp.int32)
+            for d in range(count):
+                start = start + jnp.where(giver[d] < (index ^ k) - back, given[d], 0)
+                if not whole:
+                    limit = jnp.where(giver[d] == (index ^ k), given[d], limit)
             step = lane - k * size
-            inside = (step >= 0) & (step < (size if whole else given[k]))
-            target = jnp.where(inside, start + step, target)
+            target = jnp.where((step >= 0) & (step < limit), start + step, target)
         return one_hot(rows, target)
 
     query_out[...] = placement(2 * rows // count, 0, False)
@@ -430,18 +431,30 @@
 
 def place_kernel(count, query_spread, key_spread, *refs):
     ins = refs[:count]
-    query_out, key_out, value_out = refs[count:]
-    rows, width = query_out.shape
-    depth = key_out.shape[1]
+    query_out, key_out, value_out = refs[count : count + 3]
+    query_here, key_here, value_here, sems = refs[count + 3 :]
+    rows, width = query_here.shape
+    depth = key_here.shape[1]
     heads = width // depth
     slot = 2 * rows // count
+    copies = []
+
+    def leave(here, out):
+        copies.append(pltpu.make_async_copy(here, out, sems.at[len(copies)]))
+        copies[-1].start()
+
     for h in range(heads):
+        at = slice(h * depth, (h + 1) * depth)
         taken = jnp.concatenate([ref[h * slot : (h + 1) * slot, :] for ref in ins], axis=0)
-        query_out[:, h * depth : (h + 1) * depth] = contract(query_spread[...], taken, 1, 0)
-    for n, out in enumerate((key_out, value_out)):
+        query_here[:, at] = contract(query_spread[...], taken, 1, 0)
+        leave(query_here.at[:, at], query_out.at[:, at])
+    for n, (here, out) in enumerate(((key_here, key_out), (value_here, value_out))):
         at = heads * slot + n * rows
         taken = jnp.concatenate([ref[at : at + rows, :] for ref in ins], axis=0)
-        out[...] = contract(key_spread[...], taken, 1, 0)
+        here[...] = contract(key_spread[...], taken, 1, 0)
+        leave(here, out)
+    for copy in copies:
+        copy.wait()
 
 
 def near_plan(doc_lengths, owners, queries, key_head_rows, value_head_rows, forward_out, grad_out):
@@ -489,8 +502,7 @@
         compiler_params=params,
     )(*own, packet, *near)
     received = [sent[0]] + [
-        lax.ppermute(sent[k], "ctx", [(i, (i + k) % count) for i in range(count)])
-        for k in range(1, count)
+        lax.ppermute(sent[k], "ctx", [(i, i ^ k) for i in range(count)]) for k in range(1, count)
     ]
     spreads = pl.pallas_call(
         functools.partial(order_kernel, count, halo),
@@ -501,7 +513,7 @@
         in_specs=[pl.BlockSpec(memory_space=pl.ANY)] + [whole] * (1 + halo),
         out_specs=[whole] * 2,
         compiler_params=params,
-    )(received[1], packet, *near)
+    )(received[-1], packet, *near)
     return pl.pallas_call(
         functools.partial(place_kernel, count),
         out_shape=[
@@ -510,13 +522,19 @@
             jax.ShapeDtypeStruct((rows, depth), f32),
         ],
         in_specs=[whole] * (2 + count),
-        out_specs=[whole] * 3,
+        out_specs=[pl.BlockSpec(memory_space=pl.ANY)] * 3,
+        scratch_shapes=[
+            pltpu.VMEM((rows, width), f32),
+            pltpu.VMEM((rows, depth), f32),
+            pltpu.VMEM((rows, depth), f32),
+            pltpu.SemaphoreType.DMA((heads + 2,)),
+        ],
         compiler_params=params,
     )(*spreads, *received)
 
 
 def per_device(*args):
-    if lax.axis_size("ctx") <= 4:
+    if lax.axis_size("ctx") in (2, 4):
         return near_plan(*args)
     return ring_plan(*args)
 

time: 27.2 us -> 25.7 us (0.945)
  waiting for transfers between devices: 10.6 us -> 8.56 us
  starting transfers between devices: 9.54 us -> 10.1 us
    ppermute x3, waiting for transfers between devices: 8.88 us -> 6.8 us  [near_plan(): lax.ppermute(sent[k], 'ctx', [(i, i ^ k) for i in range(count)])]
    ppermute x3, starting transfers between devices: 3.87 us -> 4.45 us  [near_plan(): lax.ppermute(sent[k], 'ctx', [(i, i ^ k) for i in range(count)])]
where the time goes in v6:
time: 25.7 us; the launch traced here: 25.6 us
  starting transfers between devices  10.1 us (39%)
  waiting for transfers between devices  8.56 us (33%)
  Pallas kernels  3.42 us (13%)
  local copies, waits for them, and re-layouts  1.82 us (7%)
  other arithmetic  0.96 us (4%)
  between operations  0.7 us (3%)
    ppermute x3, waiting for transfers between devices, near_plan(): lax.ppermute(sent[k], 'ctx', [(i, i ^ k) for i in range(count)])  6.8 us
    ppermute x2, starting transfers between devices, near_plan(): lax.ppermute(packet, 'ctx', [(i, (i + back) % count) for i in range(count)])  5.67 us
    ppermute x3, starting transfers between devices, near_plan(): lax.ppermute(sent[k], 'ctx', [(i, i ^ k) for i in range(count)])  4.45 us
    unnamed x8, local copies, waits for them, and re-layouts  1.82 us
    ppermute x2, waiting for transfers between devices, near_plan(): lax.ppermute(packet, 'ctx', [(i, (i + back) % count) for i in range(count)])  1.76 us
    pallas_call x1, Pallas kernels, near_plan(): pl.pallas_call(functools.partial(attend_kernel, count, halo), out_shape=[...  1.21 us
    pallas_call x1, Pallas kernels, near_plan(): pl.pallas_call(functools.partial(own_kernel, count, doc_lengths.shape[0])...  1.01 us
    pallas_call x1, Pallas kernels, near_plan(): pl.pallas_call(functools.partial(place_kernel, count), out_shape=[jax.Sha...  0.98 us
  transfers between devices with their start and end apart: 5, of which 3 were waited for; matrix products, arithmetic and copies ran while one was open for 0% of the time, Pallas kernels for 5%

profile of v6, /device:TPU:0, one launch (start us, length us, event | category | flops | bytes accessed | tf_op | source)
XLA Modules:
  0.0 25.6 jit_solution(17747162864542406377)
XLA Ops:
  0.6 0.0 copy-start
  0.7 0.0 copy-start.3
  0.7 0.9 %fusion.2.packet_ref.refs_6_.refs_0_ = bf16[272,128]{1,0:T(8,128)(2,1)S(1)} fusion(bf16[128,128]{1,0:T(8,128)(2,1)} %param.11, bf16[128,128]{1,0:T(8,128)(2,1)} %param.10, s32[128]{0:T(128)} %param.8, s32[272]{0:T(512)S(1)} %iota_add_fusion, pred[272]{0:T(512)(128)(4,1)S(1)} %broadcast_compare_fusion), kind=kLoop, calls=%fused_computation.4 | loop fusion | flops 348160 | bytes 137040 | tf_op jit(solution)/shard_map/jit(_where)/select_n | solution.py:474
  1.6 3.1 %collective-permute-start.1 = (bf16[272,128]{1,0:T(8,128)(2,1)S(1)}, bf16[272,128]{1,0:T(8,128)(2,1)S(1)}, u32[]{:S(2)}, u32[]{:S(2)}) collective-permute-start(bf16[272,128]{1,0:T(8,128)(2,1)S(1)} %fusion.2.packet_ref.refs_6_.refs_0_), channel_id=1, source_target_pairs={{0,4},{4,8},{8,12},{12,0},{1,5},{5,9},{9,13},{13,1},{2,6},{6,10},{... | collective-permute-start | bytes 208904 | tf_op jit(solution)/shard_map/ppermute | solution.py:480
  4.7 2.6 %collective-permute-start = (bf16[272,128]{1,0:T(8,128)(2,1)S(1)}, bf16[272,128]{1,0:T(8,128)(2,1)S(1)}, u32[]{:S(2)}, u32[]{:S(2)}) collective-permute-start(bf16[272,128]{1,0:T(8,128)(2,1)S(1)} %fusion.2.packet_ref.refs_6_.refs_0_), channel_id=1, source_target_pairs={{0,8},{4,12},{8,0},{12,4},{1,9},{5,13},{9,1},{13,5},{2,10},{6,14},... | collective-permute-start | bytes 208904 | tf_op jit(solution)/shard_map/ppermute | solution.py:480
  7.3 0.0 copy-done
  7.3 0.0 copy-done.3
  7.3 0.0 copy-start.1
  7.3 0.9 %copy-done.1 = bf16[128,512]{1,0:T(8,128)(2,1)S(1)} copy-done((bf16[128,512]{1,0:T(8,128)(2,1)S(1)}, bf16[128,512]{1,0:T(8,128)(2,1)}, u32[]{:S(2)}) %copy-start.1) | copy-done | bytes 131096
  8.2 0.0 copy-start.2
  8.2 0.9 %copy-done.2 = bf16[128,512]{1,0:T(8,128)(2,1)S(1)} copy-done((bf16[128,512]{1,0:T(8,128)(2,1)S(1)}, bf16[128,512]{1,0:T(8,128)(2,1)}, u32[]{:S(2)}) %copy-start.2) | copy-done | bytes 131096
  9.1 1.0 %shard_map.94 = (bf16[512,128]{1,0:T(8,128)(2,1)S(1)}, bf16[512,128]{1,0:T(8,128)(2,1)S(1)}, f32[128,512]{1,0:T(8,128)S(1)}, f32[128,512]{1,0:T(8,128)S(1)}, f32...) custom-call(s32[16]{0:T(128)S(1)} %copy-done.3, bf16[272,128]{1,0:T(8,128)(2,1)S(1)} %fusion.2.packet_ref.refs_6_.refs_0_, ...), custom_call_target="tpu_custom_call" | custom-call | tf_op jit(solution)/shard_map/pallas_call | solution.py:483
  10.1 0.0 collective-permute-done.1.refs_8_.refs_2_
  10.1 1.8 %collective-permute-done.refs_7_.refs_1_ = bf16[272,128]{1,0:T(8,128)(2,1)S(1)} collective-permute-done((bf16[272,128]{1,0:T(8,128)(2,1)S(1)}, bf16[272,128]{1,0:T(8,128)(2,1)S(1)}, u32[]{:S(2)}, u32[]{:S(2)}) %collective-permute-start) | collective-permute-done | bytes 69664 | tf_op jit(solution)/shard_map/ppermute | solution.py:480
  11.9 1.2 %shard_map.95 = (bf16[512,128]{1,0:T(8,128)(2,1)S(1)}, bf16[512,128]{1,0:T(8,128)(2,1)S(1)}, bf16[512,128]{1,0:T(8,128)(2,1)S(1)}, bf16[512,128]{1,0:T(8,128)(2,1)S(1)}) custom-call(bf16[512,128]{1,0:T(8,128)(2,1)S(1)} %get-tuple-element.15.refs_0_, bf16[512,128]{1,0:T(8,128)(2,1)S(1)} %get-tuple-element.16.refs_1_, ...), custom_call_target="tpu_custom_call" | custom-call | tf_op jit(solution)/shard_map/pallas_call | solution.py:497
  13.1 2.0 %collective-permute-start.2 = (bf16[512,128]{1,0:T(8,128)(2,1)S(1)}, bf16[512,128]{1,0:T(8,128)(2,1)S(1)}, u32[]{:S(2)}, u32[]{:S(2)}) collective-permute-start(bf16[512,128]{1,0:T(8,128)(2,1)S(1)} %get-tuple-element.21), channel_id=1, source_target_pairs={{0,12},{4,8},{8,4},{12,0},{1,13},{5,9},{9,5},{13,1},{2,14},{6,10},... | collective-permute-start | bytes 393224 | tf_op jit(solution)/shard_map/ppermute | solution.py:505
  15.1 0.0 collective-permute-start.3
  15.1 2.4 %collective-permute-start.4 = (bf16[512,128]{1,0:T(8,128)(2,1)S(1)}, bf16[512,128]{1,0:T(8,128)(2,1)S(1)}, u32[]{:S(2)}, u32[]{:S(2)}) collective-permute-start(bf16[512,128]{1,0:T(8,128)(2,1)S(1)} %get-tuple-element.26), channel_id=1, source_target_pairs={{0,8},{4,12},{8,0},{12,4},{1,9},{5,13},{9,1},{13,5},{2,10},{6,14},... | collective-permute-start | bytes 393224 | tf_op jit(solution)/shard_map/ppermute | solution.py:505
  17.6 3.8 %collective-permute-done.2._.refs_3_ = bf16[512,128]{1,0:T(8,128)(2,1)S(1)} collective-permute-done((bf16[512,128]{1,0:T(8,128)(2,1)S(1)}, bf16[512,128]{1,0:T(8,128)(2,1)S(1)}, u32[]{:S(2)}, u32[]{:S(2)}) %collective-permute-start.2) | collective-permute-done | bytes 131104 | tf_op jit(solution)/shard_map/ppermute | solution.py:505
  21.4 0.2 shard_map.96
  21.6 3.0 %collective-permute-done.3.refs_1_ = bf16[512,128]{1,0:T(8,128)(2,1)S(1)} collective-permute-done((bf16[512,128]{1,0:T(8,128)(2,1)S(1)}, bf16[512,128]{1,0:T(8,128)(2,1)S(1)}, u32[]{:S(2)}, u32[]{:S(2)}) %collective-permute-start.3) | collective-permute-done | bytes 131104 | tf_op jit(solution)/shard_map/ppermute | solution.py:505
  24.6 0.0 collective-permute-done.4.refs_2_
  24.6 1.0 %shard_map.97 = (f32[128,512]{1,0:T(8,128)}, f32[128,128]{1,0:T(8,128)}, f32[128,128]{1,0:T(8,128)}) custom-call(bf16[128,256]{1,0:T(8,128)(2,1)S(1)} %get-tuple-element.22.query_spread, bf16[128,512]{1,0:T(8,128)(2,1)S(1)} %get-tuple-element.23.key_spread, bf16[512,128]{1,0:T(8,128)(2,1)S(1)} %get-tuple-element.24.refs_0_, ...), custom_call_target="tpu_custom_call" | custom-call | tf_op jit(solution)/shard_map/pallas_call | solution.py:517
  (2 shorter events, 0.0 us)
Async XLA Ops:
  0.6 6.7 %copy-start = (bf16[128,512]{1,0:T(8,128)(2,1)S(1)}, bf16[128,512]{1,0:T(8,128)(2,1)}, u32[]{:S(2)}) copy-start(bf16[128,512]{1,0:T(8,128)(2,1)} %query_ref.1) | copy-start | bytes 393220
  0.7 6.6 %copy-start.3 = (s32[16]{0:T(128)S(1)}, s32[16]{0:T(128)}, u32[]{:S(2)}) copy-start(s32[16]{0:T(128)} %doc_ref.1) | copy-start | bytes 196
  1.6 8.5 %collective-permute-start.1 = (bf16[272,128]{1,0:T(8,128)(2,1)S(1)}, bf16[272,128]{1,0:T(8,128)(2,1)S(1)}, u32[]{:S(2)}, u32[]{:S(2)}) collective-permute-start(bf16[272,128]{1,0:T(8,128)(2,1)S(1)} %fusion.2.packet_ref.refs_6_.refs_0_), channel_id=1, source_target_pairs={{0,4},{4,8},{8,12},{12,0},{1,5},{5,9},{9,13},{13,1},{2,6},{6,10},{... | collective-permute-start | bytes 208904 | tf_op jit(solution)/shard_map/ppermute | solution.py:480
  4.7 7.2 %collective-permute-start = (bf16[272,128]{1,0:T(8,128)(2,1)S(1)}, bf16[272,128]{1,0:T(8,128)(2,1)S(1)}, u32[]{:S(2)}, u32[]{:S(2)}) collective-permute-start(bf16[272,128]{1,0:T(8,128)(2,1)S(1)} %fusion.2.packet_ref.refs_6_.refs_0_), channel_id=1, source_target_pairs={{0,8},{4,12},{8,0},{12,4},{1,9},{5,13},{9,1},{13,5},{2,10},{6,14},... | collective-permute-start | bytes 208904 | tf_op jit(solution)/shard_map/ppermute | solution.py:480
  7.3 0.9 %copy-start.1 = (bf16[128,512]{1,0:T(8,128)(2,1)S(1)}, bf16[128,512]{1,0:T(8,128)(2,1)}, u32[]{:S(2)}) copy-start(bf16[128,512]{1,0:T(8,128)(2,1)} %grad_ref.1) | copy-start | bytes 393220
  8.2 0.9 %copy-start.2 = (bf16[128,512]{1,0:T(8,128)(2,1)S(1)}, bf16[128,512]{1,0:T(8,128)(2,1)}, u32[]{:S(2)}) copy-start(bf16[128,512]{1,0:T(8,128)(2,1)} %saved_ref.1) | copy-start | bytes 393220
  13.1 8.3 %collective-permute-start.2 = (bf16[512,128]{1,0:T(8,128)(2,1)S(1)}, bf16[512,128]{1,0:T(8,128)(2,1)S(1)}, u32[]{:S(2)}, u32[]{:S(2)}) collective-permute-start(bf16[512,128]{1,0:T(8,128)(2,1)S(1)} %get-tuple-element.21), channel_id=1, source_target_pairs={{0,12},{4,8},{8,4},{12,0},{1,13},{5,9},{9,5},{13,1},{2,14},{6,10},... | collective-permute-start | bytes 393224 | tf_op jit(solution)/shard_map/ppermute | solution.py:505
  15.1 9.4 %collective-permute-start.3 = (bf16[512,128]{1,0:T(8,128)(2,1)S(1)}, bf16[512,128]{1,0:T(8,128)(2,1)S(1)}, u32[]{:S(2)}, u32[]{:S(2)}) collective-permute-start(bf16[512,128]{1,0:T(8,128)(2,1)S(1)} %get-tuple-element.25), channel_id=1, source_target_pairs={{0,4},{4,0},{8,12},{12,8},{1,5},{5,1},{9,13},{13,9},{2,6},{6,2},{1... | collective-permute-start | bytes 393224 | tf_op jit(solution)/shard_map/ppermute | solution.py:505
  15.1 9.4 %collective-permute-start.4 = (bf16[512,128]{1,0:T(8,128)(2,1)S(1)}, bf16[512,128]{1,0:T(8,128)(2,1)S(1)}, u32[]{:S(2)}, u32[]{:S(2)}) collective-permute-start(bf16[512,128]{1,0:T(8,128)(2,1)S(1)} %get-tuple-element.26), channel_id=1, source_target_pairs={{0,8},{4,12},{8,0},{12,4},{1,9},{5,13},{9,1},{13,5},{2,10},{6,14},... | collective-permute-start | bytes 393224 | tf_op jit(solution)/shard_map/ppermute | solution.py:505

commit v7 on v6

--- a/solution.py
+++ b/solution.py
@@ -290,6 +290,8 @@
     change_out,
     row_out,
     spread_out,
+    target_out,
+    filled_out,
 ):
     rows, width = query_ref.shape
     depth = packet_ref.shape[1]
@@ -325,62 +327,94 @@
     row_out[1:2, :] = top
     row_out[2:3, :] = jnp.sum(raised, axis=0, keepdims=True)
     row_out[3:4, :] = jnp.concatenate([first.astype(jnp.float32)] * heads, axis=1)
-    row_out[4:8, :] = jnp.zeros((4, width), jnp.float32)
+    row_out[4:8, :] = jnp.ones((4, width), jnp.float32)
     owner, counts, rank = runs_of(packet_ref[2 * rows : 2 * rows + count, :].astype(jnp.float32))
     spread_out[...] = one_hot(count * slot, (owner ^ index) * slot + rank)
-
-
-def attend_kernel(count, halo, *refs):
-    query_ref, grad_ref, raised_ref, change_ref, row_ref, spread_ref = refs[:6]
-    own = refs[6]
-    before = refs[7 : 7 + halo]
-    outs = refs[7 + halo :]
-    rows, columns = raised_ref.shape
-    depth = query_ref.shape[1]
-    heads = columns // rows
-    slot = 2 * rows // count
-    scale = 1.0 / math.sqrt(depth)
+    target_out[...] = one_hot(count * rows, (owner ^ index) * rows + rank)
+    filled_out[0:count, :] = jnp.broadcast_to(counts, (count, rows))
+    filled_out[count:, :] = jnp.zeros((8 - count, rows), jnp.float32)
+
+
+def fold(count, back, packet, queries, grads, row, filled):
+    rows = packet.shape[1]
     index = lax.axis_index("ctx")
-    delta, top, total = (row_ref[n : n + 1, :] for n in range(3))
-    first = row_ref[3:4, :].astype(jnp.int32)
-    queries = query_ref[...]
-    grads = grad_ref[...]
-
-    key_position = (index - halo) * rows + lax.broadcasted_iota(
-        jnp.int32, (halo * rows, columns), 0
-    )
-    keys = jnp.concatenate([n[0:rows, :] for n in before], axis=0)
-    values = jnp.concatenate([n[rows : 2 * rows, :] for n in before], axis=0)
-    scores = jnp.where(key_position >= first, contract(keys, queries, 1, 1) * scale, NEG)
+    delta, top, total = (row[n : n + 1, :] for n in range(3))
+    first = row[3:4, :].astype(jnp.int32)
+    position = (index - back) * rows + lax.broadcasted_iota(jnp.int32, (rows, row.shape[1]), 0)
+    scores = contract(packet[0:rows, :], queries, 1, 1) * (1.0 / math.sqrt(queries.shape[1]))
+    scores = jnp.where(position >= first, scores, NEG)
     new_top = jnp.maximum(top, jnp.max(scores, axis=0, keepdims=True))
     raised = jnp.exp(scores - new_top)
     shrink = jnp.exp(top - new_top)
-    inverse = 1.0 / (total * shrink + jnp.sum(raised, axis=0, keepdims=True))
-    weights = raised * inverse
-    own_weights = raised_ref[...] * (shrink * inverse)
-    changes = weights * (contract(values, grads, 1, 1) - delta)
-    own_changes = own_weights * change_ref[...]
-    weights = jnp.concatenate([weights, own_weights], axis=0).astype(jnp.bfloat16)
-    changes = jnp.concatenate([changes, own_changes], axis=0).astype(jnp.bfloat16)
-    keys = jnp.concatenate([keys, own[0:rows, :]], axis=0)
+    total = total * shrink + jnp.sum(raised, axis=0, keepdims=True)
+    change = contract(packet[rows : 2 * rows, :], grads, 1, 1) - delta
+    factors = row[4:8, :] * jnp.where(
+        lax.broadcasted_iota(jnp.int32, (4, row.shape[1]), 0) < back, shrink, 1.0
+    )
+    owner, counts, rank = runs_of(packet[2 * rows : 2 * rows + count, :].astype(jnp.float32))
+    base = jnp.zeros((1, rows), jnp.float32)
+    for p in range(count):
+        base = base + jnp.where(owner == p, filled[p : p + 1, :], 0.0)
+    inside = index >= back
+    target = jnp.where(inside, (owner ^ index) * rows + base.astype(jnp.int32) + rank, -1)
+    filled = filled[0:count, :] + jnp.where(inside, counts, 0.0)
+    return raised, change, (new_top, total, factors), one_hot(count * rows, target), filled
+
+
+def step_kernel(count, back, *refs):
+    query_ref, grad_ref, row_ref, filled_ref, packet_ref = refs[:5]
+    raised_out, change_out, row_out, target_out, filled_out = refs[5:]
+    raised, change, (top, total, factors), target, filled = fold(
+        count, back, packet_ref, query_ref[...], grad_ref[...], row_ref, filled_ref
+    )
+    raised_out[...] = raised
+    change_out[...] = change
+    row_out[0:1, :] = row_ref[0:1, :]
+    row_out[1:2, :] = top
+    row_out[2:3, :] = total
+    row_out[3:4, :] = row_ref[3:4, :]
+    row_out[4:8, :] = factors
+    target_out[...] = target
+    filled_out[0:count, :] = filled
+    filled_out[count:, :] = jnp.zeros_like(filled_out[count:, :])
+
+
+def attend_kernel(count, halo, *refs):
+    query_ref, grad_ref, row_ref, filled_ref, spread_ref = refs[:5]
+    raised_refs = refs[5 : 5 + halo]
+    change_refs = refs[5 + halo : 5 + 2 * halo]
+    target_refs = refs[5 + 2 * halo : 5 + 3 * halo]
+    packets = refs[5 + 3 * halo : 6 + 4 * halo]
+    outs = refs[6 + 4 * halo :]
+    rows = packets[0].shape[1]
+    depth = query_ref.shape[1]
+    heads = query_ref.shape[0] // rows
+    slot = 2 * rows // count
+    scale = 1.0 / math.sqrt(depth)
+    queries = query_ref[...]
+    grads = grad_ref[...]
+    raised, change, (_, total, factors), target, _ = fold(
+        count, halo, packets[halo], queries, grads, row_ref, filled_ref
+    )
+    factors = factors * (1.0 / total)
+    weights = []
+    changes = []
+    for block in range(halo + 1):
+        mine = raised if block == halo else raised_refs[block][...]
+        mine = mine * factors[block : block + 1, :]
+        weights.append(mine.astype(jnp.bfloat16))
+        mine = mine * (change if block == halo else change_refs[block][...])
+        changes.append(mine.astype(jnp.bfloat16))
+    weights = jnp.concatenate(weights, axis=0)
+    changes = jnp.concatenate(changes, axis=0)
+    keys = jnp.concatenate([packet[0:rows, :] for packet in packets], axis=0)
     query_grad = (contract(keys, changes, 0, 0) * scale).astype(jnp.bfloat16)
     value_parts = contract(weights, grads, 1, 0).astype(jnp.bfloat16)
     key_parts = (contract(changes, queries, 1, 0) * scale).astype(jnp.bfloat16)
 
     query_slots = contract(spread_ref[...], end_to_end(query_grad, heads), 1, 1)
     query_slots = query_slots.astype(jnp.bfloat16)
-    filled = jnp.zeros((count, 1), jnp.float32)
-    targets = []
-    for block, ref in enumerate(before + (own,)):
-        owner, counts, rank = runs_of(ref[2 * rows : 2 * rows + count, :].astype(jnp.float32))
-        base = jnp.zeros((1, rows), jnp.float32)
-        for p in range(count):
-            base = base + jnp.where(owner == p, filled[p : p + 1, :], 0.0)
-        target = (owner ^ index) * rows + base.astype(jnp.int32) + rank
-        inside = index - halo + block >= 0
-        targets.append(jnp.where(inside, target, -1))
-        filled = filled + jnp.where(inside, counts, 0.0)
-    spread = one_hot(count * rows, jnp.concatenate(targets, axis=1))
+    spread = jnp.concatenate([ref[...] for ref in target_refs] + [target], axis=1)
     key_slots = contract(spread, key_parts, 1, 0).astype(jnp.bfloat16)
     value_slots = contract(spread, value_parts, 1, 0).astype(jnp.bfloat16)
     at = heads * slot
@@ -395,7 +429,7 @@
 
 
 def order_kernel(count, halo, _, *refs):
-    packets = refs[:1] + refs[1 : 1 + halo][::-1]
+    packets = refs[: 1 + halo]
     query_out, key_out = refs[1 + halo :]
     rows = query_out.shape[0]
     index = lax.axis_index("ctx")
@@ -411,22 +445,24 @@
         given.append(rows - sum(given))
     giver = [lax.rem(index - d + count, count) for d in range(count)]
 
-    def placement(size, back, whole):
+    def placement(size, halo):
         lane = lax.broadcasted_iota(jnp.int32, (1, count * size), 1)
         target = jnp.full(lane.shape, -1, jnp.int32)
         for k in range(count):
-            start = jnp.zeros((1, 1), jnp.int32)
-            limit = jnp.full((1, 1), size, jnp.int32)
-            for d in range(count):
-                start = start + jnp.where(giver[d] < (index ^ k) - back, given[d], 0)
-                if not whole:
-                    limit = jnp.where(giver[d] == (index ^ k), given[d], limit)
             step = lane - k * size
-            target = jnp.where((step >= 0) & (step < limit), start + step, target)
+            for back in range(halo + 1):
+                block = (index ^ k) - back
+                start = jnp.zeros((1, 1), jnp.int32)
+                length = jnp.zeros((1, 1), jnp.int32)
+                for d in range(count):
+                    start = start + jnp.where(giver[d] < block, given[d], 0)
+                    length = length + jnp.where(giver[d] == block, given[d], 0)
+                target = jnp.where((step >= 0) & (step < length), start + step, target)
+                step = step - length
         return one_hot(rows, target)
 
-    query_out[...] = placement(2 * rows // count, 0, False)
-    key_out[...] = placement(rows, halo, True)
+    query_out[...] = placement(2 * rows // count, 0)
+    key_out[...] = placement(rows, halo)
 
 
 def place_kernel(count, query_spread, key_spread, *refs):
@@ -466,7 +502,6 @@
     columns = heads * rows
     halo = count // 2
     slot = 2 * rows // count
-    spread_shape = jax.ShapeDtypeStruct((count * slot, rows), bf16)
     whole = pl.BlockSpec(memory_space=pltpu.VMEM)
     params = pltpu.CompilerParams(vmem_limit_bytes=40 * 1024 * 1024)
 
@@ -478,29 +513,42 @@
     )
     near = [
         lax.ppermute(packet, "ctx", [(i, (i + back) % count) for i in range(count)])
-        for back in range(halo, 0, -1)
+        for back in range(1, halo + 1)
     ]
-    own = pl.pallas_call(
+    block_shapes = [jax.ShapeDtypeStruct((rows, columns), f32)] * 2
+    row_shape = jax.ShapeDtypeStruct((8, columns), f32)
+    target_shape = jax.ShapeDtypeStruct((count * rows, rows), bf16)
+    filled_shape = jax.ShapeDtypeStruct((8, rows), f32)
+    query_rows, grad_rows, raised, change, row, spread, target, filled = pl.pallas_call(
         functools.partial(own_kernel, count, doc_lengths.shape[0]),
-        out_shape=[
-            jax.ShapeDtypeStruct((columns, depth), bf16),
-            jax.ShapeDtypeStruct((columns, depth), bf16),
-            jax.ShapeDtypeStruct((rows, columns), f32),
-            jax.ShapeDtypeStruct((rows, columns), f32),
-            jax.ShapeDtypeStruct((8, columns), f32),
-            spread_shape,
-        ],
+        out_shape=[jax.ShapeDtypeStruct((columns, depth), bf16)] * 2
+        + block_shapes
+        + [row_shape, jax.ShapeDtypeStruct((count * slot, rows), bf16), target_shape, filled_shape],
         in_specs=[pl.BlockSpec(memory_space=pltpu.SMEM)] + [whole] * 4,
-        out_specs=[whole] * 6,
+        out_specs=[whole] * 8,
         compiler_params=params,
     )(doc_lengths, packet, queries, grad_out, forward_out)
+    raised, change, target = [raised], [change], [target]
+    for back in range(1, halo):
+        found = pl.pallas_call(
+            functools.partial(step_kernel, count, back),
+            out_shape=block_shapes + [row_shape, target_shape, filled_shape],
+            in_specs=[whole] * 5,
+            out_specs=[whole] * 5,
+            compiler_params=params,
+        )(query_rows, grad_rows, row, filled, near[back - 1])
+        raised.append(found[0])
+        change.append(found[1])
+        row = found[2]
+        target.append(found[3])
+        filled = found[4]
     sent = pl.pallas_call(
         functools.partial(attend_kernel, count, halo),
         out_shape=[jax.ShapeDtypeStruct((heads * slot + 2 * rows, depth), bf16)] * count,
-        in_specs=[whole] * (7 + halo),
+        in_specs=[whole] * (6 + 4 * halo),
         out_specs=[whole] * count,
         compiler_params=params,
-    )(*own, packet, *near)
+    )(query_rows, grad_rows, row, filled, spread, *raised, *change, *target, packet, *near)
     received = [sent[0]] + [
         lax.ppermute(sent[k], "ctx", [(i, i ^ k) for i in range(count)]) for k in range(1, count)
     ]

time: 25.7 us -> 25.6 us (level)
  waiting for transfers between devices: 8.56 us -> 8.16 us
  Pallas kernels: 3.42 us -> 3.72 us
    ppermute x2, waiting for transfers between devices: 1.76 us -> 1.42 us  [near_plan(): lax.ppermute(packet, 'ctx', [(i, (i + back) % count) for i in range(count)])]
    pallas_call x0 -> x1, Pallas kernels: none -> 0.33 us  [near_plan(): pl.pallas_call(functools.partial(step_kernel, count, back), out_shape=blo...]
  transfers between devices with their start and end apart: 5 -> 5, of which waited for: 3 -> 3; matrix products, arithmetic and copies ran while one was open for 0% -> 0% of each run, Pallas kernels for 5% -> 6%
where the time goes in v7:
time: 25.6 us; the launch traced here: 25.5 us
  starting transfers between devices  10.1 us (39%)
  waiting for transfers between devices  8.16 us (32%)
  Pallas kernels  3.72 us (15%)
  local copies, waits for them, and re-layouts  1.82 us (7%)
  other arithmetic  0.96 us (4%)
  between operations  0.7 us (3%)
    ppermute x3, waiting for transfers between devices, near_plan(): lax.ppermute(sent[k], 'ctx', [(i, i ^ k) for i in range(count)])  6.74 us
    ppermute x2, starting transfers between devices, near_plan(): lax.ppermute(packet, 'ctx', [(i, (i + back) % count) for i in range(count)])  5.67 us
    ppermute x3, starting transfers between devices, near_plan(): lax.ppermute(sent[k], 'ctx', [(i, i ^ k) for i in range(count)])  4.45 us
    unnamed x8, local copies, waits for them, and re-layouts  1.82 us
    ppermute x2, waiting for transfers between devices, near_plan(): lax.ppermute(packet, 'ctx', [(i, (i + back) % count) for i in range(count)])  1.42 us
    pallas_call x1, Pallas kernels, near_plan(): pl.pallas_call(functools.partial(attend_kernel, count, halo), out_shape=[...  1.11 us
    pallas_call x1, Pallas kernels, near_plan(): pl.pallas_call(functools.partial(own_kernel, count, doc_lengths.shape[0])...  1 us
    pallas_call x1, Pallas kernels, near_plan(): pl.pallas_call(functools.partial(place_kernel, count), out_shape=[jax.Sha...  0.98 us
  transfers between devices with their start and end apart: 5, of which 3 were waited for; matrix products, arithmetic and copies ran while one was open for 0% of the time, Pallas kernels for 6%

profile of v7, /device:TPU:0, one launch (start us, length us, event | category | flops | bytes accessed | tf_op | source)
XLA Modules:
  0.0 25.5 jit_solution(15916743689427870210)
XLA Ops:
  0.6 0.0 copy-start
  0.7 0.0 copy-start.3
  0.7 0.9 %fusion.2.packet_ref.refs_11_.refs_0_ = bf16[272,128]{1,0:T(8,128)(2,1)S(1)} fusion(bf16[128,128]{1,0:T(8,128)(2,1)} %param.11, bf16[128,128]{1,0:T(8,128)(2,1)} %param.10, s32[128]{0:T(128)} %param.8, s32[272]{0:T(512)S(1)} %iota_add_fusion, pred[272]{0:T(512)(128)(4,1)S(1)} %broadcast_compare_fusion), kind=kLoop, calls=%fused_computation.4 | loop fusion | flops 348160 | bytes 137040 | tf_op jit(solution)/shard_map/jit(_where)/select_n | solution.py:509
  1.6 3.1 %collective-permute-start = (bf16[272,128]{1,0:T(8,128)(2,1)S(1)}, bf16[272,128]{1,0:T(8,128)(2,1)S(1)}, u32[]{:S(2)}, u32[]{:S(2)}) collective-permute-start(bf16[272,128]{1,0:T(8,128)(2,1)S(1)} %fusion.2.packet_ref.refs_11_.refs_0_), channel_id=1, source_target_pairs={{0,4},{4,8},{8,12},{12,0},{1,5},{5,9},{9,13},{13,1},{2,6},{6,10},{... | collective-permute-start | bytes 208904 | tf_op jit(solution)/shard_map/ppermute | solution.py:515
  4.7 2.6 %collective-permute-start.1 = (bf16[272,128]{1,0:T(8,128)(2,1)S(1)}, bf16[272,128]{1,0:T(8,128)(2,1)S(1)}, u32[]{:S(2)}, u32[]{:S(2)}) collective-permute-start(bf16[272,128]{1,0:T(8,128)(2,1)S(1)} %fusion.2.packet_ref.refs_11_.refs_0_), channel_id=1, source_target_pairs={{0,8},{4,12},{8,0},{12,4},{1,9},{5,13},{9,1},{13,5},{2,10},{6,14},... | collective-permute-start | bytes 208904 | tf_op jit(solution)/shard_map/ppermute | solution.py:515
  7.3 0.0 copy-done
  7.3 0.0 copy-done.3
  7.3 0.0 copy-start.1
  7.3 0.9 %copy-done.1 = bf16[128,512]{1,0:T(8,128)(2,1)S(1)} copy-done((bf16[128,512]{1,0:T(8,128)(2,1)S(1)}, bf16[128,512]{1,0:T(8,128)(2,1)}, u32[]{:S(2)}) %copy-start.1) | copy-done | bytes 131096
  8.2 0.0 copy-start.2
  8.2 0.9 %copy-done.2 = bf16[128,512]{1,0:T(8,128)(2,1)S(1)} copy-done((bf16[128,512]{1,0:T(8,128)(2,1)S(1)}, bf16[128,512]{1,0:T(8,128)(2,1)}, u32[]{:S(2)}) %copy-start.2) | copy-done | bytes 131096
  9.1 1.0 %shard_map.94 = (bf16[512,128]{1,0:T(8,128)(2,1)S(1)}, bf16[512,128]{1,0:T(8,128)(2,1)S(1)}, f32[128,512]{1,0:T(8,128)S(1)}, f32[128,512]{1,0:T(8,128)S(1)}, f32...) custom-call(s32[16]{0:T(128)S(1)} %copy-done.3, ...), custom_call_target="tpu_custom_call" | custom-call | tf_op jit(solution)/shard_map/pallas_call | solution.py:522
  10.1 0.0 collective-permute-done.refs_4_.refs_12_.refs_1_
  10.1 0.3 %shard_map.95 = (f32[128,512]{1,0:T(8,128)S(1)}, f32[128,512]{1,0:T(8,128)S(1)}, f32[8,512]{1,0:T(8,128)S(1)}, bf16[512,128]{1,0:T(8,128)(2,1)S(1)}, f32[8,128]{1,0:T(8,128)S(1)}) custom-call(bf16[512,128]{1,0:T(8,128)(2,1)S(1)} %get-tuple-element.22.refs_0_, bf16[512,128]{1,0:T(8,128)(2,1)S(1)} %get-tuple-element.23.refs_1_, ...), custom_call_target="tpu_custom_call" | custom-call | tf_op jit(solution)/shard_map/pallas_call | solution.py:533
  10.5 1.4 %collective-permute-done.1.refs_13_.refs_2_ = bf16[272,128]{1,0:T(8,128)(2,1)S(1)} collective-permute-done((bf16[272,128]{1,0:T(8,128)(2,1)S(1)}, bf16[272,128]{1,0:T(8,128)(2,1)S(1)}, u32[]{:S(2)}, u32[]{:S(2)}) %collective-permute-start.1) | collective-permute-done | bytes 69664 | tf_op jit(solution)/shard_map/ppermute | solution.py:515
  11.9 1.1 %shard_map.96 = (bf16[512,128]{1,0:T(8,128)(2,1)S(1)}, bf16[512,128]{1,0:T(8,128)(2,1)S(1)}, bf16[512,128]{1,0:T(8,128)(2,1)S(1)}, bf16[512,128]{1,0:T(8,128)(2,1)S(1)}) custom-call(bf16[512,128]{1,0:T(8,128)(2,1)S(1)} %get-tuple-element.22.refs_0_, bf16[512,128]{1,0:T(8,128)(2,1)S(1)} %get-tuple-element.23.refs_1_, f32[8,512]{1,0:T(8,128)S(1)} %get-tuple-element.26.refs_2_, ...), custom_call_target="tpu_custom_call" | custom-call | tf_op jit(solution)/shard_map/pallas_call | solution.py:545
  13.0 2.0 %collective-permute-start.2 = (bf16[512,128]{1,0:T(8,128)(2,1)S(1)}, bf16[512,128]{1,0:T(8,128)(2,1)S(1)}, u32[]{:S(2)}, u32[]{:S(2)}) collective-permute-start(bf16[512,128]{1,0:T(8,128)(2,1)S(1)} %get-tuple-element.35), channel_id=1, source_target_pairs={{0,12},{4,8},{8,4},{12,0},{1,13},{5,9},{9,5},{13,1},{2,14},{6,10},... | collective-permute-start | bytes 393224 | tf_op jit(solution)/shard_map/ppermute | solution.py:553
  15.0 0.0 collective-permute-start.3
  15.0 2.4 %collective-permute-start.4 = (bf16[512,128]{1,0:T(8,128)(2,1)S(1)}, bf16[512,128]{1,0:T(8,128)(2,1)S(1)}, u32[]{:S(2)}, u32[]{:S(2)}) collective-permute-start(bf16[512,128]{1,0:T(8,128)(2,1)S(1)} %get-tuple-element.40), channel_id=1, source_target_pairs={{0,8},{4,12},{8,0},{12,4},{1,9},{5,13},{9,1},{13,5},{2,10},{6,14},... | collective-permute-start | bytes 393224 | tf_op jit(solution)/shard_map/ppermute | solution.py:553
  17.5 3.8 %collective-permute-done.2._.refs_3_ = bf16[512,128]{1,0:T(8,128)(2,1)S(1)} collective-permute-done((bf16[512,128]{1,0:T(8,128)(2,1)S(1)}, bf16[512,128]{1,0:T(8,128)(2,1)S(1)}, u32[]{:S(2)}, u32[]{:S(2)}) %collective-permute-start.2) | collective-permute-done | bytes 131104 | tf_op jit(solution)/shard_map/ppermute | solution.py:553
  21.3 0.3 %shard_map.97 = (bf16[128,256]{1,0:T(8,128)(2,1)S(1)}, bf16[128,512]{1,0:T(8,128)(2,1)S(1)}) custom-call(bf16[512,128]{1,0:T(8,128)(2,1)S(1)} %collective-permute-done.2._.refs_3_, bf16[272,128]{1,0:T(8,128)(2,1)S(1)} %fusion.2.packet_ref.refs_11_.refs_0_, bf16[272,128]{1,0:T(8,128)(2,1)S(1)} %collective-permute-done.refs_4_.refs_12_.refs_1_, ...), custom_call_target="tpu_custom_call" | custom-call | tf_op jit(solution)/shard_map/pallas_call | solution.py:555
  21.6 2.9 %collective-permute-done.3.refs_1_ = bf16[512,128]{1,0:T(8,128)(2,1)S(1)} collective-permute-done((bf16[512,128]{1,0:T(8,128)(2,1)S(1)}, bf16[512,128]{1,0:T(8,128)(2,1)S(1)}, u32[]{:S(2)}, u32[]{:S(2)}) %collective-permute-start.3) | collective-permute-done | bytes 131104 | tf_op jit(solution)/shard_map/ppermute | solution.py:553
  24.5 0.0 collective-permute-done.4.refs_2_
  24.5 1.0 %shard_map.98 = (f32[128,512]{1,0:T(8,128)}, f32[128,128]{1,0:T(8,128)}, f32[128,128]{1,0:T(8,128)}) custom-call(bf16[128,256]{1,0:T(8,128)(2,1)S(1)} %get-tuple-element.36.query_spread, bf16[128,512]{1,0:T(8,128)(2,1)S(1)} %get-tuple-element.37.key_spread, bf16[512,128]{1,0:T(8,128)(2,1)S(1)} %get-tuple-element.38.refs_0_, ...), custom_call_target="tpu_custom_call" | custom-call | tf_op jit(solution)/shard_map/pallas_call | solution.py:565
  (2 shorter events, 0.0 us)
Async XLA Ops:
  0.6 6.7 %copy-start = (bf16[128,512]{1,0:T(8,128)(2,1)S(1)}, bf16[128,512]{1,0:T(8,128)(2,1)}, u32[]{:S(2)}) copy-start(bf16[128,512]{1,0:T(8,128)(2,1)} %query_ref.1) | copy-start | bytes 393220
  0.7 6.6 %copy-start.3 = (s32[16]{0:T(128)S(1)}, s32[16]{0:T(128)}, u32[]{:S(2)}) copy-start(s32[16]{0:T(128)} %doc_ref.1) | copy-start | bytes 196
  1.6 8.5 %collective-permute-start = (bf16[272,128]{1,0:T(8,128)(2,1)S(1)}, bf16[272,128]{1,0:T(8,128)(2,1)S(1)}, u32[]{:S(2)}, u32[]{:S(2)}) collective-permute-start(bf16[272,128]{1,0:T(8,128)(2,1)S(1)} %fusion.2.packet_ref.refs_11_.refs_0_), channel_id=1, source_target_pairs={{0,4},{4,8},{8,12},{12,0},{1,5},{5,9},{9,13},{13,1},{2,6},{6,10},{... | collective-permute-start | bytes 208904 | tf_op jit(solution)/shard_map/ppermute | solution.py:515
  4.7 7.2 %collective-permute-start.1 = (bf16[272,128]{1,0:T(8,128)(2,1)S(1)}, bf16[272,128]{1,0:T(8,128)(2,1)S(1)}, u32[]{:S(2)}, u32[]{:S(2)}) collective-permute-start(bf16[272,128]{1,0:T(8,128)(2,1)S(1)} %fusion.2.packet_ref.refs_11_.refs_0_), channel_id=1, source_target_pairs={{0,8},{4,12},{8,0},{12,4},{1,9},{5,13},{9,1},{13,5},{2,10},{6,14},... | collective-permute-start | bytes 208904 | tf_op jit(solution)/shard_map/ppermute | solution.py:515
  7.3 0.9 %copy-start.1 = (bf16[128,512]{1,0:T(8,128)(2,1)S(1)}, bf16[128,512]{1,0:T(8,128)(2,1)}, u32[]{:S(2)}) copy-start(bf16[128,512]{1,0:T(8,128)(2,1)} %grad_ref.1) | copy-start | bytes 393220
  8.2 0.9 %copy-start.2 = (bf16[128,512]{1,0:T(8,128)(2,1)S(1)}, bf16[128,512]{1,0:T(8,128)(2,1)}, u32[]{:S(2)}) copy-start(bf16[128,512]{1,0:T(8,128)(2,1)} %saved_ref.1) | copy-start | bytes 393220
  13.0 8.3 %collective-permute-start.2 = (bf16[512,128]{1,0:T(8,128)(2,1)S(1)}, bf16[512,128]{1,0:T(8,128)(2,1)S(1)}, u32[]{:S(2)}, u32[]{:S(2)}) collective-permute-start(bf16[512,128]{1,0:T(8,128)(2,1)S(1)} %get-tuple-element.35), channel_id=1, source_target_pairs={{0,12},{4,8},{8,4},{12,0},{1,13},{5,9},{9,5},{13,1},{2,14},{6,10},... | collective-permute-start | bytes 393224 | tf_op jit(solution)/shard_map/ppermute | solution.py:553
  15.0 9.4 %collective-permute-start.3 = (bf16[512,128]{1,0:T(8,128)(2,1)S(1)}, bf16[512,128]{1,0:T(8,128)(2,1)S(1)}, u32[]{:S(2)}, u32[]{:S(2)}) collective-permute-start(bf16[512,128]{1,0:T(8,128)(2,1)S(1)} %get-tuple-element.39), channel_id=1, source_target_pairs={{0,4},{4,0},{8,12},{12,8},{1,5},{5,1},{9,13},{13,9},{2,6},{6,2},{1... | collective-permute-start | bytes 393224 | tf_op jit(solution)/shard_map/ppermute | solution.py:553
  15.0 9.4 %collective-permute-start.4 = (bf16[512,128]{1,0:T(8,128)(2,1)S(1)}, bf16[512,128]{1,0:T(8,128)(2,1)S(1)}, u32[]{:S(2)}, u32[]{:S(2)}) collective-permute-start(bf16[512,128]{1,0:T(8,128)(2,1)S(1)} %get-tuple-element.40), channel_id=1, source_target_pairs={{0,8},{4,12},{8,0},{12,4},{1,9},{5,13},{9,1},{13,5},{2,10},{6,14},... | collective-permute-start | bytes 393224 | tf_op jit(solution)/shard_map/ppermute | solution.py:553

commit v8 on v7

--- a/solution.py
+++ b/solution.py
@@ -335,6 +335,14 @@
     filled_out[count:, :] = jnp.zeros((8 - count, rows), jnp.float32)
 
 
+def packets_of(refs, halo):
+    even = lax.rem(lax.axis_index("ctx"), 2) == 0
+    packets = [ref[...] for ref in refs[: 1 + min(halo, 1)]]
+    for n in range(2, 2 * halo, 2):
+        packets.append(jnp.where(even, refs[n][...], refs[n + 1][...]))
+    return packets
+
+
 def fold(count, back, packet, queries, grads, row, filled):
     rows = packet.shape[1]
     index = lax.axis_index("ctx")
@@ -363,9 +371,9 @@
 
 def step_kernel(count, back, *refs):
     query_ref, grad_ref, row_ref, filled_ref, packet_ref = refs[:5]
-    raised_out, change_out, row_out, target_out, filled_out = refs[5:]
+    raised_out, change_out, row_out, target_out, filled_out = refs[-5:]
     raised, change, (top, total, factors), target, filled = fold(
-        count, back, packet_ref, query_ref[...], grad_ref[...], row_ref, filled_ref
+        count, back, packet_ref[...], query_ref[...], grad_ref[...], row_ref, filled_ref
     )
     raised_out[...] = raised
     change_out[...] = change
@@ -384,8 +392,8 @@
     raised_refs = refs[5 : 5 + halo]
     change_refs = refs[5 + halo : 5 + 2 * halo]
     target_refs = refs[5 + 2 * halo : 5 + 3 * halo]
-    packets = refs[5 + 3 * halo : 6 + 4 * halo]
-    outs = refs[6 + 4 * halo :]
+    outs = refs[-count:]
+    packets = packets_of(refs[5 + 3 * halo : -count], halo)
     rows = packets[0].shape[1]
     depth = query_ref.shape[1]
     heads = query_ref.shape[0] // rows
@@ -429,13 +437,13 @@
 
 
 def order_kernel(count, halo, _, *refs):
-    packets = refs[: 1 + halo]
-    query_out, key_out = refs[1 + halo :]
+    query_out, key_out = refs[-2:]
+    packets = packets_of(refs[:-2], halo)
     rows = query_out.shape[0]
     index = lax.axis_index("ctx")
     given = []
-    for ref in packets:
-        hot = ref[2 * rows : 2 * rows + count, :].astype(jnp.float32)
+    for packet in packets:
+        hot = packet[2 * rows : 2 * rows + count, :].astype(jnp.float32)
         counts = jnp.sum(hot, axis=1, keepdims=True)
         mine = jnp.zeros((1, 1), jnp.float32)
         for p in range(count):
@@ -511,10 +519,11 @@
         jnp.pad(jnp.concatenate([key_head_rows, value_head_rows], axis=0), ((0, META), (0, 0))),
         (owners[None, :] == mark).astype(bf16),
     )
-    near = [
-        lax.ppermute(packet, "ctx", [(i, (i + back) % count) for i in range(count)])
-        for back in range(1, halo + 1)
-    ]
+    near = [lax.ppermute(packet, "ctx", [(i, (i + 1) % count) for i in range(count)])]
+    for back in range(2, halo + 1):
+        for part in range(2):
+            pairs = [(i, (i + back) % count if i % 2 == part else i) for i in range(count)]
+            near.append(lax.ppermute(packet, "ctx", pairs))
     block_shapes = [jax.ShapeDtypeStruct((rows, columns), f32)] * 2
     row_shape = jax.ShapeDtypeStruct((8, columns), f32)
     target_shape = jax.ShapeDtypeStruct((count * rows, rows), bf16)
@@ -533,10 +542,10 @@
         found = pl.pallas_call(
             functools.partial(step_kernel, count, back),
             out_shape=block_shapes + [row_shape, target_shape, filled_shape],
-            in_specs=[whole] * 5,
+            in_specs=[whole] * 5 + [pl.BlockSpec(memory_space=pl.ANY)],
             out_specs=[whole] * 5,
             compiler_params=params,
-        )(query_rows, grad_rows, row, filled, near[back - 1])
+        )(query_rows, grad_rows, row, filled, near[back - 1], near[1])
         raised.append(found[0])
         change.append(found[1])
         row = found[2]
@@ -545,7 +554,7 @@
     sent = pl.pallas_call(
         functools.partial(attend_kernel, count, halo),
         out_shape=[jax.ShapeDtypeStruct((heads * slot + 2 * rows, depth), bf16)] * count,
-        in_specs=[whole] * (6 + 4 * halo),
+        in_specs=[whole] * (6 + 3 * halo + len(near)),
         out_specs=[whole] * count,
         compiler_params=params,
     )(query_rows, grad_rows, row, filled, spread, *raised, *change, *target, packet, *near)
@@ -558,7 +567,7 @@
             jax.ShapeDtypeStruct((rows, count * slot), bf16),
             jax.ShapeDtypeStruct((rows, count * rows), bf16),
         ],
-        in_specs=[pl.BlockSpec(memory_space=pl.ANY)] + [whole] * (1 + halo),
+        in_specs=[pl.BlockSpec(memory_space=pl.ANY)] + [whole] * (1 + len(near)),
         out_specs=[whole] * 2,
         compiler_params=params,
     )(received[-1], packet, *near)

time: 25.6 us -> 31.1 us (1.21)
  waiting for transfers between devices: 8.16 us -> 12.2 us
  starting transfers between devices: 10.1 us -> 11.5 us
    ppermute x3, waiting for transfers between devices: 6.74 us -> 9.27 us  [near_plan(): lax.ppermute(sent[k], 'ctx', [(i, i ^ k) for i in range(count)])]
    ppermute x2 -> x3, waiting for transfers between devices: 1.42 us -> 2.91 us  [the longest x1 2.9 us: near_plan(): lax.ppermute(packet, 'ctx', [(i, (i + 1) % count) for i in range(count)])]
    ppermute x2 -> x3, starting transfers between devices: 5.67 us -> 6.67 us  [the longest x2 6.61 us: near_plan(): near.append(lax.ppermute(packet, 'ctx', pairs))]
    ppermute x3, starting transfers between devices: 4.45 us -> 4.82 us  [near_plan(): lax.ppermute(sent[k], 'ctx', [(i, i ^ k) for i in range(count)])]
  transfers between devices with their start and end apart: 5 -> 6, of which waited for: 3 -> 4; matrix products, arithmetic and copies ran while one was open for 0% -> 0% of each run, Pallas kernels for 6% -> 5%
where the time goes in v8:
time: 31.1 us; the launch traced here: 30.9 us
  waiting for transfers between devices  12.2 us (39%)
  starting transfers between devices  11.5 us (37%)
  Pallas kernels  3.72 us (12%)
  local copies, waits for them, and re-layouts  1.81 us (6%)
  other arithmetic  0.96 us (3%)
  between operations  0.76 us (2%)
    ppermute x3, waiting for transfers between devices, near_plan(): lax.ppermute(sent[k], 'ctx', [(i, i ^ k) for i in range(count)])  9.27 us
    ppermute x2, starting transfers between devices, near_plan(): near.append(lax.ppermute(packet, 'ctx', pairs))  6.61 us
    ppermute x3, starting transfers between devices, near_plan(): lax.ppermute(sent[k], 'ctx', [(i, i ^ k) for i in range(count)])  4.82 us
    ppermute x1, waiting for transfers between devices, near_plan(): lax.ppermute(packet, 'ctx', [(i, (i + 1) % count) for i in range(count)])  2.9 us
    unnamed x8, local copies, waits for them, and re-layouts  1.81 us
    pallas_call x1, Pallas kernels, near_plan(): pl.pallas_call(functools.partial(attend_kernel, count, halo), out_shape=[...  1.12 us
    pallas_call x1, Pallas kernels, near_plan(): pl.pallas_call(functools.partial(own_kernel, count, doc_lengths.shape[0])...  1.01 us
    pallas_call x1, Pallas kernels, near_plan(): pl.pallas_call(functools.partial(place_kernel, count), out_shape=[jax.Sha...  0.97 us
  transfers between devices with their start and end apart: 6, of which 4 were waited for; matrix products, arithmetic and copies ran while one was open for 0% of the time, Pallas kernels for 5%

profile of v8, /device:TPU:0, one launch (start us, length us, event | category | flops | bytes accessed | tf_op | source)
XLA Modules:
  0.0 30.9 jit_solution(15282669538142540577)
XLA Ops:
  0.6 0.0 copy-start
  0.7 0.0 copy-start.3
  0.7 0.9 %fusion.2.packet_ref.refs_11_.refs_0_ = bf16[272,128]{1,0:T(8,128)(2,1)S(1)} fusion(bf16[128,128]{1,0:T(8,128)(2,1)} %param.11, bf16[128,128]{1,0:T(8,128)(2,1)} %param.10, s32[128]{0:T(128)} %param.8, s32[272]{0:T(512)S(1)} %iota_add_fusion, pred[272]{0:T(512)(128)(4,1)S(1)} %broadcast_compare_fusion), kind=kLoop, calls=%fused_computation.4 | loop fusion | flops 348160 | bytes 137040 | tf_op jit(solution)/shard_map/jit(_where)/select_n | solution.py:517
  1.6 5.9 %collective-permute-start.1 = (bf16[272,128]{1,0:T(8,128)(2,1)S(1)}, bf16[272,128]{1,0:T(8,128)(2,1)S(1)}, u32[]{:S(2)}, u32[]{:S(2)}) collective-permute-start(bf16[272,128]{1,0:T(8,128)(2,1)S(1)} %fusion.2.packet_ref.refs_11_.refs_0_), channel_id=1, source_target_pairs={{0,8},{4,4},{8,0},{12,12},{1,9},{5,5},{9,1},{13,13},{2,10},{6,6},{... | collective-permute-start | bytes 208904 | tf_op jit(solution)/shard_map/ppermute | solution.py:526
  7.6 0.1 collective-permute-start
  7.6 0.7 %collective-permute-start.2 = (bf16[272,128]{1,0:T(8,128)(2,1)S(1)}, bf16[272,128]{1,0:T(8,128)(2,1)S(1)}, u32[]{:S(2)}, u32[]{:S(2)}) collective-permute-start(bf16[272,128]{1,0:T(8,128)(2,1)S(1)} %fusion.2.packet_ref.refs_11_.refs_0_), channel_id=1, source_target_pairs={{0,0},{4,12},{8,8},{12,4},{1,1},{5,13},{9,9},{13,5},{2,2},{6,14},{... | collective-permute-start | bytes 208904 | tf_op jit(solution)/shard_map/ppermute | solution.py:526
  8.3 0.0 copy-done
  8.3 0.0 copy-start.1
  8.4 0.9 %copy-done.1 = bf16[128,512]{1,0:T(8,128)(2,1)S(1)} copy-done((bf16[128,512]{1,0:T(8,128)(2,1)S(1)}, bf16[128,512]{1,0:T(8,128)(2,1)}, u32[]{:S(2)}) %copy-start.1) | copy-done | bytes 131096
  9.2 0.9 %copy-done.2 = bf16[128,512]{1,0:T(8,128)(2,1)S(1)} copy-done((bf16[128,512]{1,0:T(8,128)(2,1)S(1)}, bf16[128,512]{1,0:T(8,128)(2,1)}, u32[]{:S(2)}) %copy-start.2) | copy-done | bytes 131096
  10.2 1.0 %shard_map.94 = (bf16[512,128]{1,0:T(8,128)(2,1)S(1)}, bf16[512,128]{1,0:T(8,128)(2,1)S(1)}, f32[128,512]{1,0:T(8,128)S(1)}, f32[128,512]{1,0:T(8,128)S(1)}, f32...) custom-call(s32[16]{0:T(128)S(1)} %copy-done.3, ...), custom_call_target="tpu_custom_call" | custom-call | tf_op jit(solution)/shard_map/pallas_call | solution.py:531
  11.2 0.0 collective-permute-done.1.refs_5_.refs_13_.refs_2_
  11.2 2.9 %collective-permute-done.refs_4_.refs_12_.refs_1_ = bf16[272,128]{1,0:T(8,128)(2,1)S(1)} collective-permute-done((bf16[272,128]{1,0:T(8,128)(2,1)S(1)}, bf16[272,128]{1,0:T(8,128)(2,1)S(1)}, u32[]{:S(2)}, u32[]{:S(2)}) %collective-permute-start) | collective-permute-done | bytes 69664 | tf_op jit(solution)/shard_map/ppermute | solution.py:522
  14.1 0.3 %shard_map.95 = (f32[128,512]{1,0:T(8,128)S(1)}, f32[128,512]{1,0:T(8,128)S(1)}, f32[8,512]{1,0:T(8,128)S(1)}, bf16[512,128]{1,0:T(8,128)(2,1)S(1)}, f32[8,128]{1,0:T(8,128)S(1)}) custom-call(bf16[512,128]{1,0:T(8,128)(2,1)S(1)} %get-tuple-element.22.refs_0_, bf16[512,128]{1,0:T(8,128)(2,1)S(1)} %get-tuple-element.23.refs_1_, ...), custom_call_target="tpu_custom_call" | custom-call | tf_op jit(solution)/shard_map/pallas_call | solution.py:542
  14.4 0.0 collective-permute-done.2.refs_14_.refs_3_
  14.4 1.1 %shard_map.96 = (bf16[512,128]{1,0:T(8,128)(2,1)S(1)}, bf16[512,128]{1,0:T(8,128)(2,1)S(1)}, bf16[512,128]{1,0:T(8,128)(2,1)S(1)}, bf16[512,128]{1,0:T(8,128)(2,1)S(1)}) custom-call(bf16[512,128]{1,0:T(8,128)(2,1)S(1)} %get-tuple-element.22.refs_0_, bf16[512,128]{1,0:T(8,128)(2,1)S(1)} %get-tuple-element.23.refs_1_, f32[8,512]{1,0:T(8,128)S(1)} %get-tuple-element.26.refs_2_, ...), custom_call_target="tpu_custom_call" | custom-call | tf_op jit(solution)/shard_map/pallas_call | solution.py:554
  15.6 4.2 %collective-permute-start.3 = (bf16[512,128]{1,0:T(8,128)(2,1)S(1)}, bf16[512,128]{1,0:T(8,128)(2,1)S(1)}, u32[]{:S(2)}, u32[]{:S(2)}) collective-permute-start(bf16[512,128]{1,0:T(8,128)(2,1)S(1)} %get-tuple-element.35), channel_id=1, source_target_pairs={{0,12},{4,8},{8,4},{12,0},{1,13},{5,9},{9,5},{13,1},{2,14},{6,10},... | collective-permute-start | bytes 393224 | tf_op jit(solution)/shard_map/ppermute | solution.py:562
  19.7 0.0 collective-permute-start.4
  19.7 0.6 %collective-permute-start.5 = (bf16[512,128]{1,0:T(8,128)(2,1)S(1)}, bf16[512,128]{1,0:T(8,128)(2,1)S(1)}, u32[]{:S(2)}, u32[]{:S(2)}) collective-permute-start(bf16[512,128]{1,0:T(8,128)(2,1)S(1)} %get-tuple-element.40), channel_id=1, source_target_pairs={{0,8},{4,12},{8,0},{12,4},{1,9},{5,13},{9,1},{13,5},{2,10},{6,14},... | collective-permute-start | bytes 393224 | tf_op jit(solution)/shard_map/ppermute | solution.py:562
  20.4 3.7 %collective-permute-done.3._.refs_3_ = bf16[512,128]{1,0:T(8,128)(2,1)S(1)} collective-permute-done((bf16[512,128]{1,0:T(8,128)(2,1)S(1)}, bf16[512,128]{1,0:T(8,128)(2,1)S(1)}, u32[]{:S(2)}, u32[]{:S(2)}) %collective-permute-start.3) | collective-permute-done | bytes 131104 | tf_op jit(solution)/shard_map/ppermute | solution.py:562
  24.0 0.3 shard_map.97
  24.3 1.1 %collective-permute-done.4.refs_1_ = bf16[512,128]{1,0:T(8,128)(2,1)S(1)} collective-permute-done((bf16[512,128]{1,0:T(8,128)(2,1)S(1)}, bf16[512,128]{1,0:T(8,128)(2,1)S(1)}, u32[]{:S(2)}, u32[]{:S(2)}) %collective-permute-start.4) | collective-permute-done | bytes 131104 | tf_op jit(solution)/shard_map/ppermute | solution.py:562
  25.4 4.5 %collective-permute-done.5.refs_2_ = bf16[512,128]{1,0:T(8,128)(2,1)S(1)} collective-permute-done((bf16[512,128]{1,0:T(8,128)(2,1)S(1)}, bf16[512,128]{1,0:T(8,128)(2,1)S(1)}, u32[]{:S(2)}, u32[]{:S(2)}) %collective-permute-start.5) | collective-permute-done | bytes 131104 | tf_op jit(solution)/shard_map/ppermute | solution.py:562
  29.9 1.0 %shard_map.98 = (f32[128,512]{1,0:T(8,128)}, f32[128,128]{1,0:T(8,128)}, f32[128,128]{1,0:T(8,128)}) custom-call(bf16[128,256]{1,0:T(8,128)(2,1)S(1)} %get-tuple-element.36.query_spread, bf16[128,512]{1,0:T(8,128)(2,1)S(1)} %get-tuple-element.37.key_spread, bf16[512,128]{1,0:T(8,128)(2,1)S(1)} %get-tuple-element.38.refs_0_, ...), custom_call_target="tpu_custom_call" | custom-call | tf_op jit(solution)/shard_map/pallas_call | solution.py:574
  (4 shorter events, 0.0 us)
Async XLA Ops:
  0.6 7.7 %copy-start = (bf16[128,512]{1,0:T(8,128)(2,1)S(1)}, bf16[128,512]{1,0:T(8,128)(2,1)}, u32[]{:S(2)}) copy-start(bf16[128,512]{1,0:T(8,128)(2,1)} %query_ref.1) | copy-start | bytes 393220
  0.7 7.7 %copy-start.3 = (s32[16]{0:T(128)S(1)}, s32[16]{0:T(128)}, u32[]{:S(2)}) copy-start(s32[16]{0:T(128)} %doc_ref.1) | copy-start | bytes 196
  1.6 9.5 %collective-permute-start.1 = (bf16[272,128]{1,0:T(8,128)(2,1)S(1)}, bf16[272,128]{1,0:T(8,128)(2,1)S(1)}, u32[]{:S(2)}, u32[]{:S(2)}) collective-permute-start(bf16[272,128]{1,0:T(8,128)(2,1)S(1)} %fusion.2.packet_ref.refs_11_.refs_0_), channel_id=1, source_target_pairs={{0,8},{4,4},{8,0},{12,12},{1,9},{5,5},{9,1},{13,13},{2,10},{6,6},{... | collective-permute-start | bytes 208904 | tf_op jit(solution)/shard_map/ppermute | solution.py:526
  7.6 6.5 %collective-permute-start = (bf16[272,128]{1,0:T(8,128)(2,1)S(1)}, bf16[272,128]{1,0:T(8,128)(2,1)S(1)}, u32[]{:S(2)}, u32[]{:S(2)}) collective-permute-start(bf16[272,128]{1,0:T(8,128)(2,1)S(1)} %fusion.2.packet_ref.refs_11_.refs_0_), channel_id=1, source_target_pairs={{0,4},{4,8},{8,12},{12,0},{1,5},{5,9},{9,13},{13,1},{2,6},{6,10},{... | collective-permute-start | bytes 208904 | tf_op jit(solution)/shard_map/ppermute | solution.py:522
  7.6 6.8 %collective-permute-start.2 = (bf16[272,128]{1,0:T(8,128)(2,1)S(1)}, bf16[272,128]{1,0:T(8,128)(2,1)S(1)}, u32[]{:S(2)}, u32[]{:S(2)}) collective-permute-start(bf16[272,128]{1,0:T(8,128)(2,1)S(1)} %fusion.2.packet_ref.refs_11_.refs_0_), channel_id=1, source_target_pairs={{0,0},{4,12},{8,8},{12,4},{1,1},{5,13},{9,9},{13,5},{2,2},{6,14},{... | collective-permute-start | bytes 208904 | tf_op jit(solution)/shard_map/ppermute | solution.py:526
  8.3 0.9 %copy-start.1 = (bf16[128,512]{1,0:T(8,128)(2,1)S(1)}, bf16[128,512]{1,0:T(8,128)(2,1)}, u32[]{:S(2)}) copy-start(bf16[128,512]{1,0:T(8,128)(2,1)} %grad_ref.1) | copy-start | bytes 393220
  9.2 0.9 %copy-start.2 = (bf16[128,512]{1,0:T(8,128)(2,1)S(1)}, bf16[128,512]{1,0:T(8,128)(2,1)}, u32[]{:S(2)}) copy-start(bf16[128,512]{1,0:T(8,128)(2,1)} %saved_ref.1) | copy-start | bytes 393220
  15.6 8.5 %collective-permute-start.3 = (bf16[512,128]{1,0:T(8,128)(2,1)S(1)}, bf16[512,128]{1,0:T(8,128)(2,1)S(1)}, u32[]{:S(2)}, u32[]{:S(2)}) collective-permute-start(bf16[512,128]{1,0:T(8,128)(2,1)S(1)} %get-tuple-element.35), channel_id=1, source_target_pairs={{0,12},{4,8},{8,4},{12,0},{1,13},{5,9},{9,5},{13,1},{2,14},{6,10},... | collective-permute-start | bytes 393224 | tf_op jit(solution)/shard_map/ppermute | solution.py:562
  19.7 5.7 %collective-permute-start.4 = (bf16[512,128]{1,0:T(8,128)(2,1)S(1)}, bf16[512,128]{1,0:T(8,128)(2,1)S(1)}, u32[]{:S(2)}, u32[]{:S(2)}) collective-permute-start(bf16[512,128]{1,0:T(8,128)(2,1)S(1)} %get-tuple-element.39), channel_id=1, source_target_pairs={{0,4},{4,0},{8,12},{12,8},{1,5},{5,1},{9,13},{13,9},{2,6},{6,2},{1... | collective-permute-start | bytes 393224 | tf_op jit(solution)/shard_map/ppermute | solution.py:562
  19.7 10.2 %collective-permute-start.5 = (bf16[512,128]{1,0:T(8,128)(2,1)S(1)}, bf16[512,128]{1,0:T(8,128)(2,1)S(1)}, u32[]{:S(2)}, u32[]{:S(2)}) collective-permute-start(bf16[512,128]{1,0:T(8,128)(2,1)S(1)} %get-tuple-element.40), channel_id=1, source_target_pairs={{0,8},{4,12},{8,0},{12,4},{1,9},{5,13},{9,1},{13,5},{2,10},{6,14},... | collective-permute-start | bytes 393224 | tf_op jit(solution)/shard_map/ppermute | solution.py:562

commit v9 on v7

--- a/solution.py
+++ b/solution.py
@@ -234,7 +234,7 @@
     return (query_grad * inverse_root, key_grad * inverse_root, value_grad)
 
 
-META = 16
+META = 8
 
 
 def contract(left, right, left_dim, right_dim, **kw):
@@ -409,14 +409,14 @@
     changes = jnp.concatenate(changes, axis=0)
     keys = jnp.concatenate([packet[0:rows, :] for packet in packets], axis=0)
     query_grad = (contract(keys, changes, 0, 0) * scale).astype(jnp.bfloat16)
-    value_parts = contract(weights, grads, 1, 0).astype(jnp.bfloat16)
-    key_parts = (contract(changes, queries, 1, 0) * scale).astype(jnp.bfloat16)
+    key_parts = contract(changes, queries, 1, 0) * scale
+    value_parts = contract(weights, grads, 1, 0)
+    parts = jnp.concatenate([key_parts, value_parts], axis=1).astype(jnp.bfloat16)
 
     query_slots = contract(spread_ref[...], end_to_end(query_grad, heads), 1, 1)
     query_slots = query_slots.astype(jnp.bfloat16)
     spread = jnp.concatenate([ref[...] for ref in target_refs] + [target], axis=1)
-    key_slots = contract(spread, key_parts, 1, 0).astype(jnp.bfloat16)
-    value_slots = contract(spread, value_parts, 1, 0).astype(jnp.bfloat16)
+    part_slots = contract(spread, parts, 1, 0).astype(jnp.bfloat16)
     at = heads * slot
     for k in range(count):
         out = outs[k]
@@ -424,8 +424,10 @@
             out[h * slot : (h + 1) * slot, :] = query_slots[
                 k * slot : (k + 1) * slot, h * depth : (h + 1) * depth
             ]
-        out[at : at + rows, :] = key_slots[k * rows : (k + 1) * rows, :]
-        out[at + rows :, :] = value_slots[k * rows : (k + 1) * rows, :]
+        for n in range(2):
+            out[at + n * rows : at + (n + 1) * rows, :] = part_slots[
+                k * rows : (k + 1) * rows, n * depth : (n + 1) * depth
+            ]
 
 
 def order_kernel(count, halo, _, *refs):
@@ -479,15 +481,23 @@
         copies.append(pltpu.make_async_copy(here, out, sems.at[len(copies)]))
         copies[-1].start()
 
-    for h in range(heads):
-        at = slice(h * depth, (h + 1) * depth)
-        taken = jnp.concatenate([ref[h * slot : (h + 1) * slot, :] for ref in ins], axis=0)
-        query_here[:, at] = contract(query_spread[...], taken, 1, 0)
-        leave(query_here.at[:, at], query_out.at[:, at])
+    def taken(first, size, pieces):
+        return jnp.concatenate(
+            [
+                jnp.concatenate(
+                    [ref[first + n * size : first + (n + 1) * size, :] for n in range(pieces)],
+                    axis=1,
+                )
+                for ref in ins
+            ],
+            axis=0,
+        )
+
+    query_here[...] = contract(query_spread[...], taken(0, slot, heads), 1, 0)
+    leave(query_here, query_out)
+    both = contract(key_spread[...], taken(heads * slot, rows, 2), 1, 0)
     for n, (here, out) in enumerate(((key_here, key_out), (value_here, value_out))):
-        at = heads * slot + n * rows
-        taken = jnp.concatenate([ref[at : at + rows, :] for ref in ins], axis=0)
-        here[...] = contract(key_spread[...], taken, 1, 0)
+        here[...] = both[:, n * depth : (n + 1) * depth]
         leave(here, out)
     for copy in copies:
         copy.wait()
@@ -575,7 +585,7 @@
             pltpu.VMEM((rows, width), f32),
             pltpu.VMEM((rows, depth), f32),
             pltpu.VMEM((rows, depth), f32),
-            pltpu.SemaphoreType.DMA((heads + 2,)),
+            pltpu.SemaphoreType.DMA((3,)),
         ],
         compiler_params=params,
     )(*spreads, *received)

time: 25.6 us -> 25.5 us (level)
  no operation moved by 1% of the time
where the time goes in v9:
time: 25.5 us; the launch traced here: 25.3 us
  starting transfers between devices  10.1 us (40%)
  waiting for transfers between devices  8.01 us (31%)
  Pallas kernels  3.67 us (14%)
  local copies, waits for them, and re-layouts  1.82 us (7%)
  other arithmetic  0.95 us (4%)
  between operations  0.71 us (3%)
    ppermute x3, waiting for transfers between devices, near_plan(): lax.ppermute(sent[k], 'ctx', [(i, i ^ k) for i in range(count)])  6.72 us
    ppermute x2, starting transfers between devices, near_plan(): lax.ppermute(packet, 'ctx', [(i, (i + back) % count) for i in range(count)])  5.67 us
    ppermute x3, starting transfers between devices, near_plan(): lax.ppermute(sent[k], 'ctx', [(i, i ^ k) for i in range(count)])  4.45 us
    unnamed x8, local copies, waits for them, and re-layouts  1.82 us
    ppermute x2, waiting for transfers between devices, near_plan(): lax.ppermute(packet, 'ctx', [(i, (i + back) % count) for i in range(count)])  1.29 us
    pallas_call x1, Pallas kernels, near_plan(): pl.pallas_call(functools.partial(attend_kernel, count, halo), out_shape=[...  1.04 us
    pallas_call x1, Pallas kernels, near_plan(): pl.pallas_call(functools.partial(place_kernel, count), out_shape=[jax.Sha...  1.01 us
    pallas_call x1, Pallas kernels, near_plan(): pl.pallas_call(functools.partial(own_kernel, count, doc_lengths.shape[0])...  1 us
  transfers between devices with their start and end apart: 5, of which 3 were waited for; matrix products, arithmetic and copies ran while one was open for 0% of the time, Pallas kernels for 6%

profile of v9, /device:TPU:0, one launch (start us, length us, event | category | flops | bytes accessed | tf_op | source)
XLA Modules:
  0.0 25.3 jit_solution(8942564751882982614)
XLA Ops:
  0.6 0.0 copy-start
  0.7 0.0 copy-start.3
  0.7 0.9 %fusion.2.packet_ref.refs_11_.refs_0_ = bf16[264,128]{1,0:T(8,128)(2,1)S(1)} fusion(bf16[128,128]{1,0:T(8,128)(2,1)} %param.11, bf16[128,128]{1,0:T(8,128)(2,1)} %param.10, s32[128]{0:T(128)} %param.8, s32[264]{0:T(512)S(1)} %iota_add_fusion, pred[264]{0:T(512)(128)(4,1)S(1)} %broadcast_compare_fusion), kind=kLoop, calls=%fused_computation.4 | loop fusion | flops 337920 | bytes 134952 | tf_op jit(solution)/shard_map/jit(_where)/select_n | solution.py:519
  1.6 3.1 %collective-permute-start = (bf16[264,128]{1,0:T(8,128)(2,1)S(1)}, bf16[264,128]{1,0:T(8,128)(2,1)S(1)}, u32[]{:S(2)}, u32[]{:S(2)}) collective-permute-start(bf16[264,128]{1,0:T(8,128)(2,1)S(1)} %fusion.2.packet_ref.refs_11_.refs_0_), channel_id=1, source_target_pairs={{0,4},{4,8},{8,12},{12,0},{1,5},{5,9},{9,13},{13,1},{2,6},{6,10},{... | collective-permute-start | bytes 202760 | tf_op jit(solution)/shard_map/ppermute | solution.py:525
  4.7 2.6 %collective-permute-start.1 = (bf16[264,128]{1,0:T(8,128)(2,1)S(1)}, bf16[264,128]{1,0:T(8,128)(2,1)S(1)}, u32[]{:S(2)}, u32[]{:S(2)}) collective-permute-start(bf16[264,128]{1,0:T(8,128)(2,1)S(1)} %fusion.2.packet_ref.refs_11_.refs_0_), channel_id=1, source_target_pairs={{0,8},{4,12},{8,0},{12,4},{1,9},{5,13},{9,1},{13,5},{2,10},{6,14},... | collective-permute-start | bytes 202760 | tf_op jit(solution)/shard_map/ppermute | solution.py:525
  7.3 0.0 copy-done
  7.3 0.0 copy-done.3
  7.3 0.0 copy-start.1
  7.3 0.9 %copy-done.1 = bf16[128,512]{1,0:T(8,128)(2,1)S(1)} copy-done((bf16[128,512]{1,0:T(8,128)(2,1)S(1)}, bf16[128,512]{1,0:T(8,128)(2,1)}, u32[]{:S(2)}) %copy-start.1) | copy-done | bytes 131096
  8.2 0.0 copy-start.2
  8.2 0.9 %copy-done.2 = bf16[128,512]{1,0:T(8,128)(2,1)S(1)} copy-done((bf16[128,512]{1,0:T(8,128)(2,1)S(1)}, bf16[128,512]{1,0:T(8,128)(2,1)}, u32[]{:S(2)}) %copy-start.2) | copy-done | bytes 131096
  9.1 1.0 %shard_map.94 = (bf16[512,128]{1,0:T(8,128)(2,1)S(1)}, bf16[512,128]{1,0:T(8,128)(2,1)S(1)}, f32[128,512]{1,0:T(8,128)S(1)}, f32[128,512]{1,0:T(8,128)S(1)}, f32...) custom-call(s32[16]{0:T(128)S(1)} %copy-done.3, ...), custom_call_target="tpu_custom_call" | custom-call | tf_op jit(solution)/shard_map/pallas_call | solution.py:532
  10.1 0.0 collective-permute-done.refs_4_.refs_12_.refs_1_
  10.1 0.3 %shard_map.95 = (f32[128,512]{1,0:T(8,128)S(1)}, f32[128,512]{1,0:T(8,128)S(1)}, f32[8,512]{1,0:T(8,128)S(1)}, bf16[512,128]{1,0:T(8,128)(2,1)S(1)}, f32[8,128]{1,0:T(8,128)S(1)}) custom-call(bf16[512,128]{1,0:T(8,128)(2,1)S(1)} %get-tuple-element.22.refs_0_, bf16[512,128]{1,0:T(8,128)(2,1)S(1)} %get-tuple-element.23.refs_1_, ...), custom_call_target="tpu_custom_call" | custom-call | tf_op jit(solution)/shard_map/pallas_call | solution.py:543
  10.5 1.3 %collective-permute-done.1.refs_13_.refs_2_ = bf16[264,128]{1,0:T(8,128)(2,1)S(1)} collective-permute-done((bf16[264,128]{1,0:T(8,128)(2,1)S(1)}, bf16[264,128]{1,0:T(8,128)(2,1)S(1)}, u32[]{:S(2)}, u32[]{:S(2)}) %collective-permute-start.1) | collective-permute-done | bytes 67616 | tf_op jit(solution)/shard_map/ppermute | solution.py:525
  11.8 1.0 %shard_map.96 = (bf16[512,128]{1,0:T(8,128)(2,1)S(1)}, bf16[512,128]{1,0:T(8,128)(2,1)S(1)}, bf16[512,128]{1,0:T(8,128)(2,1)S(1)}, bf16[512,128]{1,0:T(8,128)(2,1)S(1)}) custom-call(bf16[512,128]{1,0:T(8,128)(2,1)S(1)} %get-tuple-element.22.refs_0_, bf16[512,128]{1,0:T(8,128)(2,1)S(1)} %get-tuple-element.23.refs_1_, f32[8,512]{1,0:T(8,128)S(1)} %get-tuple-element.26.refs_2_, ...), custom_call_target="tpu_custom_call" | custom-call | tf_op jit(solution)/shard_map/pallas_call | solution.py:555
  12.8 2.1 %collective-permute-start.2 = (bf16[512,128]{1,0:T(8,128)(2,1)S(1)}, bf16[512,128]{1,0:T(8,128)(2,1)S(1)}, u32[]{:S(2)}, u32[]{:S(2)}) collective-permute-start(bf16[512,128]{1,0:T(8,128)(2,1)S(1)} %get-tuple-element.35), channel_id=1, source_target_pairs={{0,12},{4,8},{8,4},{12,0},{1,13},{5,9},{9,5},{13,1},{2,14},{6,10},... | collective-permute-start | bytes 393224 | tf_op jit(solution)/shard_map/ppermute | solution.py:563
  14.9 0.0 collective-permute-start.3
  14.9 2.4 %collective-permute-start.4 = (bf16[512,128]{1,0:T(8,128)(2,1)S(1)}, bf16[512,128]{1,0:T(8,128)(2,1)S(1)}, u32[]{:S(2)}, u32[]{:S(2)}) collective-permute-start(bf16[512,128]{1,0:T(8,128)(2,1)S(1)} %get-tuple-element.40), channel_id=1, source_target_pairs={{0,8},{4,12},{8,0},{12,4},{1,9},{5,13},{9,1},{13,5},{2,10},{6,14},... | collective-permute-start | bytes 393224 | tf_op jit(solution)/shard_map/ppermute | solution.py:563
  17.3 3.8 %collective-permute-done.2._.refs_3_ = bf16[512,128]{1,0:T(8,128)(2,1)S(1)} collective-permute-done((bf16[512,128]{1,0:T(8,128)(2,1)S(1)}, bf16[512,128]{1,0:T(8,128)(2,1)S(1)}, u32[]{:S(2)}, u32[]{:S(2)}) %collective-permute-start.2) | collective-permute-done | bytes 131104 | tf_op jit(solution)/shard_map/ppermute | solution.py:563
  21.1 0.3 %shard_map.97 = (bf16[128,256]{1,0:T(8,128)(2,1)S(1)}, bf16[128,512]{1,0:T(8,128)(2,1)S(1)}) custom-call(bf16[512,128]{1,0:T(8,128)(2,1)S(1)} %collective-permute-done.2._.refs_3_, bf16[264,128]{1,0:T(8,128)(2,1)S(1)} %fusion.2.packet_ref.refs_11_.refs_0_, bf16[264,128]{1,0:T(8,128)(2,1)S(1)} %collective-permute-done.refs_4_.refs_12_.refs_1_, ...), custom_call_target="tpu_custom_call" | custom-call | tf_op jit(solution)/shard_map/pallas_call | solution.py:565
  21.4 2.9 %collective-permute-done.3.refs_1_ = bf16[512,128]{1,0:T(8,128)(2,1)S(1)} collective-permute-done((bf16[512,128]{1,0:T(8,128)(2,1)S(1)}, bf16[512,128]{1,0:T(8,128)(2,1)S(1)}, u32[]{:S(2)}, u32[]{:S(2)}) %collective-permute-start.3) | collective-permute-done | bytes 131104 | tf_op jit(solution)/shard_map/ppermute | solution.py:563
  24.3 0.0 collective-permute-done.4.refs_2_
  24.3 1.0 %shard_map.98 = (f32[128,512]{1,0:T(8,128)}, f32[128,128]{1,0:T(8,128)}, f32[128,128]{1,0:T(8,128)}) custom-call(bf16[128,256]{1,0:T(8,128)(2,1)S(1)} %get-tuple-element.36.query_spread, bf16[128,512]{1,0:T(8,128)(2,1)S(1)} %get-tuple-element.37.key_spread, bf16[512,128]{1,0:T(8,128)(2,1)S(1)} %get-tuple-element.38.refs_0_, ...), custom_call_target="tpu_custom_call" | custom-call | tf_op jit(solution)/shard_map/pallas_call | solution.py:575
  (2 shorter events, 0.0 us)
Async XLA Ops:
  0.6 6.7 %copy-start = (bf16[128,512]{1,0:T(8,128)(2,1)S(1)}, bf16[128,512]{1,0:T(8,128)(2,1)}, u32[]{:S(2)}) copy-start(bf16[128,512]{1,0:T(8,128)(2,1)} %query_ref.1) | copy-start | bytes 393220
  0.7 6.6 %copy-start.3 = (s32[16]{0:T(128)S(1)}, s32[16]{0:T(128)}, u32[]{:S(2)}) copy-start(s32[16]{0:T(128)} %doc_ref.1) | copy-start | bytes 196
  1.6 8.5 %collective-permute-start = (bf16[264,128]{1,0:T(8,128)(2,1)S(1)}, bf16[264,128]{1,0:T(8,128)(2,1)S(1)}, u32[]{:S(2)}, u32[]{:S(2)}) collective-permute-start(bf16[264,128]{1,0:T(8,128)(2,1)S(1)} %fusion.2.packet_ref.refs_11_.refs_0_), channel_id=1, source_target_pairs={{0,4},{4,8},{8,12},{12,0},{1,5},{5,9},{9,13},{13,1},{2,6},{6,10},{... | collective-permute-start | bytes 202760 | tf_op jit(solution)/shard_map/ppermute | solution.py:525
  4.7 7.1 %collective-permute-start.1 = (bf16[264,128]{1,0:T(8,128)(2,1)S(1)}, bf16[264,128]{1,0:T(8,128)(2,1)S(1)}, u32[]{:S(2)}, u32[]{:S(2)}) collective-permute-start(bf16[264,128]{1,0:T(8,128)(2,1)S(1)} %fusion.2.packet_ref.refs_11_.refs_0_), channel_id=1, source_target_pairs={{0,8},{4,12},{8,0},{12,4},{1,9},{5,13},{9,1},{13,5},{2,10},{6,14},... | collective-permute-start | bytes 202760 | tf_op jit(solution)/shard_map/ppermute | solution.py:525
  7.3 0.9 %copy-start.1 = (bf16[128,512]{1,0:T(8,128)(2,1)S(1)}, bf16[128,512]{1,0:T(8,128)(2,1)}, u32[]{:S(2)}) copy-start(bf16[128,512]{1,0:T(8,128)(2,1)} %grad_ref.1) | copy-start | bytes 393220
  8.2 0.9 %copy-start.2 = (bf16[128,512]{1,0:T(8,128)(2,1)S(1)}, bf16[128,512]{1,0:T(8,128)(2,1)}, u32[]{:S(2)}) copy-start(bf16[128,512]{1,0:T(8,128)(2,1)} %saved_ref.1) | copy-start | bytes 393220
  12.8 8.3 %collective-permute-start.2 = (bf16[512,128]{1,0:T(8,128)(2,1)S(1)}, bf16[512,128]{1,0:T(8,128)(2,1)S(1)}, u32[]{:S(2)}, u32[]{:S(2)}) collective-permute-start(bf16[512,128]{1,0:T(8,128)(2,1)S(1)} %get-tuple-element.35), channel_id=1, source_target_pairs={{0,12},{4,8},{8,4},{12,0},{1,13},{5,9},{9,5},{13,1},{2,14},{6,10},... | collective-permute-start | bytes 393224 | tf_op jit(solution)/shard_map/ppermute | solution.py:563
  14.9 9.4 %collective-permute-start.3 = (bf16[512,128]{1,0:T(8,128)(2,1)S(1)}, bf16[512,128]{1,0:T(8,128)(2,1)S(1)}, u32[]{:S(2)}, u32[]{:S(2)}) collective-permute-start(bf16[512,128]{1,0:T(8,128)(2,1)S(1)} %get-tuple-element.39), channel_id=1, source_target_pairs={{0,4},{4,0},{8,12},{12,8},{1,5},{5,1},{9,13},{13,9},{2,6},{6,2},{1... | collective-permute-start | bytes 393224 | tf_op jit(solution)/shard_map/ppermute | solution.py:563
  14.9 9.4 %collective-permute-start.4 = (bf16[512,128]{1,0:T(8,128)(2,1)S(1)}, bf16[512,128]{1,0:T(8,128)(2,1)S(1)}, u32[]{:S(2)}, u32[]{:S(2)}) collective-permute-start(bf16[512,128]{1,0:T(8,128)(2,1)S(1)} %get-tuple-element.40), channel_id=1, source_target_pairs={{0,8},{4,12},{8,0},{12,4},{1,9},{5,13},{9,1},{13,5},{2,10},{6,14},... | collective-permute-start | bytes 393224 | tf_op jit(solution)/shard_map/ppermute | solution.py:563

commit v10 on v9

--- a/solution.py
+++ b/solution.py
@@ -380,17 +380,18 @@
 
 
 def attend_kernel(count, halo, *refs):
-    query_ref, grad_ref, row_ref, filled_ref, spread_ref = refs[:5]
-    raised_refs = refs[5 : 5 + halo]
-    change_refs = refs[5 + halo : 5 + 2 * halo]
-    target_refs = refs[5 + 2 * halo : 5 + 3 * halo]
-    packets = refs[5 + 3 * halo : 6 + 4 * halo]
-    outs = refs[6 + 4 * halo :]
+    query_ref, grad_ref, row_ref, filled_ref, spread_ref, given_ref = refs[:6]
+    raised_refs = refs[6 : 6 + halo]
+    change_refs = refs[6 + halo : 6 + 2 * halo]
+    target_refs = refs[6 + 2 * halo : 6 + 3 * halo]
+    packets = refs[6 + 3 * halo : 7 + 4 * halo]
+    outs = refs[7 + 4 * halo :]
     rows = packets[0].shape[1]
     depth = query_ref.shape[1]
     heads = query_ref.shape[0] // rows
     slot = 2 * rows // count
     scale = 1.0 / math.sqrt(depth)
+    index = lax.axis_index("ctx")
     queries = query_ref[...]
     grads = grad_ref[...]
     raised, change, (_, total, factors), target, _ = fold(
@@ -428,24 +429,29 @@
             out[at + n * rows : at + (n + 1) * rows, :] = part_slots[
                 k * rows : (k + 1) * rows, n * depth : (n + 1) * depth
             ]
-
-
-def order_kernel(count, halo, _, *refs):
-    packets = refs[: 1 + halo]
-    query_out, key_out = refs[1 + halo :]
+        given = jnp.zeros((1, rows), jnp.float32)
+        for p in range(count):
+            given = jnp.where((index ^ k) == p, given_ref[p : p + 1, :], given)
+        out[at + 2 * rows :, :] = jnp.broadcast_to(given[:, :depth], (META, depth)).astype(
+            jnp.bfloat16
+        )
+
+
+def order_kernel(count, halo, last, packet_ref, *refs):
+    ins = refs[:-2]
+    query_out, key_out = refs[-2:]
     rows = query_out.shape[0]
     index = lax.axis_index("ctx")
-    given = []
-    for ref in packets:
-        hot = ref[2 * rows : 2 * rows + count, :].astype(jnp.float32)
-        counts = jnp.sum(hot, axis=1, keepdims=True)
-        mine = jnp.zeros((1, 1), jnp.float32)
-        for p in range(count):
-            mine = jnp.where(index == p, counts[p : p + 1, :], mine)
-        given.append(mine.astype(jnp.int32))
-    if len(given) < count:
-        given.append(rows - sum(given))
-    giver = [lax.rem(index - d + count, count) for d in range(count)]
+    hot = packet_ref[2 * rows : 2 * rows + count, :].astype(jnp.float32)
+    counts = jnp.sum(hot, axis=1, keepdims=True)
+    mine = jnp.zeros((1, 1), jnp.float32)
+    for p in range(count):
+        mine = jnp.where(index == p, counts[p : p + 1, :], mine)
+    given = [mine.astype(jnp.int32)]
+    for ref in ins[::-1]:
+        at = ref.shape[0] - META
+        given.append(ref[at : at + 1, 0:1].astype(jnp.float32).astype(jnp.int32))
+    given.insert(last, rows - sum(given))
 
     def placement(size, halo):
         lane = lax.broadcasted_iota(jnp.int32, (1, count * size), 1)
@@ -456,9 +462,9 @@
                 block = (index ^ k) - back
                 start = jnp.zeros((1, 1), jnp.int32)
                 length = jnp.zeros((1, 1), jnp.int32)
-                for d in range(count):
-                    start = start + jnp.where(giver[d] < block, given[d], 0)
-                    length = length + jnp.where(giver[d] == block, given[d], 0)
+                for n in range(count):
+                    start = start + jnp.where((index ^ n) < block, given[n], 0)
+                    length = length + jnp.where((index ^ n) == block, given[n], 0)
                 target = jnp.where((step >= 0) & (step < length), start + step, target)
                 step = step - length
         return one_hot(rows, target)
@@ -521,24 +527,40 @@
         jnp.pad(jnp.concatenate([key_head_rows, value_head_rows], axis=0), ((0, META), (0, 0))),
         (owners[None, :] == mark).astype(bf16),
     )
-    near = [
-        lax.ppermute(packet, "ctx", [(i, (i + back) % count) for i in range(count)])
-        for back in range(1, halo + 1)
-    ]
+    near = [lax.ppermute(packet, "ctx", [(i, (i + 1) % count) for i in range(count)])]
     block_shapes = [jax.ShapeDtypeStruct((rows, columns), f32)] * 2
     row_shape = jax.ShapeDtypeStruct((8, columns), f32)
     target_shape = jax.ShapeDtypeStruct((count * rows, rows), bf16)
     filled_shape = jax.ShapeDtypeStruct((8, rows), f32)
-    query_rows, grad_rows, raised, change, row, spread, target, filled = pl.pallas_call(
-        functools.partial(own_kernel, count, doc_lengths.shape[0]),
-        out_shape=[jax.ShapeDtypeStruct((columns, depth), bf16)] * 2
-        + block_shapes
-        + [row_shape, jax.ShapeDtypeStruct((count * slot, rows), bf16), target_shape, filled_shape],
-        in_specs=[pl.BlockSpec(memory_space=pltpu.SMEM)] + [whole] * 4,
-        out_specs=[whole] * 8,
-        compiler_params=params,
-    )(doc_lengths, packet, queries, grad_out, forward_out)
-    raised, change, target = [raised], [change], [target]
+
+    def own_work():
+        return pl.pallas_call(
+            functools.partial(own_kernel, count, doc_lengths.shape[0]),
+            out_shape=[jax.ShapeDtypeStruct((columns, depth), bf16)] * 2
+            + block_shapes
+            + [row_shape, jax.ShapeDtypeStruct((count * slot, rows), bf16), target_shape, filled_shape],
+            in_specs=[pl.BlockSpec(memory_space=pltpu.SMEM)] + [whole] * 4,
+            out_specs=[whole] * 8,
+            compiler_params=params,
+        )(doc_lengths, packet, queries, grad_out, forward_out)
+
+    if halo == 1:
+        own = own_work()
+    else:
+        order = jnp.arange(doc_lengths.shape[0], dtype=jnp.int32)
+        ends = jnp.sum(
+            jnp.where(order[:, None] <= order[None, :], doc_lengths[:, None], 0), axis=0
+        )
+        odd = jnp.sum(((ends >= 2 * rows) & (ends <= 3 * rows)).astype(jnp.int32)) == 0
+
+        def far_and_own(part):
+            pairs = [(i, (i + 2) % count if i % 2 == part else i) for i in range(count)]
+            return lambda: (lax.ppermute(packet, "ctx", pairs), *own_work())
+
+        far, *own = lax.cond(odd, far_and_own(1), far_and_own(0))
+        near.append(far)
+    query_rows, grad_rows, raised, change, row, spread, target, filled = own
+    raised, change, target, given = [raised], [change], [target], filled
     for back in range(1, halo):
         found = pl.pallas_call(
             functools.partial(step_kernel, count, back),
@@ -554,24 +576,26 @@
         filled = found[4]
     sent = pl.pallas_call(
         functools.partial(attend_kernel, count, halo),
-        out_shape=[jax.ShapeDtypeStruct((heads * slot + 2 * rows, depth), bf16)] * count,
-        in_specs=[whole] * (6 + 4 * halo),
+        out_shape=[jax.ShapeDtypeStruct((heads * slot + 2 * rows + META, depth), bf16)] * count,
+        in_specs=[whole] * (7 + 4 * halo),
         out_specs=[whole] * count,
         compiler_params=params,
-    )(query_rows, grad_rows, row, filled, spread, *raised, *change, *target, packet, *near)
+    )(query_rows, grad_rows, row, filled, spread, given, *raised, *change, *target, packet, *near)
     received = [sent[0]] + [
         lax.ppermute(sent[k], "ctx", [(i, i ^ k) for i in range(count)]) for k in range(1, count)
     ]
+    last = count // 2
+    early = [received[k] for k in range(count - 1, 0, -1) if k != last]
     spreads = pl.pallas_call(
-        functools.partial(order_kernel, count, halo),
+        functools.partial(order_kernel, count, halo, last),
         out_shape=[
             jax.ShapeDtypeStruct((rows, count * slot), bf16),
             jax.ShapeDtypeStruct((rows, count * rows), bf16),
         ],
-        in_specs=[pl.BlockSpec(memory_space=pl.ANY)] + [whole] * (1 + halo),
+        in_specs=[whole] * (1 + len(early)),
         out_specs=[whole] * 2,
         compiler_params=params,
-    )(received[-1], packet, *near)
+    )(packet, *early)
     return pl.pallas_call(
         functools.partial(place_kernel, count),
         out_shape=[

time: 25.5 us -> 29.9 us (1.17)
  local copies, waits for them, and re-layouts: 1.82 us -> 0.01 us
  waiting for transfers between devices: 8.01 us -> 9.81 us
  starting transfers between devices: 10.1 us -> 11.8 us
  Pallas kernels: 3.67 us -> 5 us
  other arithmetic: 0.95 us -> 1.68 us
  between operations: 0.71 us -> 1.36 us
    ppermute x3, starting transfers between devices: 4.45 us -> 7.41 us  [near_plan(): lax.ppermute(sent[k], 'ctx', [(i, i ^ k) for i in range(count)])]
    ppermute x3, waiting for transfers between devices: 6.72 us -> 9.67 us  [near_plan(): lax.ppermute(sent[k], 'ctx', [(i, i ^ k) for i in range(count)])]
    unnamed x8 -> x4, local copies, waits for them, and re-layouts: 1.82 us -> 0.01 us
    ppermute x2, starting transfers between devices: 5.67 us -> 4.36 us  [the longest x1 3.08 us: near_plan(): lax.ppermute(packet, 'ctx', [(i, (i + 1) % count) for i in range(count)])]
    ppermute x2, waiting for transfers between devices: 1.29 us -> 0.14 us  [the longest x1 0.14 us: near_plan(): lax.ppermute(packet, 'ctx', [(i, (i + 1) % count) for i in range(count)])]
    pallas_call x1, Pallas kernels: 1.04 us -> 1.93 us  [near_plan(): pl.pallas_call(functools.partial(attend_kernel, count, halo), out_shape=[...]
    reduce_sum x0 -> x2, other arithmetic: none -> 0.72 us  [the longest x1 0.63 us: near_plan(): jnp.sum(((ends >= 2 * rows) & (ends <= 3 * rows)).astype(jnp.int32)) == 0]
    pallas_call x2, Pallas kernels: 1.3 us -> 1.74 us  [the longest x1 1.45 us: own_work(): pl.pallas_call(functools.partial(own_kernel, count, doc_lengths.shape[0])...]
  transfers between devices with their start and end apart: 5 -> 5, of which waited for: 3 -> 4; matrix products, arithmetic and copies ran while one was open for 0% -> 2% of each run, Pallas kernels for 6% -> 6%
where the time goes in v10:
time: 29.9 us; the launch traced here: 29.7 us
  starting transfers between devices  11.8 us (39%)
  waiting for transfers between devices  9.81 us (33%)
  Pallas kernels  5 us (17%)
  other arithmetic  1.68 us (6%)
  between operations  1.36 us (5%)
    ppermute x3, waiting for transfers between devices, near_plan(): lax.ppermute(sent[k], 'ctx', [(i, i ^ k) for i in range(count)])  9.67 us
    ppermute x3, starting transfers between devices, near_plan(): lax.ppermute(sent[k], 'ctx', [(i, i ^ k) for i in range(count)])  7.41 us
    ppermute x1, starting transfers between devices, near_plan(): lax.ppermute(packet, 'ctx', [(i, (i + 1) % count) for i in range(count)])  3.08 us
    pallas_call x1, Pallas kernels, near_plan(): pl.pallas_call(functools.partial(attend_kernel, count, halo), out_shape=[...  1.93 us
    pallas_call x1, Pallas kernels, own_work(): pl.pallas_call(functools.partial(own_kernel, count, doc_lengths.shape[0])...  1.45 us
    ppermute x1, starting transfers between devices, far_and_own(): return lambda: (lax.ppermute(packet, 'ctx', pairs), *own_work())  1.28 us
    pallas_call x1, Pallas kernels, near_plan(): pl.pallas_call(functools.partial(place_kernel, count), out_shape=[jax.Sha...  1 us
    select_n x1, other arithmetic, near_plan(): jnp.where(mark < 0, jnp.pad(jnp.concatenate([key_head_rows, value_head_ro...  0.95 us
  transfers between devices with their start and end apart: 5, of which 4 were waited for; matrix products, arithmetic and copies ran while one was open for 2% of the time, Pallas kernels for 6%

profile of v10, /device:TPU:0, one launch (start us, length us, event | category | flops | bytes accessed | tf_op | source)
XLA Modules:
  0.0 29.7 jit_solution(3266462959063666494)
XLA Ops:
  0.6 0.0 copy-start
  0.7 0.0 copy-start.1
  0.7 0.9 %fusion.2.refs_12_.packet_ref = bf16[264,128]{1,0:T(8,128)(2,1)S(1)} fusion(bf16[128,128]{1,0:T(8,128)(2,1)} %param.13, bf16[128,128]{1,0:T(8,128)(2,1)} %param.12, s32[128]{0:T(128)} %param.10, s32[264]{0:T(512)S(1)} %iota_add_fusion, pred[264]{0:T(512)(128)(4,1)S(1)} %broadcast_compare_fusion), kind=kLoop, calls=%fused_computation.4 | loop fusion | flops 337920 | bytes 134952 | tf_op jit(solution)/shard_map/jit(_where)/select_n | solution.py:525
  1.6 3.1 %collective-permute-start.2 = (bf16[264,128]{1,0:T(8,128)(2,1)S(1)}, bf16[264,128]{1,0:T(8,128)(2,1)S(1)}, u32[]{:S(2)}, u32[]{:S(2)}) collective-permute-start(bf16[264,128]{1,0:T(8,128)(2,1)S(1)} %fusion.2.refs_12_.packet_ref), channel_id=1, source_target_pairs={{0,4},{4,8},{8,12},{12,0},{1,5},{5,9},{9,13},{13,1},{2,6},{6,10},{... | collective-permute-start | bytes 202760 | tf_op jit(solution)/shard_map/ppermute | solution.py:530
  4.7 0.0 copy-done.1
  4.7 0.1 select_reduce_fusion
  4.8 0.6 %fusion.4 = s32[]{:T(128)} fusion(s32[16]{0:T(128)S(1)} %select_reduce_fusion), kind=kLoop, calls=%fused_computation.11 | loop fusion | flops 79 | bytes 68 | tf_op jit(solution)/shard_map/reduce_sum | solution.py:554
  6.1 0.0 copy-done
  6.1 2.8 %conditional.1 = (bf16[264,128]{1,0:T(8,128)(2,1)}, bf16[512,128]{1,0:T(8,128)(2,1)S(1)}, bf16[512,128]{1,0:T(8,128)(2,1)S(1)}, f32[128,512]{1,0:T(8,128)S(1)}, ...) conditional(s32[]{:T(128)} %convert_element_type.13, ...), branch_computations={%region_2.3_spmd, %region_3.4_spmd} | conditional | bytes 270448 | solution.py:560
  6.1 1.3 %collective-permute-start.1 = (bf16[264,128]{1,0:T(8,128)(2,1)S(1)}, bf16[264,128]{1,0:T(8,128)(2,1)}, u32[]{:S(2)}, u32[]{:S(2)}) collective-permute-start(bf16[264,128]{1,0:T(8,128)(2,1)S(1)} %get-tuple-element.33.packet_ref), channel_id=1, source_target_pairs={{0,0},{4,12},{8,8},{12,4},{1,1},{5,13},{9,9},{13,5},{2,2},{6,14},{... | collective-permute-start | bytes 202760 | tf_op jit(solution)/shard_map/cond/branch_1_fun/ppermute | solution.py:558
  7.4 1.4 %branch_1_fun.1 = (bf16[512,128]{1,0:T(8,128)(2,1)S(1)}, bf16[512,128]{1,0:T(8,128)(2,1)S(1)}, f32[128,512]{1,0:T(8,128)S(1)}, f32[128,512]{1,0:T(8,128)S(1)}, f...) custom-call(s32[16]{0:T(128)S(1)} %get-tuple-element.34.doc_ref, ...), custom_call_target="tpu_custom_call" | custom-call | tf_op jit(solution)/shard_map/cond/branch_1_fun/pallas_call | solution.py:537
  8.8 0.0 collective-permute-done.1
  8.9 0.1 collective-permute-done.2.refs_4_.refs_13_
  9.0 0.3 %shard_map.94 = (f32[128,512]{1,0:T(8,128)S(1)}, f32[128,512]{1,0:T(8,128)S(1)}, f32[8,512]{1,0:T(8,128)S(1)}, bf16[512,128]{1,0:T(8,128)(2,1)S(1)}, f32[8,128]{1,0:T(8,128)S(1)}) custom-call(bf16[512,128]{1,0:T(8,128)(2,1)S(1)} %get-tuple-element.69.refs_0_, bf16[512,128]{1,0:T(8,128)(2,1)S(1)} %get-tuple-element.70.refs_1_, ...), custom_call_target="tpu_custom_call" | custom-call | tf_op jit(solution)/shard_map/pallas_call | solution.py:565
  9.3 1.9 %shard_map.95 = (bf16[520,128]{1,0:T(8,128)(2,1)S(1)}, bf16[520,128]{1,0:T(8,128)(2,1)S(1)}, bf16[520,128]{1,0:T(8,128)(2,1)S(1)}, bf16[520,128]{1,0:T(8,128)(2,1)S(1)}) custom-call(bf16[512,128]{1,0:T(8,128)(2,1)S(1)} %get-tuple-element.69.refs_0_, bf16[512,128]{1,0:T(8,128)(2,1)S(1)} %get-tuple-element.70.refs_1_, f32[8,512]{1,0:T(8,128)S(1)} %get-tuple-element.73.refs_2_, ...), custom_call_target="tpu_custom_call" | custom-call | tf_op jit(solution)/shard_map/pallas_call | solution.py:577
  11.3 6.4 %collective-permute-start.3 = (bf16[520,128]{1,0:T(8,128)(2,1)S(1)}, bf16[520,128]{1,0:T(8,128)(2,1)S(1)}, u32[]{:S(2)}, u32[]{:S(2)}) collective-permute-start(bf16[520,128]{1,0:T(8,128)(2,1)S(1)} %get-tuple-element.83), channel_id=1, source_target_pairs={{0,12},{4,8},{8,4},{12,0},{1,13},{5,9},{9,5},{13,1},{2,14},{6,10},... | collective-permute-start | bytes 399368 | tf_op jit(solution)/shard_map/ppermute | solution.py:585
  17.7 0.0 collective-permute-start.4
  17.7 1.0 %collective-permute-start.5 = (bf16[520,128]{1,0:T(8,128)(2,1)S(1)}, bf16[520,128]{1,0:T(8,128)(2,1)S(1)}, u32[]{:S(2)}, u32[]{:S(2)}) collective-permute-start(bf16[520,128]{1,0:T(8,128)(2,1)S(1)} %get-tuple-element.88), channel_id=1, source_target_pairs={{0,8},{4,12},{8,0},{12,4},{1,9},{5,13},{9,1},{13,5},{2,10},{6,14},... | collective-permute-start | bytes 399368 | tf_op jit(solution)/shard_map/ppermute | solution.py:585
  18.7 3.4 %collective-permute-done.3.refs_0_.refs_3_ = bf16[520,128]{1,0:T(8,128)(2,1)S(1)} collective-permute-done((bf16[520,128]{1,0:T(8,128)(2,1)S(1)}, bf16[520,128]{1,0:T(8,128)(2,1)S(1)}, u32[]{:S(2)}, u32[]{:S(2)}) %collective-permute-start.3) | collective-permute-done | bytes 133152 | tf_op jit(solution)/shard_map/ppermute | solution.py:585
  22.1 1.6 %collective-permute-done.4.refs_1_ = bf16[520,128]{1,0:T(8,128)(2,1)S(1)} collective-permute-done((bf16[520,128]{1,0:T(8,128)(2,1)S(1)}, bf16[520,128]{1,0:T(8,128)(2,1)S(1)}, u32[]{:S(2)}, u32[]{:S(2)}) %collective-permute-start.4) | collective-permute-done | bytes 133152 | tf_op jit(solution)/shard_map/ppermute | solution.py:585
  23.7 0.3 shard_map.96
  24.0 4.7 %collective-permute-done.5.refs_2_ = bf16[520,128]{1,0:T(8,128)(2,1)S(1)} collective-permute-done((bf16[520,128]{1,0:T(8,128)(2,1)S(1)}, bf16[520,128]{1,0:T(8,128)(2,1)S(1)}, u32[]{:S(2)}, u32[]{:S(2)}) %collective-permute-start.5) | collective-permute-done | bytes 133152 | tf_op jit(solution)/shard_map/ppermute | solution.py:585
  28.7 1.0 %shard_map.97 = (f32[128,512]{1,0:T(8,128)}, f32[128,128]{1,0:T(8,128)}, f32[128,128]{1,0:T(8,128)}) custom-call(bf16[128,256]{1,0:T(8,128)(2,1)S(1)} %get-tuple-element.85.query_spread, bf16[128,512]{1,0:T(8,128)(2,1)S(1)} %get-tuple-element.86.key_spread, bf16[520,128]{1,0:T(8,128)(2,1)S(1)} %get-tuple-element.87.refs_0_, ...), custom_call_target="tpu_custom_call" | custom-call | tf_op jit(solution)/shard_map/pallas_call | solution.py:599
  (2 shorter events, 0.0 us)
Async XLA Ops:
  0.6 5.5 %copy-start = (bf16[128,512]{1,0:T(8,128)(2,1)S(1)}, bf16[128,512]{1,0:T(8,128)(2,1)}, u32[]{:S(2)}) copy-start(bf16[128,512]{1,0:T(8,128)(2,1)} %param.11) | copy-start | bytes 393220
  0.7 4.0 %copy-start.1 = (s32[16]{0:T(128)S(1)}, s32[16]{0:T(128)}, u32[]{:S(2)}) copy-start(s32[16]{0:T(128)} %param.9) | copy-start | bytes 196
  1.6 7.4 %collective-permute-start.2 = (bf16[264,128]{1,0:T(8,128)(2,1)S(1)}, bf16[264,128]{1,0:T(8,128)(2,1)S(1)}, u32[]{:S(2)}, u32[]{:S(2)}) collective-permute-start(bf16[264,128]{1,0:T(8,128)(2,1)S(1)} %fusion.2.refs_12_.packet_ref), channel_id=1, source_target_pairs={{0,4},{4,8},{8,12},{12,0},{1,5},{5,9},{9,13},{13,1},{2,6},{6,10},{... | collective-permute-start | bytes 202760 | tf_op jit(solution)/shard_map/ppermute | solution.py:530
  6.1 2.7 %collective-permute-start.1 = (bf16[264,128]{1,0:T(8,128)(2,1)S(1)}, bf16[264,128]{1,0:T(8,128)(2,1)}, u32[]{:S(2)}, u32[]{:S(2)}) collective-permute-start(bf16[264,128]{1,0:T(8,128)(2,1)S(1)} %get-tuple-element.33.packet_ref), channel_id=1, source_target_pairs={{0,0},{4,12},{8,8},{12,4},{1,1},{5,13},{9,9},{13,5},{2,2},{6,14},{... | collective-permute-start | bytes 202760 | tf_op jit(solution)/shard_map/cond/branch_1_fun/ppermute | solution.py:558
  11.3 10.8 %collective-permute-start.3 = (bf16[520,128]{1,0:T(8,128)(2,1)S(1)}, bf16[520,128]{1,0:T(8,128)(2,1)S(1)}, u32[]{:S(2)}, u32[]{:S(2)}) collective-permute-start(bf16[520,128]{1,0:T(8,128)(2,1)S(1)} %get-tuple-element.83), channel_id=1, source_target_pairs={{0,12},{4,8},{8,4},{12,0},{1,13},{5,9},{9,5},{13,1},{2,14},{6,10},... | collective-permute-start | bytes 399368 | tf_op jit(solution)/shard_map/ppermute | solution.py:585
  17.7 6.0 %collective-permute-start.4 = (bf16[520,128]{1,0:T(8,128)(2,1)S(1)}, bf16[520,128]{1,0:T(8,128)(2,1)S(1)}, u32[]{:S(2)}, u32[]{:S(2)}) collective-permute-start(bf16[520,128]{1,0:T(8,128)(2,1)S(1)} %get-tuple-element.84), channel_id=1, source_target_pairs={{0,4},{4,0},{8,12},{12,8},{1,5},{5,1},{9,13},{13,9},{2,6},{6,2},{1... | collective-permute-start | bytes 399368 | tf_op jit(solution)/shard_map/ppermute | solution.py:585
  17.7 11.0 %collective-permute-start.5 = (bf16[520,128]{1,0:T(8,128)(2,1)S(1)}, bf16[520,128]{1,0:T(8,128)(2,1)S(1)}, u32[]{:S(2)}, u32[]{:S(2)}) collective-permute-start(bf16[520,128]{1,0:T(8,128)(2,1)S(1)} %get-tuple-element.88), channel_id=1, source_target_pairs={{0,8},{4,12},{8,0},{12,4},{1,9},{5,13},{9,1},{13,5},{2,10},{6,14},... | collective-permute-start | bytes 399368 | tf_op jit(solution)/shard_map/ppermute | solution.py:585

commit v11 on v9

--- a/solution.py
+++ b/solution.py
@@ -468,7 +468,8 @@
 
 
 def place_kernel(count, query_spread, key_spread, *refs):
-    ins = refs[:count]
+    half = (count + 1) // 2
+    ins = [refs[k // 2 + half * (k % 2)] for k in range(count)]
     query_out, key_out, value_out = refs[count : count + 3]
     query_here, key_here, value_here, sems = refs[count + 3 :]
     rows, width = query_here.shape
@@ -588,7 +589,7 @@
             pltpu.SemaphoreType.DMA((3,)),
         ],
         compiler_params=params,
-    )(*spreads, *received)
+    )(*spreads, *received[::2], *received[1::2])
 
 
 def per_device(*args):

time: 25.5 us -> 26.7 us (1.047)
  waiting for transfers between devices: 8.01 us -> 9.27 us
    ppermute x3, waiting for transfers between devices: 6.72 us -> 7.98 us  [near_plan(): lax.ppermute(sent[k], 'ctx', [(i, i ^ k) for i in range(count)])]
where the time goes in v11:
time: 26.7 us; the launch traced here: 26.5 us
  starting transfers between devices  10.1 us (38%)
  waiting for transfers between devices  9.27 us (35%)
  Pallas kernels  3.68 us (14%)
  local copies, waits for them, and re-layouts  1.82 us (7%)
  other arithmetic  0.95 us (4%)
  between operations  0.71 us (3%)
    ppermute x3, waiting for transfers between devices, near_plan(): lax.ppermute(sent[k], 'ctx', [(i, i ^ k) for i in range(count)])  7.98 us
    ppermute x2, starting transfers between devices, near_plan(): lax.ppermute(packet, 'ctx', [(i, (i + back) % count) for i in range(count)])  5.67 us
    ppermute x3, starting transfers between devices, near_plan(): lax.ppermute(sent[k], 'ctx', [(i, i ^ k) for i in range(count)])  4.45 us
    unnamed x8, local copies, waits for them, and re-layouts  1.82 us
    ppermute x2, waiting for transfers between devices, near_plan(): lax.ppermute(packet, 'ctx', [(i, (i + back) % count) for i in range(count)])  1.29 us
    pallas_call x1, Pallas kernels, near_plan(): pl.pallas_call(functools.partial(attend_kernel, count, halo), out_shape=[...  1.04 us
    pallas_call x1, Pallas kernels, near_plan(): pl.pallas_call(functools.partial(place_kernel, count), out_shape=[jax.Sha...  1.01 us
    pallas_call x1, Pallas kernels, near_plan(): pl.pallas_call(functools.partial(own_kernel, count, doc_lengths.shape[0])...  1 us
  transfers between devices with their start and end apart: 5, of which 3 were waited for; matrix products, arithmetic and copies ran while one was open for 0% of the time, Pallas kernels for 6%

profile of v11, /device:TPU:0, one launch (start us, length us, event | category | flops | bytes accessed | tf_op | source)
XLA Modules:
  0.0 26.5 jit_solution(16943854559642419370)
XLA Ops:
  0.6 0.0 copy-start
  0.7 0.0 copy-start.3
  0.7 0.9 %fusion.2.packet_ref.refs_11_.refs_0_ = bf16[264,128]{1,0:T(8,128)(2,1)S(1)} fusion(bf16[128,128]{1,0:T(8,128)(2,1)} %param.11, bf16[128,128]{1,0:T(8,128)(2,1)} %param.10, s32[128]{0:T(128)} %param.8, s32[264]{0:T(512)S(1)} %iota_add_fusion, pred[264]{0:T(512)(128)(4,1)S(1)} %broadcast_compare_fusion), kind=kLoop, calls=%fused_computation.4 | loop fusion | flops 337920 | bytes 134952 | tf_op jit(solution)/shard_map/jit(_where)/select_n | solution.py:520
  1.6 3.1 %collective-permute-start = (bf16[264,128]{1,0:T(8,128)(2,1)S(1)}, bf16[264,128]{1,0:T(8,128)(2,1)S(1)}, u32[]{:S(2)}, u32[]{:S(2)}) collective-permute-start(bf16[264,128]{1,0:T(8,128)(2,1)S(1)} %fusion.2.packet_ref.refs_11_.refs_0_), channel_id=1, source_target_pairs={{0,4},{4,8},{8,12},{12,0},{1,5},{5,9},{9,13},{13,1},{2,6},{6,10},{... | collective-permute-start | bytes 202760 | tf_op jit(solution)/shard_map/ppermute | solution.py:526
  4.7 2.6 %collective-permute-start.1 = (bf16[264,128]{1,0:T(8,128)(2,1)S(1)}, bf16[264,128]{1,0:T(8,128)(2,1)S(1)}, u32[]{:S(2)}, u32[]{:S(2)}) collective-permute-start(bf16[264,128]{1,0:T(8,128)(2,1)S(1)} %fusion.2.packet_ref.refs_11_.refs_0_), channel_id=1, source_target_pairs={{0,8},{4,12},{8,0},{12,4},{1,9},{5,13},{9,1},{13,5},{2,10},{6,14},... | collective-permute-start | bytes 202760 | tf_op jit(solution)/shard_map/ppermute | solution.py:526
  7.3 0.0 copy-done
  7.3 0.0 copy-done.3
  7.3 0.0 copy-start.1
  7.3 0.9 %copy-done.1 = bf16[128,512]{1,0:T(8,128)(2,1)S(1)} copy-done((bf16[128,512]{1,0:T(8,128)(2,1)S(1)}, bf16[128,512]{1,0:T(8,128)(2,1)}, u32[]{:S(2)}) %copy-start.1) | copy-done | bytes 131096
  8.2 0.0 copy-start.2
  8.2 0.9 %copy-done.2 = bf16[128,512]{1,0:T(8,128)(2,1)S(1)} copy-done((bf16[128,512]{1,0:T(8,128)(2,1)S(1)}, bf16[128,512]{1,0:T(8,128)(2,1)}, u32[]{:S(2)}) %copy-start.2) | copy-done | bytes 131096
  9.1 1.0 %shard_map.94 = (bf16[512,128]{1,0:T(8,128)(2,1)S(1)}, bf16[512,128]{1,0:T(8,128)(2,1)S(1)}, f32[128,512]{1,0:T(8,128)S(1)}, f32[128,512]{1,0:T(8,128)S(1)}, f32...) custom-call(s32[16]{0:T(128)S(1)} %copy-done.3, ...), custom_call_target="tpu_custom_call" | custom-call | tf_op jit(solution)/shard_map/pallas_call | solution.py:533
  10.1 0.0 collective-permute-done.refs_4_.refs_12_.refs_1_
  10.1 0.3 %shard_map.95 = (f32[128,512]{1,0:T(8,128)S(1)}, f32[128,512]{1,0:T(8,128)S(1)}, f32[8,512]{1,0:T(8,128)S(1)}, bf16[512,128]{1,0:T(8,128)(2,1)S(1)}, f32[8,128]{1,0:T(8,128)S(1)}) custom-call(bf16[512,128]{1,0:T(8,128)(2,1)S(1)} %get-tuple-element.22.refs_0_, bf16[512,128]{1,0:T(8,128)(2,1)S(1)} %get-tuple-element.23.refs_1_, ...), custom_call_target="tpu_custom_call" | custom-call | tf_op jit(solution)/shard_map/pallas_call | solution.py:544
  10.5 1.3 %collective-permute-done.1.refs_13_.refs_2_ = bf16[264,128]{1,0:T(8,128)(2,1)S(1)} collective-permute-done((bf16[264,128]{1,0:T(8,128)(2,1)S(1)}, bf16[264,128]{1,0:T(8,128)(2,1)S(1)}, u32[]{:S(2)}, u32[]{:S(2)}) %collective-permute-start.1) | collective-permute-done | bytes 67616 | tf_op jit(solution)/shard_map/ppermute | solution.py:526
  11.8 1.0 %shard_map.96 = (bf16[512,128]{1,0:T(8,128)(2,1)S(1)}, bf16[512,128]{1,0:T(8,128)(2,1)S(1)}, bf16[512,128]{1,0:T(8,128)(2,1)S(1)}, bf16[512,128]{1,0:T(8,128)(2,1)S(1)}) custom-call(bf16[512,128]{1,0:T(8,128)(2,1)S(1)} %get-tuple-element.22.refs_0_, bf16[512,128]{1,0:T(8,128)(2,1)S(1)} %get-tuple-element.23.refs_1_, f32[8,512]{1,0:T(8,128)S(1)} %get-tuple-element.26.refs_2_, ...), custom_call_target="tpu_custom_call" | custom-call | tf_op jit(solution)/shard_map/pallas_call | solution.py:556
  12.8 2.1 %collective-permute-start.2 = (bf16[512,128]{1,0:T(8,128)(2,1)S(1)}, bf16[512,128]{1,0:T(8,128)(2,1)S(1)}, u32[]{:S(2)}, u32[]{:S(2)}) collective-permute-start(bf16[512,128]{1,0:T(8,128)(2,1)S(1)} %get-tuple-element.35), channel_id=1, source_target_pairs={{0,12},{4,8},{8,4},{12,0},{1,13},{5,9},{9,5},{13,1},{2,14},{6,10},... | collective-permute-start | bytes 393224 | tf_op jit(solution)/shard_map/ppermute | solution.py:564
  14.9 0.0 collective-permute-start.3
  14.9 2.4 %collective-permute-start.4 = (bf16[512,128]{1,0:T(8,128)(2,1)S(1)}, bf16[512,128]{1,0:T(8,128)(2,1)S(1)}, u32[]{:S(2)}, u32[]{:S(2)}) collective-permute-start(bf16[512,128]{1,0:T(8,128)(2,1)S(1)} %get-tuple-element.40), channel_id=1, source_target_pairs={{0,4},{4,0},{8,12},{12,8},{1,5},{5,1},{9,13},{13,9},{2,6},{6,2},{1... | collective-permute-start | bytes 393224 | tf_op jit(solution)/shard_map/ppermute | solution.py:564
  17.3 3.9 %collective-permute-done.2._.refs_3_ = bf16[512,128]{1,0:T(8,128)(2,1)S(1)} collective-permute-done((bf16[512,128]{1,0:T(8,128)(2,1)S(1)}, bf16[512,128]{1,0:T(8,128)(2,1)S(1)}, u32[]{:S(2)}, u32[]{:S(2)}) %collective-permute-start.2) | collective-permute-done | bytes 131104 | tf_op jit(solution)/shard_map/ppermute | solution.py:564
  21.1 0.3 %shard_map.97 = (bf16[128,256]{1,0:T(8,128)(2,1)S(1)}, bf16[128,512]{1,0:T(8,128)(2,1)S(1)}) custom-call(bf16[512,128]{1,0:T(8,128)(2,1)S(1)} %collective-permute-done.2._.refs_3_, bf16[264,128]{1,0:T(8,128)(2,1)S(1)} %fusion.2.packet_ref.refs_11_.refs_0_, bf16[264,128]{1,0:T(8,128)(2,1)S(1)} %collective-permute-done.refs_4_.refs_12_.refs_1_, ...), custom_call_target="tpu_custom_call" | custom-call | tf_op jit(solution)/shard_map/pallas_call | solution.py:566
  21.4 4.1 %collective-permute-done.3.refs_1_ = bf16[512,128]{1,0:T(8,128)(2,1)S(1)} collective-permute-done((bf16[512,128]{1,0:T(8,128)(2,1)S(1)}, bf16[512,128]{1,0:T(8,128)(2,1)S(1)}, u32[]{:S(2)}, u32[]{:S(2)}) %collective-permute-start.3) | collective-permute-done | bytes 131104 | tf_op jit(solution)/shard_map/ppermute | solution.py:564
  25.5 0.0 collective-permute-done.4.refs_2_
  25.5 1.0 %shard_map.98 = (f32[128,512]{1,0:T(8,128)}, f32[128,128]{1,0:T(8,128)}, f32[128,128]{1,0:T(8,128)}) custom-call(bf16[128,256]{1,0:T(8,128)(2,1)S(1)} %get-tuple-element.36.query_spread, bf16[128,512]{1,0:T(8,128)(2,1)S(1)} %get-tuple-element.37.key_spread, bf16[512,128]{1,0:T(8,128)(2,1)S(1)} %get-tuple-element.38.refs_0_, ...), custom_call_target="tpu_custom_call" | custom-call | tf_op jit(solution)/shard_map/pallas_call | solution.py:576
  (2 shorter events, 0.0 us)
Async XLA Ops:
  0.6 6.7 %copy-start = (bf16[128,512]{1,0:T(8,128)(2,1)S(1)}, bf16[128,512]{1,0:T(8,128)(2,1)}, u32[]{:S(2)}) copy-start(bf16[128,512]{1,0:T(8,128)(2,1)} %query_ref.1) | copy-start | bytes 393220
  0.7 6.6 %copy-start.3 = (s32[16]{0:T(128)S(1)}, s32[16]{0:T(128)}, u32[]{:S(2)}) copy-start(s32[16]{0:T(128)} %doc_ref.1) | copy-start | bytes 196
  1.6 8.5 %collective-permute-start = (bf16[264,128]{1,0:T(8,128)(2,1)S(1)}, bf16[264,128]{1,0:T(8,128)(2,1)S(1)}, u32[]{:S(2)}, u32[]{:S(2)}) collective-permute-start(bf16[264,128]{1,0:T(8,128)(2,1)S(1)} %fusion.2.packet_ref.refs_11_.refs_0_), channel_id=1, source_target_pairs={{0,4},{4,8},{8,12},{12,0},{1,5},{5,9},{9,13},{13,1},{2,6},{6,10},{... | collective-permute-start | bytes 202760 | tf_op jit(solution)/shard_map/ppermute | solution.py:526
  4.7 7.1 %collective-permute-start.1 = (bf16[264,128]{1,0:T(8,128)(2,1)S(1)}, bf16[264,128]{1,0:T(8,128)(2,1)S(1)}, u32[]{:S(2)}, u32[]{:S(2)}) collective-permute-start(bf16[264,128]{1,0:T(8,128)(2,1)S(1)} %fusion.2.packet_ref.refs_11_.refs_0_), channel_id=1, source_target_pairs={{0,8},{4,12},{8,0},{12,4},{1,9},{5,13},{9,1},{13,5},{2,10},{6,14},... | collective-permute-start | bytes 202760 | tf_op jit(solution)/shard_map/ppermute | solution.py:526
  7.3 0.9 %copy-start.1 = (bf16[128,512]{1,0:T(8,128)(2,1)S(1)}, bf16[128,512]{1,0:T(8,128)(2,1)}, u32[]{:S(2)}) copy-start(bf16[128,512]{1,0:T(8,128)(2,1)} %grad_ref.1) | copy-start | bytes 393220
  8.2 0.9 %copy-start.2 = (bf16[128,512]{1,0:T(8,128)(2,1)S(1)}, bf16[128,512]{1,0:T(8,128)(2,1)}, u32[]{:S(2)}) copy-start(bf16[128,512]{1,0:T(8,128)(2,1)} %saved_ref.1) | copy-start | bytes 393220
  12.8 8.3 %collective-permute-start.2 = (bf16[512,128]{1,0:T(8,128)(2,1)S(1)}, bf16[512,128]{1,0:T(8,128)(2,1)S(1)}, u32[]{:S(2)}, u32[]{:S(2)}) collective-permute-start(bf16[512,128]{1,0:T(8,128)(2,1)S(1)} %get-tuple-element.35), channel_id=1, source_target_pairs={{0,12},{4,8},{8,4},{12,0},{1,13},{5,9},{9,5},{13,1},{2,14},{6,10},... | collective-permute-start | bytes 393224 | tf_op jit(solution)/shard_map/ppermute | solution.py:564
  14.9 10.7 %collective-permute-start.3 = (bf16[512,128]{1,0:T(8,128)(2,1)S(1)}, bf16[512,128]{1,0:T(8,128)(2,1)S(1)}, u32[]{:S(2)}, u32[]{:S(2)}) collective-permute-start(bf16[512,128]{1,0:T(8,128)(2,1)S(1)} %get-tuple-element.39), channel_id=1, source_target_pairs={{0,8},{4,12},{8,0},{12,4},{1,9},{5,13},{9,1},{13,5},{2,10},{6,14},... | collective-permute-start | bytes 393224 | tf_op jit(solution)/shard_map/ppermute | solution.py:564
  14.9 10.7 %collective-permute-start.4 = (bf16[512,128]{1,0:T(8,128)(2,1)S(1)}, bf16[512,128]{1,0:T(8,128)(2,1)S(1)}, u32[]{:S(2)}, u32[]{:S(2)}) collective-permute-start(bf16[512,128]{1,0:T(8,128)(2,1)S(1)} %get-tuple-element.40), channel_id=1, source_target_pairs={{0,4},{4,0},{8,12},{12,8},{1,5},{5,1},{9,13},{13,9},{2,6},{6,2},{1... | collective-permute-start | bytes 393224 | tf_op jit(solution)/shard_map/ppermute | solution.py:564

commit v12 on v9

--- a/solution.py
+++ b/solution.py
@@ -380,12 +380,12 @@
 
 
 def attend_kernel(count, halo, *refs):
-    query_ref, grad_ref, row_ref, filled_ref, spread_ref = refs[:5]
-    raised_refs = refs[5 : 5 + halo]
-    change_refs = refs[5 + halo : 5 + 2 * halo]
-    target_refs = refs[5 + 2 * halo : 5 + 3 * halo]
-    packets = refs[5 + 3 * halo : 6 + 4 * halo]
-    outs = refs[6 + 4 * halo :]
+    query_ref, grad_ref, row_ref, filled_ref, spread_ref, given_ref = refs[:6]
+    raised_refs = refs[6 : 6 + halo]
+    change_refs = refs[6 + halo : 6 + 2 * halo]
+    target_refs = refs[6 + 2 * halo : 6 + 3 * halo]
+    packets = refs[6 + 3 * halo : 7 + 4 * halo]
+    outs = refs[7 + 4 * halo :]
     rows = packets[0].shape[1]
     depth = query_ref.shape[1]
     heads = query_ref.shape[0] // rows
@@ -428,24 +428,31 @@
             out[at + n * rows : at + (n + 1) * rows, :] = part_slots[
                 k * rows : (k + 1) * rows, n * depth : (n + 1) * depth
             ]
-
-
-def order_kernel(count, halo, _, *refs):
-    packets = refs[: 1 + halo]
-    query_out, key_out = refs[1 + halo :]
+    half = count // 2
+    given = jnp.zeros((1, depth), jnp.float32)
+    for p in range(count):
+        given = jnp.where((lax.axis_index("ctx") ^ half) == p, given_ref[p : p + 1, 0:depth], given)
+    outs[half][at + 2 * rows :, :] = jnp.broadcast_to(given, (META, depth)).astype(jnp.bfloat16)
+
+
+def order_kernel(count, halo, half_ref, packet_ref, near_ref, query_out, key_out):
     rows = query_out.shape[0]
     index = lax.axis_index("ctx")
+    giver = [index, lax.rem(index + count - 1, count)]
     given = []
-    for ref in packets:
+    for ref in (packet_ref, near_ref):
         hot = ref[2 * rows : 2 * rows + count, :].astype(jnp.float32)
         counts = jnp.sum(hot, axis=1, keepdims=True)
         mine = jnp.zeros((1, 1), jnp.float32)
         for p in range(count):
             mine = jnp.where(index == p, counts[p : p + 1, :], mine)
         given.append(mine.astype(jnp.int32))
-    if len(given) < count:
+    if count == 4:
+        at = half_ref.shape[0] - META
+        given.append(half_ref[at : at + 1, 0:1].astype(jnp.float32).astype(jnp.int32))
+        giver.append(index ^ 2)
         given.append(rows - sum(given))
-    giver = [lax.rem(index - d + count, count) for d in range(count)]
+        giver.append(6 - sum(giver))
 
     def placement(size, halo):
         lane = lax.broadcasted_iota(jnp.int32, (1, count * size), 1)
@@ -456,9 +463,9 @@
                 block = (index ^ k) - back
                 start = jnp.zeros((1, 1), jnp.int32)
                 length = jnp.zeros((1, 1), jnp.int32)
-                for d in range(count):
-                    start = start + jnp.where(giver[d] < block, given[d], 0)
-                    length = length + jnp.where(giver[d] == block, given[d], 0)
+                for n in range(count):
+                    start = start + jnp.where(giver[n] < block, given[n], 0)
+                    length = length + jnp.where(giver[n] == block, given[n], 0)
                 target = jnp.where((step >= 0) & (step < length), start + step, target)
                 step = step - length
         return one_hot(rows, target)
@@ -522,8 +529,14 @@
         (owners[None, :] == mark).astype(bf16),
     )
     near = [
-        lax.ppermute(packet, "ctx", [(i, (i + back) % count) for i in range(count)])
-        for back in range(1, halo + 1)
+        lax.ppermute(packet, "ctx", [(i, (i + 1) % count) for i in range(count)])
+    ] + [
+        lax.ppermute(
+            packet,
+            "ctx",
+            [(i, i + back if i + back < count else count - 1 - i) for i in range(count)],
+        )
+        for back in range(2, halo + 1)
     ]
     block_shapes = [jax.ShapeDtypeStruct((rows, columns), f32)] * 2
     row_shape = jax.ShapeDtypeStruct((8, columns), f32)
@@ -538,7 +551,7 @@
         out_specs=[whole] * 8,
         compiler_params=params,
     )(doc_lengths, packet, queries, grad_out, forward_out)
-    raised, change, target = [raised], [change], [target]
+    raised, change, target, given = [raised], [change], [target], filled
     for back in range(1, halo):
         found = pl.pallas_call(
             functools.partial(step_kernel, count, back),
@@ -554,11 +567,16 @@
         filled = found[4]
     sent = pl.pallas_call(
         functools.partial(attend_kernel, count, halo),
-        out_shape=[jax.ShapeDtypeStruct((heads * slot + 2 * rows, depth), bf16)] * count,
-        in_specs=[whole] * (6 + 4 * halo),
+        out_shape=[
+            jax.ShapeDtypeStruct(
+                (heads * slot + 2 * rows + (META if k == count // 2 else 0), depth), bf16
+            )
+            for k in range(count)
+        ],
+        in_specs=[whole] * (7 + 4 * halo),
         out_specs=[whole] * count,
         compiler_params=params,
-    )(query_rows, grad_rows, row, filled, spread, *raised, *change, *target, packet, *near)
+    )(query_rows, grad_rows, row, filled, spread, given, *raised, *change, *target, packet, *near)
     received = [sent[0]] + [
         lax.ppermute(sent[k], "ctx", [(i, i ^ k) for i in range(count)]) for k in range(1, count)
     ]
@@ -568,10 +586,10 @@
             jax.ShapeDtypeStruct((rows, count * slot), bf16),
             jax.ShapeDtypeStruct((rows, count * rows), bf16),
         ],
-        in_specs=[pl.BlockSpec(memory_space=pl.ANY)] + [whole] * (1 + halo),
+        in_specs=[whole] * 3,
         out_specs=[whole] * 2,
         compiler_params=params,
-    )(received[-1], packet, *near)
+    )(received[count // 2], packet, near[0])
     return pl.pallas_call(
         functools.partial(place_kernel, count),
         out_shape=[

time: 25.5 us -> 26.1 us (1.024)
  waiting for transfers between devices: 8.01 us -> 8.64 us
    ppermute x3, waiting for transfers between devices: 6.72 us -> 8.26 us  [near_plan(): lax.ppermute(sent[k], 'ctx', [(i, i ^ k) for i in range(count)])]
    ppermute x2, waiting for transfers between devices: 1.29 us -> 0.38 us  [the longest x1 0.37 us: near_plan(): lax.ppermute(packet, 'ctx', [(i, i + back if i + back < count else count...]
where the time goes in v12:
time: 26.1 us; the launch traced here: 25.9 us
  starting transfers between devices  10.1 us (39%)
  waiting for transfers between devices  8.64 us (33%)
  Pallas kernels  3.66 us (14%)
  local copies, waits for them, and re-layouts  1.82 us (7%)
  other arithmetic  0.95 us (4%)
  between operations  0.72 us (3%)
    ppermute x3, waiting for transfers between devices, near_plan(): lax.ppermute(sent[k], 'ctx', [(i, i ^ k) for i in range(count)])  8.26 us
    ppermute x3, starting transfers between devices, near_plan(): lax.ppermute(sent[k], 'ctx', [(i, i ^ k) for i in range(count)])  4.45 us
    ppermute x1, starting transfers between devices, near_plan(): lax.ppermute(packet, 'ctx', [(i, (i + 1) % count) for i in range(count)])  3.08 us
    ppermute x1, starting transfers between devices, near_plan(): lax.ppermute(packet, 'ctx', [(i, i + back if i + back < count else count...  2.59 us
    unnamed x8, local copies, waits for them, and re-layouts  1.82 us
    pallas_call x1, Pallas kernels, near_plan(): pl.pallas_call(functools.partial(attend_kernel, count, halo), out_shape=[...  1.05 us
    pallas_call x1, Pallas kernels, near_plan(): pl.pallas_call(functools.partial(own_kernel, count, doc_lengths.shape[0])...  1.01 us
    pallas_call x1, Pallas kernels, near_plan(): pl.pallas_call(functools.partial(place_kernel, count), out_shape=[jax.Sha...  1 us
  transfers between devices with their start and end apart: 5, of which 3 were waited for; matrix products, arithmetic and copies ran while one was open for 0% of the time, Pallas kernels for 6%

profile of v12, /device:TPU:0, one launch (start us, length us, event | category | flops | bytes accessed | tf_op | source)
XLA Modules:
  0.0 25.9 jit_solution(16161566281730370296)
XLA Ops:
  0.6 0.0 copy-start
  0.7 0.0 copy-start.3
  0.7 0.9 %fusion.2.packet_ref.refs_12_ = bf16[264,128]{1,0:T(8,128)(2,1)S(1)} fusion(bf16[128,128]{1,0:T(8,128)(2,1)} %param.11, bf16[128,128]{1,0:T(8,128)(2,1)} %param.10, s32[128]{0:T(128)} %param.8, s32[264]{0:T(512)S(1)} %iota_add_fusion, pred[264]{0:T(512)(128)(4,1)S(1)} %broadcast_compare_fusion), kind=kLoop, calls=%fused_computation.4 | loop fusion | flops 337920 | bytes 134952 | tf_op jit(solution)/shard_map/jit(_where)/select_n | solution.py:526
  1.6 3.1 %collective-permute-start = (bf16[264,128]{1,0:T(8,128)(2,1)S(1)}, bf16[264,128]{1,0:T(8,128)(2,1)S(1)}, u32[]{:S(2)}, u32[]{:S(2)}) collective-permute-start(bf16[264,128]{1,0:T(8,128)(2,1)S(1)} %fusion.2.packet_ref.refs_12_), channel_id=1, source_target_pairs={{0,4},{4,8},{8,12},{12,0},{1,5},{5,9},{9,13},{13,1},{2,6},{6,10},{... | collective-permute-start | bytes 202760 | tf_op jit(solution)/shard_map/ppermute | solution.py:532
  4.7 2.6 %collective-permute-start.1 = (bf16[264,128]{1,0:T(8,128)(2,1)S(1)}, bf16[264,128]{1,0:T(8,128)(2,1)S(1)}, u32[]{:S(2)}, u32[]{:S(2)}) collective-permute-start(bf16[264,128]{1,0:T(8,128)(2,1)S(1)} %fusion.2.packet_ref.refs_12_), channel_id=1, source_target_pairs={{0,8},{4,12},{8,4},{12,0},{1,9},{5,13},{9,5},{13,1},{2,10},{6,14},... | collective-permute-start | bytes 202760 | tf_op jit(solution)/shard_map/ppermute | solution.py:534
  7.3 0.0 copy-done
  7.3 0.0 copy-done.3
  7.3 0.0 copy-start.1
  7.3 0.9 %copy-done.1 = bf16[128,512]{1,0:T(8,128)(2,1)S(1)} copy-done((bf16[128,512]{1,0:T(8,128)(2,1)S(1)}, bf16[128,512]{1,0:T(8,128)(2,1)}, u32[]{:S(2)}) %copy-start.1) | copy-done | bytes 131096
  8.2 0.0 copy-start.2
  8.2 0.9 %copy-done.2 = bf16[128,512]{1,0:T(8,128)(2,1)S(1)} copy-done((bf16[128,512]{1,0:T(8,128)(2,1)S(1)}, bf16[128,512]{1,0:T(8,128)(2,1)}, u32[]{:S(2)}) %copy-start.2) | copy-done | bytes 131096
  9.1 1.0 %shard_map.94 = (bf16[512,128]{1,0:T(8,128)(2,1)S(1)}, bf16[512,128]{1,0:T(8,128)(2,1)S(1)}, f32[128,512]{1,0:T(8,128)S(1)}, f32[128,512]{1,0:T(8,128)S(1)}, f32...) custom-call(s32[16]{0:T(128)S(1)} %copy-done.3, ...), custom_call_target="tpu_custom_call" | custom-call | tf_op jit(solution)/shard_map/pallas_call | solution.py:545
  10.1 0.0 collective-permute-done.refs_4_.refs_13_.near_ref
  10.1 0.3 %shard_map.95 = (f32[128,512]{1,0:T(8,128)S(1)}, f32[128,512]{1,0:T(8,128)S(1)}, f32[8,512]{1,0:T(8,128)S(1)}, bf16[512,128]{1,0:T(8,128)(2,1)S(1)}, f32[8,128]{1,0:T(8,128)S(1)}) custom-call(bf16[512,128]{1,0:T(8,128)(2,1)S(1)} %get-tuple-element.22.refs_0_, bf16[512,128]{1,0:T(8,128)(2,1)S(1)} %get-tuple-element.23.refs_1_, ...), custom_call_target="tpu_custom_call" | custom-call | tf_op jit(solution)/shard_map/pallas_call | solution.py:556
  10.5 0.4 %collective-permute-done.1.refs_14_ = bf16[264,128]{1,0:T(8,128)(2,1)S(1)} collective-permute-done((bf16[264,128]{1,0:T(8,128)(2,1)S(1)}, bf16[264,128]{1,0:T(8,128)(2,1)S(1)}, u32[]{:S(2)}, u32[]{:S(2)}) %collective-permute-start.1) | collective-permute-done | bytes 67616 | tf_op jit(solution)/shard_map/ppermute | solution.py:534
  10.8 1.0 %shard_map.96 = (bf16[512,128]{1,0:T(8,128)(2,1)S(1)}, bf16[512,128]{1,0:T(8,128)(2,1)S(1)}, bf16[520,128]{1,0:T(8,128)(2,1)S(1)}, bf16[512,128]{1,0:T(8,128)(2,1)S(1)}) custom-call(bf16[512,128]{1,0:T(8,128)(2,1)S(1)} %get-tuple-element.22.refs_0_, bf16[512,128]{1,0:T(8,128)(2,1)S(1)} %get-tuple-element.23.refs_1_, f32[8,512]{1,0:T(8,128)S(1)} %get-tuple-element.26.refs_2_, ...), custom_call_target="tpu_custom_call" | custom-call | tf_op jit(solution)/shard_map/pallas_call | solution.py:568
  11.9 1.8 %collective-permute-start.2 = (bf16[520,128]{1,0:T(8,128)(2,1)S(1)}, bf16[520,128]{1,0:T(8,128)(2,1)S(1)}, u32[]{:S(2)}, u32[]{:S(2)}) collective-permute-start(bf16[520,128]{1,0:T(8,128)(2,1)S(1)} %get-tuple-element.35), channel_id=1, source_target_pairs={{0,8},{4,12},{8,0},{12,4},{1,9},{5,13},{9,1},{13,5},{2,10},{6,14},... | collective-permute-start | bytes 399368 | tf_op jit(solution)/shard_map/ppermute | solution.py:581
  13.7 1.7 %collective-permute-start.3 = (bf16[512,128]{1,0:T(8,128)(2,1)S(1)}, bf16[512,128]{1,0:T(8,128)(2,1)S(1)}, u32[]{:S(2)}, u32[]{:S(2)}) collective-permute-start(bf16[512,128]{1,0:T(8,128)(2,1)S(1)} %get-tuple-element.39), channel_id=1, source_target_pairs={{0,4},{4,0},{8,12},{12,8},{1,5},{5,1},{9,13},{13,9},{2,6},{6,2},{1... | collective-permute-start | bytes 393224 | tf_op jit(solution)/shard_map/ppermute | solution.py:581
  15.4 0.9 %collective-permute-start.4 = (bf16[512,128]{1,0:T(8,128)(2,1)S(1)}, bf16[512,128]{1,0:T(8,128)(2,1)S(1)}, u32[]{:S(2)}, u32[]{:S(2)}) collective-permute-start(bf16[512,128]{1,0:T(8,128)(2,1)S(1)} %get-tuple-element.40), channel_id=1, source_target_pairs={{0,12},{4,8},{8,4},{12,0},{1,13},{5,9},{9,5},{13,1},{2,14},{6,10},... | collective-permute-start | bytes 393224 | tf_op jit(solution)/shard_map/ppermute | solution.py:581
  16.4 6.7 %collective-permute-done.2.half_ref.refs_2_ = bf16[520,128]{1,0:T(8,128)(2,1)S(1)} collective-permute-done((bf16[520,128]{1,0:T(8,128)(2,1)S(1)}, bf16[520,128]{1,0:T(8,128)(2,1)S(1)}, u32[]{:S(2)}, u32[]{:S(2)}) %collective-permute-start.2) | collective-permute-done | bytes 133152 | tf_op jit(solution)/shard_map/ppermute | solution.py:581
  23.0 0.3 %shard_map.97 = (bf16[128,256]{1,0:T(8,128)(2,1)S(1)}, bf16[128,512]{1,0:T(8,128)(2,1)S(1)}) custom-call(bf16[520,128]{1,0:T(8,128)(2,1)S(1)} %collective-permute-done.2.half_ref.refs_2_, bf16[264,128]{1,0:T(8,128)(2,1)S(1)} %fusion.2.packet_ref.refs_12_, bf16[264,128]{1,0:T(8,128)(2,1)S(1)} %collective-permute-done.refs_4_.refs_13_.near_ref), custom_call_target="tpu_custom_call" | custom-call | tf_op jit(solution)/shard_map/pallas_call | solution.py:583
  23.3 0.0 collective-permute-done.3.refs_1_
  23.3 1.6 %collective-permute-done.4.refs_3_ = bf16[512,128]{1,0:T(8,128)(2,1)S(1)} collective-permute-done((bf16[512,128]{1,0:T(8,128)(2,1)S(1)}, bf16[512,128]{1,0:T(8,128)(2,1)S(1)}, u32[]{:S(2)}, u32[]{:S(2)}) %collective-permute-start.4) | collective-permute-done | bytes 131104 | tf_op jit(solution)/shard_map/ppermute | solution.py:581
  24.9 1.0 %shard_map.98 = (f32[128,512]{1,0:T(8,128)}, f32[128,128]{1,0:T(8,128)}, f32[128,128]{1,0:T(8,128)}) custom-call(bf16[128,256]{1,0:T(8,128)(2,1)S(1)} %get-tuple-element.36.query_spread, bf16[128,512]{1,0:T(8,128)(2,1)S(1)} %get-tuple-element.37.key_spread, bf16[512,128]{1,0:T(8,128)(2,1)S(1)} %get-tuple-element.38.refs_0_, ...), custom_call_target="tpu_custom_call" | custom-call | tf_op jit(solution)/shard_map/pallas_call | solution.py:593
  (2 shorter events, 0.0 us)
Async XLA Ops:
  0.6 6.7 %copy-start = (bf16[128,512]{1,0:T(8,128)(2,1)S(1)}, bf16[128,512]{1,0:T(8,128)(2,1)}, u32[]{:S(2)}) copy-start(bf16[128,512]{1,0:T(8,128)(2,1)} %query_ref.1) | copy-start | bytes 393220
  0.7 6.6 %copy-start.3 = (s32[16]{0:T(128)S(1)}, s32[16]{0:T(128)}, u32[]{:S(2)}) copy-start(s32[16]{0:T(128)} %doc_ref.1) | copy-start | bytes 196
  1.6 8.5 %collective-permute-start = (bf16[264,128]{1,0:T(8,128)(2,1)S(1)}, bf16[264,128]{1,0:T(8,128)(2,1)S(1)}, u32[]{:S(2)}, u32[]{:S(2)}) collective-permute-start(bf16[264,128]{1,0:T(8,128)(2,1)S(1)} %fusion.2.packet_ref.refs_12_), channel_id=1, source_target_pairs={{0,4},{4,8},{8,12},{12,0},{1,5},{5,9},{9,13},{13,1},{2,6},{6,10},{... | collective-permute-start | bytes 202760 | tf_op jit(solution)/shard_map/ppermute | solution.py:532
  4.7 6.1 %collective-permute-start.1 = (bf16[264,128]{1,0:T(8,128)(2,1)S(1)}, bf16[264,128]{1,0:T(8,128)(2,1)S(1)}, u32[]{:S(2)}, u32[]{:S(2)}) collective-permute-start(bf16[264,128]{1,0:T(8,128)(2,1)S(1)} %fusion.2.packet_ref.refs_12_), channel_id=1, source_target_pairs={{0,8},{4,12},{8,4},{12,0},{1,9},{5,13},{9,5},{13,1},{2,10},{6,14},... | collective-permute-start | bytes 202760 | tf_op jit(solution)/shard_map/ppermute | solution.py:534
  7.3 0.9 %copy-start.1 = (bf16[128,512]{1,0:T(8,128)(2,1)S(1)}, bf16[128,512]{1,0:T(8,128)(2,1)}, u32[]{:S(2)}) copy-start(bf16[128,512]{1,0:T(8,128)(2,1)} %grad_ref.1) | copy-start | bytes 393220
  8.2 0.9 %copy-start.2 = (bf16[128,512]{1,0:T(8,128)(2,1)S(1)}, bf16[128,512]{1,0:T(8,128)(2,1)}, u32[]{:S(2)}) copy-start(bf16[128,512]{1,0:T(8,128)(2,1)} %saved_ref.1) | copy-start | bytes 393220
  11.9 11.1 %collective-permute-start.2 = (bf16[520,128]{1,0:T(8,128)(2,1)S(1)}, bf16[520,128]{1,0:T(8,128)(2,1)S(1)}, u32[]{:S(2)}, u32[]{:S(2)}) collective-permute-start(bf16[520,128]{1,0:T(8,128)(2,1)S(1)} %get-tuple-element.35), channel_id=1, source_target_pairs={{0,8},{4,12},{8,0},{12,4},{1,9},{5,13},{9,1},{13,5},{2,10},{6,14},... | collective-permute-start | bytes 399368 | tf_op jit(solution)/shard_map/ppermute | solution.py:581
  13.7 9.6 %collective-permute-start.3 = (bf16[512,128]{1,0:T(8,128)(2,1)S(1)}, bf16[512,128]{1,0:T(8,128)(2,1)S(1)}, u32[]{:S(2)}, u32[]{:S(2)}) collective-permute-start(bf16[512,128]{1,0:T(8,128)(2,1)S(1)} %get-tuple-element.39), channel_id=1, source_target_pairs={{0,4},{4,0},{8,12},{12,8},{1,5},{5,1},{9,13},{13,9},{2,6},{6,2},{1... | collective-permute-start | bytes 393224 | tf_op jit(solution)/shard_map/ppermute | solution.py:581
  15.4 9.5 %collective-permute-start.4 = (bf16[512,128]{1,0:T(8,128)(2,1)S(1)}, bf16[512,128]{1,0:T(8,128)(2,1)S(1)}, u32[]{:S(2)}, u32[]{:S(2)}) collective-permute-start(bf16[512,128]{1,0:T(8,128)(2,1)S(1)} %get-tuple-element.40), channel_id=1, source_target_pairs={{0,12},{4,8},{8,4},{12,0},{1,13},{5,9},{9,5},{13,1},{2,14},{6,10},... | collective-permute-start | bytes 393224 | tf_op jit(solution)/shard_map/ppermute | solution.py:581

commit v13 on v9

--- a/solution.py
+++ b/solution.py
@@ -276,23 +276,8 @@
     return owner, counts, lane - earlier.astype(jnp.int32)
 
 
-def own_kernel(
-    count,
-    docs,
-    doc_ref,
-    packet_ref,
-    query_ref,
-    grad_ref,
-    saved_ref,
-    query_out,
-    grad_out,
-    raised_out,
-    change_out,
-    row_out,
-    spread_out,
-    target_out,
-    filled_out,
-):
+def own_scores(count, docs, doc_ref, packet_ref, query_ref, outs):
+    query_out, raised_out, row_out, spread_out, target_out, filled_out = outs
     rows, width = query_ref.shape
     depth = packet_ref.shape[1]
     heads = width // depth
@@ -316,14 +301,7 @@
     top = jnp.max(scores, axis=0, keepdims=True)
     raised = jnp.exp(scores - top)
     raised_out[...] = raised
-    grads = end_to_end(grad_ref[...], heads)
-    grad_out[...] = grads
-    product = grads.astype(jnp.float32) * end_to_end(saved_ref[...], heads).astype(jnp.float32)
-    delta = contract(
-        jnp.ones((8, depth), jnp.float32), product, 1, 1, precision=lax.Precision.HIGHEST
-    )[0:1, :]
-    change_out[...] = contract(packet_ref[rows : 2 * rows, :], grads, 1, 1) - delta
-    row_out[0:1, :] = delta
+    row_out[0:1, :] = jnp.zeros((1, width), jnp.float32)
     row_out[1:2, :] = top
     row_out[2:3, :] = jnp.sum(raised, axis=0, keepdims=True)
     row_out[3:4, :] = jnp.concatenate([first.astype(jnp.float32)] * heads, axis=1)
@@ -333,6 +311,41 @@
     target_out[...] = one_hot(count * rows, (owner ^ index) * rows + rank)
     filled_out[0:count, :] = jnp.broadcast_to(counts, (count, rows))
     filled_out[count:, :] = jnp.zeros((8 - count, rows), jnp.float32)
+
+
+def odd_kernel(count, docs, doc_ref, packet_ref, query_ref, packet_out, *outs):
+    packet_out[...] = packet_ref[...]
+
+    @pl.when(lax.rem(lax.axis_index("ctx"), 2) == 1)
+    def _():
+        own_scores(count, docs, doc_ref, packet_ref, query_ref, outs)
+
+
+def own_kernel(count, docs, doc_ref, packet_ref, query_ref, grad_ref, saved_ref, *refs):
+    done, outs = refs[:6], refs[6:12]
+    grad_out, change_out = refs[12:]
+    rows, width = query_ref.shape
+    depth = packet_ref.shape[1]
+    heads = width // depth
+    odd = lax.rem(lax.axis_index("ctx"), 2) == 1
+
+    @pl.when(odd)
+    def _():
+        for here, out in zip(done, outs, strict=True):
+            out[...] = here[...]
+
+    @pl.when(jnp.logical_not(odd))
+    def _():
+        own_scores(count, docs, doc_ref, packet_ref, query_ref, outs)
+
+    grads = end_to_end(grad_ref[...], heads)
+    grad_out[...] = grads
+    product = grads.astype(jnp.float32) * end_to_end(saved_ref[...], heads).astype(jnp.float32)
+    delta = contract(
+        jnp.ones((8, depth), jnp.float32), product, 1, 1, precision=lax.Precision.HIGHEST
+    )[0:1, :]
+    change_out[...] = contract(packet_ref[rows : 2 * rows, :], grads, 1, 1) - delta
+    outs[2][0:1, :] = delta
 
 
 def fold(count, back, packet, queries, grads, row, filled):
@@ -521,23 +534,37 @@
         jnp.pad(jnp.concatenate([key_head_rows, value_head_rows], axis=0), ((0, META), (0, 0))),
         (owners[None, :] == mark).astype(bf16),
     )
-    near = [
-        lax.ppermute(packet, "ctx", [(i, (i + back) % count) for i in range(count)])
-        for back in range(1, halo + 1)
-    ]
     block_shapes = [jax.ShapeDtypeStruct((rows, columns), f32)] * 2
     row_shape = jax.ShapeDtypeStruct((8, columns), f32)
     target_shape = jax.ShapeDtypeStruct((count * rows, rows), bf16)
     filled_shape = jax.ShapeDtypeStruct((8, rows), f32)
-    query_rows, grad_rows, raised, change, row, spread, target, filled = pl.pallas_call(
+    score_shapes = [
+        jax.ShapeDtypeStruct((columns, depth), bf16),
+        block_shapes[0],
+        row_shape,
+        jax.ShapeDtypeStruct((count * slot, rows), bf16),
+        target_shape,
+        filled_shape,
+    ]
+    near = [lax.ppermute(packet, "ctx", [(i, (i + 1) % count) for i in range(count)])]
+    far, *scored = pl.pallas_call(
+        functools.partial(odd_kernel, count, doc_lengths.shape[0]),
+        out_shape=[jax.ShapeDtypeStruct(packet.shape, bf16)] + score_shapes,
+        in_specs=[pl.BlockSpec(memory_space=pltpu.SMEM)] + [whole] * 2,
+        out_specs=[whole] * 7,
+        compiler_params=params,
+    )(doc_lengths, packet, queries)
+    near += [
+        lax.ppermute(far, "ctx", [(i, (i + back) % count) for i in range(count)])
+        for back in range(2, halo + 1)
+    ]
+    query_rows, raised, row, spread, target, filled, grad_rows, change = pl.pallas_call(
         functools.partial(own_kernel, count, doc_lengths.shape[0]),
-        out_shape=[jax.ShapeDtypeStruct((columns, depth), bf16)] * 2
-        + block_shapes
-        + [row_shape, jax.ShapeDtypeStruct((count * slot, rows), bf16), target_shape, filled_shape],
-        in_specs=[pl.BlockSpec(memory_space=pltpu.SMEM)] + [whole] * 4,
+        out_shape=score_shapes + [jax.ShapeDtypeStruct((columns, depth), bf16), block_shapes[1]],
+        in_specs=[pl.BlockSpec(memory_space=pltpu.SMEM)] + [whole] * 10,
         out_specs=[whole] * 8,
         compiler_params=params,
-    )(doc_lengths, packet, queries, grad_out, forward_out)
+    )(doc_lengths, packet, queries, grad_out, forward_out, *scored)
     raised, change, target = [raised], [change], [target]
     for back in range(1, halo):
         found = pl.pallas_call(

time: 25.5 us -> 26.5 us (1.039)
  waiting for transfers between devices: 8.01 us -> 8.99 us
  local copies, waits for them, and re-layouts: 1.82 us -> 0.92 us
  Pallas kernels: 3.67 us -> 4.53 us
    ppermute x3, waiting for transfers between devices: 6.72 us -> 8.3 us  [near_plan(): lax.ppermute(sent[k], 'ctx', [(i, i ^ k) for i in range(count)])]
    unnamed x8, local copies, waits for them, and re-layouts: 1.82 us -> 0.92 us
    ppermute x2, waiting for transfers between devices: 1.29 us -> 0.69 us  [the longest x1 0.69 us: near_plan(): lax.ppermute(far, 'ctx', [(i, (i + back) % count) for i in range(count)])]
    pallas_call x0 -> x1, Pallas kernels: none -> 0.56 us  [near_plan(): pl.pallas_call(functools.partial(odd_kernel, count, doc_lengths.shape[0])...]
    pallas_call x1, Pallas kernels: 1 us -> 1.3 us  [near_plan(): pl.pallas_call(functools.partial(own_kernel, count, doc_lengths.shape[0])...]
  transfers between devices with their start and end apart: 5 -> 5, of which waited for: 3 -> 4; matrix products, arithmetic and copies ran while one was open for 0% -> 0% of each run, Pallas kernels for 6% -> 9%
where the time goes in v13:
time: 26.5 us; the launch traced here: 26.3 us
  starting transfers between devices  10.2 us (38%)
  waiting for transfers between devices  8.99 us (34%)
  Pallas kernels  4.53 us (17%)
  other arithmetic  0.95 us (4%)
  local copies, waits for them, and re-layouts  0.92 us (3%)
  between operations  0.72 us (3%)
    ppermute x3, waiting for transfers between devices, near_plan(): lax.ppermute(sent[k], 'ctx', [(i, i ^ k) for i in range(count)])  8.3 us
    ppermute x3, starting transfers between devices, near_plan(): lax.ppermute(sent[k], 'ctx', [(i, i ^ k) for i in range(count)])  4.45 us
    ppermute x1, starting transfers between devices, near_plan(): lax.ppermute(packet, 'ctx', [(i, (i + 1) % count) for i in range(count)])  3.08 us
    ppermute x1, starting transfers between devices, near_plan(): lax.ppermute(far, 'ctx', [(i, (i + back) % count) for i in range(count)])  2.65 us
    pallas_call x1, Pallas kernels, near_plan(): pl.pallas_call(functools.partial(own_kernel, count, doc_lengths.shape[0])...  1.3 us
    pallas_call x1, Pallas kernels, near_plan(): pl.pallas_call(functools.partial(attend_kernel, count, halo), out_shape=[...  1.05 us
    pallas_call x1, Pallas kernels, near_plan(): pl.pallas_call(functools.partial(place_kernel, count), out_shape=[jax.Sha...  1 us
    select_n x1, other arithmetic, near_plan(): jnp.where(mark < 0, jnp.pad(jnp.concatenate([key_head_rows, value_head_ro...  0.94 us
  transfers between devices with their start and end apart: 5, of which 4 were waited for; matrix products, arithmetic and copies ran while one was open for 0% of the time, Pallas kernels for 9%

profile of v13, /device:TPU:0, one launch (start us, length us, event | category | flops | bytes accessed | tf_op | source)
XLA Modules:
  0.0 26.3 jit_solution(15858591120028930895)
XLA Ops:
  0.6 0.0 copy-start
  0.7 0.0 copy-start.3
  0.7 0.9 %fusion.2.packet_ref.refs_11_.refs_0_ = bf16[264,128]{1,0:T(8,128)(2,1)S(1)} fusion(bf16[128,128]{1,0:T(8,128)(2,1)} %param.11, bf16[128,128]{1,0:T(8,128)(2,1)} %param.10, s32[128]{0:T(128)} %param.8, s32[264]{0:T(512)S(1)} %iota_add_fusion, pred[264]{0:T(512)(128)(4,1)S(1)} %broadcast_compare_fusion), kind=kLoop, calls=%fused_computation.4 | loop fusion | flops 337920 | bytes 134952 | tf_op jit(solution)/shard_map/jit(_where)/select_n | solution.py:532
  1.6 0.0 copy-start.1
  1.6 3.1 %collective-permute-start = (bf16[264,128]{1,0:T(8,128)(2,1)S(1)}, bf16[264,128]{1,0:T(8,128)(2,1)S(1)}, u32[]{:S(2)}, u32[]{:S(2)}) collective-permute-start(bf16[264,128]{1,0:T(8,128)(2,1)S(1)} %fusion.2.packet_ref.refs_11_.refs_0_), channel_id=1, source_target_pairs={{0,4},{4,8},{8,12},{12,0},{1,5},{5,9},{9,13},{13,1},{2,6},{6,10},{... | collective-permute-start | bytes 202760 | tf_op jit(solution)/shard_map/ppermute | solution.py:549
  4.7 0.0 copy-done
  4.7 0.0 copy-done.3
  4.7 0.6 %shard_map.94 = (bf16[264,128]{1,0:T(8,128)(2,1)S(1)}, bf16[512,128]{1,0:T(8,128)(2,1)S(1)}, f32[128,512]{1,0:T(8,128)S(1)}, f32[8,512]{1,0:T(8,128)S(1)}, bf16[...) custom-call(s32[16]{0:T(128)S(1)} %copy-done.3, ...), custom_call_target="tpu_custom_call" | custom-call | tf_op jit(solution)/shard_map/pallas_call | solution.py:550
  5.3 2.7 %collective-permute-start.1 = (bf16[264,128]{1,0:T(8,128)(2,1)S(1)}, bf16[264,128]{1,0:T(8,128)(2,1)S(1)}, u32[]{:S(2)}, u32[]{:S(2)}) collective-permute-start(bf16[264,128]{1,0:T(8,128)(2,1)S(1)} %get-tuple-element.48), channel_id=1, source_target_pairs={{0,8},{4,12},{8,0},{12,4},{1,9},{5,13},{9,1},{13,5},{2,10},{6,14},... | collective-permute-start | bytes 202760 | tf_op jit(solution)/shard_map/ppermute | solution.py:558
  7.9 0.0 copy-done.1
  7.9 0.9 %copy-done.2 = bf16[128,512]{1,0:T(8,128)(2,1)S(1)} copy-done((bf16[128,512]{1,0:T(8,128)(2,1)S(1)}, bf16[128,512]{1,0:T(8,128)(2,1)}, u32[]{:S(2)}) %copy-start.2) | copy-done | bytes 131096
  8.8 1.3 %shard_map.95 = (bf16[512,128]{1,0:T(8,128)(2,1)S(1)}, f32[128,512]{1,0:T(8,128)S(1)}, f32[8,512]{1,0:T(8,128)S(1)}, bf16[256,128]{1,0:T(8,128)(2,1)S(1)}, bf16[...) custom-call(s32[16]{0:T(128)S(1)} %copy-done.3, ...), custom_call_target="tpu_custom_call" | custom-call | tf_op jit(solution)/shard_map/pallas_call | solution.py:561
  10.2 0.0 collective-permute-done.refs_4_.refs_12_.refs_1_
  10.2 0.3 %shard_map.96 = (f32[128,512]{1,0:T(8,128)S(1)}, f32[128,512]{1,0:T(8,128)S(1)}, f32[8,512]{1,0:T(8,128)S(1)}, bf16[512,128]{1,0:T(8,128)(2,1)S(1)}, f32[8,128]{1,0:T(8,128)S(1)}) custom-call(bf16[512,128]{1,0:T(8,128)(2,1)S(1)} %get-tuple-element.35.refs_0_, bf16[512,128]{1,0:T(8,128)(2,1)S(1)} %get-tuple-element.36.refs_1_, ...), custom_call_target="tpu_custom_call" | custom-call | tf_op jit(solution)/shard_map/pallas_call | solution.py:570
  10.5 0.7 %collective-permute-done.1.refs_13_.refs_2_ = bf16[264,128]{1,0:T(8,128)(2,1)S(1)} collective-permute-done((bf16[264,128]{1,0:T(8,128)(2,1)S(1)}, bf16[264,128]{1,0:T(8,128)(2,1)S(1)}, u32[]{:S(2)}, u32[]{:S(2)}) %collective-permute-start.1) | collective-permute-done | bytes 67616 | tf_op jit(solution)/shard_map/ppermute | solution.py:558
  11.2 1.1 %shard_map.97 = (bf16[512,128]{1,0:T(8,128)(2,1)S(1)}, bf16[512,128]{1,0:T(8,128)(2,1)S(1)}, bf16[512,128]{1,0:T(8,128)(2,1)S(1)}, bf16[512,128]{1,0:T(8,128)(2,1)S(1)}) custom-call(bf16[512,128]{1,0:T(8,128)(2,1)S(1)} %get-tuple-element.35.refs_0_, bf16[512,128]{1,0:T(8,128)(2,1)S(1)} %get-tuple-element.36.refs_1_, f32[8,512]{1,0:T(8,128)S(1)} %get-tuple-element.39.refs_2_, ...), custom_call_target="tpu_custom_call" | custom-call | tf_op jit(solution)/shard_map/pallas_call | solution.py:582
  12.3 2.2 %collective-permute-start.2 = (bf16[512,128]{1,0:T(8,128)(2,1)S(1)}, bf16[512,128]{1,0:T(8,128)(2,1)S(1)}, u32[]{:S(2)}, u32[]{:S(2)}) collective-permute-start(bf16[512,128]{1,0:T(8,128)(2,1)S(1)} %get-tuple-element.49), channel_id=1, source_target_pairs={{0,12},{4,8},{8,4},{12,0},{1,13},{5,9},{9,5},{13,1},{2,14},{6,10},... | collective-permute-start | bytes 393224 | tf_op jit(solution)/shard_map/ppermute | solution.py:590
  14.5 0.4 %collective-permute-start.3 = (bf16[512,128]{1,0:T(8,128)(2,1)S(1)}, bf16[512,128]{1,0:T(8,128)(2,1)S(1)}, u32[]{:S(2)}, u32[]{:S(2)}) collective-permute-start(bf16[512,128]{1,0:T(8,128)(2,1)S(1)} %get-tuple-element.53), channel_id=1, source_target_pairs={{0,4},{4,0},{8,12},{12,8},{1,5},{5,1},{9,13},{13,9},{2,6},{6,2},{1... | collective-permute-start | bytes 393224 | tf_op jit(solution)/shard_map/ppermute | solution.py:590
  14.8 1.9 %collective-permute-start.4 = (bf16[512,128]{1,0:T(8,128)(2,1)S(1)}, bf16[512,128]{1,0:T(8,128)(2,1)S(1)}, u32[]{:S(2)}, u32[]{:S(2)}) collective-permute-start(bf16[512,128]{1,0:T(8,128)(2,1)S(1)} %get-tuple-element.54), channel_id=1, source_target_pairs={{0,8},{4,12},{8,0},{12,4},{1,9},{5,13},{9,1},{13,5},{2,10},{6,14},... | collective-permute-start | bytes 393224 | tf_op jit(solution)/shard_map/ppermute | solution.py:590
  16.7 3.9 %collective-permute-done.2._.refs_3_ = bf16[512,128]{1,0:T(8,128)(2,1)S(1)} collective-permute-done((bf16[512,128]{1,0:T(8,128)(2,1)S(1)}, bf16[512,128]{1,0:T(8,128)(2,1)S(1)}, u32[]{:S(2)}, u32[]{:S(2)}) %collective-permute-start.2) | collective-permute-done | bytes 131104 | tf_op jit(solution)/shard_map/ppermute | solution.py:590
  20.7 0.3 %shard_map.98 = (bf16[128,256]{1,0:T(8,128)(2,1)S(1)}, bf16[128,512]{1,0:T(8,128)(2,1)S(1)}) custom-call(bf16[512,128]{1,0:T(8,128)(2,1)S(1)} %collective-permute-done.2._.refs_3_, bf16[264,128]{1,0:T(8,128)(2,1)S(1)} %fusion.2.packet_ref.refs_11_.refs_0_, bf16[264,128]{1,0:T(8,128)(2,1)S(1)} %collective-permute-done.refs_4_.refs_12_.refs_1_, ...), custom_call_target="tpu_custom_call" | custom-call | tf_op jit(solution)/shard_map/pallas_call | solution.py:592
  20.9 0.6 %collective-permute-done.3.refs_1_ = bf16[512,128]{1,0:T(8,128)(2,1)S(1)} collective-permute-done((bf16[512,128]{1,0:T(8,128)(2,1)S(1)}, bf16[512,128]{1,0:T(8,128)(2,1)S(1)}, u32[]{:S(2)}, u32[]{:S(2)}) %collective-permute-start.3) | collective-permute-done | bytes 131104 | tf_op jit(solution)/shard_map/ppermute | solution.py:590
  21.6 3.7 %collective-permute-done.4.refs_2_ = bf16[512,128]{1,0:T(8,128)(2,1)S(1)} collective-permute-done((bf16[512,128]{1,0:T(8,128)(2,1)S(1)}, bf16[512,128]{1,0:T(8,128)(2,1)S(1)}, u32[]{:S(2)}, u32[]{:S(2)}) %collective-permute-start.4) | collective-permute-done | bytes 131104 | tf_op jit(solution)/shard_map/ppermute | solution.py:590
  25.3 1.0 %shard_map.99 = (f32[128,512]{1,0:T(8,128)}, f32[128,128]{1,0:T(8,128)}, f32[128,128]{1,0:T(8,128)}) custom-call(bf16[128,256]{1,0:T(8,128)(2,1)S(1)} %get-tuple-element.50.query_spread, bf16[128,512]{1,0:T(8,128)(2,1)S(1)} %get-tuple-element.51.key_spread, bf16[512,128]{1,0:T(8,128)(2,1)S(1)} %get-tuple-element.52.refs_0_, ...), custom_call_target="tpu_custom_call" | custom-call | tf_op jit(solution)/shard_map/pallas_call | solution.py:602
  (3 shorter events, 0.0 us)
Async XLA Ops:
  0.6 4.1 %copy-start = (bf16[128,512]{1,0:T(8,128)(2,1)S(1)}, bf16[128,512]{1,0:T(8,128)(2,1)}, u32[]{:S(2)}) copy-start(bf16[128,512]{1,0:T(8,128)(2,1)} %query_ref.3) | copy-start | bytes 393220
  0.7 4.1 %copy-start.3 = (s32[16]{0:T(128)S(1)}, s32[16]{0:T(128)}, u32[]{:S(2)}) copy-start(s32[16]{0:T(128)} %doc_ref.3) | copy-start | bytes 196
  1.6 6.3 %copy-start.1 = (bf16[128,512]{1,0:T(8,128)(2,1)S(1)}, bf16[128,512]{1,0:T(8,128)(2,1)}, u32[]{:S(2)}) copy-start(bf16[128,512]{1,0:T(8,128)(2,1)} %grad_ref.1) | copy-start | bytes 393220
  1.6 8.5 %collective-permute-start = (bf16[264,128]{1,0:T(8,128)(2,1)S(1)}, bf16[264,128]{1,0:T(8,128)(2,1)S(1)}, u32[]{:S(2)}, u32[]{:S(2)}) collective-permute-start(bf16[264,128]{1,0:T(8,128)(2,1)S(1)} %fusion.2.packet_ref.refs_11_.refs_0_), channel_id=1, source_target_pairs={{0,4},{4,8},{8,12},{12,0},{1,5},{5,9},{9,13},{13,1},{2,6},{6,10},{... | collective-permute-start | bytes 202760 | tf_op jit(solution)/shard_map/ppermute | solution.py:549
  5.3 5.9 %collective-permute-start.1 = (bf16[264,128]{1,0:T(8,128)(2,1)S(1)}, bf16[264,128]{1,0:T(8,128)(2,1)S(1)}, u32[]{:S(2)}, u32[]{:S(2)}) collective-permute-start(bf16[264,128]{1,0:T(8,128)(2,1)S(1)} %get-tuple-element.48), channel_id=1, source_target_pairs={{0,8},{4,12},{8,0},{12,4},{1,9},{5,13},{9,1},{13,5},{2,10},{6,14},... | collective-permute-start | bytes 202760 | tf_op jit(solution)/shard_map/ppermute | solution.py:558
  7.9 0.9 %copy-start.2 = (bf16[128,512]{1,0:T(8,128)(2,1)S(1)}, bf16[128,512]{1,0:T(8,128)(2,1)}, u32[]{:S(2)}) copy-start(bf16[128,512]{1,0:T(8,128)(2,1)} %saved_ref.1) | copy-start | bytes 393220
  12.3 8.4 %collective-permute-start.2 = (bf16[512,128]{1,0:T(8,128)(2,1)S(1)}, bf16[512,128]{1,0:T(8,128)(2,1)S(1)}, u32[]{:S(2)}, u32[]{:S(2)}) collective-permute-start(bf16[512,128]{1,0:T(8,128)(2,1)S(1)} %get-tuple-element.49), channel_id=1, source_target_pairs={{0,12},{4,8},{8,4},{12,0},{1,13},{5,9},{9,5},{13,1},{2,14},{6,10},... | collective-permute-start | bytes 393224 | tf_op jit(solution)/shard_map/ppermute | solution.py:590
  14.5 7.1 %collective-permute-start.3 = (bf16[512,128]{1,0:T(8,128)(2,1)S(1)}, bf16[512,128]{1,0:T(8,128)(2,1)S(1)}, u32[]{:S(2)}, u32[]{:S(2)}) collective-permute-start(bf16[512,128]{1,0:T(8,128)(2,1)S(1)} %get-tuple-element.53), channel_id=1, source_target_pairs={{0,4},{4,0},{8,12},{12,8},{1,5},{5,1},{9,13},{13,9},{2,6},{6,2},{1... | collective-permute-start | bytes 393224 | tf_op jit(solution)/shard_map/ppermute | solution.py:590
  14.8 10.5 %collective-permute-start.4 = (bf16[512,128]{1,0:T(8,128)(2,1)S(1)}, bf16[512,128]{1,0:T(8,128)(2,1)S(1)}, u32[]{:S(2)}, u32[]{:S(2)}) collective-permute-start(bf16[512,128]{1,0:T(8,128)(2,1)S(1)} %get-tuple-element.54), channel_id=1, source_target_pairs={{0,8},{4,12},{8,0},{12,4},{1,9},{5,13},{9,1},{13,5},{2,10},{6,14},... | collective-permute-start | bytes 393224 | tf_op jit(solution)/shard_map/ppermute | solution.py:590

commit v14 on v13

--- a/solution.py
+++ b/solution.py
@@ -285,11 +285,12 @@
     index = lax.axis_index("ctx")
     lane = lax.broadcasted_iota(jnp.int32, (1, rows), 1)
     position = index * rows + lane
-    first = jnp.zeros((1, rows), jnp.int32)
-    end = jnp.int32(0)
-    for d in range(docs):
-        end = end + doc_ref[d]
-        first = jnp.where(end <= position, end, first)
+    earlier = lax.broadcasted_iota(jnp.int32, (docs, docs), 1) <= lax.broadcasted_iota(
+        jnp.int32, (docs, docs), 0
+    )
+    lengths = doc_ref[...].astype(jnp.float32)
+    ends = jnp.sum(jnp.where(earlier, lengths, 0.0), axis=1, keepdims=True).astype(jnp.int32)
+    first = jnp.max(jnp.where(ends <= position, ends, 0), axis=0, keepdims=True)
     key_position = index * rows + lax.broadcasted_iota(jnp.int32, (rows, rows), 0)
     allowed = (key_position >= first) & (key_position <= position)
     allowed = jnp.concatenate([allowed] * heads, axis=1)
@@ -481,9 +482,12 @@
 
 
 def place_kernel(count, query_spread, key_spread, *refs):
-    ins = refs[:count]
-    query_out, key_out, value_out = refs[count : count + 3]
-    query_here, key_here, value_here, sems = refs[count + 3 :]
+    query_out, key_out, value_out, query_here, key_here, value_here, sems = refs[-7:]
+    even = lax.rem(lax.axis_index("ctx"), 2) == 0
+    ins = []
+    for k in range(count):
+        here = refs[len(ins) + sum(n % 2 == 0 for n in range(1, k)) :]
+        ins.append(jnp.where(even, here[1][...], here[0][...]) if k and k % 2 == 0 else here[0])
     rows, width = query_here.shape
     depth = key_here.shape[1]
     heads = width // depth
@@ -550,10 +554,10 @@
     far, *scored = pl.pallas_call(
         functools.partial(odd_kernel, count, doc_lengths.shape[0]),
         out_shape=[jax.ShapeDtypeStruct(packet.shape, bf16)] + score_shapes,
-        in_specs=[pl.BlockSpec(memory_space=pltpu.SMEM)] + [whole] * 2,
+        in_specs=[whole] * 3,
         out_specs=[whole] * 7,
         compiler_params=params,
-    )(doc_lengths, packet, queries)
+    )(doc_lengths.reshape(1, -1), packet, queries)
     near += [
         lax.ppermute(far, "ctx", [(i, (i + back) % count) for i in range(count)])
         for back in range(2, halo + 1)
@@ -561,10 +565,10 @@
     query_rows, raised, row, spread, target, filled, grad_rows, change = pl.pallas_call(
         functools.partial(own_kernel, count, doc_lengths.shape[0]),
         out_shape=score_shapes + [jax.ShapeDtypeStruct((columns, depth), bf16), block_shapes[1]],
-        in_specs=[pl.BlockSpec(memory_space=pltpu.SMEM)] + [whole] * 10,
+        in_specs=[whole] * 11,
         out_specs=[whole] * 8,
         compiler_params=params,
-    )(doc_lengths, packet, queries, grad_out, forward_out, *scored)
+    )(doc_lengths.reshape(1, -1), packet, queries, grad_out, forward_out, *scored)
     raised, change, target = [raised], [change], [target]
     for back in range(1, halo):
         found = pl.pallas_call(
@@ -586,9 +590,17 @@
         out_specs=[whole] * count,
         compiler_params=params,
     )(query_rows, grad_rows, row, filled, spread, *raised, *change, *target, packet, *near)
-    received = [sent[0]] + [
-        lax.ppermute(sent[k], "ctx", [(i, i ^ k) for i in range(count)]) for k in range(1, count)
-    ]
+    received = [[sent[0]]]
+    for k in range(1, count):
+        parts = (1, 0) if k % 2 == 0 else (None,)
+        received.append(
+            [
+                lax.ppermute(
+                    sent[k], "ctx", [(i, i ^ k if part in (None, i % 2) else i) for i in range(count)]
+                )
+                for part in parts
+            ]
+        )
     spreads = pl.pallas_call(
         functools.partial(order_kernel, count, halo),
         out_shape=[
@@ -598,7 +610,7 @@
         in_specs=[pl.BlockSpec(memory_space=pl.ANY)] + [whole] * (1 + halo),
         out_specs=[whole] * 2,
         compiler_params=params,
-    )(received[-1], packet, *near)
+    )(received[-1][0], packet, *near)
     return pl.pallas_call(
         functools.partial(place_kernel, count),
         out_shape=[
@@ -606,7 +618,7 @@
             jax.ShapeDtypeStruct((rows, depth), f32),
             jax.ShapeDtypeStruct((rows, depth), f32),
         ],
-        in_specs=[whole] * (2 + count),
+        in_specs=[whole] * (2 + sum(map(len, received))),
         out_specs=[pl.BlockSpec(memory_space=pl.ANY)] * 3,
         scratch_shapes=[
             pltpu.VMEM((rows, width), f32),
@@ -615,7 +627,7 @@
             pltpu.SemaphoreType.DMA((3,)),
         ],
         compiler_params=params,
-    )(*spreads, *received)
+    )(*spreads, *sum(received, []))
 
 
 def per_device(*args):

time: 26.5 us -> 27.1 us (1.023)
  starting transfers between devices: 10.2 us -> 12.7 us
  Pallas kernels: 4.53 us -> 3.43 us
  waiting for transfers between devices: 8.99 us -> 8.15 us
    ppermute x3 -> x4, starting transfers between devices: 4.45 us -> 7.02 us  [near_plan(): lax.ppermute(sent[k], 'ctx', [(i, i ^ k if part in (None, i % 2) else i)...]
    ppermute x3 -> x4, waiting for transfers between devices: 8.3 us -> 5.77 us  [near_plan(): lax.ppermute(sent[k], 'ctx', [(i, i ^ k if part in (None, i % 2) else i)...]
    ppermute x1, waiting for transfers between devices: 0.69 us -> 2.38 us  [near_plan(): lax.ppermute(far, 'ctx', [(i, (i + back) % count) for i in range(count)])]
    pallas_call x1, Pallas kernels: 1.3 us -> 0.74 us  [near_plan(): pl.pallas_call(functools.partial(own_kernel, count, doc_lengths.shape[0])...]
    pallas_call x1, Pallas kernels: 0.56 us -> 0.01 us  [near_plan(): pl.pallas_call(functools.partial(odd_kernel, count, doc_lengths.shape[0])...]
  transfers between devices with their start and end apart: 5 -> 6, of which waited for: 4 -> 4; matrix products, arithmetic and copies ran while one was open for 0% -> 0% of each run, Pallas kernels for 9% -> 5%
where the time goes in v14:
time: 27.1 us; the launch traced here: 27 us
  starting transfers between devices  12.7 us (47%)
  waiting for transfers between devices  8.15 us (30%)
  Pallas kernels  3.43 us (13%)
  other arithmetic  0.95 us (4%)
  local copies, waits for them, and re-layouts  0.92 us (3%)
  between operations  0.74 us (3%)
    ppermute x4, starting transfers between devices, near_plan(): lax.ppermute(sent[k], 'ctx', [(i, i ^ k if part in (None, i % 2) else i)...  7.02 us
    ppermute x4, waiting for transfers between devices, near_plan(): lax.ppermute(sent[k], 'ctx', [(i, i ^ k if part in (None, i % 2) else i)...  5.77 us
    ppermute x1, starting transfers between devices, near_plan(): lax.ppermute(packet, 'ctx', [(i, (i + 1) % count) for i in range(count)])  3.08 us
    ppermute x1, starting transfers between devices, near_plan(): lax.ppermute(far, 'ctx', [(i, (i + back) % count) for i in range(count)])  2.65 us
    ppermute x1, waiting for transfers between devices, near_plan(): lax.ppermute(far, 'ctx', [(i, (i + back) % count) for i in range(count)])  2.38 us
    pallas_call x1, Pallas kernels, near_plan(): pl.pallas_call(functools.partial(attend_kernel, count, halo), out_shape=[...  1.05 us
    pallas_call x1, Pallas kernels, near_plan(): pl.pallas_call(functools.partial(place_kernel, count), out_shape=[jax.Sha...  1.01 us
    select_n x1, other arithmetic, near_plan(): jnp.where(mark < 0, jnp.pad(jnp.concatenate([key_head_rows, value_head_ro...  0.94 us
  transfers between devices with their start and end apart: 6, of which 4 were waited for; matrix products, arithmetic and copies ran while one was open for 0% of the time, Pallas kernels for 5%

profile of v14, /device:TPU:0, one launch (start us, length us, event | category | flops | bytes accessed | tf_op | source)
XLA Modules:
  0.0 27.0 jit_solution(12642875127719536746)
XLA Ops:
  0.6 0.0 copy-start
  0.7 0.0 copy-start.3
  0.7 0.9 %fusion.2.packet_ref.refs_11_.refs_0_ = bf16[264,128]{1,0:T(8,128)(2,1)S(1)} fusion(bf16[128,128]{1,0:T(8,128)(2,1)} %param.11, bf16[128,128]{1,0:T(8,128)(2,1)} %param.10, s32[128]{0:T(128)} %param.8, s32[264]{0:T(512)S(1)} %iota_add_fusion, pred[264]{0:T(512)(128)(4,1)S(1)} %broadcast_compare_fusion), kind=kLoop, calls=%fused_computation.4 | loop fusion | flops 337920 | bytes 134952 | tf_op jit(solution)/shard_map/jit(_where)/select_n | solution.py:536
  1.6 0.0 copy-start.1
  1.6 3.1 %collective-permute-start = (bf16[264,128]{1,0:T(8,128)(2,1)S(1)}, bf16[264,128]{1,0:T(8,128)(2,1)S(1)}, u32[]{:S(2)}, u32[]{:S(2)}) collective-permute-start(bf16[264,128]{1,0:T(8,128)(2,1)S(1)} %fusion.2.packet_ref.refs_11_.refs_0_), channel_id=1, source_target_pairs={{0,4},{4,8},{8,12},{12,0},{1,5},{5,9},{9,13},{13,1},{2,6},{6,10},{... | collective-permute-start | bytes 202760 | tf_op jit(solution)/shard_map/ppermute | solution.py:553
  4.7 0.0 copy-done
  4.7 0.0 copy-done.3
  4.7 2.7 %collective-permute-start.1 = (bf16[264,128]{1,0:T(8,128)(2,1)S(1)}, bf16[264,128]{1,0:T(8,128)(2,1)S(1)}, u32[]{:S(2)}, u32[]{:S(2)}) collective-permute-start(bf16[264,128]{1,0:T(8,128)(2,1)S(1)} %get-tuple-element.48), channel_id=1, source_target_pairs={{0,8},{4,12},{8,0},{12,4},{1,9},{5,13},{9,1},{13,5},{2,10},{6,14},... | collective-permute-start | bytes 202760 | tf_op jit(solution)/shard_map/ppermute | solution.py:562
  7.4 0.9 %copy-done.2 = bf16[128,512]{1,0:T(8,128)(2,1)S(1)} copy-done((bf16[128,512]{1,0:T(8,128)(2,1)S(1)}, bf16[128,512]{1,0:T(8,128)(2,1)}, u32[]{:S(2)}) %copy-start.2) | copy-done | bytes 131096
  8.3 0.7 %shard_map.95 = (bf16[512,128]{1,0:T(8,128)(2,1)S(1)}, f32[128,512]{1,0:T(8,128)S(1)}, f32[8,512]{1,0:T(8,128)S(1)}, bf16[256,128]{1,0:T(8,128)(2,1)S(1)}, bf16[...) custom-call(s32[1,16]{1,0:T(1,128)S(1)} %bitcast.2, ...), custom_call_target="tpu_custom_call" | custom-call | tf_op jit(solution)/shard_map/pallas_call | solution.py:565
  9.0 0.0 collective-permute-done.refs_4_.refs_12_.refs_1_
  9.1 0.3 %shard_map.96 = (f32[128,512]{1,0:T(8,128)S(1)}, f32[128,512]{1,0:T(8,128)S(1)}, f32[8,512]{1,0:T(8,128)S(1)}, bf16[512,128]{1,0:T(8,128)(2,1)S(1)}, f32[8,128]{1,0:T(8,128)S(1)}) custom-call(bf16[512,128]{1,0:T(8,128)(2,1)S(1)} %get-tuple-element.35.refs_0_, bf16[512,128]{1,0:T(8,128)(2,1)S(1)} %get-tuple-element.36.refs_1_, ...), custom_call_target="tpu_custom_call" | custom-call | tf_op jit(solution)/shard_map/pallas_call | solution.py:574
  9.4 2.4 %collective-permute-done.1.refs_13_.refs_2_ = bf16[264,128]{1,0:T(8,128)(2,1)S(1)} collective-permute-done((bf16[264,128]{1,0:T(8,128)(2,1)S(1)}, bf16[264,128]{1,0:T(8,128)(2,1)S(1)}, u32[]{:S(2)}, u32[]{:S(2)}) %collective-permute-start.1) | collective-permute-done | bytes 67616 | tf_op jit(solution)/shard_map/ppermute | solution.py:562
  11.8 1.1 %shard_map.97 = (bf16[512,128]{1,0:T(8,128)(2,1)S(1)}, bf16[512,128]{1,0:T(8,128)(2,1)S(1)}, bf16[512,128]{1,0:T(8,128)(2,1)S(1)}, bf16[512,128]{1,0:T(8,128)(2,1)S(1)}) custom-call(bf16[512,128]{1,0:T(8,128)(2,1)S(1)} %get-tuple-element.35.refs_0_, bf16[512,128]{1,0:T(8,128)(2,1)S(1)} %get-tuple-element.36.refs_1_, f32[8,512]{1,0:T(8,128)S(1)} %get-tuple-element.39.refs_2_, ...), custom_call_target="tpu_custom_call" | custom-call | tf_op jit(solution)/shard_map/pallas_call | solution.py:586
  12.8 2.1 %collective-permute-start.2 = (bf16[512,128]{1,0:T(8,128)(2,1)S(1)}, bf16[512,128]{1,0:T(8,128)(2,1)S(1)}, u32[]{:S(2)}, u32[]{:S(2)}) collective-permute-start(bf16[512,128]{1,0:T(8,128)(2,1)S(1)} %get-tuple-element.49), channel_id=1, source_target_pairs={{0,12},{4,8},{8,4},{12,0},{1,13},{5,9},{9,5},{13,1},{2,14},{6,10},... | collective-permute-start | bytes 393224 | tf_op jit(solution)/shard_map/ppermute | solution.py:598
  14.9 0.0 collective-permute-start.3
  14.9 4.2 %collective-permute-start.5 = (bf16[512,128]{1,0:T(8,128)(2,1)S(1)}, bf16[512,128]{1,0:T(8,128)(2,1)S(1)}, u32[]{:S(2)}, u32[]{:S(2)}) collective-permute-start(bf16[512,128]{1,0:T(8,128)(2,1)S(1)} %get-tuple-element.54), channel_id=1, source_target_pairs={{0,8},{4,4},{8,0},{12,12},{1,9},{5,5},{9,1},{13,13},{2,10},{6,6},{... | collective-permute-start | bytes 393224 | tf_op jit(solution)/shard_map/ppermute | solution.py:598
  19.2 0.7 %collective-permute-start.4 = (bf16[512,128]{1,0:T(8,128)(2,1)S(1)}, bf16[512,128]{1,0:T(8,128)(2,1)S(1)}, u32[]{:S(2)}, u32[]{:S(2)}) collective-permute-start(bf16[512,128]{1,0:T(8,128)(2,1)S(1)} %get-tuple-element.54), channel_id=1, source_target_pairs={{0,0},{4,12},{8,8},{12,4},{1,1},{5,13},{9,9},{13,5},{2,2},{6,14},{... | collective-permute-start | bytes 393224 | tf_op jit(solution)/shard_map/ppermute | solution.py:598
  19.9 1.3 %collective-permute-done.2._.refs_4_ = bf16[512,128]{1,0:T(8,128)(2,1)S(1)} collective-permute-done((bf16[512,128]{1,0:T(8,128)(2,1)S(1)}, bf16[512,128]{1,0:T(8,128)(2,1)S(1)}, u32[]{:S(2)}, u32[]{:S(2)}) %collective-permute-start.2) | collective-permute-done | bytes 131104 | tf_op jit(solution)/shard_map/ppermute | solution.py:598
  21.1 0.3 %shard_map.98 = (bf16[128,256]{1,0:T(8,128)(2,1)S(1)}, bf16[128,512]{1,0:T(8,128)(2,1)S(1)}) custom-call(bf16[512,128]{1,0:T(8,128)(2,1)S(1)} %collective-permute-done.2._.refs_4_, bf16[264,128]{1,0:T(8,128)(2,1)S(1)} %fusion.2.packet_ref.refs_11_.refs_0_, bf16[264,128]{1,0:T(8,128)(2,1)S(1)} %collective-permute-done.refs_4_.refs_12_.refs_1_, ...), custom_call_target="tpu_custom_call" | custom-call | tf_op jit(solution)/shard_map/pallas_call | solution.py:604
  21.4 2.8 %collective-permute-done.3.refs_1_ = bf16[512,128]{1,0:T(8,128)(2,1)S(1)} collective-permute-done((bf16[512,128]{1,0:T(8,128)(2,1)S(1)}, bf16[512,128]{1,0:T(8,128)(2,1)S(1)}, u32[]{:S(2)}, u32[]{:S(2)}) %collective-permute-start.3) | collective-permute-done | bytes 131104 | tf_op jit(solution)/shard_map/ppermute | solution.py:598
  24.3 1.7 %collective-permute-done.5.refs_3_ = bf16[512,128]{1,0:T(8,128)(2,1)S(1)} collective-permute-done((bf16[512,128]{1,0:T(8,128)(2,1)S(1)}, bf16[512,128]{1,0:T(8,128)(2,1)S(1)}, u32[]{:S(2)}, u32[]{:S(2)}) %collective-permute-start.5) | collective-permute-done | bytes 131104 | tf_op jit(solution)/shard_map/ppermute | solution.py:598
  25.9 0.0 collective-permute-done.4.refs_2_
  25.9 1.0 %shard_map.99 = (f32[128,512]{1,0:T(8,128)}, f32[128,128]{1,0:T(8,128)}, f32[128,128]{1,0:T(8,128)}) custom-call(bf16[128,256]{1,0:T(8,128)(2,1)S(1)} %get-tuple-element.50.query_spread, bf16[128,512]{1,0:T(8,128)(2,1)S(1)} %get-tuple-element.51.key_spread, bf16[512,128]{1,0:T(8,128)(2,1)S(1)} %get-tuple-element.52.refs_0_, ...), custom_call_target="tpu_custom_call" | custom-call | tf_op jit(solution)/shard_map/pallas_call | solution.py:614
  (5 shorter events, 0.0 us)
Async XLA Ops:
  0.6 4.1 %copy-start = (bf16[128,512]{1,0:T(8,128)(2,1)S(1)}, bf16[128,512]{1,0:T(8,128)(2,1)}, u32[]{:S(2)}) copy-start(bf16[128,512]{1,0:T(8,128)(2,1)} %query_ref.3) | copy-start | bytes 393220
  0.7 4.1 %copy-start.3 = (s32[16]{0:T(128)S(1)}, s32[16]{0:T(128)}, u32[]{:S(2)}) copy-start(s32[16]{0:T(128)} %param.7) | copy-start | bytes 196
  1.6 5.8 %copy-start.1 = (bf16[128,512]{1,0:T(8,128)(2,1)S(1)}, bf16[128,512]{1,0:T(8,128)(2,1)}, u32[]{:S(2)}) copy-start(bf16[128,512]{1,0:T(8,128)(2,1)} %grad_ref.1) | copy-start | bytes 393220
  1.6 7.4 %collective-permute-start = (bf16[264,128]{1,0:T(8,128)(2,1)S(1)}, bf16[264,128]{1,0:T(8,128)(2,1)S(1)}, u32[]{:S(2)}, u32[]{:S(2)}) collective-permute-start(bf16[264,128]{1,0:T(8,128)(2,1)S(1)} %fusion.2.packet_ref.refs_11_.refs_0_), channel_id=1, source_target_pairs={{0,4},{4,8},{8,12},{12,0},{1,5},{5,9},{9,13},{13,1},{2,6},{6,10},{... | collective-permute-start | bytes 202760 | tf_op jit(solution)/shard_map/ppermute | solution.py:553
  4.7 7.0 %collective-permute-start.1 = (bf16[264,128]{1,0:T(8,128)(2,1)S(1)}, bf16[264,128]{1,0:T(8,128)(2,1)S(1)}, u32[]{:S(2)}, u32[]{:S(2)}) collective-permute-start(bf16[264,128]{1,0:T(8,128)(2,1)S(1)} %get-tuple-element.48), channel_id=1, source_target_pairs={{0,8},{4,12},{8,0},{12,4},{1,9},{5,13},{9,1},{13,5},{2,10},{6,14},... | collective-permute-start | bytes 202760 | tf_op jit(solution)/shard_map/ppermute | solution.py:562
  7.4 0.9 %copy-start.2 = (bf16[128,512]{1,0:T(8,128)(2,1)S(1)}, bf16[128,512]{1,0:T(8,128)(2,1)}, u32[]{:S(2)}) copy-start(bf16[128,512]{1,0:T(8,128)(2,1)} %saved_ref.1) | copy-start | bytes 393220
  12.8 8.3 %collective-permute-start.2 = (bf16[512,128]{1,0:T(8,128)(2,1)S(1)}, bf16[512,128]{1,0:T(8,128)(2,1)S(1)}, u32[]{:S(2)}, u32[]{:S(2)}) collective-permute-start(bf16[512,128]{1,0:T(8,128)(2,1)S(1)} %get-tuple-element.49), channel_id=1, source_target_pairs={{0,12},{4,8},{8,4},{12,0},{1,13},{5,9},{9,5},{13,1},{2,14},{6,10},... | collective-permute-start | bytes 393224 | tf_op jit(solution)/shard_map/ppermute | solution.py:598
  14.9 9.3 %collective-permute-start.3 = (bf16[512,128]{1,0:T(8,128)(2,1)S(1)}, bf16[512,128]{1,0:T(8,128)(2,1)S(1)}, u32[]{:S(2)}, u32[]{:S(2)}) collective-permute-start(bf16[512,128]{1,0:T(8,128)(2,1)S(1)} %get-tuple-element.53), channel_id=1, source_target_pairs={{0,4},{4,0},{8,12},{12,8},{1,5},{5,1},{9,13},{13,9},{2,6},{6,2},{1... | collective-permute-start | bytes 393224 | tf_op jit(solution)/shard_map/ppermute | solution.py:598
  14.9 11.0 %collective-permute-start.5 = (bf16[512,128]{1,0:T(8,128)(2,1)S(1)}, bf16[512,128]{1,0:T(8,128)(2,1)S(1)}, u32[]{:S(2)}, u32[]{:S(2)}) collective-permute-start(bf16[512,128]{1,0:T(8,128)(2,1)S(1)} %get-tuple-element.54), channel_id=1, source_target_pairs={{0,8},{4,4},{8,0},{12,12},{1,9},{5,5},{9,1},{13,13},{2,10},{6,6},{... | collective-permute-start | bytes 393224 | tf_op jit(solution)/shard_map/ppermute | solution.py:598
  19.2 6.7 %collective-permute-start.4 = (bf16[512,128]{1,0:T(8,128)(2,1)S(1)}, bf16[512,128]{1,0:T(8,128)(2,1)S(1)}, u32[]{:S(2)}, u32[]{:S(2)}) collective-permute-start(bf16[512,128]{1,0:T(8,128)(2,1)S(1)} %get-tuple-element.54), channel_id=1, source_target_pairs={{0,0},{4,12},{8,8},{12,4},{1,1},{5,13},{9,9},{13,5},{2,2},{6,14},{... | collective-permute-start | bytes 393224 | tf_op jit(solution)/shard_map/ppermute | solution.py:598

commit v15 on v9

--- a/solution.py
+++ b/solution.py
@@ -262,6 +262,23 @@
     return jnp.concatenate([matrix[:, h * width : (h + 1) * width] for h in range(heads)], axis=0)
 
 
+def target_of(index, k, count):
+    if count == 4 and k in (1, 2):
+        return (2 * index + 1) % 5 if k == 1 else (3 * index + 2) % 5
+    return index ^ k
+
+
+def source_of(index, k, count):
+    return target_of(index, 3 - k if count == 4 and k in (1, 2) else k, count)
+
+
+def exchange_of(owner, index, count):
+    found = jnp.zeros_like(owner)
+    for k in range(1, count):
+        found = jnp.where(owner == target_of(index, k, count), k, found)
+    return found
+
+
 def runs_of(hot):
     count, rows = hot.shape
     counts = jnp.sum(hot, axis=1, keepdims=True)
@@ -300,11 +317,12 @@
     index = lax.axis_index("ctx")
     lane = lax.broadcasted_iota(jnp.int32, (1, rows), 1)
     position = index * rows + lane
-    first = jnp.zeros((1, rows), jnp.int32)
-    end = jnp.int32(0)
-    for d in range(docs):
-        end = end + doc_ref[d]
-        first = jnp.where(end <= position, end, first)
+    earlier = lax.broadcasted_iota(jnp.int32, (docs, docs), 1) <= lax.broadcasted_iota(
+        jnp.int32, (docs, docs), 0
+    )
+    lengths = doc_ref[...].astype(jnp.float32)
+    ends = jnp.sum(jnp.where(earlier, lengths, 0.0), axis=1, keepdims=True).astype(jnp.int32)
+    first = jnp.max(jnp.where(ends <= position, ends, 0), axis=0, keepdims=True)
     key_position = index * rows + lax.broadcasted_iota(jnp.int32, (rows, rows), 0)
     allowed = (key_position >= first) & (key_position <= position)
     allowed = jnp.concatenate([allowed] * heads, axis=1)
@@ -329,8 +347,9 @@
     row_out[3:4, :] = jnp.concatenate([first.astype(jnp.float32)] * heads, axis=1)
     row_out[4:8, :] = jnp.ones((4, width), jnp.float32)
     owner, counts, rank = runs_of(packet_ref[2 * rows : 2 * rows + count, :].astype(jnp.float32))
-    spread_out[...] = one_hot(count * slot, (owner ^ index) * slot + rank)
-    target_out[...] = one_hot(count * rows, (owner ^ index) * rows + rank)
+    at = exchange_of(owner, index, count)
+    spread_out[...] = one_hot(count * slot, at * slot + rank)
+    target_out[...] = one_hot(count * rows, at * rows + rank)
     filled_out[0:count, :] = jnp.broadcast_to(counts, (count, rows))
     filled_out[count:, :] = jnp.zeros((8 - count, rows), jnp.float32)
 
@@ -356,7 +375,8 @@
     for p in range(count):
         base = base + jnp.where(owner == p, filled[p : p + 1, :], 0.0)
     inside = index >= back
-    target = jnp.where(inside, (owner ^ index) * rows + base.astype(jnp.int32) + rank, -1)
+    at = exchange_of(owner, index, count)
+    target = jnp.where(inside, at * rows + base.astype(jnp.int32) + rank, -1)
     filled = filled[0:count, :] + jnp.where(inside, counts, 0.0)
     return raised, change, (new_top, total, factors), one_hot(count * rows, target), filled
 
@@ -453,7 +473,7 @@
         for k in range(count):
             step = lane - k * size
             for back in range(halo + 1):
-                block = (index ^ k) - back
+                block = source_of(index, k, count) - back
                 start = jnp.zeros((1, 1), jnp.int32)
                 length = jnp.zeros((1, 1), jnp.int32)
                 for d in range(count):
@@ -534,10 +554,10 @@
         out_shape=[jax.ShapeDtypeStruct((columns, depth), bf16)] * 2
         + block_shapes
         + [row_shape, jax.ShapeDtypeStruct((count * slot, rows), bf16), target_shape, filled_shape],
-        in_specs=[pl.BlockSpec(memory_space=pltpu.SMEM)] + [whole] * 4,
+        in_specs=[whole] * 5,
         out_specs=[whole] * 8,
         compiler_params=params,
-    )(doc_lengths, packet, queries, grad_out, forward_out)
+    )(doc_lengths.reshape(1, -1), packet, queries, grad_out, forward_out)
     raised, change, target = [raised], [change], [target]
     for back in range(1, halo):
         found = pl.pallas_call(
@@ -560,7 +580,8 @@
         compiler_params=params,
     )(query_rows, grad_rows, row, filled, spread, *raised, *change, *target, packet, *near)
     received = [sent[0]] + [
-        lax.ppermute(sent[k], "ctx", [(i, i ^ k) for i in range(count)]) for k in range(1, count)
+        lax.ppermute(sent[k], "ctx", [(i, target_of(i, k, count)) for i in range(count)])
+        for k in range(1, count)
     ]
     spreads = pl.pallas_call(
         functools.partial(order_kernel, count, halo),

time: 25.5 us -> 26.5 us (1.039)
  waiting for transfers between devices: 8.01 us -> 9.03 us
  starting transfers between devices: 10.1 us -> 10.7 us
  Pallas kernels: 3.67 us -> 3.14 us
    ppermute x2, waiting for transfers between devices: 1.29 us -> 1.83 us  [near_plan(): lax.ppermute(packet, 'ctx', [(i, (i + back) % count) for i in range(count)])]
    ppermute x3, starting transfers between devices: 4.45 us -> 4.99 us  [near_plan(): lax.ppermute(sent[k], 'ctx', [(i, target_of(i, k, count)) for i in range(...]
    pallas_call x1, Pallas kernels: 1 us -> 0.47 us  [near_plan(): pl.pallas_call(functools.partial(own_kernel, count, doc_lengths.shape[0])...]
    ppermute x3, waiting for transfers between devices: 6.72 us -> 7.2 us  [near_plan(): lax.ppermute(sent[k], 'ctx', [(i, target_of(i, k, count)) for i in range(...]
  transfers between devices with their start and end apart: 5 -> 5, of which waited for: 3 -> 4; matrix products, arithmetic and copies ran while one was open for 0% -> 0% of each run, Pallas kernels for 6% -> 4%
where the time goes in v15:
time: 26.5 us; the launch traced here: 26.3 us
  starting transfers between devices  10.7 us (40%)
  waiting for transfers between devices  9.03 us (34%)
  Pallas kernels  3.14 us (12%)
  local copies, waits for them, and re-layouts  1.82 us (7%)
  other arithmetic  0.96 us (4%)
  between operations  0.7 us (3%)
    ppermute x3, waiting for transfers between devices, near_plan(): lax.ppermute(sent[k], 'ctx', [(i, target_of(i, k, count)) for i in range(...  7.2 us
    ppermute x2, starting transfers between devices, near_plan(): lax.ppermute(packet, 'ctx', [(i, (i + back) % count) for i in range(count)])  5.67 us
    ppermute x3, starting transfers between devices, near_plan(): lax.ppermute(sent[k], 'ctx', [(i, target_of(i, k, count)) for i in range(...  4.99 us
    ppermute x2, waiting for transfers between devices, near_plan(): lax.ppermute(packet, 'ctx', [(i, (i + back) % count) for i in range(count)])  1.83 us
    unnamed x8, local copies, waits for them, and re-layouts  1.82 us
    pallas_call x1, Pallas kernels, near_plan(): pl.pallas_call(functools.partial(attend_kernel, count, halo), out_shape=[...  1.04 us
    pallas_call x1, Pallas kernels, near_plan(): pl.pallas_call(functools.partial(place_kernel, count), out_shape=[jax.Sha...  1 us
    select_n x1, other arithmetic, near_plan(): jnp.where(mark < 0, jnp.pad(jnp.concatenate([key_head_rows, value_head_ro...  0.94 us
  transfers between devices with their start and end apart: 5, of which 4 were waited for; matrix products, arithmetic and copies ran while one was open for 0% of the time, Pallas kernels for 4%

profile of v15, /device:TPU:0, one launch (start us, length us, event | category | flops | bytes accessed | tf_op | source)
XLA Modules:
  0.0 26.3 jit_solution(9551675916800974450)
XLA Ops:
  0.6 0.0 copy-start
  0.7 0.9 %fusion.2.packet_ref.refs_11_.refs_0_ = bf16[264,128]{1,0:T(8,128)(2,1)S(1)} fusion(bf16[128,128]{1,0:T(8,128)(2,1)} %param.11, bf16[128,128]{1,0:T(8,128)(2,1)} %param.10, s32[128]{0:T(128)} %param.8, s32[264]{0:T(512)S(1)} %iota_add_fusion, pred[264]{0:T(512)(128)(4,1)S(1)} %broadcast_compare_fusion), kind=kLoop, calls=%fused_computation.4 | loop fusion | flops 337920 | bytes 134952 | tf_op jit(solution)/shard_map/jit(_where)/select_n | solution.py:539
  1.6 0.0 copy-start.3
  1.6 3.1 %collective-permute-start = (bf16[264,128]{1,0:T(8,128)(2,1)S(1)}, bf16[264,128]{1,0:T(8,128)(2,1)S(1)}, u32[]{:S(2)}, u32[]{:S(2)}) collective-permute-start(bf16[264,128]{1,0:T(8,128)(2,1)S(1)} %fusion.2.packet_ref.refs_11_.refs_0_), channel_id=1, source_target_pairs={{0,4},{4,8},{8,12},{12,0},{1,5},{5,9},{9,13},{13,1},{2,6},{6,10},{... | collective-permute-start | bytes 202760 | tf_op jit(solution)/shard_map/ppermute | solution.py:545
  4.7 2.6 %collective-permute-start.1 = (bf16[264,128]{1,0:T(8,128)(2,1)S(1)}, bf16[264,128]{1,0:T(8,128)(2,1)S(1)}, u32[]{:S(2)}, u32[]{:S(2)}) collective-permute-start(bf16[264,128]{1,0:T(8,128)(2,1)S(1)} %fusion.2.packet_ref.refs_11_.refs_0_), channel_id=1, source_target_pairs={{0,8},{4,12},{8,0},{12,4},{1,9},{5,13},{9,1},{13,5},{2,10},{6,14},... | collective-permute-start | bytes 202760 | tf_op jit(solution)/shard_map/ppermute | solution.py:545
  7.3 0.0 copy-done
  7.3 0.0 copy-done.3
  7.3 0.0 copy-start.1
  7.3 0.9 %copy-done.1 = bf16[128,512]{1,0:T(8,128)(2,1)S(1)} copy-done((bf16[128,512]{1,0:T(8,128)(2,1)S(1)}, bf16[128,512]{1,0:T(8,128)(2,1)}, u32[]{:S(2)}) %copy-start.1) | copy-done | bytes 131096
  8.2 0.0 copy-start.2
  8.2 0.9 %copy-done.2 = bf16[128,512]{1,0:T(8,128)(2,1)S(1)} copy-done((bf16[128,512]{1,0:T(8,128)(2,1)S(1)}, bf16[128,512]{1,0:T(8,128)(2,1)}, u32[]{:S(2)}) %copy-start.2) | copy-done | bytes 131096
  9.1 0.5 %shard_map.94 = (bf16[512,128]{1,0:T(8,128)(2,1)S(1)}, bf16[512,128]{1,0:T(8,128)(2,1)S(1)}, f32[128,512]{1,0:T(8,128)S(1)}, f32[128,512]{1,0:T(8,128)S(1)}, f32...) custom-call(s32[1,16]{1,0:T(1,128)S(1)} %bitcast.1, ...), custom_call_target="tpu_custom_call" | custom-call | tf_op jit(solution)/shard_map/pallas_call | solution.py:552
  9.6 0.0 collective-permute-done.refs_4_.refs_12_.refs_1_
  9.6 0.3 %shard_map.95 = (f32[128,512]{1,0:T(8,128)S(1)}, f32[128,512]{1,0:T(8,128)S(1)}, f32[8,512]{1,0:T(8,128)S(1)}, bf16[512,128]{1,0:T(8,128)(2,1)S(1)}, f32[8,128]{1,0:T(8,128)S(1)}) custom-call(bf16[512,128]{1,0:T(8,128)(2,1)S(1)} %get-tuple-element.22.refs_0_, bf16[512,128]{1,0:T(8,128)(2,1)S(1)} %get-tuple-element.23.refs_1_, ...), custom_call_target="tpu_custom_call" | custom-call | tf_op jit(solution)/shard_map/pallas_call | solution.py:563
  9.9 1.8 %collective-permute-done.1.refs_13_.refs_2_ = bf16[264,128]{1,0:T(8,128)(2,1)S(1)} collective-permute-done((bf16[264,128]{1,0:T(8,128)(2,1)S(1)}, bf16[264,128]{1,0:T(8,128)(2,1)S(1)}, u32[]{:S(2)}, u32[]{:S(2)}) %collective-permute-start.1) | collective-permute-done | bytes 67616 | tf_op jit(solution)/shard_map/ppermute | solution.py:545
  11.8 1.0 %shard_map.96 = (bf16[512,128]{1,0:T(8,128)(2,1)S(1)}, bf16[512,128]{1,0:T(8,128)(2,1)S(1)}, bf16[512,128]{1,0:T(8,128)(2,1)S(1)}, bf16[512,128]{1,0:T(8,128)(2,1)S(1)}) custom-call(bf16[512,128]{1,0:T(8,128)(2,1)S(1)} %get-tuple-element.22.refs_0_, bf16[512,128]{1,0:T(8,128)(2,1)S(1)} %get-tuple-element.23.refs_1_, f32[8,512]{1,0:T(8,128)S(1)} %get-tuple-element.26.refs_2_, ...), custom_call_target="tpu_custom_call" | custom-call | tf_op jit(solution)/shard_map/pallas_call | solution.py:575
  12.8 2.1 %collective-permute-start.2 = (bf16[512,128]{1,0:T(8,128)(2,1)S(1)}, bf16[512,128]{1,0:T(8,128)(2,1)S(1)}, u32[]{:S(2)}, u32[]{:S(2)}) collective-permute-start(bf16[512,128]{1,0:T(8,128)(2,1)S(1)} %get-tuple-element.35), channel_id=1, source_target_pairs={{0,12},{4,8},{8,4},{12,0},{1,13},{5,9},{9,5},{13,1},{2,14},{6,10},... | collective-permute-start | bytes 393224 | tf_op jit(solution)/shard_map/ppermute | solution.py:583
  14.9 0.0 collective-permute-start.3
  14.9 2.9 %collective-permute-start.4 = (bf16[512,128]{1,0:T(8,128)(2,1)S(1)}, bf16[512,128]{1,0:T(8,128)(2,1)S(1)}, u32[]{:S(2)}, u32[]{:S(2)}) collective-permute-start(bf16[512,128]{1,0:T(8,128)(2,1)S(1)} %get-tuple-element.40), channel_id=1, source_target_pairs={{0,8},{4,0},{8,12},{12,4},{1,9},{5,1},{9,13},{13,5},{2,10},{6,2},{... | collective-permute-start | bytes 393224 | tf_op jit(solution)/shard_map/ppermute | solution.py:583
  17.8 3.3 %collective-permute-done.2._.refs_3_ = bf16[512,128]{1,0:T(8,128)(2,1)S(1)} collective-permute-done((bf16[512,128]{1,0:T(8,128)(2,1)S(1)}, bf16[512,128]{1,0:T(8,128)(2,1)S(1)}, u32[]{:S(2)}, u32[]{:S(2)}) %collective-permute-start.2) | collective-permute-done | bytes 131104 | tf_op jit(solution)/shard_map/ppermute | solution.py:583
  21.1 0.3 %shard_map.97 = (bf16[128,256]{1,0:T(8,128)(2,1)S(1)}, bf16[128,512]{1,0:T(8,128)(2,1)S(1)}) custom-call(bf16[512,128]{1,0:T(8,128)(2,1)S(1)} %collective-permute-done.2._.refs_3_, bf16[264,128]{1,0:T(8,128)(2,1)S(1)} %fusion.2.packet_ref.refs_11_.refs_0_, bf16[264,128]{1,0:T(8,128)(2,1)S(1)} %collective-permute-done.refs_4_.refs_12_.refs_1_, ...), custom_call_target="tpu_custom_call" | custom-call | tf_op jit(solution)/shard_map/pallas_call | solution.py:586
  21.4 2.1 %collective-permute-done.3.refs_1_ = bf16[512,128]{1,0:T(8,128)(2,1)S(1)} collective-permute-done((bf16[512,128]{1,0:T(8,128)(2,1)S(1)}, bf16[512,128]{1,0:T(8,128)(2,1)S(1)}, u32[]{:S(2)}, u32[]{:S(2)}) %collective-permute-start.3) | collective-permute-done | bytes 131104 | tf_op jit(solution)/shard_map/ppermute | solution.py:583
  23.5 1.8 %collective-permute-done.4.refs_2_ = bf16[512,128]{1,0:T(8,128)(2,1)S(1)} collective-permute-done((bf16[512,128]{1,0:T(8,128)(2,1)S(1)}, bf16[512,128]{1,0:T(8,128)(2,1)S(1)}, u32[]{:S(2)}, u32[]{:S(2)}) %collective-permute-start.4) | collective-permute-done | bytes 131104 | tf_op jit(solution)/shard_map/ppermute | solution.py:583
  25.3 1.0 %shard_map.98 = (f32[128,512]{1,0:T(8,128)}, f32[128,128]{1,0:T(8,128)}, f32[128,128]{1,0:T(8,128)}) custom-call(bf16[128,256]{1,0:T(8,128)(2,1)S(1)} %get-tuple-element.36.query_spread, bf16[128,512]{1,0:T(8,128)(2,1)S(1)} %get-tuple-element.37.key_spread, bf16[512,128]{1,0:T(8,128)(2,1)S(1)} %get-tuple-element.38.refs_0_, ...), custom_call_target="tpu_custom_call" | custom-call | tf_op jit(solution)/shard_map/pallas_call | solution.py:596
  (2 shorter events, 0.0 us)
Async XLA Ops:
  0.6 6.7 %copy-start = (bf16[128,512]{1,0:T(8,128)(2,1)S(1)}, bf16[128,512]{1,0:T(8,128)(2,1)}, u32[]{:S(2)}) copy-start(bf16[128,512]{1,0:T(8,128)(2,1)} %query_ref.1) | copy-start | bytes 393220
  1.6 5.7 %copy-start.3 = (s32[16]{0:T(128)S(1)}, s32[16]{0:T(128)}, u32[]{:S(2)}) copy-start(s32[16]{0:T(128)} %param.7) | copy-start | bytes 196
  1.6 8.0 %collective-permute-start = (bf16[264,128]{1,0:T(8,128)(2,1)S(1)}, bf16[264,128]{1,0:T(8,128)(2,1)S(1)}, u32[]{:S(2)}, u32[]{:S(2)}) collective-permute-start(bf16[264,128]{1,0:T(8,128)(2,1)S(1)} %fusion.2.packet_ref.refs_11_.refs_0_), channel_id=1, source_target_pairs={{0,4},{4,8},{8,12},{12,0},{1,5},{5,9},{9,13},{13,1},{2,6},{6,10},{... | collective-permute-start | bytes 202760 | tf_op jit(solution)/shard_map/ppermute | solution.py:545
  4.7 7.1 %collective-permute-start.1 = (bf16[264,128]{1,0:T(8,128)(2,1)S(1)}, bf16[264,128]{1,0:T(8,128)(2,1)S(1)}, u32[]{:S(2)}, u32[]{:S(2)}) collective-permute-start(bf16[264,128]{1,0:T(8,128)(2,1)S(1)} %fusion.2.packet_ref.refs_11_.refs_0_), channel_id=1, source_target_pairs={{0,8},{4,12},{8,0},{12,4},{1,9},{5,13},{9,1},{13,5},{2,10},{6,14},... | collective-permute-start | bytes 202760 | tf_op jit(solution)/shard_map/ppermute | solution.py:545
  7.3 0.9 %copy-start.1 = (bf16[128,512]{1,0:T(8,128)(2,1)S(1)}, bf16[128,512]{1,0:T(8,128)(2,1)}, u32[]{:S(2)}) copy-start(bf16[128,512]{1,0:T(8,128)(2,1)} %grad_ref.1) | copy-start | bytes 393220
  8.2 0.9 %copy-start.2 = (bf16[128,512]{1,0:T(8,128)(2,1)S(1)}, bf16[128,512]{1,0:T(8,128)(2,1)}, u32[]{:S(2)}) copy-start(bf16[128,512]{1,0:T(8,128)(2,1)} %saved_ref.1) | copy-start | bytes 393220
  12.8 8.3 %collective-permute-start.2 = (bf16[512,128]{1,0:T(8,128)(2,1)S(1)}, bf16[512,128]{1,0:T(8,128)(2,1)S(1)}, u32[]{:S(2)}, u32[]{:S(2)}) collective-permute-start(bf16[512,128]{1,0:T(8,128)(2,1)S(1)} %get-tuple-element.35), channel_id=1, source_target_pairs={{0,12},{4,8},{8,4},{12,0},{1,13},{5,9},{9,5},{13,1},{2,14},{6,10},... | collective-permute-start | bytes 393224 | tf_op jit(solution)/shard_map/ppermute | solution.py:583
  14.9 8.6 %collective-permute-start.3 = (bf16[512,128]{1,0:T(8,128)(2,1)S(1)}, bf16[512,128]{1,0:T(8,128)(2,1)S(1)}, u32[]{:S(2)}, u32[]{:S(2)}) collective-permute-start(bf16[512,128]{1,0:T(8,128)(2,1)S(1)} %get-tuple-element.39), channel_id=1, source_target_pairs={{0,4},{4,12},{8,0},{12,8},{1,5},{5,13},{9,1},{13,9},{2,6},{6,14},{... | collective-permute-start | bytes 393224 | tf_op jit(solution)/shard_map/ppermute | solution.py:583
  14.9 10.4 %collective-permute-start.4 = (bf16[512,128]{1,0:T(8,128)(2,1)S(1)}, bf16[512,128]{1,0:T(8,128)(2,1)S(1)}, u32[]{:S(2)}, u32[]{:S(2)}) collective-permute-start(bf16[512,128]{1,0:T(8,128)(2,1)S(1)} %get-tuple-element.40), channel_id=1, source_target_pairs={{0,8},{4,0},{8,12},{12,4},{1,9},{5,1},{9,13},{13,5},{2,10},{6,2},{... | collective-permute-start | bytes 393224 | tf_op jit(solution)/shard_map/ppermute | solution.py:583

commit v16 on v13

--- a/solution.py
+++ b/solution.py
@@ -262,6 +262,23 @@
     return jnp.concatenate([matrix[:, h * width : (h + 1) * width] for h in range(heads)], axis=0)
 
 
+def target_of(index, k, count):
+    if count == 4 and k in (1, 2):
+        return (2 * index + 1) % 5 if k == 1 else (3 * index + 2) % 5
+    return index ^ k
+
+
+def source_of(index, k, count):
+    return target_of(index, 3 - k if count == 4 and k in (1, 2) else k, count)
+
+
+def exchange_of(owner, index, count):
+    found = jnp.zeros_like(owner)
+    for k in range(1, count):
+        found = jnp.where(owner == target_of(index, k, count), k, found)
+    return found
+
+
 def runs_of(hot):
     count, rows = hot.shape
     counts = jnp.sum(hot, axis=1, keepdims=True)
@@ -285,11 +302,12 @@
     index = lax.axis_index("ctx")
     lane = lax.broadcasted_iota(jnp.int32, (1, rows), 1)
     position = index * rows + lane
-    first = jnp.zeros((1, rows), jnp.int32)
-    end = jnp.int32(0)
-    for d in range(docs):
-        end = end + doc_ref[d]
-        first = jnp.where(end <= position, end, first)
+    earlier = lax.broadcasted_iota(jnp.int32, (docs, docs), 1) <= lax.broadcasted_iota(
+        jnp.int32, (docs, docs), 0
+    )
+    lengths = doc_ref[...].astype(jnp.float32)
+    ends = jnp.sum(jnp.where(earlier, lengths, 0.0), axis=1, keepdims=True).astype(jnp.int32)
+    first = jnp.max(jnp.where(ends <= position, ends, 0), axis=0, keepdims=True)
     key_position = index * rows + lax.broadcasted_iota(jnp.int32, (rows, rows), 0)
     allowed = (key_position >= first) & (key_position <= position)
     allowed = jnp.concatenate([allowed] * heads, axis=1)
@@ -307,37 +325,22 @@
     row_out[3:4, :] = jnp.concatenate([first.astype(jnp.float32)] * heads, axis=1)
     row_out[4:8, :] = jnp.ones((4, width), jnp.float32)
     owner, counts, rank = runs_of(packet_ref[2 * rows : 2 * rows + count, :].astype(jnp.float32))
-    spread_out[...] = one_hot(count * slot, (owner ^ index) * slot + rank)
-    target_out[...] = one_hot(count * rows, (owner ^ index) * rows + rank)
+    at = exchange_of(owner, index, count)
+    spread_out[...] = one_hot(count * slot, at * slot + rank)
+    target_out[...] = one_hot(count * rows, at * rows + rank)
     filled_out[0:count, :] = jnp.broadcast_to(counts, (count, rows))
     filled_out[count:, :] = jnp.zeros((8 - count, rows), jnp.float32)
 
 
-def odd_kernel(count, docs, doc_ref, packet_ref, query_ref, packet_out, *outs):
+def scores_kernel(count, docs, doc_ref, packet_ref, query_ref, packet_out, *outs):
     packet_out[...] = packet_ref[...]
-
-    @pl.when(lax.rem(lax.axis_index("ctx"), 2) == 1)
-    def _():
-        own_scores(count, docs, doc_ref, packet_ref, query_ref, outs)
-
-
-def own_kernel(count, docs, doc_ref, packet_ref, query_ref, grad_ref, saved_ref, *refs):
-    done, outs = refs[:6], refs[6:12]
-    grad_out, change_out = refs[12:]
-    rows, width = query_ref.shape
+    own_scores(count, docs, doc_ref, packet_ref, query_ref, outs)
+
+
+def own_kernel(packet_ref, grad_ref, saved_ref, row_ref, grad_out, change_out, row_out):
+    rows, width = grad_ref.shape
     depth = packet_ref.shape[1]
     heads = width // depth
-    odd = lax.rem(lax.axis_index("ctx"), 2) == 1
-
-    @pl.when(odd)
-    def _():
-        for here, out in zip(done, outs, strict=True):
-            out[...] = here[...]
-
-    @pl.when(jnp.logical_not(odd))
-    def _():
-        own_scores(count, docs, doc_ref, packet_ref, query_ref, outs)
-
     grads = end_to_end(grad_ref[...], heads)
     grad_out[...] = grads
     product = grads.astype(jnp.float32) * end_to_end(saved_ref[...], heads).astype(jnp.float32)
@@ -345,7 +348,8 @@
         jnp.ones((8, depth), jnp.float32), product, 1, 1, precision=lax.Precision.HIGHEST
     )[0:1, :]
     change_out[...] = contract(packet_ref[rows : 2 * rows, :], grads, 1, 1) - delta
-    outs[2][0:1, :] = delta
+    row_out[0:1, :] = delta
+    row_out[1:, :] = row_ref[1:, :]
 
 
 def fold(count, back, packet, queries, grads, row, filled):
@@ -369,7 +373,8 @@
     for p in range(count):
         base = base + jnp.where(owner == p, filled[p : p + 1, :], 0.0)
     inside = index >= back
-    target = jnp.where(inside, (owner ^ index) * rows + base.astype(jnp.int32) + rank, -1)
+    at = exchange_of(owner, index, count)
+    target = jnp.where(inside, at * rows + base.astype(jnp.int32) + rank, -1)
     filled = filled[0:count, :] + jnp.where(inside, counts, 0.0)
     return raised, change, (new_top, total, factors), one_hot(count * rows, target), filled
 
@@ -466,7 +471,7 @@
         for k in range(count):
             step = lane - k * size
             for back in range(halo + 1):
-                block = (index ^ k) - back
+                block = source_of(index, k, count) - back
                 start = jnp.zeros((1, 1), jnp.int32)
                 length = jnp.zeros((1, 1), jnp.int32)
                 for d in range(count):
@@ -548,23 +553,24 @@
     ]
     near = [lax.ppermute(packet, "ctx", [(i, (i + 1) % count) for i in range(count)])]
     far, *scored = pl.pallas_call(
-        functools.partial(odd_kernel, count, doc_lengths.shape[0]),
+        functools.partial(scores_kernel, count, doc_lengths.shape[0]),
         out_shape=[jax.ShapeDtypeStruct(packet.shape, bf16)] + score_shapes,
-        in_specs=[pl.BlockSpec(memory_space=pltpu.SMEM)] + [whole] * 2,
+        in_specs=[whole] * 3,
         out_specs=[whole] * 7,
         compiler_params=params,
-    )(doc_lengths, packet, queries)
+    )(doc_lengths.reshape(1, -1), packet, queries)
     near += [
         lax.ppermute(far, "ctx", [(i, (i + back) % count) for i in range(count)])
         for back in range(2, halo + 1)
     ]
-    query_rows, raised, row, spread, target, filled, grad_rows, change = pl.pallas_call(
-        functools.partial(own_kernel, count, doc_lengths.shape[0]),
-        out_shape=score_shapes + [jax.ShapeDtypeStruct((columns, depth), bf16), block_shapes[1]],
-        in_specs=[pl.BlockSpec(memory_space=pltpu.SMEM)] + [whole] * 10,
-        out_specs=[whole] * 8,
+    query_rows, raised, row, spread, target, filled = scored
+    grad_rows, change, row = pl.pallas_call(
+        own_kernel,
+        out_shape=[jax.ShapeDtypeStruct((columns, depth), bf16), block_shapes[1], row_shape],
+        in_specs=[whole] * 4,
+        out_specs=[whole] * 3,
         compiler_params=params,
-    )(doc_lengths, packet, queries, grad_out, forward_out, *scored)
+    )(packet, grad_out, forward_out, row)
     raised, change, target = [raised], [change], [target]
     for back in range(1, halo):
         found = pl.pallas_call(
@@ -587,7 +593,8 @@
         compiler_params=params,
     )(query_rows, grad_rows, row, filled, spread, *raised, *change, *target, packet, *near)
     received = [sent[0]] + [
-        lax.ppermute(sent[k], "ctx", [(i, i ^ k) for i in range(count)]) for k in range(1, count)
+        lax.ppermute(sent[k], "ctx", [(i, target_of(i, k, count)) for i in range(count)])
+        for k in range(1, count)
     ]
     spreads = pl.pallas_call(
         functools.partial(order_kernel, count, halo),

time: 26.5 us -> 27.1 us (1.023)
  waiting for transfers between devices: 8.99 us -> 10.9 us
  Pallas kernels: 4.53 us -> 3.4 us
    ppermute x1, waiting for transfers between devices: 0.69 us -> 2.33 us  [near_plan(): lax.ppermute(far, 'ctx', [(i, (i + back) % count) for i in range(count)])]
    pallas_call x2, Pallas kernels: 1.85 us -> 0.73 us  [the longest x1 0.42 us: near_plan(): pl.pallas_call(own_kernel, out_shape=[jax.ShapeDtypeStruct((columns, dept...]
  transfers between devices with their start and end apart: 5 -> 5, of which waited for: 4 -> 4; matrix products, arithmetic and copies ran while one was open for 0% -> 0% of each run, Pallas kernels for 9% -> 5%
where the time goes in v16:
time: 27.1 us; the launch traced here: 26.9 us
  waiting for transfers between devices  10.9 us (40%)
  starting transfers between devices  10 us (37%)
  Pallas kernels  3.4 us (13%)
  other arithmetic  0.95 us (4%)
  local copies, waits for them, and re-layouts  0.92 us (3%)
  between operations  0.71 us (3%)
    ppermute x3, waiting for transfers between devices, near_plan(): lax.ppermute(sent[k], 'ctx', [(i, target_of(i, k, count)) for i in range(...  8.49 us
    ppermute x3, starting transfers between devices, near_plan(): lax.ppermute(sent[k], 'ctx', [(i, target_of(i, k, count)) for i in range(...  4.31 us
    ppermute x1, starting transfers between devices, near_plan(): lax.ppermute(packet, 'ctx', [(i, (i + 1) % count) for i in range(count)])  3.08 us
    ppermute x1, starting transfers between devices, near_plan(): lax.ppermute(far, 'ctx', [(i, (i + back) % count) for i in range(count)])  2.66 us
    ppermute x1, waiting for transfers between devices, near_plan(): lax.ppermute(far, 'ctx', [(i, (i + back) % count) for i in range(count)])  2.33 us
    pallas_call x1, Pallas kernels, near_plan(): pl.pallas_call(functools.partial(attend_kernel, count, halo), out_shape=[...  1.04 us
    pallas_call x1, Pallas kernels, near_plan(): pl.pallas_call(functools.partial(place_kernel, count), out_shape=[jax.Sha...  1 us
    select_n x1, other arithmetic, near_plan(): jnp.where(mark < 0, jnp.pad(jnp.concatenate([key_head_rows, value_head_ro...  0.94 us
  transfers between devices with their start and end apart: 5, of which 4 were waited for; matrix products, arithmetic and copies ran while one was open for 0% of the time, Pallas kernels for 5%

profile of v16, /device:TPU:0, one launch (start us, length us, event | category | flops | bytes accessed | tf_op | source)
XLA Modules:
  0.0 26.9 jit_solution(3274533203701663355)
XLA Ops:
  0.6 0.0 copy-start
  0.7 0.0 copy-start.3
  0.7 0.9 %fusion.2.packet_ref.refs_11_.refs_0_ = bf16[264,128]{1,0:T(8,128)(2,1)S(1)} fusion(bf16[128,128]{1,0:T(8,128)(2,1)} %param.11, bf16[128,128]{1,0:T(8,128)(2,1)} %param.10, s32[128]{0:T(128)} %param.8, s32[264]{0:T(512)S(1)} %iota_add_fusion, pred[264]{0:T(512)(128)(4,1)S(1)} %broadcast_compare_fusion), kind=kLoop, calls=%fused_computation.4 | loop fusion | flops 337920 | bytes 134952 | tf_op jit(solution)/shard_map/jit(_where)/select_n | solution.py:537
  1.6 0.0 copy-start.1
  1.6 3.1 %collective-permute-start = (bf16[264,128]{1,0:T(8,128)(2,1)S(1)}, bf16[264,128]{1,0:T(8,128)(2,1)S(1)}, u32[]{:S(2)}, u32[]{:S(2)}) collective-permute-start(bf16[264,128]{1,0:T(8,128)(2,1)S(1)} %fusion.2.packet_ref.refs_11_.refs_0_), channel_id=1, source_target_pairs={{0,4},{4,8},{8,12},{12,0},{1,5},{5,9},{9,13},{13,1},{2,6},{6,10},{... | collective-permute-start | bytes 202760 | tf_op jit(solution)/shard_map/ppermute | solution.py:554
  4.7 0.0 copy-done
  4.7 0.0 copy-done.3
  4.7 0.3 %shard_map.94 = (bf16[264,128]{1,0:T(8,128)(2,1)S(1)}, bf16[512,128]{1,0:T(8,128)(2,1)S(1)}, f32[128,512]{1,0:T(8,128)S(1)}, f32[8,512]{1,0:T(8,128)S(1)}, bf16[...) custom-call(s32[1,16]{1,0:T(1,128)S(1)} %bitcast.1, ...), custom_call_target="tpu_custom_call" | custom-call | tf_op jit(solution)/shard_map/pallas_call | solution.py:555
  5.0 2.7 %collective-permute-start.1 = (bf16[264,128]{1,0:T(8,128)(2,1)S(1)}, bf16[264,128]{1,0:T(8,128)(2,1)S(1)}, u32[]{:S(2)}, u32[]{:S(2)}) collective-permute-start(bf16[264,128]{1,0:T(8,128)(2,1)S(1)} %get-tuple-element.38), channel_id=1, source_target_pairs={{0,8},{4,12},{8,0},{12,4},{1,9},{5,13},{9,1},{13,5},{2,10},{6,14},... | collective-permute-start | bytes 202760 | tf_op jit(solution)/shard_map/ppermute | solution.py:563
  7.7 0.0 copy-done.1
  7.7 0.9 %copy-done.2 = bf16[128,512]{1,0:T(8,128)(2,1)S(1)} copy-done((bf16[128,512]{1,0:T(8,128)(2,1)S(1)}, bf16[128,512]{1,0:T(8,128)(2,1)}, u32[]{:S(2)}) %copy-start.2) | copy-done | bytes 131096
  8.6 0.4 %shard_map.95 = (bf16[512,128]{1,0:T(8,128)(2,1)S(1)}, f32[128,512]{1,0:T(8,128)S(1)}, f32[8,512]{1,0:T(8,128)S(1)}) custom-call(bf16[264,128]{1,0:T(8,128)(2,1)S(1)} %fusion.2.packet_ref.refs_11_.refs_0_, bf16[128,512]{1,0:T(8,128)(2,1)S(1)} %copy-done.1, bf16[128,512]{1,0:T(8,128)(2,1)S(1)} %copy-done.2, f32[8,512]{1,0:T(8,128)S(1)} %get-tuple-element.25.row_ref), custom_call_target="tpu_custom_call" | custom-call | tf_op jit(solution)/shard_map/pallas_call | solution.py:567
  9.0 0.1 collective-permute-done.refs_4_.refs_12_.refs_1_
  9.1 0.3 %shard_map.96 = (f32[128,512]{1,0:T(8,128)S(1)}, f32[128,512]{1,0:T(8,128)S(1)}, f32[8,512]{1,0:T(8,128)S(1)}, bf16[512,128]{1,0:T(8,128)(2,1)S(1)}, f32[8,128]{1,0:T(8,128)S(1)}) custom-call(bf16[512,128]{1,0:T(8,128)(2,1)S(1)} %get-tuple-element.24.refs_0_, bf16[512,128]{1,0:T(8,128)(2,1)S(1)} %get-tuple-element.26.refs_1_, ...), custom_call_target="tpu_custom_call" | custom-call | tf_op jit(solution)/shard_map/pallas_call | solution.py:576
  9.4 2.3 %collective-permute-done.1.refs_13_.refs_2_ = bf16[264,128]{1,0:T(8,128)(2,1)S(1)} collective-permute-done((bf16[264,128]{1,0:T(8,128)(2,1)S(1)}, bf16[264,128]{1,0:T(8,128)(2,1)S(1)}, u32[]{:S(2)}, u32[]{:S(2)}) %collective-permute-start.1) | collective-permute-done | bytes 67616 | tf_op jit(solution)/shard_map/ppermute | solution.py:563
  11.8 1.0 %shard_map.97 = (bf16[512,128]{1,0:T(8,128)(2,1)S(1)}, bf16[512,128]{1,0:T(8,128)(2,1)S(1)}, bf16[512,128]{1,0:T(8,128)(2,1)S(1)}, bf16[512,128]{1,0:T(8,128)(2,1)S(1)}) custom-call(bf16[512,128]{1,0:T(8,128)(2,1)S(1)} %get-tuple-element.24.refs_0_, bf16[512,128]{1,0:T(8,128)(2,1)S(1)} %get-tuple-element.26.refs_1_, f32[8,512]{1,0:T(8,128)S(1)} %get-tuple-element.29.refs_2_, ...), custom_call_target="tpu_custom_call" | custom-call | tf_op jit(solution)/shard_map/pallas_call | solution.py:588
  12.8 1.4 %collective-permute-start.2 = (bf16[512,128]{1,0:T(8,128)(2,1)S(1)}, bf16[512,128]{1,0:T(8,128)(2,1)S(1)}, u32[]{:S(2)}, u32[]{:S(2)}) collective-permute-start(bf16[512,128]{1,0:T(8,128)(2,1)S(1)} %get-tuple-element.39), channel_id=1, source_target_pairs={{0,12},{4,8},{8,4},{12,0},{1,13},{5,9},{9,5},{13,1},{2,14},{6,10},... | collective-permute-start | bytes 393224 | tf_op jit(solution)/shard_map/ppermute | solution.py:596
  14.2 0.4 %collective-permute-start.3 = (bf16[512,128]{1,0:T(8,128)(2,1)S(1)}, bf16[512,128]{1,0:T(8,128)(2,1)S(1)}, u32[]{:S(2)}, u32[]{:S(2)}) collective-permute-start(bf16[512,128]{1,0:T(8,128)(2,1)S(1)} %get-tuple-element.43), channel_id=1, source_target_pairs={{0,4},{4,12},{8,0},{12,8},{1,5},{5,13},{9,1},{13,9},{2,6},{6,14},{... | collective-permute-start | bytes 393224 | tf_op jit(solution)/shard_map/ppermute | solution.py:596
  14.6 2.5 %collective-permute-start.4 = (bf16[512,128]{1,0:T(8,128)(2,1)S(1)}, bf16[512,128]{1,0:T(8,128)(2,1)S(1)}, u32[]{:S(2)}, u32[]{:S(2)}) collective-permute-start(bf16[512,128]{1,0:T(8,128)(2,1)S(1)} %get-tuple-element.44), channel_id=1, source_target_pairs={{0,8},{4,0},{8,12},{12,4},{1,9},{5,1},{9,13},{13,5},{2,10},{6,2},{... | collective-permute-start | bytes 393224 | tf_op jit(solution)/shard_map/ppermute | solution.py:596
  17.1 3.9 %collective-permute-done.2._.refs_3_ = bf16[512,128]{1,0:T(8,128)(2,1)S(1)} collective-permute-done((bf16[512,128]{1,0:T(8,128)(2,1)S(1)}, bf16[512,128]{1,0:T(8,128)(2,1)S(1)}, u32[]{:S(2)}, u32[]{:S(2)}) %collective-permute-start.2) | collective-permute-done | bytes 131104 | tf_op jit(solution)/shard_map/ppermute | solution.py:596
  21.1 0.3 %shard_map.98 = (bf16[128,256]{1,0:T(8,128)(2,1)S(1)}, bf16[128,512]{1,0:T(8,128)(2,1)S(1)}) custom-call(bf16[512,128]{1,0:T(8,128)(2,1)S(1)} %collective-permute-done.2._.refs_3_, bf16[264,128]{1,0:T(8,128)(2,1)S(1)} %fusion.2.packet_ref.refs_11_.refs_0_, bf16[264,128]{1,0:T(8,128)(2,1)S(1)} %collective-permute-done.refs_4_.refs_12_.refs_1_, ...), custom_call_target="tpu_custom_call" | custom-call | tf_op jit(solution)/shard_map/pallas_call | solution.py:599
  21.4 4.6 %collective-permute-done.3.refs_1_ = bf16[512,128]{1,0:T(8,128)(2,1)S(1)} collective-permute-done((bf16[512,128]{1,0:T(8,128)(2,1)S(1)}, bf16[512,128]{1,0:T(8,128)(2,1)S(1)}, u32[]{:S(2)}, u32[]{:S(2)}) %collective-permute-start.3) | collective-permute-done | bytes 131104 | tf_op jit(solution)/shard_map/ppermute | solution.py:596
  25.9 0.0 collective-permute-done.4.refs_2_
  25.9 1.0 %shard_map.99 = (f32[128,512]{1,0:T(8,128)}, f32[128,128]{1,0:T(8,128)}, f32[128,128]{1,0:T(8,128)}) custom-call(bf16[128,256]{1,0:T(8,128)(2,1)S(1)} %get-tuple-element.40.query_spread, bf16[128,512]{1,0:T(8,128)(2,1)S(1)} %get-tuple-element.41.key_spread, bf16[512,128]{1,0:T(8,128)(2,1)S(1)} %get-tuple-element.42.refs_0_, ...), custom_call_target="tpu_custom_call" | custom-call | tf_op jit(solution)/shard_map/pallas_call | solution.py:609
  (3 shorter events, 0.0 us)
Async XLA Ops:
  0.6 4.1 %copy-start = (bf16[128,512]{1,0:T(8,128)(2,1)S(1)}, bf16[128,512]{1,0:T(8,128)(2,1)}, u32[]{:S(2)}) copy-start(bf16[128,512]{1,0:T(8,128)(2,1)} %query_ref.1) | copy-start | bytes 393220
  0.7 4.1 %copy-start.3 = (s32[16]{0:T(128)S(1)}, s32[16]{0:T(128)}, u32[]{:S(2)}) copy-start(s32[16]{0:T(128)} %param.7) | copy-start | bytes 196
  1.6 6.1 %copy-start.1 = (bf16[128,512]{1,0:T(8,128)(2,1)S(1)}, bf16[128,512]{1,0:T(8,128)(2,1)}, u32[]{:S(2)}) copy-start(bf16[128,512]{1,0:T(8,128)(2,1)} %grad_ref.1) | copy-start | bytes 393220
  1.6 7.5 %collective-permute-start = (bf16[264,128]{1,0:T(8,128)(2,1)S(1)}, bf16[264,128]{1,0:T(8,128)(2,1)S(1)}, u32[]{:S(2)}, u32[]{:S(2)}) collective-permute-start(bf16[264,128]{1,0:T(8,128)(2,1)S(1)} %fusion.2.packet_ref.refs_11_.refs_0_), channel_id=1, source_target_pairs={{0,4},{4,8},{8,12},{12,0},{1,5},{5,9},{9,13},{13,1},{2,6},{6,10},{... | collective-permute-start | bytes 202760 | tf_op jit(solution)/shard_map/ppermute | solution.py:554
  5.0 6.7 %collective-permute-start.1 = (bf16[264,128]{1,0:T(8,128)(2,1)S(1)}, bf16[264,128]{1,0:T(8,128)(2,1)S(1)}, u32[]{:S(2)}, u32[]{:S(2)}) collective-permute-start(bf16[264,128]{1,0:T(8,128)(2,1)S(1)} %get-tuple-element.38), channel_id=1, source_target_pairs={{0,8},{4,12},{8,0},{12,4},{1,9},{5,13},{9,1},{13,5},{2,10},{6,14},... | collective-permute-start | bytes 202760 | tf_op jit(solution)/shard_map/ppermute | solution.py:563
  7.7 0.9 %copy-start.2 = (bf16[128,512]{1,0:T(8,128)(2,1)S(1)}, bf16[128,512]{1,0:T(8,128)(2,1)}, u32[]{:S(2)}) copy-start(bf16[128,512]{1,0:T(8,128)(2,1)} %saved_ref.1) | copy-start | bytes 393220
  12.8 8.2 %collective-permute-start.2 = (bf16[512,128]{1,0:T(8,128)(2,1)S(1)}, bf16[512,128]{1,0:T(8,128)(2,1)S(1)}, u32[]{:S(2)}, u32[]{:S(2)}) collective-permute-start(bf16[512,128]{1,0:T(8,128)(2,1)S(1)} %get-tuple-element.39), channel_id=1, source_target_pairs={{0,12},{4,8},{8,4},{12,0},{1,13},{5,9},{9,5},{13,1},{2,14},{6,10},... | collective-permute-start | bytes 393224 | tf_op jit(solution)/shard_map/ppermute | solution.py:596
  14.2 11.7 %collective-permute-start.3 = (bf16[512,128]{1,0:T(8,128)(2,1)S(1)}, bf16[512,128]{1,0:T(8,128)(2,1)S(1)}, u32[]{:S(2)}, u32[]{:S(2)}) collective-permute-start(bf16[512,128]{1,0:T(8,128)(2,1)S(1)} %get-tuple-element.43), channel_id=1, source_target_pairs={{0,4},{4,12},{8,0},{12,8},{1,5},{5,13},{9,1},{13,9},{2,6},{6,14},{... | collective-permute-start | bytes 393224 | tf_op jit(solution)/shard_map/ppermute | solution.py:596
  14.6 11.3 %collective-permute-start.4 = (bf16[512,128]{1,0:T(8,128)(2,1)S(1)}, bf16[512,128]{1,0:T(8,128)(2,1)S(1)}, u32[]{:S(2)}, u32[]{:S(2)}) collective-permute-start(bf16[512,128]{1,0:T(8,128)(2,1)S(1)} %get-tuple-element.44), channel_id=1, source_target_pairs={{0,8},{4,0},{8,12},{12,4},{1,9},{5,1},{9,13},{13,5},{2,10},{6,2},{... | collective-permute-start | bytes 393224 | tf_op jit(solution)/shard_map/ppermute | solution.py:596

commit v17 on v9

--- a/solution.py
+++ b/solution.py
@@ -300,11 +300,12 @@
     index = lax.axis_index("ctx")
     lane = lax.broadcasted_iota(jnp.int32, (1, rows), 1)
     position = index * rows + lane
-    first = jnp.zeros((1, rows), jnp.int32)
-    end = jnp.int32(0)
-    for d in range(docs):
-        end = end + doc_ref[d]
-        first = jnp.where(end <= position, end, first)
+    earlier = lax.broadcasted_iota(jnp.int32, (docs, docs), 1) <= lax.broadcasted_iota(
+        jnp.int32, (docs, docs), 0
+    )
+    lengths = doc_ref[...].astype(jnp.float32)
+    ends = jnp.sum(jnp.where(earlier, lengths, 0.0), axis=1, keepdims=True).astype(jnp.int32)
+    first = jnp.max(jnp.where(ends <= position, ends, 0), axis=0, keepdims=True)
     key_position = index * rows + lax.broadcasted_iota(jnp.int32, (rows, rows), 0)
     allowed = (key_position >= first) & (key_position <= position)
     allowed = jnp.concatenate([allowed] * heads, axis=1)
@@ -380,6 +381,16 @@
 
 
 def attend_kernel(count, halo, *refs):
+    index = lax.axis_index("ctx")
+    for blocks in range(1, halo + 2):
+        here = index == blocks - 1 if blocks <= halo else index >= halo
+
+        @pl.when(here)
+        def _(blocks=blocks):
+            attend(count, halo, blocks, refs)
+
+
+def attend(count, halo, blocks, refs):
     query_ref, grad_ref, row_ref, filled_ref, spread_ref = refs[:5]
     raised_refs = refs[5 : 5 + halo]
     change_refs = refs[5 + halo : 5 + 2 * halo]
@@ -393,21 +404,24 @@
     scale = 1.0 / math.sqrt(depth)
     queries = query_ref[...]
     grads = grad_ref[...]
-    raised, change, (_, total, factors), target, _ = fold(
-        count, halo, packets[halo], queries, grads, row_ref, filled_ref
-    )
+    raised = [ref[...] for ref in raised_refs[:blocks]]
+    change = [ref[...] for ref in change_refs[:blocks]]
+    targets = [ref[...] for ref in target_refs[:blocks]]
+    total = row_ref[2:3, :]
+    factors = row_ref[4:8, :]
+    if blocks > halo:
+        raised_far, change_far, (_, total, factors), target_far, _ = fold(
+            count, halo, packets[halo], queries, grads, row_ref, filled_ref
+        )
+        raised.append(raised_far)
+        change.append(change_far)
+        targets.append(target_far)
     factors = factors * (1.0 / total)
-    weights = []
-    changes = []
-    for block in range(halo + 1):
-        mine = raised if block == halo else raised_refs[block][...]
-        mine = mine * factors[block : block + 1, :]
-        weights.append(mine.astype(jnp.bfloat16))
-        mine = mine * (change if block == halo else change_refs[block][...])
-        changes.append(mine.astype(jnp.bfloat16))
-    weights = jnp.concatenate(weights, axis=0)
-    changes = jnp.concatenate(changes, axis=0)
-    keys = jnp.concatenate([packet[0:rows, :] for packet in packets], axis=0)
+    weights = [raised[n] * factors[n : n + 1, :] for n in range(blocks)]
+    changes = [weights[n] * change[n] for n in range(blocks)]
+    weights = jnp.concatenate([part.astype(jnp.bfloat16) for part in weights], axis=0)
+    changes = jnp.concatenate([part.astype(jnp.bfloat16) for part in changes], axis=0)
+    keys = jnp.concatenate([packet[0:rows, :] for packet in packets[:blocks]], axis=0)
     query_grad = (contract(keys, changes, 0, 0) * scale).astype(jnp.bfloat16)
     key_parts = contract(changes, queries, 1, 0) * scale
     value_parts = contract(weights, grads, 1, 0)
@@ -415,8 +429,7 @@
 
     query_slots = contract(spread_ref[...], end_to_end(query_grad, heads), 1, 1)
     query_slots = query_slots.astype(jnp.bfloat16)
-    spread = jnp.concatenate([ref[...] for ref in target_refs] + [target], axis=1)
-    part_slots = contract(spread, parts, 1, 0).astype(jnp.bfloat16)
+    part_slots = contract(jnp.concatenate(targets, axis=1), parts, 1, 0).astype(jnp.bfloat16)
     at = heads * slot
     for k in range(count):
         out = outs[k]
@@ -534,10 +547,10 @@
         out_shape=[jax.ShapeDtypeStruct((columns, depth), bf16)] * 2
         + block_shapes
         + [row_shape, jax.ShapeDtypeStruct((count * slot, rows), bf16), target_shape, filled_shape],
-        in_specs=[pl.BlockSpec(memory_space=pltpu.SMEM)] + [whole] * 4,
+        in_specs=[whole] * 5,
         out_specs=[whole] * 8,
         compiler_params=params,
-    )(doc_lengths, packet, queries, grad_out, forward_out)
+    )(doc_lengths.reshape(1, -1), packet, queries, grad_out, forward_out)
     raised, change, target = [raised], [change], [target]
     for back in range(1, halo):
         found = pl.pallas_call(

time: 25.5 us -> 25.1 us (0.984)
  Pallas kernels: 3.67 us -> 2.65 us
  waiting for transfers between devices: 8.01 us -> 8.7 us
    ppermute x2, waiting for transfers between devices: 1.29 us -> 1.83 us  [near_plan(): lax.ppermute(packet, 'ctx', [(i, (i + back) % count) for i in range(count)])]
    pallas_call x1, Pallas kernels: 1 us -> 0.47 us  [near_plan(): pl.pallas_call(functools.partial(own_kernel, count, doc_lengths.shape[0])...]
    pallas_call x1, Pallas kernels: 1.04 us -> 0.55 us  [near_plan(): pl.pallas_call(functools.partial(attend_kernel, count, halo), out_shape=[...]
  transfers between devices with their start and end apart: 5 -> 5, of which waited for: 3 -> 3; matrix products, arithmetic and copies ran while one was open for 0% -> 0% of each run, Pallas kernels for 6% -> 4%
where the time goes in v17:
time: 25.1 us; the launch traced here: 24.9 us
  starting transfers between devices  10.1 us (40%)
  waiting for transfers between devices  8.7 us (35%)
  Pallas kernels  2.65 us (11%)
  local copies, waits for them, and re-layouts  1.82 us (7%)
  other arithmetic  0.96 us (4%)
  between operations  0.7 us (3%)
    ppermute x3, waiting for transfers between devices, near_plan(): lax.ppermute(sent[k], 'ctx', [(i, i ^ k) for i in range(count)])  6.87 us
    ppermute x2, starting transfers between devices, near_plan(): lax.ppermute(packet, 'ctx', [(i, (i + back) % count) for i in range(count)])  5.67 us
    ppermute x3, starting transfers between devices, near_plan(): lax.ppermute(sent[k], 'ctx', [(i, i ^ k) for i in range(count)])  4.45 us
    ppermute x2, waiting for transfers between devices, near_plan(): lax.ppermute(packet, 'ctx', [(i, (i + back) % count) for i in range(count)])  1.83 us
    unnamed x8, local copies, waits for them, and re-layouts  1.82 us
    pallas_call x1, Pallas kernels, near_plan(): pl.pallas_call(functools.partial(place_kernel, count), out_shape=[jax.Sha...  1 us
    select_n x1, other arithmetic, near_plan(): jnp.where(mark < 0, jnp.pad(jnp.concatenate([key_head_rows, value_head_ro...  0.94 us
    pallas_call x1, Pallas kernels, near_plan(): pl.pallas_call(functools.partial(attend_kernel, count, halo), out_shape=[...  0.55 us
  transfers between devices with their start and end apart: 5, of which 3 were waited for; matrix products, arithmetic and copies ran while one was open for 0% of the time, Pallas kernels for 4%

profile of v17, /device:TPU:0, one launch (start us, length us, event | category | flops | bytes accessed | tf_op | source)
XLA Modules:
  0.0 24.9 jit_solution(14438928404877952770)
XLA Ops:
  0.6 0.0 copy-start
  0.7 0.9 %fusion.2.packet_ref.refs_11_.refs_0_ = bf16[264,128]{1,0:T(8,128)(2,1)S(1)} fusion(bf16[128,128]{1,0:T(8,128)(2,1)} %param.11, bf16[128,128]{1,0:T(8,128)(2,1)} %param.10, s32[128]{0:T(128)} %param.8, s32[264]{0:T(512)S(1)} %iota_add_fusion, pred[264]{0:T(512)(128)(4,1)S(1)} %broadcast_compare_fusion), kind=kLoop, calls=%fused_computation.4 | loop fusion | flops 337920 | bytes 134952 | tf_op jit(solution)/shard_map/jit(_where)/select_n | solution.py:532
  1.6 0.0 copy-start.3
  1.6 3.1 %collective-permute-start = (bf16[264,128]{1,0:T(8,128)(2,1)S(1)}, bf16[264,128]{1,0:T(8,128)(2,1)S(1)}, u32[]{:S(2)}, u32[]{:S(2)}) collective-permute-start(bf16[264,128]{1,0:T(8,128)(2,1)S(1)} %fusion.2.packet_ref.refs_11_.refs_0_), channel_id=1, source_target_pairs={{0,4},{4,8},{8,12},{12,0},{1,5},{5,9},{9,13},{13,1},{2,6},{6,10},{... | collective-permute-start | bytes 202760 | tf_op jit(solution)/shard_map/ppermute | solution.py:538
  4.7 2.6 %collective-permute-start.1 = (bf16[264,128]{1,0:T(8,128)(2,1)S(1)}, bf16[264,128]{1,0:T(8,128)(2,1)S(1)}, u32[]{:S(2)}, u32[]{:S(2)}) collective-permute-start(bf16[264,128]{1,0:T(8,128)(2,1)S(1)} %fusion.2.packet_ref.refs_11_.refs_0_), channel_id=1, source_target_pairs={{0,8},{4,12},{8,0},{12,4},{1,9},{5,13},{9,1},{13,5},{2,10},{6,14},... | collective-permute-start | bytes 202760 | tf_op jit(solution)/shard_map/ppermute | solution.py:538
  7.3 0.0 copy-done
  7.3 0.0 copy-done.3
  7.3 0.0 copy-start.1
  7.3 0.9 %copy-done.1 = bf16[128,512]{1,0:T(8,128)(2,1)S(1)} copy-done((bf16[128,512]{1,0:T(8,128)(2,1)S(1)}, bf16[128,512]{1,0:T(8,128)(2,1)}, u32[]{:S(2)}) %copy-start.1) | copy-done | bytes 131096
  8.2 0.0 copy-start.2
  8.2 0.9 %copy-done.2 = bf16[128,512]{1,0:T(8,128)(2,1)S(1)} copy-done((bf16[128,512]{1,0:T(8,128)(2,1)S(1)}, bf16[128,512]{1,0:T(8,128)(2,1)}, u32[]{:S(2)}) %copy-start.2) | copy-done | bytes 131096
  9.1 0.5 %shard_map.94 = (bf16[512,128]{1,0:T(8,128)(2,1)S(1)}, bf16[512,128]{1,0:T(8,128)(2,1)S(1)}, f32[128,512]{1,0:T(8,128)S(1)}, f32[128,512]{1,0:T(8,128)S(1)}, f32...) custom-call(s32[1,16]{1,0:T(1,128)S(1)} %bitcast.1, ...), custom_call_target="tpu_custom_call" | custom-call | tf_op jit(solution)/shard_map/pallas_call | solution.py:545
  9.6 0.0 collective-permute-done.refs_4_.refs_12_.refs_1_
  9.6 0.3 %shard_map.95 = (f32[128,512]{1,0:T(8,128)S(1)}, f32[128,512]{1,0:T(8,128)S(1)}, f32[8,512]{1,0:T(8,128)S(1)}, bf16[512,128]{1,0:T(8,128)(2,1)S(1)}, f32[8,128]{1,0:T(8,128)S(1)}) custom-call(bf16[512,128]{1,0:T(8,128)(2,1)S(1)} %get-tuple-element.22.refs_0_, bf16[512,128]{1,0:T(8,128)(2,1)S(1)} %get-tuple-element.23.refs_1_, ...), custom_call_target="tpu_custom_call" | custom-call | tf_op jit(solution)/shard_map/pallas_call | solution.py:556
  9.9 1.8 %collective-permute-done.1.refs_13_.refs_2_ = bf16[264,128]{1,0:T(8,128)(2,1)S(1)} collective-permute-done((bf16[264,128]{1,0:T(8,128)(2,1)S(1)}, bf16[264,128]{1,0:T(8,128)(2,1)S(1)}, u32[]{:S(2)}, u32[]{:S(2)}) %collective-permute-start.1) | collective-permute-done | bytes 67616 | tf_op jit(solution)/shard_map/ppermute | solution.py:538
  11.8 0.5 %shard_map.96 = (bf16[512,128]{1,0:T(8,128)(2,1)S(1)}, bf16[512,128]{1,0:T(8,128)(2,1)S(1)}, bf16[512,128]{1,0:T(8,128)(2,1)S(1)}, bf16[512,128]{1,0:T(8,128)(2,1)S(1)}) custom-call(bf16[512,128]{1,0:T(8,128)(2,1)S(1)} %get-tuple-element.22.refs_0_, bf16[512,128]{1,0:T(8,128)(2,1)S(1)} %get-tuple-element.23.refs_1_, f32[8,512]{1,0:T(8,128)S(1)} %get-tuple-element.26.refs_2_, ...), custom_call_target="tpu_custom_call" | custom-call | tf_op jit(solution)/shard_map/pallas_call | solution.py:568
  12.3 2.6 %collective-permute-start.2 = (bf16[512,128]{1,0:T(8,128)(2,1)S(1)}, bf16[512,128]{1,0:T(8,128)(2,1)S(1)}, u32[]{:S(2)}, u32[]{:S(2)}) collective-permute-start(bf16[512,128]{1,0:T(8,128)(2,1)S(1)} %get-tuple-element.35), channel_id=1, source_target_pairs={{0,12},{4,8},{8,4},{12,0},{1,13},{5,9},{9,5},{13,1},{2,14},{6,10},... | collective-permute-start | bytes 393224 | tf_op jit(solution)/shard_map/ppermute | solution.py:576
  14.9 0.0 collective-permute-start.3
  14.9 1.9 %collective-permute-start.4 = (bf16[512,128]{1,0:T(8,128)(2,1)S(1)}, bf16[512,128]{1,0:T(8,128)(2,1)S(1)}, u32[]{:S(2)}, u32[]{:S(2)}) collective-permute-start(bf16[512,128]{1,0:T(8,128)(2,1)S(1)} %get-tuple-element.40), channel_id=1, source_target_pairs={{0,8},{4,12},{8,0},{12,4},{1,9},{5,13},{9,1},{13,5},{2,10},{6,14},... | collective-permute-start | bytes 393224 | tf_op jit(solution)/shard_map/ppermute | solution.py:576
  16.8 3.9 %collective-permute-done.2._.refs_3_ = bf16[512,128]{1,0:T(8,128)(2,1)S(1)} collective-permute-done((bf16[512,128]{1,0:T(8,128)(2,1)S(1)}, bf16[512,128]{1,0:T(8,128)(2,1)S(1)}, u32[]{:S(2)}, u32[]{:S(2)}) %collective-permute-start.2) | collective-permute-done | bytes 131104 | tf_op jit(solution)/shard_map/ppermute | solution.py:576
  20.6 0.3 %shard_map.97 = (bf16[128,256]{1,0:T(8,128)(2,1)S(1)}, bf16[128,512]{1,0:T(8,128)(2,1)S(1)}) custom-call(bf16[512,128]{1,0:T(8,128)(2,1)S(1)} %collective-permute-done.2._.refs_3_, bf16[264,128]{1,0:T(8,128)(2,1)S(1)} %fusion.2.packet_ref.refs_11_.refs_0_, bf16[264,128]{1,0:T(8,128)(2,1)S(1)} %collective-permute-done.refs_4_.refs_12_.refs_1_, ...), custom_call_target="tpu_custom_call" | custom-call | tf_op jit(solution)/shard_map/pallas_call | solution.py:578
  20.9 3.0 %collective-permute-done.3.refs_1_ = bf16[512,128]{1,0:T(8,128)(2,1)S(1)} collective-permute-done((bf16[512,128]{1,0:T(8,128)(2,1)S(1)}, bf16[512,128]{1,0:T(8,128)(2,1)S(1)}, u32[]{:S(2)}, u32[]{:S(2)}) %collective-permute-start.3) | collective-permute-done | bytes 131104 | tf_op jit(solution)/shard_map/ppermute | solution.py:576
  23.9 0.0 collective-permute-done.4.refs_2_
  23.9 1.0 %shard_map.98 = (f32[128,512]{1,0:T(8,128)}, f32[128,128]{1,0:T(8,128)}, f32[128,128]{1,0:T(8,128)}) custom-call(bf16[128,256]{1,0:T(8,128)(2,1)S(1)} %get-tuple-element.36.query_spread, bf16[128,512]{1,0:T(8,128)(2,1)S(1)} %get-tuple-element.37.key_spread, bf16[512,128]{1,0:T(8,128)(2,1)S(1)} %get-tuple-element.38.refs_0_, ...), custom_call_target="tpu_custom_call" | custom-call | tf_op jit(solution)/shard_map/pallas_call | solution.py:588
  (2 shorter events, 0.0 us)
Async XLA Ops:
  0.6 6.7 %copy-start = (bf16[128,512]{1,0:T(8,128)(2,1)S(1)}, bf16[128,512]{1,0:T(8,128)(2,1)}, u32[]{:S(2)}) copy-start(bf16[128,512]{1,0:T(8,128)(2,1)} %query_ref.1) | copy-start | bytes 393220
  1.6 5.7 %copy-start.3 = (s32[16]{0:T(128)S(1)}, s32[16]{0:T(128)}, u32[]{:S(2)}) copy-start(s32[16]{0:T(128)} %param.7) | copy-start | bytes 196
  1.6 8.0 %collective-permute-start = (bf16[264,128]{1,0:T(8,128)(2,1)S(1)}, bf16[264,128]{1,0:T(8,128)(2,1)S(1)}, u32[]{:S(2)}, u32[]{:S(2)}) collective-permute-start(bf16[264,128]{1,0:T(8,128)(2,1)S(1)} %fusion.2.packet_ref.refs_11_.refs_0_), channel_id=1, source_target_pairs={{0,4},{4,8},{8,12},{12,0},{1,5},{5,9},{9,13},{13,1},{2,6},{6,10},{... | collective-permute-start | bytes 202760 | tf_op jit(solution)/shard_map/ppermute | solution.py:538
  4.7 7.1 %collective-permute-start.1 = (bf16[264,128]{1,0:T(8,128)(2,1)S(1)}, bf16[264,128]{1,0:T(8,128)(2,1)S(1)}, u32[]{:S(2)}, u32[]{:S(2)}) collective-permute-start(bf16[264,128]{1,0:T(8,128)(2,1)S(1)} %fusion.2.packet_ref.refs_11_.refs_0_), channel_id=1, source_target_pairs={{0,8},{4,12},{8,0},{12,4},{1,9},{5,13},{9,1},{13,5},{2,10},{6,14},... | collective-permute-start | bytes 202760 | tf_op jit(solution)/shard_map/ppermute | solution.py:538
  7.3 0.9 %copy-start.1 = (bf16[128,512]{1,0:T(8,128)(2,1)S(1)}, bf16[128,512]{1,0:T(8,128)(2,1)}, u32[]{:S(2)}) copy-start(bf16[128,512]{1,0:T(8,128)(2,1)} %grad_ref.1) | copy-start | bytes 393220
  8.2 0.9 %copy-start.2 = (bf16[128,512]{1,0:T(8,128)(2,1)S(1)}, bf16[128,512]{1,0:T(8,128)(2,1)}, u32[]{:S(2)}) copy-start(bf16[128,512]{1,0:T(8,128)(2,1)} %saved_ref.1) | copy-start | bytes 393220
  12.3 8.3 %collective-permute-start.2 = (bf16[512,128]{1,0:T(8,128)(2,1)S(1)}, bf16[512,128]{1,0:T(8,128)(2,1)S(1)}, u32[]{:S(2)}, u32[]{:S(2)}) collective-permute-start(bf16[512,128]{1,0:T(8,128)(2,1)S(1)} %get-tuple-element.35), channel_id=1, source_target_pairs={{0,12},{4,8},{8,4},{12,0},{1,13},{5,9},{9,5},{13,1},{2,14},{6,10},... | collective-permute-start | bytes 393224 | tf_op jit(solution)/shard_map/ppermute | solution.py:576
  14.9 9.1 %collective-permute-start.3 = (bf16[512,128]{1,0:T(8,128)(2,1)S(1)}, bf16[512,128]{1,0:T(8,128)(2,1)S(1)}, u32[]{:S(2)}, u32[]{:S(2)}) collective-permute-start(bf16[512,128]{1,0:T(8,128)(2,1)S(1)} %get-tuple-element.39), channel_id=1, source_target_pairs={{0,4},{4,0},{8,12},{12,8},{1,5},{5,1},{9,13},{13,9},{2,6},{6,2},{1... | collective-permute-start | bytes 393224 | tf_op jit(solution)/shard_map/ppermute | solution.py:576
  14.9 9.1 %collective-permute-start.4 = (bf16[512,128]{1,0:T(8,128)(2,1)S(1)}, bf16[512,128]{1,0:T(8,128)(2,1)S(1)}, u32[]{:S(2)}, u32[]{:S(2)}) collective-permute-start(bf16[512,128]{1,0:T(8,128)(2,1)S(1)} %get-tuple-element.40), channel_id=1, source_target_pairs={{0,8},{4,12},{8,0},{12,4},{1,9},{5,13},{9,1},{13,5},{2,10},{6,14},... | collective-permute-start | bytes 393224 | tf_op jit(solution)/shard_map/ppermute | solution.py:576

commit v18 on v17

--- a/solution.py
+++ b/solution.py
@@ -364,7 +364,7 @@
 
 def step_kernel(count, back, *refs):
     query_ref, grad_ref, row_ref, filled_ref, packet_ref = refs[:5]
-    raised_out, change_out, row_out, target_out, filled_out = refs[5:]
+    raised_out, change_out, row_out, target_out, filled_out, given_out = refs[5:]
     raised, change, (top, total, factors), target, filled = fold(
         count, back, packet_ref, query_ref[...], grad_ref[...], row_ref, filled_ref
     )
@@ -378,10 +378,21 @@
     target_out[...] = target
     filled_out[0:count, :] = filled
     filled_out[count:, :] = jnp.zeros_like(filled_out[count:, :])
-
-
-def attend_kernel(count, halo, *refs):
+    rows = packet_ref.shape[1]
+    hot = packet_ref[2 * rows : 2 * rows + count, :].astype(jnp.float32)
+    given_out[0:count, :] = jnp.broadcast_to(jnp.sum(hot, axis=1, keepdims=True), (count, rows))
+    given_out[count:, :] = jnp.zeros_like(given_out[count:, :])
+
+
+def attend_kernel(count, halo, given_ref, *refs):
     index = lax.axis_index("ctx")
+    last = refs[-1]
+    given = jnp.zeros((1, last.shape[1]), jnp.float32)
+    for p in range(count):
+        given = jnp.where((index ^ (count - 1)) == p, given_ref[p : p + 1, 0 : last.shape[1]], given)
+    last[last.shape[0] - META :, :] = jnp.broadcast_to(given, (META, last.shape[1])).astype(
+        jnp.bfloat16
+    )
     for blocks in range(1, halo + 2):
         here = index == blocks - 1 if blocks <= halo else index >= halo
 
@@ -443,11 +454,12 @@
             ]
 
 
-def order_kernel(count, halo, _, *refs):
+def order_kernel(count, halo, last_ref, *refs):
     packets = refs[: 1 + halo]
     query_out, key_out = refs[1 + halo :]
     rows = query_out.shape[0]
     index = lax.axis_index("ctx")
+    giver = [index, lax.rem(index + count - 1, count)]
     given = []
     for ref in packets:
         hot = ref[2 * rows : 2 * rows + count, :].astype(jnp.float32)
@@ -456,9 +468,14 @@
         for p in range(count):
             mine = jnp.where(index == p, counts[p : p + 1, :], mine)
         given.append(mine.astype(jnp.int32))
-    if len(given) < count:
+    if count == 4:
+        at = last_ref.shape[0] - META
+        told = last_ref[at : at + 1, 0:1].astype(jnp.float32).astype(jnp.int32)
+        even = lax.rem(index, 2) == 0
+        given[2] = jnp.where(even, told, given[2])
+        giver.append(jnp.where(even, lax.rem((index ^ 3) + 3, 4), jnp.where(index == 1, 2, 1)))
         given.append(rows - sum(given))
-    giver = [lax.rem(index - d + count, count) for d in range(count)]
+        giver.append(6 - sum(giver))
 
     def placement(size, halo):
         lane = lax.broadcasted_iota(jnp.int32, (1, count * size), 1)
@@ -535,8 +552,14 @@
         (owners[None, :] == mark).astype(bf16),
     )
     near = [
-        lax.ppermute(packet, "ctx", [(i, (i + back) % count) for i in range(count)])
-        for back in range(1, halo + 1)
+        lax.ppermute(packet, "ctx", [(i, (i + 1) % count) for i in range(count)])
+    ] + [
+        lax.ppermute(
+            packet,
+            "ctx",
+            [(i, i + back if i + back < count else count - 1 - i) for i in range(count)],
+        )
+        for back in range(2, halo + 1)
     ]
     block_shapes = [jax.ShapeDtypeStruct((rows, columns), f32)] * 2
     row_shape = jax.ShapeDtypeStruct((8, columns), f32)
@@ -551,27 +574,32 @@
         out_specs=[whole] * 8,
         compiler_params=params,
     )(doc_lengths.reshape(1, -1), packet, queries, grad_out, forward_out)
-    raised, change, target = [raised], [change], [target]
+    raised, change, target, given = [raised], [change], [target], filled
     for back in range(1, halo):
         found = pl.pallas_call(
             functools.partial(step_kernel, count, back),
-            out_shape=block_shapes + [row_shape, target_shape, filled_shape],
+            out_shape=block_shapes + [row_shape, target_shape, filled_shape, filled_shape],
             in_specs=[whole] * 5,
-            out_specs=[whole] * 5,
+            out_specs=[whole] * 6,
             compiler_params=params,
         )(query_rows, grad_rows, row, filled, near[back - 1])
         raised.append(found[0])
         change.append(found[1])
         row = found[2]
         target.append(found[3])
-        filled = found[4]
+        filled, given = found[4:]
     sent = pl.pallas_call(
         functools.partial(attend_kernel, count, halo),
-        out_shape=[jax.ShapeDtypeStruct((heads * slot + 2 * rows, depth), bf16)] * count,
-        in_specs=[whole] * (6 + 4 * halo),
+        out_shape=[
+            jax.ShapeDtypeStruct(
+                (heads * slot + 2 * rows + (META if k == count - 1 else 0), depth), bf16
+            )
+            for k in range(count)
+        ],
+        in_specs=[whole] * (7 + 4 * halo),
         out_specs=[whole] * count,
         compiler_params=params,
-    )(query_rows, grad_rows, row, filled, spread, *raised, *change, *target, packet, *near)
+    )(given, query_rows, grad_rows, row, filled, spread, *raised, *change, *target, packet, *near)
     received = [sent[0]] + [
         lax.ppermute(sent[k], "ctx", [(i, i ^ k) for i in range(count)]) for k in range(1, count)
     ]
@@ -581,7 +609,7 @@
             jax.ShapeDtypeStruct((rows, count * slot), bf16),
             jax.ShapeDtypeStruct((rows, count * rows), bf16),
         ],
-        in_specs=[pl.BlockSpec(memory_space=pl.ANY)] + [whole] * (1 + halo),
+        in_specs=[whole] * (2 + halo),
         out_specs=[whole] * 2,
         compiler_params=params,
     )(received[-1], packet, *near)

time: 25.1 us -> 27.1 us (1.080)
  waiting for transfers between devices: 8.7 us -> 10.7 us
    ppermute x3, waiting for transfers between devices: 6.87 us -> 9.78 us  [near_plan(): lax.ppermute(sent[k], 'ctx', [(i, i ^ k) for i in range(count)])]
    ppermute x2, waiting for transfers between devices: 1.83 us -> 0.92 us  [the longest x1 0.92 us: near_plan(): lax.ppermute(packet, 'ctx', [(i, i + back if i + back < count else count...]
  transfers between devices with their start and end apart: 5 -> 5, of which waited for: 3 -> 4; matrix products, arithmetic and copies ran while one was open for 0% -> 0% of each run, Pallas kernels for 4% -> 4%
where the time goes in v18:
time: 27.1 us; the launch traced here: 26.9 us
  waiting for transfers between devices  10.7 us (39%)
  starting transfers between devices  10.1 us (37%)
  Pallas kernels  2.65 us (10%)
  local copies, waits for them, and re-layouts  1.82 us (7%)
  other arithmetic  0.96 us (4%)
  between operations  0.7 us (3%)
    ppermute x3, waiting for transfers between devices, near_plan(): lax.ppermute(sent[k], 'ctx', [(i, i ^ k) for i in range(count)])  9.78 us
    ppermute x3, starting transfers between devices, near_plan(): lax.ppermute(sent[k], 'ctx', [(i, i ^ k) for i in range(count)])  4.45 us
    ppermute x1, starting transfers between devices, near_plan(): lax.ppermute(packet, 'ctx', [(i, (i + 1) % count) for i in range(count)])  3.08 us
    ppermute x1, starting transfers between devices, near_plan(): lax.ppermute(packet, 'ctx', [(i, i + back if i + back < count else count...  2.59 us
    unnamed x8, local copies, waits for them, and re-layouts  1.82 us
    pallas_call x1, Pallas kernels, near_plan(): pl.pallas_call(functools.partial(place_kernel, count), out_shape=[jax.Sha...  1 us
    select_n x1, other arithmetic, near_plan(): jnp.where(mark < 0, jnp.pad(jnp.concatenate([key_head_rows, value_head_ro...  0.94 us
    ppermute x1, waiting for transfers between devices, near_plan(): lax.ppermute(packet, 'ctx', [(i, i + back if i + back < count else count...  0.92 us
  transfers between devices with their start and end apart: 5, of which 4 were waited for; matrix products, arithmetic and copies ran while one was open for 0% of the time, Pallas kernels for 4%

profile of v18, /device:TPU:0, one launch (start us, length us, event | category | flops | bytes accessed | tf_op | source)
XLA Modules:
  0.0 26.9 jit_solution(7174066005113338398)
XLA Ops:
  0.6 0.0 copy-start
  0.7 0.9 %fusion.2.packet_ref.refs_11_.refs_0_ = bf16[264,128]{1,0:T(8,128)(2,1)S(1)} fusion(bf16[128,128]{1,0:T(8,128)(2,1)} %param.11, bf16[128,128]{1,0:T(8,128)(2,1)} %param.10, s32[128]{0:T(128)} %param.8, s32[264]{0:T(512)S(1)} %iota_add_fusion, pred[264]{0:T(512)(128)(4,1)S(1)} %broadcast_compare_fusion), kind=kLoop, calls=%fused_computation.4 | loop fusion | flops 337920 | bytes 134952 | tf_op jit(solution)/shard_map/jit(_where)/select_n | solution.py:549
  1.6 0.0 copy-start.3
  1.6 3.1 %collective-permute-start = (bf16[264,128]{1,0:T(8,128)(2,1)S(1)}, bf16[264,128]{1,0:T(8,128)(2,1)S(1)}, u32[]{:S(2)}, u32[]{:S(2)}) collective-permute-start(bf16[264,128]{1,0:T(8,128)(2,1)S(1)} %fusion.2.packet_ref.refs_11_.refs_0_), channel_id=1, source_target_pairs={{0,4},{4,8},{8,12},{12,0},{1,5},{5,9},{9,13},{13,1},{2,6},{6,10},{... | collective-permute-start | bytes 202760 | tf_op jit(solution)/shard_map/ppermute | solution.py:555
  4.7 2.6 %collective-permute-start.1 = (bf16[264,128]{1,0:T(8,128)(2,1)S(1)}, bf16[264,128]{1,0:T(8,128)(2,1)S(1)}, u32[]{:S(2)}, u32[]{:S(2)}) collective-permute-start(bf16[264,128]{1,0:T(8,128)(2,1)S(1)} %fusion.2.packet_ref.refs_11_.refs_0_), channel_id=1, source_target_pairs={{0,8},{4,12},{8,4},{12,0},{1,9},{5,13},{9,5},{13,1},{2,10},{6,14},... | collective-permute-start | bytes 202760 | tf_op jit(solution)/shard_map/ppermute | solution.py:557
  7.3 0.0 copy-done
  7.3 0.0 copy-done.3
  7.3 0.0 copy-start.1
  7.3 0.9 %copy-done.1 = bf16[128,512]{1,0:T(8,128)(2,1)S(1)} copy-done((bf16[128,512]{1,0:T(8,128)(2,1)S(1)}, bf16[128,512]{1,0:T(8,128)(2,1)}, u32[]{:S(2)}) %copy-start.1) | copy-done | bytes 131096
  8.2 0.0 copy-start.2
  8.2 0.9 %copy-done.2 = bf16[128,512]{1,0:T(8,128)(2,1)S(1)} copy-done((bf16[128,512]{1,0:T(8,128)(2,1)S(1)}, bf16[128,512]{1,0:T(8,128)(2,1)}, u32[]{:S(2)}) %copy-start.2) | copy-done | bytes 131096
  9.1 0.5 %shard_map.94 = (bf16[512,128]{1,0:T(8,128)(2,1)S(1)}, bf16[512,128]{1,0:T(8,128)(2,1)S(1)}, f32[128,512]{1,0:T(8,128)S(1)}, f32[128,512]{1,0:T(8,128)S(1)}, f32...) custom-call(s32[1,16]{1,0:T(1,128)S(1)} %bitcast.1, ...), custom_call_target="tpu_custom_call" | custom-call | tf_op jit(solution)/shard_map/pallas_call | solution.py:568
  9.6 0.0 collective-permute-done.refs_4_.refs_12_.refs_1_
  9.6 0.3 %shard_map.95 = (f32[128,512]{1,0:T(8,128)S(1)}, f32[128,512]{1,0:T(8,128)S(1)}, f32[8,512]{1,0:T(8,128)S(1)}, bf16[512,128]{1,0:T(8,128)(2,1)S(1)}, f32[8,128]{1,0:T(8,128)S(1)}, /*index=5*/f32[8,128]{1,0:T(8,128)S(1)}) custom-call(bf16[512,128]{1,0:T(8,128)(2,1)S(1)} %get-tuple-element.23.refs_0_, bf16[512,128]{1,0:T(8,128)(2,1)S(1)} %get-tuple-element.24.refs_1_, ...), custom_call_target="tpu_custom_call" | custom-call | tf_op jit(solution)/shard_map/pallas_call | solution.py:579
  9.9 0.9 %collective-permute-done.1.refs_13_.refs_2_ = bf16[264,128]{1,0:T(8,128)(2,1)S(1)} collective-permute-done((bf16[264,128]{1,0:T(8,128)(2,1)S(1)}, bf16[264,128]{1,0:T(8,128)(2,1)S(1)}, u32[]{:S(2)}, u32[]{:S(2)}) %collective-permute-start.1) | collective-permute-done | bytes 67616 | tf_op jit(solution)/shard_map/ppermute | solution.py:557
  10.8 0.6 %shard_map.96 = (bf16[512,128]{1,0:T(8,128)(2,1)S(1)}, bf16[512,128]{1,0:T(8,128)(2,1)S(1)}, bf16[512,128]{1,0:T(8,128)(2,1)S(1)}, bf16[520,128]{1,0:T(8,128)(2,1)S(1)}) custom-call(f32[8,128]{1,0:T(8,128)S(1)} %get-tuple-element.27.given_ref, bf16[512,128]{1,0:T(8,128)(2,1)S(1)} %get-tuple-element.23.refs_0_, ...), custom_call_target="tpu_custom_call" | custom-call | tf_op jit(solution)/shard_map/pallas_call | solution.py:591
  11.4 3.5 %collective-permute-start.2 = (bf16[520,128]{1,0:T(8,128)(2,1)S(1)}, bf16[520,128]{1,0:T(8,128)(2,1)S(1)}, u32[]{:S(2)}, u32[]{:S(2)}) collective-permute-start(bf16[520,128]{1,0:T(8,128)(2,1)S(1)} %get-tuple-element.37), channel_id=1, source_target_pairs={{0,12},{4,8},{8,4},{12,0},{1,13},{5,9},{9,5},{13,1},{2,14},{6,10},... | collective-permute-start | bytes 399368 | tf_op jit(solution)/shard_map/ppermute | solution.py:604
  14.9 0.0 collective-permute-start.3
  14.9 1.0 %collective-permute-start.4 = (bf16[512,128]{1,0:T(8,128)(2,1)S(1)}, bf16[512,128]{1,0:T(8,128)(2,1)S(1)}, u32[]{:S(2)}, u32[]{:S(2)}) collective-permute-start(bf16[512,128]{1,0:T(8,128)(2,1)S(1)} %get-tuple-element.42), channel_id=1, source_target_pairs={{0,8},{4,12},{8,0},{12,4},{1,9},{5,13},{9,1},{13,5},{2,10},{6,14},... | collective-permute-start | bytes 393224 | tf_op jit(solution)/shard_map/ppermute | solution.py:604
  15.9 3.8 %collective-permute-done.2.last_ref.refs_3_ = bf16[520,128]{1,0:T(8,128)(2,1)S(1)} collective-permute-done((bf16[520,128]{1,0:T(8,128)(2,1)S(1)}, bf16[520,128]{1,0:T(8,128)(2,1)S(1)}, u32[]{:S(2)}, u32[]{:S(2)}) %collective-permute-start.2) | collective-permute-done | bytes 133152 | tf_op jit(solution)/shard_map/ppermute | solution.py:604
  19.7 0.3 %shard_map.97 = (bf16[128,256]{1,0:T(8,128)(2,1)S(1)}, bf16[128,512]{1,0:T(8,128)(2,1)S(1)}) custom-call(bf16[520,128]{1,0:T(8,128)(2,1)S(1)} %collective-permute-done.2.last_ref.refs_3_, bf16[264,128]{1,0:T(8,128)(2,1)S(1)} %fusion.2.packet_ref.refs_11_.refs_0_, bf16[264,128]{1,0:T(8,128)(2,1)S(1)} %collective-permute-done.refs_4_.refs_12_.refs_1_, ...), custom_call_target="tpu_custom_call" | custom-call | tf_op jit(solution)/shard_map/pallas_call | solution.py:606
  20.0 0.5 %collective-permute-done.3.refs_1_ = bf16[512,128]{1,0:T(8,128)(2,1)S(1)} collective-permute-done((bf16[512,128]{1,0:T(8,128)(2,1)S(1)}, bf16[512,128]{1,0:T(8,128)(2,1)S(1)}, u32[]{:S(2)}, u32[]{:S(2)}) %collective-permute-start.3) | collective-permute-done | bytes 131104 | tf_op jit(solution)/shard_map/ppermute | solution.py:604
  20.4 5.5 %collective-permute-done.4.refs_2_ = bf16[512,128]{1,0:T(8,128)(2,1)S(1)} collective-permute-done((bf16[512,128]{1,0:T(8,128)(2,1)S(1)}, bf16[512,128]{1,0:T(8,128)(2,1)S(1)}, u32[]{:S(2)}, u32[]{:S(2)}) %collective-permute-start.4) | collective-permute-done | bytes 131104 | tf_op jit(solution)/shard_map/ppermute | solution.py:604
  25.9 1.0 %shard_map.98 = (f32[128,512]{1,0:T(8,128)}, f32[128,128]{1,0:T(8,128)}, f32[128,128]{1,0:T(8,128)}) custom-call(bf16[128,256]{1,0:T(8,128)(2,1)S(1)} %get-tuple-element.38.query_spread, bf16[128,512]{1,0:T(8,128)(2,1)S(1)} %get-tuple-element.39.key_spread, bf16[512,128]{1,0:T(8,128)(2,1)S(1)} %get-tuple-element.40.refs_0_, ...), custom_call_target="tpu_custom_call" | custom-call | tf_op jit(solution)/shard_map/pallas_call | solution.py:616
  (2 shorter events, 0.0 us)
Async XLA Ops:
  0.6 6.7 %copy-start = (bf16[128,512]{1,0:T(8,128)(2,1)S(1)}, bf16[128,512]{1,0:T(8,128)(2,1)}, u32[]{:S(2)}) copy-start(bf16[128,512]{1,0:T(8,128)(2,1)} %query_ref.1) | copy-start | bytes 393220
  1.6 5.7 %copy-start.3 = (s32[16]{0:T(128)S(1)}, s32[16]{0:T(128)}, u32[]{:S(2)}) copy-start(s32[16]{0:T(128)} %param.7) | copy-start | bytes 196
  1.6 8.0 %collective-permute-start = (bf16[264,128]{1,0:T(8,128)(2,1)S(1)}, bf16[264,128]{1,0:T(8,128)(2,1)S(1)}, u32[]{:S(2)}, u32[]{:S(2)}) collective-permute-start(bf16[264,128]{1,0:T(8,128)(2,1)S(1)} %fusion.2.packet_ref.refs_11_.refs_0_), channel_id=1, source_target_pairs={{0,4},{4,8},{8,12},{12,0},{1,5},{5,9},{9,13},{13,1},{2,6},{6,10},{... | collective-permute-start | bytes 202760 | tf_op jit(solution)/shard_map/ppermute | solution.py:555
  4.7 6.1 %collective-permute-start.1 = (bf16[264,128]{1,0:T(8,128)(2,1)S(1)}, bf16[264,128]{1,0:T(8,128)(2,1)S(1)}, u32[]{:S(2)}, u32[]{:S(2)}) collective-permute-start(bf16[264,128]{1,0:T(8,128)(2,1)S(1)} %fusion.2.packet_ref.refs_11_.refs_0_), channel_id=1, source_target_pairs={{0,8},{4,12},{8,4},{12,0},{1,9},{5,13},{9,5},{13,1},{2,10},{6,14},... | collective-permute-start | bytes 202760 | tf_op jit(solution)/shard_map/ppermute | solution.py:557
  7.3 0.9 %copy-start.1 = (bf16[128,512]{1,0:T(8,128)(2,1)S(1)}, bf16[128,512]{1,0:T(8,128)(2,1)}, u32[]{:S(2)}) copy-start(bf16[128,512]{1,0:T(8,128)(2,1)} %grad_ref.1) | copy-start | bytes 393220
  8.2 0.9 %copy-start.2 = (bf16[128,512]{1,0:T(8,128)(2,1)S(1)}, bf16[128,512]{1,0:T(8,128)(2,1)}, u32[]{:S(2)}) copy-start(bf16[128,512]{1,0:T(8,128)(2,1)} %saved_ref.1) | copy-start | bytes 393220
  11.4 8.3 %collective-permute-start.2 = (bf16[520,128]{1,0:T(8,128)(2,1)S(1)}, bf16[520,128]{1,0:T(8,128)(2,1)S(1)}, u32[]{:S(2)}, u32[]{:S(2)}) collective-permute-start(bf16[520,128]{1,0:T(8,128)(2,1)S(1)} %get-tuple-element.37), channel_id=1, source_target_pairs={{0,12},{4,8},{8,4},{12,0},{1,13},{5,9},{9,5},{13,1},{2,14},{6,10},... | collective-permute-start | bytes 399368 | tf_op jit(solution)/shard_map/ppermute | solution.py:604
  14.9 5.6 %collective-permute-start.3 = (bf16[512,128]{1,0:T(8,128)(2,1)S(1)}, bf16[512,128]{1,0:T(8,128)(2,1)S(1)}, u32[]{:S(2)}, u32[]{:S(2)}) collective-permute-start(bf16[512,128]{1,0:T(8,128)(2,1)S(1)} %get-tuple-element.41), channel_id=1, source_target_pairs={{0,4},{4,0},{8,12},{12,8},{1,5},{5,1},{9,13},{13,9},{2,6},{6,2},{1... | collective-permute-start | bytes 393224 | tf_op jit(solution)/shard_map/ppermute | solution.py:604
  14.9 11.1 %collective-permute-start.4 = (bf16[512,128]{1,0:T(8,128)(2,1)S(1)}, bf16[512,128]{1,0:T(8,128)(2,1)S(1)}, u32[]{:S(2)}, u32[]{:S(2)}) collective-permute-start(bf16[512,128]{1,0:T(8,128)(2,1)S(1)} %get-tuple-element.42), channel_id=1, source_target_pairs={{0,8},{4,12},{8,0},{12,4},{1,9},{5,13},{9,1},{13,5},{2,10},{6,14},... | collective-permute-start | bytes 393224 | tf_op jit(solution)/shard_map/ppermute | solution.py:604

commit v19 on v17

--- a/solution.py
+++ b/solution.py
@@ -443,10 +443,25 @@
             ]
 
 
-def order_kernel(count, halo, _, *refs):
-    packets = refs[: 1 + halo]
-    query_out, key_out = refs[1 + halo :]
-    rows = query_out.shape[0]
+def slots_of(refs, first, size, pieces):
+    return jnp.concatenate(
+        [
+            jnp.concatenate(
+                [ref[first + n * size : first + (n + 1) * size, :] for n in range(pieces)], axis=1
+            )
+            for ref in refs
+        ],
+        axis=0,
+    )
+
+
+def order_kernel(count, halo, early, late, *refs):
+    ins, packets = refs[: len(early)], refs[len(early) : len(early) + 1 + halo]
+    query_out, key_out, query_base, key_base = refs[-4:]
+    rows, width = query_base.shape
+    depth = ins[0].shape[1]
+    heads = width // depth
+    slot = 2 * rows // count
     index = lax.axis_index("ctx")
     given = []
     for ref in packets:
@@ -460,11 +475,11 @@
         given.append(rows - sum(given))
     giver = [lax.rem(index - d + count, count) for d in range(count)]
 
-    def placement(size, halo):
-        lane = lax.broadcasted_iota(jnp.int32, (1, count * size), 1)
+    def placement(size, halo, exchanges):
+        lane = lax.broadcasted_iota(jnp.int32, (1, len(exchanges) * size), 1)
         target = jnp.full(lane.shape, -1, jnp.int32)
-        for k in range(count):
-            step = lane - k * size
+        for n, k in enumerate(exchanges):
+            step = lane - n * size
             for back in range(halo + 1):
                 block = (index ^ k) - back
                 start = jnp.zeros((1, 1), jnp.int32)
@@ -476,14 +491,17 @@
                 step = step - length
         return one_hot(rows, target)
 
-    query_out[...] = placement(2 * rows // count, 0)
-    key_out[...] = placement(rows, halo)
-
-
-def place_kernel(count, query_spread, key_spread, *refs):
-    ins = refs[:count]
-    query_out, key_out, value_out = refs[count : count + 3]
-    query_here, key_here, value_here, sems = refs[count + 3 :]
+    query_out[...] = placement(slot, 0, late)
+    key_out[...] = placement(rows, halo, late)
+    query_base[...] = contract(placement(slot, 0, early), slots_of(ins, 0, slot, heads), 1, 0)
+    key_base[...] = contract(
+        placement(rows, halo, early), slots_of(ins, heads * slot, rows, 2), 1, 0
+    )
+
+
+def place_kernel(count, query_spread, key_spread, query_base, key_base, *refs):
+    ins = refs[:-7]
+    query_out, key_out, value_out, query_here, key_here, value_here, sems = refs[-7:]
     rows, width = query_here.shape
     depth = key_here.shape[1]
     heads = width // depth
@@ -494,21 +512,13 @@
         copies.append(pltpu.make_async_copy(here, out, sems.at[len(copies)]))
         copies[-1].start()
 
-    def taken(first, size, pieces):
-        return jnp.concatenate(
-            [
-                jnp.concatenate(
-                    [ref[first + n * size : first + (n + 1) * size, :] for n in range(pieces)],
-                    axis=1,
-                )
-                for ref in ins
-            ],
-            axis=0,
-        )
-
-    query_here[...] = contract(query_spread[...], taken(0, slot, heads), 1, 0)
+    query_here[...] = query_base[...] + contract(
+        query_spread[...], slots_of(ins, 0, slot, heads), 1, 0
+    )
     leave(query_here, query_out)
-    both = contract(key_spread[...], taken(heads * slot, rows, 2), 1, 0)
+    both = key_base[...] + contract(
+        key_spread[...], slots_of(ins, heads * slot, rows, 2), 1, 0
+    )
     for n, (here, out) in enumerate(((key_here, key_out), (value_here, value_out))):
         here[...] = both[:, n * depth : (n + 1) * depth]
         leave(here, out)
@@ -575,16 +585,20 @@
     received = [sent[0]] + [
         lax.ppermute(sent[k], "ctx", [(i, i ^ k) for i in range(count)]) for k in range(1, count)
     ]
-    spreads = pl.pallas_call(
-        functools.partial(order_kernel, count, halo),
+    early = (0, 3) if count == 4 else (0,)
+    late = tuple(k for k in range(count) if k not in early)
+    placed = pl.pallas_call(
+        functools.partial(order_kernel, count, halo, early, late),
         out_shape=[
-            jax.ShapeDtypeStruct((rows, count * slot), bf16),
-            jax.ShapeDtypeStruct((rows, count * rows), bf16),
+            jax.ShapeDtypeStruct((rows, len(late) * slot), bf16),
+            jax.ShapeDtypeStruct((rows, len(late) * rows), bf16),
+            jax.ShapeDtypeStruct((rows, width), f32),
+            jax.ShapeDtypeStruct((rows, 2 * depth), f32),
         ],
-        in_specs=[pl.BlockSpec(memory_space=pl.ANY)] + [whole] * (1 + halo),
-        out_specs=[whole] * 2,
+        in_specs=[whole] * (len(early) + 1 + halo),
+        out_specs=[whole] * 4,
         compiler_params=params,
-    )(received[-1], packet, *near)
+    )(*[received[k] for k in early], packet, *near)
     return pl.pallas_call(
         functools.partial(place_kernel, count),
         out_shape=[
@@ -592,7 +606,7 @@
             jax.ShapeDtypeStruct((rows, depth), f32),
             jax.ShapeDtypeStruct((rows, depth), f32),
         ],
-        in_specs=[whole] * (2 + count),
+        in_specs=[whole] * (4 + len(late)),
         out_specs=[pl.BlockSpec(memory_space=pl.ANY)] * 3,
         scratch_shapes=[
             pltpu.VMEM((rows, width), f32),
@@ -601,7 +615,7 @@
             pltpu.SemaphoreType.DMA((3,)),
         ],
         compiler_params=params,
-    )(*spreads, *received)
+    )(*placed, *[received[k] for k in late])
 
 
 def per_device(*args):

time: 25.1 us -> 25.1 us (level)
  transfers between devices with their start and end apart: 5 -> 5, of which waited for: 3 -> 3; matrix products, arithmetic and copies ran while one was open for 0% -> 0% of each run, Pallas kernels for 4% -> 5%
where the time goes in v19:
time: 25.1 us; the launch traced here: 24.9 us
  starting transfers between devices  10.1 us (40%)
  waiting for transfers between devices  8.6 us (34%)
  Pallas kernels  2.68 us (11%)
  local copies, waits for them, and re-layouts  1.82 us (7%)
  other arithmetic  0.96 us (4%)
  between operations  0.71 us (3%)
    ppermute x3, waiting for transfers between devices, near_plan(): lax.ppermute(sent[k], 'ctx', [(i, i ^ k) for i in range(count)])  6.77 us
    ppermute x2, starting transfers between devices, near_plan(): lax.ppermute(packet, 'ctx', [(i, (i + back) % count) for i in range(count)])  5.67 us
    ppermute x3, starting transfers between devices, near_plan(): lax.ppermute(sent[k], 'ctx', [(i, i ^ k) for i in range(count)])  4.45 us
    ppermute x2, waiting for transfers between devices, near_plan(): lax.ppermute(packet, 'ctx', [(i, (i + back) % count) for i in range(count)])  1.83 us
    unnamed x8, local copies, waits for them, and re-layouts  1.82 us
    select_n x1, other arithmetic, near_plan(): jnp.where(mark < 0, jnp.pad(jnp.concatenate([key_head_rows, value_head_ro...  0.94 us
    pallas_call x1, Pallas kernels, near_plan(): pl.pallas_call(functools.partial(place_kernel, count), out_shape=[jax.Sha...  0.94 us
    pallas_call x1, Pallas kernels, near_plan(): pl.pallas_call(functools.partial(attend_kernel, count, halo), out_shape=[...  0.55 us
  transfers between devices with their start and end apart: 5, of which 3 were waited for; matrix products, arithmetic and copies ran while one was open for 0% of the time, Pallas kernels for 5%

profile of v19, /device:TPU:0, one launch (start us, length us, event | category | flops | bytes accessed | tf_op | source)
XLA Modules:
  0.0 24.9 jit_solution(2169519082907257640)
XLA Ops:
  0.6 0.0 copy-start
  0.7 0.9 %fusion.2.packet_ref.refs_11_.refs_2_ = bf16[264,128]{1,0:T(8,128)(2,1)S(1)} fusion(bf16[128,128]{1,0:T(8,128)(2,1)} %param.11, bf16[128,128]{1,0:T(8,128)(2,1)} %param.10, s32[128]{0:T(128)} %param.8, s32[264]{0:T(512)S(1)} %iota_add_fusion, pred[264]{0:T(512)(128)(4,1)S(1)} %broadcast_compare_fusion), kind=kLoop, calls=%fused_computation.4 | loop fusion | flops 337920 | bytes 134952 | tf_op jit(solution)/shard_map/jit(_where)/select_n | solution.py:542
  1.6 0.0 copy-start.3
  1.6 3.1 %collective-permute-start = (bf16[264,128]{1,0:T(8,128)(2,1)S(1)}, bf16[264,128]{1,0:T(8,128)(2,1)S(1)}, u32[]{:S(2)}, u32[]{:S(2)}) collective-permute-start(bf16[264,128]{1,0:T(8,128)(2,1)S(1)} %fusion.2.packet_ref.refs_11_.refs_2_), channel_id=1, source_target_pairs={{0,4},{4,8},{8,12},{12,0},{1,5},{5,9},{9,13},{13,1},{2,6},{6,10},{... | collective-permute-start | bytes 202760 | tf_op jit(solution)/shard_map/ppermute | solution.py:548
  4.7 2.6 %collective-permute-start.1 = (bf16[264,128]{1,0:T(8,128)(2,1)S(1)}, bf16[264,128]{1,0:T(8,128)(2,1)S(1)}, u32[]{:S(2)}, u32[]{:S(2)}) collective-permute-start(bf16[264,128]{1,0:T(8,128)(2,1)S(1)} %fusion.2.packet_ref.refs_11_.refs_2_), channel_id=1, source_target_pairs={{0,8},{4,12},{8,0},{12,4},{1,9},{5,13},{9,1},{13,5},{2,10},{6,14},... | collective-permute-start | bytes 202760 | tf_op jit(solution)/shard_map/ppermute | solution.py:548
  7.3 0.0 copy-done
  7.3 0.0 copy-done.3
  7.3 0.0 copy-start.1
  7.3 0.9 %copy-done.1 = bf16[128,512]{1,0:T(8,128)(2,1)S(1)} copy-done((bf16[128,512]{1,0:T(8,128)(2,1)S(1)}, bf16[128,512]{1,0:T(8,128)(2,1)}, u32[]{:S(2)}) %copy-start.1) | copy-done | bytes 131096
  8.2 0.0 copy-start.2
  8.2 0.9 %copy-done.2 = bf16[128,512]{1,0:T(8,128)(2,1)S(1)} copy-done((bf16[128,512]{1,0:T(8,128)(2,1)S(1)}, bf16[128,512]{1,0:T(8,128)(2,1)}, u32[]{:S(2)}) %copy-start.2) | copy-done | bytes 131096
  9.1 0.5 %shard_map.94 = (bf16[512,128]{1,0:T(8,128)(2,1)S(1)}, bf16[512,128]{1,0:T(8,128)(2,1)S(1)}, f32[128,512]{1,0:T(8,128)S(1)}, f32[128,512]{1,0:T(8,128)S(1)}, f32...) custom-call(s32[1,16]{1,0:T(1,128)S(1)} %bitcast.1, ...), custom_call_target="tpu_custom_call" | custom-call | tf_op jit(solution)/shard_map/pallas_call | solution.py:555
  9.6 0.0 collective-permute-done.refs_4_.refs_12_.refs_3_
  9.6 0.3 %shard_map.95 = (f32[128,512]{1,0:T(8,128)S(1)}, f32[128,512]{1,0:T(8,128)S(1)}, f32[8,512]{1,0:T(8,128)S(1)}, bf16[512,128]{1,0:T(8,128)(2,1)S(1)}, f32[8,128]{1,0:T(8,128)S(1)}) custom-call(bf16[512,128]{1,0:T(8,128)(2,1)S(1)} %get-tuple-element.24.refs_0_, bf16[512,128]{1,0:T(8,128)(2,1)S(1)} %get-tuple-element.25.refs_1_, ...), custom_call_target="tpu_custom_call" | custom-call | tf_op jit(solution)/shard_map/pallas_call | solution.py:566
  9.9 1.8 %collective-permute-done.1.refs_13_.refs_4_ = bf16[264,128]{1,0:T(8,128)(2,1)S(1)} collective-permute-done((bf16[264,128]{1,0:T(8,128)(2,1)S(1)}, bf16[264,128]{1,0:T(8,128)(2,1)S(1)}, u32[]{:S(2)}, u32[]{:S(2)}) %collective-permute-start.1) | collective-permute-done | bytes 67616 | tf_op jit(solution)/shard_map/ppermute | solution.py:548
  11.8 0.5 %shard_map.96 = (bf16[512,128]{1,0:T(8,128)(2,1)S(1)}, bf16[512,128]{1,0:T(8,128)(2,1)S(1)}, bf16[512,128]{1,0:T(8,128)(2,1)S(1)}, bf16[512,128]{1,0:T(8,128)(2,1)S(1)}) custom-call(bf16[512,128]{1,0:T(8,128)(2,1)S(1)} %get-tuple-element.24.refs_0_, bf16[512,128]{1,0:T(8,128)(2,1)S(1)} %get-tuple-element.25.refs_1_, f32[8,512]{1,0:T(8,128)S(1)} %get-tuple-element.28.refs_2_, ...), custom_call_target="tpu_custom_call" | custom-call | tf_op jit(solution)/shard_map/pallas_call | solution.py:578
  12.3 2.6 %collective-permute-start.2 = (bf16[512,128]{1,0:T(8,128)(2,1)S(1)}, bf16[512,128]{1,0:T(8,128)(2,1)S(1)}, u32[]{:S(2)}, u32[]{:S(2)}) collective-permute-start(bf16[512,128]{1,0:T(8,128)(2,1)S(1)} %get-tuple-element.38), channel_id=1, source_target_pairs={{0,12},{4,8},{8,4},{12,0},{1,13},{5,9},{9,5},{13,1},{2,14},{6,10},... | collective-permute-start | bytes 393224 | tf_op jit(solution)/shard_map/ppermute | solution.py:586
  14.9 0.0 collective-permute-start.3
  14.9 1.9 %collective-permute-start.4 = (bf16[512,128]{1,0:T(8,128)(2,1)S(1)}, bf16[512,128]{1,0:T(8,128)(2,1)S(1)}, u32[]{:S(2)}, u32[]{:S(2)}) collective-permute-start(bf16[512,128]{1,0:T(8,128)(2,1)S(1)} %get-tuple-element.44), channel_id=1, source_target_pairs={{0,8},{4,12},{8,0},{12,4},{1,9},{5,13},{9,1},{13,5},{2,10},{6,14},... | collective-permute-start | bytes 393224 | tf_op jit(solution)/shard_map/ppermute | solution.py:586
  16.8 3.9 %collective-permute-done.2.refs_1_ = bf16[512,128]{1,0:T(8,128)(2,1)S(1)} collective-permute-done((bf16[512,128]{1,0:T(8,128)(2,1)S(1)}, bf16[512,128]{1,0:T(8,128)(2,1)S(1)}, u32[]{:S(2)}, u32[]{:S(2)}) %collective-permute-start.2) | collective-permute-done | bytes 131104 | tf_op jit(solution)/shard_map/ppermute | solution.py:586
  20.6 0.4 %shard_map.97 = (bf16[128,128]{1,0:T(8,128)(2,1)S(1)}, bf16[128,256]{1,0:T(8,128)(2,1)S(1)}, f32[128,512]{1,0:T(8,128)S(1)}, f32[128,256]{1,0:T(8,128)S(1)}) custom-call(bf16[512,128]{1,0:T(8,128)(2,1)S(1)} %get-tuple-element.37.refs_0_, bf16[512,128]{1,0:T(8,128)(2,1)S(1)} %collective-permute-done.2.refs_1_, ...), custom_call_target="tpu_custom_call" | custom-call | tf_op jit(solution)/shard_map/pallas_call | solution.py:590
  21.0 2.9 %collective-permute-done.3.refs_0_ = bf16[512,128]{1,0:T(8,128)(2,1)S(1)} collective-permute-done((bf16[512,128]{1,0:T(8,128)(2,1)S(1)}, bf16[512,128]{1,0:T(8,128)(2,1)S(1)}, u32[]{:S(2)}, u32[]{:S(2)}) %collective-permute-start.3) | collective-permute-done | bytes 131104 | tf_op jit(solution)/shard_map/ppermute | solution.py:586
  23.9 0.0 collective-permute-done.4.refs_1_
  23.9 0.9 %shard_map.98 = (f32[128,512]{1,0:T(8,128)}, f32[128,128]{1,0:T(8,128)}, f32[128,128]{1,0:T(8,128)}) custom-call(bf16[128,128]{1,0:T(8,128)(2,1)S(1)} %get-tuple-element.39.query_spread, bf16[128,256]{1,0:T(8,128)(2,1)S(1)} %get-tuple-element.40.key_spread, f32[128,512]{1,0:T(8,128)S(1)} %get-tuple-element.41.query_base, ...), custom_call_target="tpu_custom_call" | custom-call | tf_op jit(solution)/shard_map/pallas_call | solution.py:602
  (2 shorter events, 0.0 us)
Async XLA Ops:
  0.6 6.7 %copy-start = (bf16[128,512]{1,0:T(8,128)(2,1)S(1)}, bf16[128,512]{1,0:T(8,128)(2,1)}, u32[]{:S(2)}) copy-start(bf16[128,512]{1,0:T(8,128)(2,1)} %query_ref.1) | copy-start | bytes 393220
  1.6 5.7 %copy-start.3 = (s32[16]{0:T(128)S(1)}, s32[16]{0:T(128)}, u32[]{:S(2)}) copy-start(s32[16]{0:T(128)} %param.7) | copy-start | bytes 196
  1.6 8.0 %collective-permute-start = (bf16[264,128]{1,0:T(8,128)(2,1)S(1)}, bf16[264,128]{1,0:T(8,128)(2,1)S(1)}, u32[]{:S(2)}, u32[]{:S(2)}) collective-permute-start(bf16[264,128]{1,0:T(8,128)(2,1)S(1)} %fusion.2.packet_ref.refs_11_.refs_2_), channel_id=1, source_target_pairs={{0,4},{4,8},{8,12},{12,0},{1,5},{5,9},{9,13},{13,1},{2,6},{6,10},{... | collective-permute-start | bytes 202760 | tf_op jit(solution)/shard_map/ppermute | solution.py:548
  4.7 7.1 %collective-permute-start.1 = (bf16[264,128]{1,0:T(8,128)(2,1)S(1)}, bf16[264,128]{1,0:T(8,128)(2,1)S(1)}, u32[]{:S(2)}, u32[]{:S(2)}) collective-permute-start(bf16[264,128]{1,0:T(8,128)(2,1)S(1)} %fusion.2.packet_ref.refs_11_.refs_2_), channel_id=1, source_target_pairs={{0,8},{4,12},{8,0},{12,4},{1,9},{5,13},{9,1},{13,5},{2,10},{6,14},... | collective-permute-start | bytes 202760 | tf_op jit(solution)/shard_map/ppermute | solution.py:548
  7.3 0.9 %copy-start.1 = (bf16[128,512]{1,0:T(8,128)(2,1)S(1)}, bf16[128,512]{1,0:T(8,128)(2,1)}, u32[]{:S(2)}) copy-start(bf16[128,512]{1,0:T(8,128)(2,1)} %grad_ref.1) | copy-start | bytes 393220
  8.2 0.9 %copy-start.2 = (bf16[128,512]{1,0:T(8,128)(2,1)S(1)}, bf16[128,512]{1,0:T(8,128)(2,1)}, u32[]{:S(2)}) copy-start(bf16[128,512]{1,0:T(8,128)(2,1)} %saved_ref.1) | copy-start | bytes 393220
  12.3 8.3 %collective-permute-start.2 = (bf16[512,128]{1,0:T(8,128)(2,1)S(1)}, bf16[512,128]{1,0:T(8,128)(2,1)S(1)}, u32[]{:S(2)}, u32[]{:S(2)}) collective-permute-start(bf16[512,128]{1,0:T(8,128)(2,1)S(1)} %get-tuple-element.38), channel_id=1, source_target_pairs={{0,12},{4,8},{8,4},{12,0},{1,13},{5,9},{9,5},{13,1},{2,14},{6,10},... | collective-permute-start | bytes 393224 | tf_op jit(solution)/shard_map/ppermute | solution.py:586
  14.9 9.1 %collective-permute-start.3 = (bf16[512,128]{1,0:T(8,128)(2,1)S(1)}, bf16[512,128]{1,0:T(8,128)(2,1)S(1)}, u32[]{:S(2)}, u32[]{:S(2)}) collective-permute-start(bf16[512,128]{1,0:T(8,128)(2,1)S(1)} %get-tuple-element.43), channel_id=1, source_target_pairs={{0,4},{4,0},{8,12},{12,8},{1,5},{5,1},{9,13},{13,9},{2,6},{6,2},{1... | collective-permute-start | bytes 393224 | tf_op jit(solution)/shard_map/ppermute | solution.py:586
  14.9 9.1 %collective-permute-start.4 = (bf16[512,128]{1,0:T(8,128)(2,1)S(1)}, bf16[512,128]{1,0:T(8,128)(2,1)S(1)}, u32[]{:S(2)}, u32[]{:S(2)}) collective-permute-start(bf16[512,128]{1,0:T(8,128)(2,1)S(1)} %get-tuple-element.44), channel_id=1, source_target_pairs={{0,8},{4,12},{8,0},{12,4},{1,9},{5,13},{9,1},{13,5},{2,10},{6,14},... | collective-permute-start | bytes 393224 | tf_op jit(solution)/shard_map/ppermute | solution.py:586

commit v20 on v19

--- a/solution.py
+++ b/solution.py
@@ -362,11 +362,16 @@
     return raised, change, (new_top, total, factors), one_hot(count * rows, target), filled
 
 
-def step_kernel(count, back, *refs):
-    query_ref, grad_ref, row_ref, filled_ref, packet_ref = refs[:5]
-    raised_out, change_out, row_out, target_out, filled_out = refs[5:]
+def step_kernel(count, halo, back, *refs):
+    query_ref, grad_ref, row_ref, filled_ref, spread_ref = refs[:5]
+    raised_refs = refs[5 : 5 + back]
+    change_refs = refs[5 + back : 5 + 2 * back]
+    target_refs = refs[5 + 2 * back : 5 + 3 * back]
+    packets = refs[5 + 3 * back : 6 + 4 * back]
+    raised_out, change_out, row_out, target_out, filled_out = refs[6 + 4 * back : 11 + 4 * back]
+    outs = refs[11 + 4 * back :]
     raised, change, (top, total, factors), target, filled = fold(
-        count, back, packet_ref, query_ref[...], grad_ref[...], row_ref, filled_ref
+        count, back, packets[back], query_ref[...], grad_ref[...], row_ref, filled_ref
     )
     raised_out[...] = raised
     change_out[...] = change
@@ -378,16 +383,39 @@
     target_out[...] = target
     filled_out[0:count, :] = filled
     filled_out[count:, :] = jnp.zeros_like(filled_out[count:, :])
-
-
-def attend_kernel(count, halo, *refs):
-    index = lax.axis_index("ctx")
-    for blocks in range(1, halo + 2):
-        here = index == blocks - 1 if blocks <= halo else index >= halo
-
-        @pl.when(here)
+    if outs:
+        attend_first(
+            count,
+            halo,
+            (query_ref, grad_ref, row_out, filled_out, spread_ref)
+            + (*raised_refs, raised_out, *change_refs, change_out, *target_refs, target_out)
+            + (*packets, None, *outs),
+        )
+
+
+def attend_first(count, halo, refs):
+    for blocks in range(1, halo + 1):
+
+        @pl.when(lax.axis_index("ctx") == blocks - 1)
         def _(blocks=blocks):
             attend(count, halo, blocks, refs)
+
+
+def attend_kernel(count, halo, *refs):
+    ready, refs = refs[: count * (halo > 1)], refs[count * (halo > 1) :]
+    held = lax.axis_index("ctx") >= halo
+
+    @pl.when(held)
+    def _():
+        attend(count, halo, halo + 1, refs)
+
+    if not ready:
+        return attend_first(count, halo, refs)
+
+    @pl.when(jnp.logical_not(held))
+    def _():
+        for here, out in zip(ready, refs[-count:], strict=True):
+            out[...] = here[...]
 
 
 def attend(count, halo, blocks, refs):
@@ -562,26 +590,31 @@
         compiler_params=params,
     )(doc_lengths.reshape(1, -1), packet, queries, grad_out, forward_out)
     raised, change, target = [raised], [change], [target]
+    slot_shapes = [jax.ShapeDtypeStruct((heads * slot + 2 * rows, depth), bf16)] * count
+    ready = []
     for back in range(1, halo):
         found = pl.pallas_call(
-            functools.partial(step_kernel, count, back),
-            out_shape=block_shapes + [row_shape, target_shape, filled_shape],
-            in_specs=[whole] * 5,
-            out_specs=[whole] * 5,
+            functools.partial(step_kernel, count, halo, back),
+            out_shape=block_shapes
+            + [row_shape, target_shape, filled_shape]
+            + slot_shapes * (back == halo - 1),
+            in_specs=[whole] * (6 + 4 * back),
+            out_specs=[whole] * (5 + count * (back == halo - 1)),
             compiler_params=params,
-        )(query_rows, grad_rows, row, filled, near[back - 1])
+        )(query_rows, grad_rows, row, filled, spread, *raised, *change, *target, packet, *near[:back])
         raised.append(found[0])
         change.append(found[1])
         row = found[2]
         target.append(found[3])
         filled = found[4]
+        ready = found[5:]
     sent = pl.pallas_call(
         functools.partial(attend_kernel, count, halo),
-        out_shape=[jax.ShapeDtypeStruct((heads * slot + 2 * rows, depth), bf16)] * count,
-        in_specs=[whole] * (6 + 4 * halo),
+        out_shape=slot_shapes,
+        in_specs=[whole] * (len(ready) + 6 + 4 * halo),
         out_specs=[whole] * count,
         compiler_params=params,
-    )(query_rows, grad_rows, row, filled, spread, *raised, *change, *target, packet, *near)
+    )(*ready, query_rows, grad_rows, row, filled, spread, *raised, *change, *target, packet, *near)
     received = [sent[0]] + [
         lax.ppermute(sent[k], "ctx", [(i, i ^ k) for i in range(count)]) for k in range(1, count)
     ]

time: 25.1 us -> 26.2 us (1.044)
  waiting for transfers between devices: 8.6 us -> 9.7 us
    ppermute x3, waiting for transfers between devices: 6.77 us -> 8.42 us  [near_plan(): lax.ppermute(sent[k], 'ctx', [(i, i ^ k) for i in range(count)])]
    ppermute x2, waiting for transfers between devices: 1.83 us -> 1.27 us  [near_plan(): lax.ppermute(packet, 'ctx', [(i, (i + back) % count) for i in range(count)])]
  transfers between devices with their start and end apart: 5 -> 5, of which waited for: 3 -> 4; matrix products, arithmetic and copies ran while one was open for 0% -> 0% of each run, Pallas kernels for 5% -> 7%
where the time goes in v20:
time: 26.2 us; the launch traced here: 26 us
  starting transfers between devices  10.1 us (39%)
  waiting for transfers between devices  9.7 us (37%)
  Pallas kernels  2.73 us (10%)
  local copies, waits for them, and re-layouts  1.82 us (7%)
  other arithmetic  0.96 us (4%)
  between operations  0.7 us (3%)
    ppermute x3, waiting for transfers between devices, near_plan(): lax.ppermute(sent[k], 'ctx', [(i, i ^ k) for i in range(count)])  8.42 us
    ppermute x2, starting transfers between devices, near_plan(): lax.ppermute(packet, 'ctx', [(i, (i + back) % count) for i in range(count)])  5.67 us
    ppermute x3, starting transfers between devices, near_plan(): lax.ppermute(sent[k], 'ctx', [(i, i ^ k) for i in range(count)])  4.45 us
    unnamed x8, local copies, waits for them, and re-layouts  1.82 us
    ppermute x2, waiting for transfers between devices, near_plan(): lax.ppermute(packet, 'ctx', [(i, (i + back) % count) for i in range(count)])  1.27 us
    select_n x1, other arithmetic, near_plan(): jnp.where(mark < 0, jnp.pad(jnp.concatenate([key_head_rows, value_head_ro...  0.94 us
    pallas_call x1, Pallas kernels, near_plan(): pl.pallas_call(functools.partial(place_kernel, count), out_shape=[jax.Sha...  0.94 us
    pallas_call x1, Pallas kernels, near_plan(): pl.pallas_call(functools.partial(step_kernel, count, halo, back), out_sha...  0.89 us
  transfers between devices with their start and end apart: 5, of which 4 were waited for; matrix products, arithmetic and copies ran while one was open for 0% of the time, Pallas kernels for 7%

profile of v20, /device:TPU:0, one launch (start us, length us, event | category | flops | bytes accessed | tf_op | source)
XLA Modules:
  0.0 26.0 jit_solution(9280899238027656738)
XLA Ops:
  0.6 0.0 copy-start
  0.7 0.9 %fusion.2.packet_ref.refs_8_.refs_15_.refs_2_ = bf16[264,128]{1,0:T(8,128)(2,1)S(1)} fusion(bf16[128,128]{1,0:T(8,128)(2,1)} %param.11, bf16[128,128]{1,0:T(8,128)(2,1)} %param.10, s32[128]{0:T(128)} %param.8, s32[264]{0:T(512)S(1)} %iota_add_fusion, pred[264]{0:T(512)(128)(4,1)S(1)} %broadcast_compare_fusion), kind=kLoop, calls=%fused_computation.4 | loop fusion | flops 337920 | bytes 134952 | tf_op jit(solution)/shard_map/jit(_where)/select_n | solution.py:570
  1.6 0.0 copy-start.3
  1.6 3.1 %collective-permute-start = (bf16[264,128]{1,0:T(8,128)(2,1)S(1)}, bf16[264,128]{1,0:T(8,128)(2,1)S(1)}, u32[]{:S(2)}, u32[]{:S(2)}) collective-permute-start(bf16[264,128]{1,0:T(8,128)(2,1)S(1)} %fusion.2.packet_ref.refs_8_.refs_15_.refs_2_), channel_id=1, source_target_pairs={{0,4},{4,8},{8,12},{12,0},{1,5},{5,9},{9,13},{13,1},{2,6},{6,10},{... | collective-permute-start | bytes 202760 | tf_op jit(solution)/shard_map/ppermute | solution.py:576
  4.7 2.6 %collective-permute-start.1 = (bf16[264,128]{1,0:T(8,128)(2,1)S(1)}, bf16[264,128]{1,0:T(8,128)(2,1)S(1)}, u32[]{:S(2)}, u32[]{:S(2)}) collective-permute-start(bf16[264,128]{1,0:T(8,128)(2,1)S(1)} %fusion.2.packet_ref.refs_8_.refs_15_.refs_2_), channel_id=1, source_target_pairs={{0,8},{4,12},{8,0},{12,4},{1,9},{5,13},{9,1},{13,5},{2,10},{6,14},... | collective-permute-start | bytes 202760 | tf_op jit(solution)/shard_map/ppermute | solution.py:576
  7.3 0.0 copy-done
  7.3 0.0 copy-done.3
  7.3 0.0 copy-start.1
  7.3 0.9 %copy-done.1 = bf16[128,512]{1,0:T(8,128)(2,1)S(1)} copy-done((bf16[128,512]{1,0:T(8,128)(2,1)S(1)}, bf16[128,512]{1,0:T(8,128)(2,1)}, u32[]{:S(2)}) %copy-start.1) | copy-done | bytes 131096
  8.2 0.0 copy-start.2
  8.2 0.9 %copy-done.2 = bf16[128,512]{1,0:T(8,128)(2,1)S(1)} copy-done((bf16[128,512]{1,0:T(8,128)(2,1)S(1)}, bf16[128,512]{1,0:T(8,128)(2,1)}, u32[]{:S(2)}) %copy-start.2) | copy-done | bytes 131096
  9.1 0.5 %shard_map.94 = (bf16[512,128]{1,0:T(8,128)(2,1)S(1)}, bf16[512,128]{1,0:T(8,128)(2,1)S(1)}, f32[128,512]{1,0:T(8,128)S(1)}, f32[128,512]{1,0:T(8,128)S(1)}, f32...) custom-call(s32[1,16]{1,0:T(1,128)S(1)} %bitcast.1, ...), custom_call_target="tpu_custom_call" | custom-call | tf_op jit(solution)/shard_map/pallas_call | solution.py:583
  9.6 0.0 collective-permute-done.refs_9_.refs_16_.refs_3_
  9.6 0.9 %shard_map.95 = (f32[128,512]{1,0:T(8,128)S(1)}, f32[128,512]{1,0:T(8,128)S(1)}, f32[8,512]{1,0:T(8,128)S(1)}, bf16[512,128]{1,0:T(8,128)(2,1)S(1)}, f32[8,128]{...) custom-call(bf16[512,128]{1,0:T(8,128)(2,1)S(1)} %get-tuple-element., ...), custom_call_target="tpu_custom_call" | custom-call | tf_op jit(solution)/shard_map/pallas_call | solution.py:596
  10.5 1.3 %collective-permute-done.1.refs_17_.refs_4_ = bf16[264,128]{1,0:T(8,128)(2,1)S(1)} collective-permute-done((bf16[264,128]{1,0:T(8,128)(2,1)S(1)}, bf16[264,128]{1,0:T(8,128)(2,1)S(1)}, u32[]{:S(2)}, u32[]{:S(2)}) %collective-permute-start.1) | collective-permute-done | bytes 67616 | tf_op jit(solution)/shard_map/ppermute | solution.py:576
  11.8 3.1 %collective-permute-start.2 = (bf16[512,128]{1,0:T(8,128)(2,1)S(1)}, bf16[512,128]{1,0:T(8,128)(2,1)S(1)}, u32[]{:S(2)}, u32[]{:S(2)}) collective-permute-start(bf16[512,128]{1,0:T(8,128)(2,1)S(1)} %get-tuple-element.46), channel_id=1, source_target_pairs={{0,12},{4,8},{8,4},{12,0},{1,13},{5,9},{9,5},{13,1},{2,14},{6,10},... | collective-permute-start | bytes 393224 | tf_op jit(solution)/shard_map/ppermute | solution.py:619
  14.9 0.0 collective-permute-start.3
  14.9 1.4 %collective-permute-start.4 = (bf16[512,128]{1,0:T(8,128)(2,1)S(1)}, bf16[512,128]{1,0:T(8,128)(2,1)S(1)}, u32[]{:S(2)}, u32[]{:S(2)}) collective-permute-start(bf16[512,128]{1,0:T(8,128)(2,1)S(1)} %get-tuple-element.52), channel_id=1, source_target_pairs={{0,8},{4,12},{8,0},{12,4},{1,9},{5,13},{9,1},{13,5},{2,10},{6,14},... | collective-permute-start | bytes 393224 | tf_op jit(solution)/shard_map/ppermute | solution.py:619
  16.3 3.8 %collective-permute-done.2.refs_1_ = bf16[512,128]{1,0:T(8,128)(2,1)S(1)} collective-permute-done((bf16[512,128]{1,0:T(8,128)(2,1)S(1)}, bf16[512,128]{1,0:T(8,128)(2,1)S(1)}, u32[]{:S(2)}, u32[]{:S(2)}) %collective-permute-start.2) | collective-permute-done | bytes 131104 | tf_op jit(solution)/shard_map/ppermute | solution.py:619
  20.1 0.4 %shard_map.97 = (bf16[128,128]{1,0:T(8,128)(2,1)S(1)}, bf16[128,256]{1,0:T(8,128)(2,1)S(1)}, f32[128,512]{1,0:T(8,128)S(1)}, f32[128,256]{1,0:T(8,128)S(1)}) custom-call(bf16[512,128]{1,0:T(8,128)(2,1)S(1)} %get-tuple-element.45.refs_0_, bf16[512,128]{1,0:T(8,128)(2,1)S(1)} %collective-permute-done.2.refs_1_, ...), custom_call_target="tpu_custom_call" | custom-call | tf_op jit(solution)/shard_map/pallas_call | solution.py:623
  20.5 3.2 %collective-permute-done.3.refs_0_ = bf16[512,128]{1,0:T(8,128)(2,1)S(1)} collective-permute-done((bf16[512,128]{1,0:T(8,128)(2,1)S(1)}, bf16[512,128]{1,0:T(8,128)(2,1)S(1)}, u32[]{:S(2)}, u32[]{:S(2)}) %collective-permute-start.3) | collective-permute-done | bytes 131104 | tf_op jit(solution)/shard_map/ppermute | solution.py:619
  23.7 1.4 %collective-permute-done.4.refs_1_ = bf16[512,128]{1,0:T(8,128)(2,1)S(1)} collective-permute-done((bf16[512,128]{1,0:T(8,128)(2,1)S(1)}, bf16[512,128]{1,0:T(8,128)(2,1)S(1)}, u32[]{:S(2)}, u32[]{:S(2)}) %collective-permute-start.4) | collective-permute-done | bytes 131104 | tf_op jit(solution)/shard_map/ppermute | solution.py:619
  25.1 0.9 %shard_map.98 = (f32[128,512]{1,0:T(8,128)}, f32[128,128]{1,0:T(8,128)}, f32[128,128]{1,0:T(8,128)}) custom-call(bf16[128,128]{1,0:T(8,128)(2,1)S(1)} %get-tuple-element.47.query_spread, bf16[128,256]{1,0:T(8,128)(2,1)S(1)} %get-tuple-element.48.key_spread, f32[128,512]{1,0:T(8,128)S(1)} %get-tuple-element.49.query_base, ...), custom_call_target="tpu_custom_call" | custom-call | tf_op jit(solution)/shard_map/pallas_call | solution.py:635
  (3 shorter events, 0.0 us)
Async XLA Ops:
  0.6 6.7 %copy-start = (bf16[128,512]{1,0:T(8,128)(2,1)S(1)}, bf16[128,512]{1,0:T(8,128)(2,1)}, u32[]{:S(2)}) copy-start(bf16[128,512]{1,0:T(8,128)(2,1)} %query_ref.1) | copy-start | bytes 393220
  1.6 5.7 %copy-start.3 = (s32[16]{0:T(128)S(1)}, s32[16]{0:T(128)}, u32[]{:S(2)}) copy-start(s32[16]{0:T(128)} %param.7) | copy-start | bytes 196
  1.6 8.0 %collective-permute-start = (bf16[264,128]{1,0:T(8,128)(2,1)S(1)}, bf16[264,128]{1,0:T(8,128)(2,1)S(1)}, u32[]{:S(2)}, u32[]{:S(2)}) collective-permute-start(bf16[264,128]{1,0:T(8,128)(2,1)S(1)} %fusion.2.packet_ref.refs_8_.refs_15_.refs_2_), channel_id=1, source_target_pairs={{0,4},{4,8},{8,12},{12,0},{1,5},{5,9},{9,13},{13,1},{2,6},{6,10},{... | collective-permute-start | bytes 202760 | tf_op jit(solution)/shard_map/ppermute | solution.py:576
  4.7 7.1 %collective-permute-start.1 = (bf16[264,128]{1,0:T(8,128)(2,1)S(1)}, bf16[264,128]{1,0:T(8,128)(2,1)S(1)}, u32[]{:S(2)}, u32[]{:S(2)}) collective-permute-start(bf16[264,128]{1,0:T(8,128)(2,1)S(1)} %fusion.2.packet_ref.refs_8_.refs_15_.refs_2_), channel_id=1, source_target_pairs={{0,8},{4,12},{8,0},{12,4},{1,9},{5,13},{9,1},{13,5},{2,10},{6,14},... | collective-permute-start | bytes 202760 | tf_op jit(solution)/shard_map/ppermute | solution.py:576
  7.3 0.9 %copy-start.1 = (bf16[128,512]{1,0:T(8,128)(2,1)S(1)}, bf16[128,512]{1,0:T(8,128)(2,1)}, u32[]{:S(2)}) copy-start(bf16[128,512]{1,0:T(8,128)(2,1)} %grad_ref.1) | copy-start | bytes 393220
  8.2 0.9 %copy-start.2 = (bf16[128,512]{1,0:T(8,128)(2,1)S(1)}, bf16[128,512]{1,0:T(8,128)(2,1)}, u32[]{:S(2)}) copy-start(bf16[128,512]{1,0:T(8,128)(2,1)} %saved_ref.1) | copy-start | bytes 393220
  11.8 8.3 %collective-permute-start.2 = (bf16[512,128]{1,0:T(8,128)(2,1)S(1)}, bf16[512,128]{1,0:T(8,128)(2,1)S(1)}, u32[]{:S(2)}, u32[]{:S(2)}) collective-permute-start(bf16[512,128]{1,0:T(8,128)(2,1)S(1)} %get-tuple-element.46), channel_id=1, source_target_pairs={{0,12},{4,8},{8,4},{12,0},{1,13},{5,9},{9,5},{13,1},{2,14},{6,10},... | collective-permute-start | bytes 393224 | tf_op jit(solution)/shard_map/ppermute | solution.py:619
  14.9 8.8 %collective-permute-start.3 = (bf16[512,128]{1,0:T(8,128)(2,1)S(1)}, bf16[512,128]{1,0:T(8,128)(2,1)S(1)}, u32[]{:S(2)}, u32[]{:S(2)}) collective-permute-start(bf16[512,128]{1,0:T(8,128)(2,1)S(1)} %get-tuple-element.51), channel_id=1, source_target_pairs={{0,4},{4,0},{8,12},{12,8},{1,5},{5,1},{9,13},{13,9},{2,6},{6,2},{1... | collective-permute-start | bytes 393224 | tf_op jit(solution)/shard_map/ppermute | solution.py:619
  14.9 10.2 %collective-permute-start.4 = (bf16[512,128]{1,0:T(8,128)(2,1)S(1)}, bf16[512,128]{1,0:T(8,128)(2,1)S(1)}, u32[]{:S(2)}, u32[]{:S(2)}) collective-permute-start(bf16[512,128]{1,0:T(8,128)(2,1)S(1)} %get-tuple-element.52), channel_id=1, source_target_pairs={{0,8},{4,12},{8,0},{12,4},{1,9},{5,13},{9,1},{13,5},{2,10},{6,14},... | collective-permute-start | bytes 393224 | tf_op jit(solution)/shard_map/ppermute | solution.py:619

commit v21 on v20

--- a/solution.py
+++ b/solution.py
@@ -386,15 +386,16 @@
     if outs:
         attend_first(
             count,
-            halo,
+            (1,),
             (query_ref, grad_ref, row_out, filled_out, spread_ref)
             + (*raised_refs, raised_out, *change_refs, change_out, *target_refs, target_out)
             + (*packets, None, *outs),
         )
 
 
-def attend_first(count, halo, refs):
-    for blocks in range(1, halo + 1):
+def attend_first(count, several, refs):
+    halo = count // 2
+    for blocks in several:
 
         @pl.when(lax.axis_index("ctx") == blocks - 1)
         def _(blocks=blocks):
@@ -409,10 +410,11 @@
     def _():
         attend(count, halo, halo + 1, refs)
 
+    attend_first(count, range(2 if ready else 1, halo + 1), refs)
     if not ready:
-        return attend_first(count, halo, refs)
-
-    @pl.when(jnp.logical_not(held))
+        return
+
+    @pl.when(lax.axis_index("ctx") == 0)
     def _():
         for here, out in zip(ready, refs[-count:], strict=True):
             out[...] = here[...]

time: 26.2 us -> 26.3 us (level)
  no operation moved by 1% of the time
where the time goes in v21:
time: 26.3 us; the launch traced here: 26.1 us
  starting transfers between devices  10.1 us (38%)
  waiting for transfers between devices  9.79 us (37%)
  Pallas kernels  2.72 us (10%)
  local copies, waits for them, and re-layouts  1.82 us (7%)
  other arithmetic  0.96 us (4%)
  between operations  0.7 us (3%)
    ppermute x3, waiting for transfers between devices, near_plan(): lax.ppermute(sent[k], 'ctx', [(i, i ^ k) for i in range(count)])  8.51 us
    ppermute x2, starting transfers between devices, near_plan(): lax.ppermute(packet, 'ctx', [(i, (i + back) % count) for i in range(count)])  5.67 us
    ppermute x3, starting transfers between devices, near_plan(): lax.ppermute(sent[k], 'ctx', [(i, i ^ k) for i in range(count)])  4.45 us
    unnamed x8, local copies, waits for them, and re-layouts  1.82 us
    ppermute x2, waiting for transfers between devices, near_plan(): lax.ppermute(packet, 'ctx', [(i, (i + back) % count) for i in range(count)])  1.28 us
    select_n x1, other arithmetic, near_plan(): jnp.where(mark < 0, jnp.pad(jnp.concatenate([key_head_rows, value_head_ro...  0.94 us
    pallas_call x1, Pallas kernels, near_plan(): pl.pallas_call(functools.partial(place_kernel, count), out_shape=[jax.Sha...  0.94 us
    pallas_call x1, Pallas kernels, near_plan(): pl.pallas_call(functools.partial(step_kernel, count, halo, back), out_sha...  0.88 us
  transfers between devices with their start and end apart: 5, of which 4 were waited for; matrix products, arithmetic and copies ran while one was open for 0% of the time, Pallas kernels for 7%

profile of v21, /device:TPU:0, one launch (start us, length us, event | category | flops | bytes accessed | tf_op | source)
XLA Modules:
  0.0 26.1 jit_solution(5629560007832795617)
XLA Ops:
  0.6 0.0 copy-start
  0.7 0.9 %fusion.2.packet_ref.refs_8_.refs_15_.refs_2_ = bf16[264,128]{1,0:T(8,128)(2,1)S(1)} fusion(bf16[128,128]{1,0:T(8,128)(2,1)} %param.11, bf16[128,128]{1,0:T(8,128)(2,1)} %param.10, s32[128]{0:T(128)} %param.8, s32[264]{0:T(512)S(1)} %iota_add_fusion, pred[264]{0:T(512)(128)(4,1)S(1)} %broadcast_compare_fusion), kind=kLoop, calls=%fused_computation.4 | loop fusion | flops 337920 | bytes 134952 | tf_op jit(solution)/shard_map/jit(_where)/select_n | solution.py:572
  1.6 0.0 copy-start.3
  1.6 3.1 %collective-permute-start = (bf16[264,128]{1,0:T(8,128)(2,1)S(1)}, bf16[264,128]{1,0:T(8,128)(2,1)S(1)}, u32[]{:S(2)}, u32[]{:S(2)}) collective-permute-start(bf16[264,128]{1,0:T(8,128)(2,1)S(1)} %fusion.2.packet_ref.refs_8_.refs_15_.refs_2_), channel_id=1, source_target_pairs={{0,4},{4,8},{8,12},{12,0},{1,5},{5,9},{9,13},{13,1},{2,6},{6,10},{... | collective-permute-start | bytes 202760 | tf_op jit(solution)/shard_map/ppermute | solution.py:578
  4.7 2.6 %collective-permute-start.1 = (bf16[264,128]{1,0:T(8,128)(2,1)S(1)}, bf16[264,128]{1,0:T(8,128)(2,1)S(1)}, u32[]{:S(2)}, u32[]{:S(2)}) collective-permute-start(bf16[264,128]{1,0:T(8,128)(2,1)S(1)} %fusion.2.packet_ref.refs_8_.refs_15_.refs_2_), channel_id=1, source_target_pairs={{0,8},{4,12},{8,0},{12,4},{1,9},{5,13},{9,1},{13,5},{2,10},{6,14},... | collective-permute-start | bytes 202760 | tf_op jit(solution)/shard_map/ppermute | solution.py:578
  7.3 0.0 copy-done
  7.3 0.0 copy-done.3
  7.3 0.0 copy-start.1
  7.3 0.9 %copy-done.1 = bf16[128,512]{1,0:T(8,128)(2,1)S(1)} copy-done((bf16[128,512]{1,0:T(8,128)(2,1)S(1)}, bf16[128,512]{1,0:T(8,128)(2,1)}, u32[]{:S(2)}) %copy-start.1) | copy-done | bytes 131096
  8.2 0.0 copy-start.2
  8.2 0.9 %copy-done.2 = bf16[128,512]{1,0:T(8,128)(2,1)S(1)} copy-done((bf16[128,512]{1,0:T(8,128)(2,1)S(1)}, bf16[128,512]{1,0:T(8,128)(2,1)}, u32[]{:S(2)}) %copy-start.2) | copy-done | bytes 131096
  9.1 0.5 %shard_map.94 = (bf16[512,128]{1,0:T(8,128)(2,1)S(1)}, bf16[512,128]{1,0:T(8,128)(2,1)S(1)}, f32[128,512]{1,0:T(8,128)S(1)}, f32[128,512]{1,0:T(8,128)S(1)}, f32...) custom-call(s32[1,16]{1,0:T(1,128)S(1)} %bitcast.1, ...), custom_call_target="tpu_custom_call" | custom-call | tf_op jit(solution)/shard_map/pallas_call | solution.py:585
  9.6 0.0 collective-permute-done.refs_9_.refs_16_.refs_3_
  9.6 0.9 %shard_map.95 = (f32[128,512]{1,0:T(8,128)S(1)}, f32[128,512]{1,0:T(8,128)S(1)}, f32[8,512]{1,0:T(8,128)S(1)}, bf16[512,128]{1,0:T(8,128)(2,1)S(1)}, f32[8,128]{...) custom-call(bf16[512,128]{1,0:T(8,128)(2,1)S(1)} %get-tuple-element., ...), custom_call_target="tpu_custom_call" | custom-call | tf_op jit(solution)/shard_map/pallas_call | solution.py:598
  10.5 1.3 %collective-permute-done.1.refs_17_.refs_4_ = bf16[264,128]{1,0:T(8,128)(2,1)S(1)} collective-permute-done((bf16[264,128]{1,0:T(8,128)(2,1)S(1)}, bf16[264,128]{1,0:T(8,128)(2,1)S(1)}, u32[]{:S(2)}, u32[]{:S(2)}) %collective-permute-start.1) | collective-permute-done | bytes 67616 | tf_op jit(solution)/shard_map/ppermute | solution.py:578
  11.8 3.1 %collective-permute-start.2 = (bf16[512,128]{1,0:T(8,128)(2,1)S(1)}, bf16[512,128]{1,0:T(8,128)(2,1)S(1)}, u32[]{:S(2)}, u32[]{:S(2)}) collective-permute-start(bf16[512,128]{1,0:T(8,128)(2,1)S(1)} %get-tuple-element.46), channel_id=1, source_target_pairs={{0,12},{4,8},{8,4},{12,0},{1,13},{5,9},{9,5},{13,1},{2,14},{6,10},... | collective-permute-start | bytes 393224 | tf_op jit(solution)/shard_map/ppermute | solution.py:621
  14.9 0.0 collective-permute-start.3
  14.9 1.4 %collective-permute-start.4 = (bf16[512,128]{1,0:T(8,128)(2,1)S(1)}, bf16[512,128]{1,0:T(8,128)(2,1)S(1)}, u32[]{:S(2)}, u32[]{:S(2)}) collective-permute-start(bf16[512,128]{1,0:T(8,128)(2,1)S(1)} %get-tuple-element.52), channel_id=1, source_target_pairs={{0,8},{4,12},{8,0},{12,4},{1,9},{5,13},{9,1},{13,5},{2,10},{6,14},... | collective-permute-start | bytes 393224 | tf_op jit(solution)/shard_map/ppermute | solution.py:621
  16.3 3.8 %collective-permute-done.2.refs_1_ = bf16[512,128]{1,0:T(8,128)(2,1)S(1)} collective-permute-done((bf16[512,128]{1,0:T(8,128)(2,1)S(1)}, bf16[512,128]{1,0:T(8,128)(2,1)S(1)}, u32[]{:S(2)}, u32[]{:S(2)}) %collective-permute-start.2) | collective-permute-done | bytes 131104 | tf_op jit(solution)/shard_map/ppermute | solution.py:621
  20.1 0.4 %shard_map.97 = (bf16[128,128]{1,0:T(8,128)(2,1)S(1)}, bf16[128,256]{1,0:T(8,128)(2,1)S(1)}, f32[128,512]{1,0:T(8,128)S(1)}, f32[128,256]{1,0:T(8,128)S(1)}) custom-call(bf16[512,128]{1,0:T(8,128)(2,1)S(1)} %get-tuple-element.45.refs_0_, bf16[512,128]{1,0:T(8,128)(2,1)S(1)} %collective-permute-done.2.refs_1_, ...), custom_call_target="tpu_custom_call" | custom-call | tf_op jit(solution)/shard_map/pallas_call | solution.py:625
  20.5 3.1 %collective-permute-done.3.refs_0_ = bf16[512,128]{1,0:T(8,128)(2,1)S(1)} collective-permute-done((bf16[512,128]{1,0:T(8,128)(2,1)S(1)}, bf16[512,128]{1,0:T(8,128)(2,1)S(1)}, u32[]{:S(2)}, u32[]{:S(2)}) %collective-permute-start.3) | collective-permute-done | bytes 131104 | tf_op jit(solution)/shard_map/ppermute | solution.py:621
  23.6 1.6 %collective-permute-done.4.refs_1_ = bf16[512,128]{1,0:T(8,128)(2,1)S(1)} collective-permute-done((bf16[512,128]{1,0:T(8,128)(2,1)S(1)}, bf16[512,128]{1,0:T(8,128)(2,1)S(1)}, u32[]{:S(2)}, u32[]{:S(2)}) %collective-permute-start.4) | collective-permute-done | bytes 131104 | tf_op jit(solution)/shard_map/ppermute | solution.py:621
  25.2 0.9 %shard_map.98 = (f32[128,512]{1,0:T(8,128)}, f32[128,128]{1,0:T(8,128)}, f32[128,128]{1,0:T(8,128)}) custom-call(bf16[128,128]{1,0:T(8,128)(2,1)S(1)} %get-tuple-element.47.query_spread, bf16[128,256]{1,0:T(8,128)(2,1)S(1)} %get-tuple-element.48.key_spread, f32[128,512]{1,0:T(8,128)S(1)} %get-tuple-element.49.query_base, ...), custom_call_target="tpu_custom_call" | custom-call | tf_op jit(solution)/shard_map/pallas_call | solution.py:637
  (3 shorter events, 0.0 us)
Async XLA Ops:
  0.6 6.7 %copy-start = (bf16[128,512]{1,0:T(8,128)(2,1)S(1)}, bf16[128,512]{1,0:T(8,128)(2,1)}, u32[]{:S(2)}) copy-start(bf16[128,512]{1,0:T(8,128)(2,1)} %query_ref.1) | copy-start | bytes 393220
  1.6 5.7 %copy-start.3 = (s32[16]{0:T(128)S(1)}, s32[16]{0:T(128)}, u32[]{:S(2)}) copy-start(s32[16]{0:T(128)} %param.7) | copy-start | bytes 196
  1.6 8.0 %collective-permute-start = (bf16[264,128]{1,0:T(8,128)(2,1)S(1)}, bf16[264,128]{1,0:T(8,128)(2,1)S(1)}, u32[]{:S(2)}, u32[]{:S(2)}) collective-permute-start(bf16[264,128]{1,0:T(8,128)(2,1)S(1)} %fusion.2.packet_ref.refs_8_.refs_15_.refs_2_), channel_id=1, source_target_pairs={{0,4},{4,8},{8,12},{12,0},{1,5},{5,9},{9,13},{13,1},{2,6},{6,10},{... | collective-permute-start | bytes 202760 | tf_op jit(solution)/shard_map/ppermute | solution.py:578
  4.7 7.1 %collective-permute-start.1 = (bf16[264,128]{1,0:T(8,128)(2,1)S(1)}, bf16[264,128]{1,0:T(8,128)(2,1)S(1)}, u32[]{:S(2)}, u32[]{:S(2)}) collective-permute-start(bf16[264,128]{1,0:T(8,128)(2,1)S(1)} %fusion.2.packet_ref.refs_8_.refs_15_.refs_2_), channel_id=1, source_target_pairs={{0,8},{4,12},{8,0},{12,4},{1,9},{5,13},{9,1},{13,5},{2,10},{6,14},... | collective-permute-start | bytes 202760 | tf_op jit(solution)/shard_map/ppermute | solution.py:578
  7.3 0.9 %copy-start.1 = (bf16[128,512]{1,0:T(8,128)(2,1)S(1)}, bf16[128,512]{1,0:T(8,128)(2,1)}, u32[]{:S(2)}) copy-start(bf16[128,512]{1,0:T(8,128)(2,1)} %grad_ref.1) | copy-start | bytes 393220
  8.2 0.9 %copy-start.2 = (bf16[128,512]{1,0:T(8,128)(2,1)S(1)}, bf16[128,512]{1,0:T(8,128)(2,1)}, u32[]{:S(2)}) copy-start(bf16[128,512]{1,0:T(8,128)(2,1)} %saved_ref.1) | copy-start | bytes 393220
  11.8 8.3 %collective-permute-start.2 = (bf16[512,128]{1,0:T(8,128)(2,1)S(1)}, bf16[512,128]{1,0:T(8,128)(2,1)S(1)}, u32[]{:S(2)}, u32[]{:S(2)}) collective-permute-start(bf16[512,128]{1,0:T(8,128)(2,1)S(1)} %get-tuple-element.46), channel_id=1, source_target_pairs={{0,12},{4,8},{8,4},{12,0},{1,13},{5,9},{9,5},{13,1},{2,14},{6,10},... | collective-permute-start | bytes 393224 | tf_op jit(solution)/shard_map/ppermute | solution.py:621
  14.9 8.7 %collective-permute-start.3 = (bf16[512,128]{1,0:T(8,128)(2,1)S(1)}, bf16[512,128]{1,0:T(8,128)(2,1)S(1)}, u32[]{:S(2)}, u32[]{:S(2)}) collective-permute-start(bf16[512,128]{1,0:T(8,128)(2,1)S(1)} %get-tuple-element.51), channel_id=1, source_target_pairs={{0,4},{4,0},{8,12},{12,8},{1,5},{5,1},{9,13},{13,9},{2,6},{6,2},{1... | collective-permute-start | bytes 393224 | tf_op jit(solution)/shard_map/ppermute | solution.py:621
  14.9 10.3 %collective-permute-start.4 = (bf16[512,128]{1,0:T(8,128)(2,1)S(1)}, bf16[512,128]{1,0:T(8,128)(2,1)S(1)}, u32[]{:S(2)}, u32[]{:S(2)}) collective-permute-start(bf16[512,128]{1,0:T(8,128)(2,1)S(1)} %get-tuple-element.52), channel_id=1, source_target_pairs={{0,8},{4,12},{8,0},{12,4},{1,9},{5,13},{9,1},{13,5},{2,10},{6,14},... | collective-permute-start | bytes 393224 | tf_op jit(solution)/shard_map/ppermute | solution.py:621

commit v22 on v21

--- a/solution.py
+++ b/solution.py
@@ -386,7 +386,7 @@
     if outs:
         attend_first(
             count,
-            (1,),
+            (halo,),
             (query_ref, grad_ref, row_out, filled_out, spread_ref)
             + (*raised_refs, raised_out, *change_refs, change_out, *target_refs, target_out)
             + (*packets, None, *outs),
@@ -410,11 +410,11 @@
     def _():
         attend(count, halo, halo + 1, refs)
 
-    attend_first(count, range(2 if ready else 1, halo + 1), refs)
+    attend_first(count, range(1, halo + (not ready)), refs)
     if not ready:
         return
 
-    @pl.when(lax.axis_index("ctx") == 0)
+    @pl.when(lax.axis_index("ctx") == halo - 1)
     def _():
         for here, out in zip(ready, refs[-count:], strict=True):
             out[...] = here[...]

time: 26.3 us -> 25.1 us (0.954)
  waiting for transfers between devices: 9.79 us -> 8.6 us
    ppermute x3, waiting for transfers between devices: 8.51 us -> 6.78 us  [near_plan(): lax.ppermute(sent[k], 'ctx', [(i, i ^ k) for i in range(count)])]
    pallas_call x1, Pallas kernels: 0.88 us -> 0.34 us  [near_plan(): pl.pallas_call(functools.partial(step_kernel, count, halo, back), out_sha...]
    ppermute x2, waiting for transfers between devices: 1.28 us -> 1.82 us  [near_plan(): lax.ppermute(packet, 'ctx', [(i, (i + back) % count) for i in range(count)])]
    pallas_call x1, Pallas kernels: 0.03 us -> 0.54 us  [near_plan(): pl.pallas_call(functools.partial(attend_kernel, count, halo), out_shape=s...]
  transfers between devices with their start and end apart: 5 -> 5, of which waited for: 4 -> 3; matrix products, arithmetic and copies ran while one was open for 0% -> 0% of each run, Pallas kernels for 7% -> 5%
where the time goes in v22:
time: 25.1 us; the launch traced here: 24.9 us
  starting transfers between devices  10.1 us (40%)
  waiting for transfers between devices  8.6 us (34%)
  Pallas kernels  2.69 us (11%)
  local copies, waits for them, and re-layouts  1.82 us (7%)
  other arithmetic  0.96 us (4%)
  between operations  0.71 us (3%)
    ppermute x3, waiting for transfers between devices, near_plan(): lax.ppermute(sent[k], 'ctx', [(i, i ^ k) for i in range(count)])  6.78 us
    ppermute x2, starting transfers between devices, near_plan(): lax.ppermute(packet, 'ctx', [(i, (i + back) % count) for i in range(count)])  5.67 us
    ppermute x3, starting transfers between devices, near_plan(): lax.ppermute(sent[k], 'ctx', [(i, i ^ k) for i in range(count)])  4.45 us
    ppermute x2, waiting for transfers between devices, near_plan(): lax.ppermute(packet, 'ctx', [(i, (i + back) % count) for i in range(count)])  1.82 us
    unnamed x8, local copies, waits for them, and re-layouts  1.82 us
    select_n x1, other arithmetic, near_plan(): jnp.where(mark < 0, jnp.pad(jnp.concatenate([key_head_rows, value_head_ro...  0.94 us
    pallas_call x1, Pallas kernels, near_plan(): pl.pallas_call(functools.partial(place_kernel, count), out_shape=[jax.Sha...  0.94 us
    pallas_call x1, Pallas kernels, near_plan(): pl.pallas_call(functools.partial(attend_kernel, count, halo), out_shape=s...  0.54 us
  transfers between devices with their start and end apart: 5, of which 3 were waited for; matrix products, arithmetic and copies ran while one was open for 0% of the time, Pallas kernels for 5%

profile of v22, /device:TPU:0, one launch (start us, length us, event | category | flops | bytes accessed | tf_op | source)
XLA Modules:
  0.0 24.9 jit_solution(12298454487957306674)
XLA Ops:
  0.6 0.0 copy-start
  0.7 0.9 %fusion.2.packet_ref.refs_8_.refs_15_.refs_2_ = bf16[264,128]{1,0:T(8,128)(2,1)S(1)} fusion(bf16[128,128]{1,0:T(8,128)(2,1)} %param.11, bf16[128,128]{1,0:T(8,128)(2,1)} %param.10, s32[128]{0:T(128)} %param.8, s32[264]{0:T(512)S(1)} %iota_add_fusion, pred[264]{0:T(512)(128)(4,1)S(1)} %broadcast_compare_fusion), kind=kLoop, calls=%fused_computation.4 | loop fusion | flops 337920 | bytes 134952 | tf_op jit(solution)/shard_map/jit(_where)/select_n | solution.py:572
  1.6 0.0 copy-start.3
  1.6 3.1 %collective-permute-start = (bf16[264,128]{1,0:T(8,128)(2,1)S(1)}, bf16[264,128]{1,0:T(8,128)(2,1)S(1)}, u32[]{:S(2)}, u32[]{:S(2)}) collective-permute-start(bf16[264,128]{1,0:T(8,128)(2,1)S(1)} %fusion.2.packet_ref.refs_8_.refs_15_.refs_2_), channel_id=1, source_target_pairs={{0,4},{4,8},{8,12},{12,0},{1,5},{5,9},{9,13},{13,1},{2,6},{6,10},{... | collective-permute-start | bytes 202760 | tf_op jit(solution)/shard_map/ppermute | solution.py:578
  4.7 2.6 %collective-permute-start.1 = (bf16[264,128]{1,0:T(8,128)(2,1)S(1)}, bf16[264,128]{1,0:T(8,128)(2,1)S(1)}, u32[]{:S(2)}, u32[]{:S(2)}) collective-permute-start(bf16[264,128]{1,0:T(8,128)(2,1)S(1)} %fusion.2.packet_ref.refs_8_.refs_15_.refs_2_), channel_id=1, source_target_pairs={{0,8},{4,12},{8,0},{12,4},{1,9},{5,13},{9,1},{13,5},{2,10},{6,14},... | collective-permute-start | bytes 202760 | tf_op jit(solution)/shard_map/ppermute | solution.py:578
  7.3 0.0 copy-done
  7.3 0.0 copy-done.3
  7.3 0.0 copy-start.1
  7.3 0.9 %copy-done.1 = bf16[128,512]{1,0:T(8,128)(2,1)S(1)} copy-done((bf16[128,512]{1,0:T(8,128)(2,1)S(1)}, bf16[128,512]{1,0:T(8,128)(2,1)}, u32[]{:S(2)}) %copy-start.1) | copy-done | bytes 131096
  8.2 0.0 copy-start.2
  8.2 0.9 %copy-done.2 = bf16[128,512]{1,0:T(8,128)(2,1)S(1)} copy-done((bf16[128,512]{1,0:T(8,128)(2,1)S(1)}, bf16[128,512]{1,0:T(8,128)(2,1)}, u32[]{:S(2)}) %copy-start.2) | copy-done | bytes 131096
  9.1 0.5 %shard_map.94 = (bf16[512,128]{1,0:T(8,128)(2,1)S(1)}, bf16[512,128]{1,0:T(8,128)(2,1)S(1)}, f32[128,512]{1,0:T(8,128)S(1)}, f32[128,512]{1,0:T(8,128)S(1)}, f32...) custom-call(s32[1,16]{1,0:T(1,128)S(1)} %bitcast.1, ...), custom_call_target="tpu_custom_call" | custom-call | tf_op jit(solution)/shard_map/pallas_call | solution.py:585
  9.6 0.0 collective-permute-done.refs_9_.refs_16_.refs_3_
  9.6 0.3 %shard_map.95 = (f32[128,512]{1,0:T(8,128)S(1)}, f32[128,512]{1,0:T(8,128)S(1)}, f32[8,512]{1,0:T(8,128)S(1)}, bf16[512,128]{1,0:T(8,128)(2,1)S(1)}, f32[8,128]{...) custom-call(bf16[512,128]{1,0:T(8,128)(2,1)S(1)} %get-tuple-element., ...), custom_call_target="tpu_custom_call" | custom-call | tf_op jit(solution)/shard_map/pallas_call | solution.py:598
  9.9 1.8 %collective-permute-done.1.refs_17_.refs_4_ = bf16[264,128]{1,0:T(8,128)(2,1)S(1)} collective-permute-done((bf16[264,128]{1,0:T(8,128)(2,1)S(1)}, bf16[264,128]{1,0:T(8,128)(2,1)S(1)}, u32[]{:S(2)}, u32[]{:S(2)}) %collective-permute-start.1) | collective-permute-done | bytes 67616 | tf_op jit(solution)/shard_map/ppermute | solution.py:578
  11.8 0.5 %shard_map.96 = (bf16[512,128]{1,0:T(8,128)(2,1)S(1)}, bf16[512,128]{1,0:T(8,128)(2,1)S(1)}, bf16[512,128]{1,0:T(8,128)(2,1)S(1)}, bf16[512,128]{1,0:T(8,128)(2,1)S(1)}) custom-call(bf16[512,128]{1,0:T(8,128)(2,1)S(1)} %get-tuple-element.36.refs_0_, bf16[512,128]{1,0:T(8,128)(2,1)S(1)} %get-tuple-element.37.refs_1_, ...), custom_call_target="tpu_custom_call" | custom-call | tf_op jit(solution)/shard_map/pallas_call | solution.py:613
  12.3 2.6 %collective-permute-start.2 = (bf16[512,128]{1,0:T(8,128)(2,1)S(1)}, bf16[512,128]{1,0:T(8,128)(2,1)S(1)}, u32[]{:S(2)}, u32[]{:S(2)}) collective-permute-start(bf16[512,128]{1,0:T(8,128)(2,1)S(1)} %get-tuple-element.46), channel_id=1, source_target_pairs={{0,12},{4,8},{8,4},{12,0},{1,13},{5,9},{9,5},{13,1},{2,14},{6,10},... | collective-permute-start | bytes 393224 | tf_op jit(solution)/shard_map/ppermute | solution.py:621
  14.9 0.0 collective-permute-start.3
  14.9 1.9 %collective-permute-start.4 = (bf16[512,128]{1,0:T(8,128)(2,1)S(1)}, bf16[512,128]{1,0:T(8,128)(2,1)S(1)}, u32[]{:S(2)}, u32[]{:S(2)}) collective-permute-start(bf16[512,128]{1,0:T(8,128)(2,1)S(1)} %get-tuple-element.52), channel_id=1, source_target_pairs={{0,8},{4,12},{8,0},{12,4},{1,9},{5,13},{9,1},{13,5},{2,10},{6,14},... | collective-permute-start | bytes 393224 | tf_op jit(solution)/shard_map/ppermute | solution.py:621
  16.8 3.9 %collective-permute-done.2.refs_1_ = bf16[512,128]{1,0:T(8,128)(2,1)S(1)} collective-permute-done((bf16[512,128]{1,0:T(8,128)(2,1)S(1)}, bf16[512,128]{1,0:T(8,128)(2,1)S(1)}, u32[]{:S(2)}, u32[]{:S(2)}) %collective-permute-start.2) | collective-permute-done | bytes 131104 | tf_op jit(solution)/shard_map/ppermute | solution.py:621
  20.6 0.4 %shard_map.97 = (bf16[128,128]{1,0:T(8,128)(2,1)S(1)}, bf16[128,256]{1,0:T(8,128)(2,1)S(1)}, f32[128,512]{1,0:T(8,128)S(1)}, f32[128,256]{1,0:T(8,128)S(1)}) custom-call(bf16[512,128]{1,0:T(8,128)(2,1)S(1)} %get-tuple-element.45.refs_0_, bf16[512,128]{1,0:T(8,128)(2,1)S(1)} %collective-permute-done.2.refs_1_, ...), custom_call_target="tpu_custom_call" | custom-call | tf_op jit(solution)/shard_map/pallas_call | solution.py:625
  21.0 2.9 %collective-permute-done.3.refs_0_ = bf16[512,128]{1,0:T(8,128)(2,1)S(1)} collective-permute-done((bf16[512,128]{1,0:T(8,128)(2,1)S(1)}, bf16[512,128]{1,0:T(8,128)(2,1)S(1)}, u32[]{:S(2)}, u32[]{:S(2)}) %collective-permute-start.3) | collective-permute-done | bytes 131104 | tf_op jit(solution)/shard_map/ppermute | solution.py:621
  23.9 0.0 collective-permute-done.4.refs_1_
  23.9 0.9 %shard_map.98 = (f32[128,512]{1,0:T(8,128)}, f32[128,128]{1,0:T(8,128)}, f32[128,128]{1,0:T(8,128)}) custom-call(bf16[128,128]{1,0:T(8,128)(2,1)S(1)} %get-tuple-element.47.query_spread, bf16[128,256]{1,0:T(8,128)(2,1)S(1)} %get-tuple-element.48.key_spread, f32[128,512]{1,0:T(8,128)S(1)} %get-tuple-element.49.query_base, ...), custom_call_target="tpu_custom_call" | custom-call | tf_op jit(solution)/shard_map/pallas_call | solution.py:637
  (2 shorter events, 0.0 us)
Async XLA Ops:
  0.6 6.7 %copy-start = (bf16[128,512]{1,0:T(8,128)(2,1)S(1)}, bf16[128,512]{1,0:T(8,128)(2,1)}, u32[]{:S(2)}) copy-start(bf16[128,512]{1,0:T(8,128)(2,1)} %query_ref.1) | copy-start | bytes 393220
  1.6 5.7 %copy-start.3 = (s32[16]{0:T(128)S(1)}, s32[16]{0:T(128)}, u32[]{:S(2)}) copy-start(s32[16]{0:T(128)} %param.7) | copy-start | bytes 196
  1.6 8.0 %collective-permute-start = (bf16[264,128]{1,0:T(8,128)(2,1)S(1)}, bf16[264,128]{1,0:T(8,128)(2,1)S(1)}, u32[]{:S(2)}, u32[]{:S(2)}) collective-permute-start(bf16[264,128]{1,0:T(8,128)(2,1)S(1)} %fusion.2.packet_ref.refs_8_.refs_15_.refs_2_), channel_id=1, source_target_pairs={{0,4},{4,8},{8,12},{12,0},{1,5},{5,9},{9,13},{13,1},{2,6},{6,10},{... | collective-permute-start | bytes 202760 | tf_op jit(solution)/shard_map/ppermute | solution.py:578
  4.7 7.1 %collective-permute-start.1 = (bf16[264,128]{1,0:T(8,128)(2,1)S(1)}, bf16[264,128]{1,0:T(8,128)(2,1)S(1)}, u32[]{:S(2)}, u32[]{:S(2)}) collective-permute-start(bf16[264,128]{1,0:T(8,128)(2,1)S(1)} %fusion.2.packet_ref.refs_8_.refs_15_.refs_2_), channel_id=1, source_target_pairs={{0,8},{4,12},{8,0},{12,4},{1,9},{5,13},{9,1},{13,5},{2,10},{6,14},... | collective-permute-start | bytes 202760 | tf_op jit(solution)/shard_map/ppermute | solution.py:578
  7.3 0.9 %copy-start.1 = (bf16[128,512]{1,0:T(8,128)(2,1)S(1)}, bf16[128,512]{1,0:T(8,128)(2,1)}, u32[]{:S(2)}) copy-start(bf16[128,512]{1,0:T(8,128)(2,1)} %grad_ref.1) | copy-start | bytes 393220
  8.2 0.9 %copy-start.2 = (bf16[128,512]{1,0:T(8,128)(2,1)S(1)}, bf16[128,512]{1,0:T(8,128)(2,1)}, u32[]{:S(2)}) copy-start(bf16[128,512]{1,0:T(8,128)(2,1)} %saved_ref.1) | copy-start | bytes 393220
  12.3 8.3 %collective-permute-start.2 = (bf16[512,128]{1,0:T(8,128)(2,1)S(1)}, bf16[512,128]{1,0:T(8,128)(2,1)S(1)}, u32[]{:S(2)}, u32[]{:S(2)}) collective-permute-start(bf16[512,128]{1,0:T(8,128)(2,1)S(1)} %get-tuple-element.46), channel_id=1, source_target_pairs={{0,12},{4,8},{8,4},{12,0},{1,13},{5,9},{9,5},{13,1},{2,14},{6,10},... | collective-permute-start | bytes 393224 | tf_op jit(solution)/shard_map/ppermute | solution.py:621
  14.9 9.1 %collective-permute-start.3 = (bf16[512,128]{1,0:T(8,128)(2,1)S(1)}, bf16[512,128]{1,0:T(8,128)(2,1)S(1)}, u32[]{:S(2)}, u32[]{:S(2)}) collective-permute-start(bf16[512,128]{1,0:T(8,128)(2,1)S(1)} %get-tuple-element.51), channel_id=1, source_target_pairs={{0,4},{4,0},{8,12},{12,8},{1,5},{5,1},{9,13},{13,9},{2,6},{6,2},{1... | collective-permute-start | bytes 393224 | tf_op jit(solution)/shard_map/ppermute | solution.py:621
  14.9 9.1 %collective-permute-start.4 = (bf16[512,128]{1,0:T(8,128)(2,1)S(1)}, bf16[512,128]{1,0:T(8,128)(2,1)S(1)}, u32[]{:S(2)}, u32[]{:S(2)}) collective-permute-start(bf16[512,128]{1,0:T(8,128)(2,1)S(1)} %get-tuple-element.52), channel_id=1, source_target_pairs={{0,8},{4,12},{8,0},{12,4},{1,9},{5,13},{9,1},{13,5},{2,10},{6,14},... | collective-permute-start | bytes 393224 | tf_op jit(solution)/shard_map/ppermute | solution.py:621
